TPU v7x, 32 devices: a whole 2x2x4 slice. The times are simulated.
32 devices in a mesh: var: 4 (over z), samp: 8 (over y, x, core).
Axes of the slice: x: 2, y: 2, z: 4, core: 2. Of those that a mesh axis runs over, the one named last changes fastest.
Arguments:
- genotypes: int32 [3072, 24576], P('var', 'samp'), may hold values from 0 to 2, as said below
- called: int32 [3072, 24576], P('var', 'samp'), may hold values from 0 to 1
- dosage: int32 [24576, 1024], P(('samp', 'var')), may hold values from 0 to 200
- sample_order: int32 [32, 768], P(('samp', 'var')), may hold values from 0 to 767, each once within a row
- noise_ratio: float32 [16], replicated, may hold values from 0.5 to 4
- solution: float32 [24576, 16], P(('samp', 'var')), may hold values from -13 to 13
- residual: float32 [24576, 16], P(('samp', 'var')), may hold values from -13 to 13
- direction: float32 [24576, 16], P(('samp', 'var')), may hold values from -13 to 13
Outputs:
- solution_new: float32 [24576, 16], P(('samp', 'var'))
- residual_new: float32 [24576, 16], P(('samp', 'var'))
- direction_new: float32 [24576, 16], P(('samp', 'var'))
- scores: float32 [1024, 16], P(('var', 'samp'))
Inputs may be any that keep to these rules, and one draw needn't show every extreme that they name: `genotypes`: where called is 1, the count of one allele. `sample_order`: each row lists 0 to 767 once.
All inputs are finite; a program needn't handle non-finite values.
Results may differ from a plain program's by a relative error of at most 0.023.
Values may be sent and summed in bfloat16 or wider, within the bound.
No kernel may reach another device: no remote copies, remote signals or barrier semaphores. Data moves between devices by JAX's collectives and lax.ppermute only.
A program may use at most 128 MiB of HBM per device.

v0:
```python
import math

import jax
import jax.numpy as jnp
from jax import lax
from jax.sharding import PartitionSpec as P

VARIANTS = 3072


def standard_form(raw_proj, called_proj, allele_sum, called_count):
    frequency = (allele_sum + 1.0) / (2.0 * called_count + 2.0)
    spread = jnp.sqrt(2.0 * frequency * (1.0 - frequency))
    loading = (raw_proj - 2.0 * frequency[:, None] * called_proj) / spread[:, None]
    return (frequency, spread, loading)


def body(genotypes, called, dosage, sample_order, noise_ratio, solution, residual, direction):
    coded = genotypes * called
    coded_b = coded.astype(jnp.bfloat16)
    called_b = called.astype(jnp.bfloat16)
    allele_sum = jnp.sum(coded, axis=1).astype(jnp.float32)
    called_count = jnp.sum(called, axis=1).astype(jnp.float32)
    quarter = direction.shape[0]
    samples = quarter * lax.axis_size("samp") * lax.axis_size("var")
    dosage_b = dosage.astype(jnp.bfloat16)
    dosage_sum = jnp.sum(dosage, axis=0).astype(jnp.float32)
    order_row = sample_order[0]
    direction_b = direction.astype(jnp.bfloat16)
    piece = lax.all_gather(direction_b, "var", axis=0, tiled=True)
    coded_cols = coded_b
    called_cols = called_b
    raw_proj = jnp.dot(coded_cols, piece, preferred_element_type=jnp.float32)
    called_proj = jnp.dot(called_cols, piece, preferred_element_type=jnp.float32)
    raw_proj, called_proj, allele_sum, called_count = (
        lax.psum(raw_proj.astype(jnp.bfloat16), "samp").astype(jnp.float32),
        lax.psum(called_proj.astype(jnp.bfloat16), "samp").astype(jnp.float32),
        lax.psum(allele_sum.astype(jnp.bfloat16), "samp").astype(jnp.float32),
        lax.psum(called_count.astype(jnp.bfloat16), "samp").astype(jnp.float32),
    )
    frequency, spread, loading = standard_form(raw_proj, called_proj, allele_sum, called_count)
    scaled_a = (loading / spread[:, None]).astype(jnp.bfloat16)
    scaled_b = (2.0 * frequency[:, None] * loading / spread[:, None]).astype(jnp.bfloat16)
    coded_cols = coded_b
    called_cols = called_b
    term = jnp.einsum("vs,vc->sc", coded_cols, scaled_a, preferred_element_type=jnp.float32)
    term = term - jnp.einsum("vs,vc->sc", called_cols, scaled_b, preferred_element_type=jnp.float32)
    back = lax.psum_scatter(
        (term / VARIANTS).astype(jnp.bfloat16), "var", scatter_dimension=0, tiled=True
    ).astype(jnp.float32)
    applied = noise_ratio[None, :] * direction + back
    res_norm, curvature = lax.psum(
        (jnp.sum(residual * residual, axis=0), jnp.sum(direction * applied, axis=0)),
        ("var", "samp"),
    )
    step_size = res_norm / (curvature + 1e-06)
    solution_new = solution + step_size[None, :] * direction
    residual_new = residual - step_size[None, :] * applied
    res_square = jnp.sum(residual_new * residual_new, axis=0)
    res_new_norm, sol_sum, sol_square = lax.psum(
        (res_square, jnp.sum(solution_new, axis=0), jnp.sum(solution_new * solution_new, axis=0)),
        ("var", "samp"),
    )
    picked = jnp.take(solution_new, order_row, axis=0).astype(jnp.bfloat16)
    cross_local = jnp.einsum("ij,ic->jc", dosage_b, picked, preferred_element_type=jnp.float32)
    cross_sum, dosage_sum = (
        lax.psum_scatter(cross_local, ("var", "samp"), scatter_dimension=0, tiled=True),
        lax.psum_scatter(dosage_sum, ("var", "samp"), scatter_dimension=0, tiled=True),
    )
    direction_new = residual_new + (res_new_norm / (res_norm + 1e-06))[None, :] * direction
    dose_freq = (dosage_sum / 100.0 + 1.0) / (2.0 * samples + 2.0)
    dose_spread = jnp.sqrt(2.0 * dose_freq * (1.0 - dose_freq))
    scale_norm = math.sqrt(samples) * jnp.sqrt(sol_square / samples + 1e-06)
    scores = (cross_sum / 100.0 - 2.0 * dose_freq[:, None] * sol_sum[None, :]) / (
        dose_spread[:, None] * scale_norm[None, :]
    )
    return (solution_new, residual_new, direction_new, scores)


def solution(mesh):
    placed = (
        P("var", "samp"),
        P("var", "samp"),
        P(("samp", "var"), None),
        P(("samp", "var"), None),
        P(),
        P(("samp", "var"), None),
        P(("samp", "var"), None),
        P(("samp", "var"), None),
    )
    return jax.shard_map(
        body,
        mesh=mesh,
        in_specs=placed,
        out_specs=(
            P(("samp", "var"), None),
            P(("samp", "var"), None),
            P(("samp", "var"), None),
            P(("var", "samp"), None),
        ),
        check_vma=False,
    )
```

profile of v0, /device:TPU:0, one launch (start us, length us, event | category | flops | bytes accessed | tf_op | source)
XLA Modules:
  0.0 276.4 jit_solution(308824428564435516)
XLA Ops:
  7.2 0.0 reduce-scatter.5.cloned.1.call-start
  7.2 0.8 convert_element_type.61
  8.0 15.0 %all_gather.3 = bf16[3072,16]{0,1:T(8,128)(2,1)S(1)} all-gather(bf16[768,16]{0,1:T(8,128)(2,1)S(1)} %convert_element_type.61), channel_id=1, replica_groups=mesh['var'=4,'samp'=8] {'var'}, dimensions={0}, use_global_device_ids=true | all-gather | bytes 122880 | tf_op jit(solution)/shard_map/all_gather | solution.py:30
  23.0 10.1 %multiply_reduce_fusion = (s32[768]{0:T(1024)S(1)}, s32[768]{0:T(1024)S(1)}, bf16[768,3072]{1,0:T(8,128)(2,1)}) fusion(s32[768,3072]{1,0:T(8,128)} %param.8, s32[768,3072]{1,0:T(8,128)} %param.9), kind=kLoop, calls=%fused_computation.1 | loop fusion | flops 9435648 | bytes 23599104 | tf_op jit(solution)/shard_map/reduce_sum | solution.py:22
  33.1 5.1 %fusion.10 = bf16[768,16]{0,1:T(8,128)(2,1)S(1)} fusion(bf16[3072,16]{0,1:T(8,128)(2,1)S(1)} %all_gather.3, s32[768,3072]{1,0:T(8,128)} %param.9), kind=kOutput, calls=%fused_computation.13 | convolution fusion | flops 77869056 | bytes 9560064 | tf_op jit(solution)/shard_map/dot_general | solution.py:34
  38.3 1.3 convolution_convert_fusion
  39.6 22.8 %all-reduce.3 = (bf16[768,16]{0,1:T(8,128)(2,1)S(1)}, bf16[768,16]{0,1:T(8,128)(2,1)S(1)}, bf16[768]{0:T(1024)(128)(2,1)S(1)}, bf16[768]{0:T(1024)(128)(2,1)S(1)}) all-reduce(bf16[768,16]{0,1:T(8,128)(2,1)S(1)} %fusion.10, bf16[768,16]{0,1:T(8,128)(2,1)S(1)} %convolution_convert_fusion, ...), channel_id=1, replica_groups=mesh['var'=4,'samp'=8] {'samp'}, use_global_device_ids=true, to_apply=%region_7.0 | all-reduce | flops 26112 | bytes 104448 | tf_op jit(solution)/shard_map/psum | solution.py:37
  62.5 4.6 %convolution_bitcast_fusion = f32[3072,16]{0,1:T(8,128)S(1)} fusion(s32[768,3072]{1,0:T(8,128)} %param.9, bf16[768,16]{0,1:T(8,128)(2,1)S(1)} %get-tuple-element.14, bf16[768,16]{0,1:T(8,128)(2,1)S(1)} %get-tuple-element.15, f32[768]{0:T(1024)S(1)} %get-tuple-element.28, f32[768]{0:T(1024)S(1)} %get-tuple-element.29), kind=kOutput, calls=%fused_computation.5 | convolution fusion | flops 77955072 | bytes 9689088 | tf_op jit(solution)/shard_map/vs,vc->sc/dot_general | solution.py:47
  67.1 0.0 copy-start.5
  67.1 0.3 slice-done.1
  67.4 1.4 fusion.1
  68.7 0.0 reduce-scatter.5.cloned.1.call-update
  68.7 0.0 reduce-scatter.7.cloned.1.call-start
  68.8 0.1 multiply_reduce_fusion.4
  69.0 2.3 reduce_sum.77
  71.3 16.9 %reduce-scatter.5.cloned.1.call-done = bf16[768,16]{0,1:T(8,128)(2,1)} async-done(((bf16[3072,16]{0,1:T(8,128)(2,1)}), bf16[768,16]{0,1:T(8,128)(2,1)}) %reduce-scatter.5.cloned.1.call-update) | async-done | bytes 24592 | tf_op jit(solution)/shard_map/reduce_scatter | solution.py:48
  88.2 0.9 multiply_reduce_fusion.3
  89.1 38.5 %all-reduce.2 = (f32[16]{0:T(128)S(1)}, f32[16]{0:T(128)S(1)}) all-reduce(f32[16]{0:T(128)S(1)} %multiply_reduce_fusion.4, f32[16]{0:T(128)S(1)} %multiply_reduce_fusion.3), channel_id=1, replica_groups=mesh['var'=4,'samp'=8] {'var','samp'}, use_global_device_ids=true, to_apply=%region_1.0 | all-reduce | flops 32 | bytes 256 | tf_op jit(solution)/shard_map/psum | solution.py:52
  127.6 2.1 multiply_reduce_fusion.2
  129.7 0.6 copy-done.4
  130.3 0.2 copy.14
  130.5 1.9 gather_fusion
  132.4 0.5 fusion.7
  132.8 1.0 copy.15
  133.9 0.0 reduce-scatter.7.cloned.1.call-update
  133.9 41.2 %all-reduce.1 = (f32[16]{0:T(128)S(1)}, f32[16]{0:T(128)S(1)}, f32[1024]{0:T(1024)S(1)}, f32[16]{0:T(128)S(1)}) all-reduce(f32[16]{0:T(128)S(1)} %get-tuple-element.19, f32[16]{0:T(128)} %get-tuple-element.22, f32[1024]{0:T(1024)S(1)} %convert_element_type.79, f32[16]{0:T(128)} %get-tuple-element.23), channel_id=1, replica_groups=mesh['var'=4,'samp'=8] {'var','samp'}, use_global_device_ids=true, to_apply=%region_12.0 | all-reduce | flops 1072 | bytes 8576 | tf_op jit(solution)/shard_map/psum | solution.py:60
  175.1 0.6 add_divide_fusion.1
  175.7 1.5 multiply_add_fusion
  177.2 0.1 broadcast_multiply_fusion.1
  177.3 90.7 %reduce-scatter.7.cloned.1.call-done = f32[32,16]{1,0:T(8,128)} async-done(((f32[1024,16]{1,0:T(8,128)}), f32[32,16]{1,0:T(8,128)}) %reduce-scatter.7.cloned.1.call-update) | async-done | bytes 2064
  268.1 0.8 copy.16
  268.8 0.7 multiply_divide_fusion
  (29 shorter events, 0.1 us)
Async XLA Ops:
  7.2 81.0 %reduce-scatter.5.cloned.1.call-start = ((), (), s32[]{:S(2)}) async-start(), calls=%async_computation.2 | async-start | bytes 122880 | tf_op jit(solution)/shard_map/reduce_scatter | solution.py:48
  33.1 5.2 %copy-start = (bf16[768,3072]{1,0:T(8,128)(2,1)S(1)}, bf16[768,3072]{1,0:T(8,128)(2,1)}, u32[]{:S(2)}) copy-start(bf16[768,3072]{1,0:T(8,128)(2,1)} %get-tuple-element.21) | copy-start | bytes 14155780
  38.3 28.8 %slice-start = ((s8[4718592]{0:T(1024)(128)(4,1)}), s8[524288]{0:T(1024)(128)(4,1)S(1)}, s32[]{:S(2)}) async-start(s8[4718592]{0:T(1024)(128)(4,1)} %bitcast.11), calls=%async_computation.4 | async-start | bytes 1048576
  62.5 4.9 %slice-start.1 = ((s8[4718592]{0:T(1024)(128)(4,1)}), s8[4194304]{0:T(1024)(128)(4,1)S(1)}, s32[]{:S(2)}) async-start(s8[4718592]{0:T(1024)(128)(4,1)} %bitcast.11), calls=%async_computation.5 | async-start | bytes 8388608
  67.0 1.8 copy-start.3
  67.0 1.9 copy-start.6
  67.0 21.1 %copy-start.2 = (f32[768,16]{0,1:T(8,128)S(1)}, f32[768,16]{0,1:T(8,128)}, u32[]{:S(2)}) copy-start(f32[768,16]{0,1:T(8,128)} %param.15) | copy-start | bytes 147460
  67.1 21.1 %copy-start.7 = (f32[16]{0:T(128)S(1)}, f32[16]{0:T(128)}, u32[]{:S(2)}) copy-start(f32[16]{0:T(128)} %param.12) | copy-start | bytes 196
  67.1 60.5 %copy-start.5 = (f32[768,16]{0,1:T(8,128)S(1)}, f32[768,16]{0,1:T(8,128)}, u32[]{:S(2)}) copy-start(f32[768,16]{0,1:T(8,128)} %param.13) | copy-start | bytes 147460
  68.7 63.6 %copy-start.1 = (s32[768,1024]{1,0:T(8,128)S(1)}, s32[768,1024]{1,0:T(8,128)}, u32[]{:S(2)}) copy-start(s32[768,1024]{1,0:T(8,128)} %param.10) | copy-start | bytes 9437188
  68.7 199.3 %reduce-scatter.7.cloned.1.call-start = ((), (), s32[]{:S(2)}) async-start(), calls=%async_computation.3 | async-start | bytes 540672
  127.6 2.1 copy-start.8
  129.7 0.6 copy-start.4
Sparse Core Ops, SparseCore 0:
  68.9 19.2 reduce-scatter.4
  134.0 134.0 reduce-scatter.6
where the time goes:
time: 277 us; the launch traced here: 276 us
  blocking collectives  118 us (43%)
  waiting for transfers between devices  108 us (39%)
  other arithmetic  19.2 us (7%)
  between operations  14.2 us (5%)
  matrix products  12.9 us (5%)
  local copies, waits for them, and re-layouts  4.75 us (2%)
    unnamed x3, waiting for transfers between devices  90.8 us
    psum x1, blocking collectives, body(): lax.psum((res_square, jnp.sum(solution_new, axis=0), jnp.sum(solution_new...  41.2 us
    psum x1, blocking collectives, body(): lax.psum((jnp.sum(residual * residual, axis=0), jnp.sum(direction * appli...  38.5 us
    psum x1, blocking collectives, body(): lax.psum(called_proj.astype(jnp.bfloat16), 'samp').astype(jnp.float32)  22.8 us
    reduce_scatter x1, waiting for transfers between devices, body(): lax.psum_scatter((term / VARIANTS).astype(jnp.bfloat16), 'var', scatter_d...  16.9 us
    all_gather x1, blocking collectives, body(): piece = lax.all_gather(direction_b, 'var', axis=0, tiled=True)  15 us
    reduce_sum x1, other arithmetic, body(): allele_sum = jnp.sum(coded, axis=1).astype(jnp.float32)  10.1 us
  transfers between devices with their start and end apart: 2, of which 2 were waited for; matrix products, arithmetic and copies ran while one was open for 2% of the time, Pallas kernels for 0%

commit v1 on v0

v1 whole, which is shorter than its diff:
```python
import math

import jax
import jax.numpy as jnp
from jax import lax
from jax.sharding import PartitionSpec as P

BF16 = jnp.bfloat16
F32 = jnp.float32


def swap(values, axis, distance):
    size = lax.axis_size(axis)
    return lax.ppermute(values, axis, [(i, i ^ distance) for i in range(size)])


def sum_over(values, axis, stages):
    for distances in stages:
        total = values
        for arrived in [swap(values, axis, distance) for distance in distances]:
            total = total + arrived
        values = total
    return values


def stages_of(size, radices):
    stages = []
    step = 1
    while step < size:
        radix = min(radices[min(len(stages), len(radices) - 1)], size // step)
        stages.append([step * k for k in range(1, radix)])
        step *= radix
    return stages


def split2(values):
    high = lax.reduce_precision(values, 8, 7)
    return high.astype(BF16), (values - high).astype(BF16)


def body(genotypes, called, dosage, sample_order, noise_ratio, solution, residual, direction):
    var = lax.axis_index("var")
    samp = lax.axis_index("samp")
    n_var = lax.axis_size("var")
    n_samp = lax.axis_size("samp")
    own, rhs = direction.shape
    variants = genotypes.shape[0] * n_var
    samples = own * n_samp * n_var
    imputed = dosage.shape[1]
    var_all = list(range(1, n_var))
    samp_stages = stages_of(n_samp, [2, 4])

    direction_t = direction.T
    residual_t = residual.T
    solution_t = solution.T

    direction_b = direction_t.astype(BF16)
    pieces = jnp.stack([direction_b] + [swap(direction_b, "var", k) for k in var_all])
    piece = jnp.concatenate(
        [lax.dynamic_index_in_dim(pieces, p ^ var, keepdims=False) for p in range(n_var)], axis=1
    )

    coded = genotypes * called
    coded_b = coded.astype(BF16)
    called_b = called.astype(BF16)
    allele_part = jnp.sum(coded, axis=1).astype(F32)
    called_part = jnp.sum(called, axis=1).astype(F32)

    order_row = sample_order[0]
    both = jnp.concatenate([solution_t, direction_t], axis=0)
    picked = jnp.take(both, order_row, axis=1)
    picked_high, picked_low = split2(picked)
    dosage_b = dosage.astype(BF16)
    stack = jnp.concatenate([picked_high, picked_low, jnp.ones((16, own), BF16)], axis=0)
    cross = jnp.dot(stack, dosage_b, preferred_element_type=F32)
    cross = jnp.concatenate([cross[: 2 * rhs] + cross[2 * rhs : 4 * rhs], cross[4 * rhs : 4 * rhs + 8]])

    sums = jnp.concatenate(
        [
            jnp.sum(residual_t * residual_t, axis=1),
            jnp.sum(direction_t * direction_t, axis=1),
            jnp.sum(solution_t, axis=1),
            jnp.sum(solution_t * solution_t, axis=1),
            jnp.sum(solution_t * direction_t, axis=1),
            jnp.sum(direction_t, axis=1),
        ]
    )
    rows = genotypes.shape[0]
    extra = jnp.zeros((6, rows), F32).at[0, : 6 * rhs].set(sums)

    nt = (((1,), (1,)), ((), ()))
    raw_part = lax.dot_general(piece, coded_b, nt, preferred_element_type=F32)
    called_proj_part = lax.dot_general(piece, called_b, nt, preferred_element_type=F32)
    message = jnp.concatenate([raw_part, called_proj_part, allele_part[None], called_part[None], extra])
    total = sum_over(message, "samp", samp_stages)
    raw_proj = total[:rhs]
    called_proj = total[rhs : 2 * rhs]
    allele_sum = total[2 * rhs]
    called_count = total[2 * rhs + 1]
    sums = total[2 * rhs + 2, : 6 * rhs]

    frequency = (allele_sum + 1.0) / (2.0 * called_count + 2.0)
    spread = jnp.sqrt(2.0 * frequency * (1.0 - frequency))
    loading = (raw_proj - 2.0 * frequency * called_proj) / spread
    scaled = loading / spread
    scaled_a = scaled.astype(BF16)
    scaled_b = (2.0 * frequency * scaled).astype(BF16)

    small = jnp.concatenate([sums, jnp.sum(loading * loading, axis=1)])
    small = sum_over(small, "var", [var_all])

    term = jnp.dot(scaled_a, coded_b, preferred_element_type=F32)
    term = term - jnp.dot(scaled_b, called_b, preferred_element_type=F32)
    term = (term / variants).astype(BF16)
    term = term.reshape(rhs, n_var, own)
    take = lambda p: lax.dynamic_index_in_dim(term, p, axis=1, keepdims=False)
    back = take(var).astype(F32)
    for arrived in [swap(take(var ^ k), "var", k) for k in var_all]:
        back = back + arrived.astype(F32)

    res_norm, dir_norm, sol_one, sol_two, sol_dir, dir_one, load_square = small.reshape(7, rhs)
    applied = noise_ratio[:, None] * direction_t + back
    curvature = noise_ratio * dir_norm + load_square / variants
    step_size = res_norm / (curvature + 1e-06)
    solution_new = solution_t + step_size[:, None] * direction_t
    residual_new = residual_t - step_size[:, None] * applied
    res_new_norm = jnp.sum(residual_new * residual_new, axis=1)
    res_new_norm = sum_over(res_new_norm, "samp", [list(range(1, n_samp))] if n_samp <= 8 else samp_stages)
    res_new_norm = sum_over(res_new_norm, "var", [var_all])
    direction_new = residual_new + (res_new_norm / (res_norm + 1e-06))[:, None] * direction_t

    wide = imputed // n_var
    cross = cross.reshape(cross.shape[0], n_var, wide)
    take_cross = lambda p: lax.dynamic_index_in_dim(cross, p, axis=1, keepdims=False)
    mine = take_cross(var)
    for arrived in [swap(take_cross(var ^ k), "var", k) for k in var_all]:
        mine = mine + arrived
    mine = sum_over(mine, "samp", samp_stages)
    narrow = wide // n_samp
    mine = lax.dynamic_slice_in_dim(mine, samp * narrow, narrow, axis=1)
    cross_sum = mine[:rhs] + step_size[:, None] * mine[rhs : 2 * rhs]
    dosage_sum = mine[2 * rhs]
    sol_sum = sol_one + step_size * dir_one
    sol_square = sol_two + 2.0 * step_size * sol_dir + step_size * (step_size * dir_norm)
    dose_freq = (dosage_sum / 100.0 + 1.0) / (2.0 * samples + 2.0)
    dose_spread = jnp.sqrt(2.0 * dose_freq * (1.0 - dose_freq))
    scale_norm = math.sqrt(samples) * jnp.sqrt(sol_square / samples + 1e-06)
    scores = (cross_sum / 100.0 - 2.0 * dose_freq[None, :] * sol_sum[:, None]) / (
        dose_spread[None, :] * scale_norm[:, None]
    )
    return (solution_new.T, residual_new.T, direction_new.T, scores.T)


def solution(mesh):
    placed = (
        P("var", "samp"),
        P("var", "samp"),
        P(("samp", "var"), None),
        P(("samp", "var"), None),
        P(),
        P(("samp", "var"), None),
        P(("samp", "var"), None),
        P(("samp", "var"), None),
    )
    return jax.shard_map(
        body,
        mesh=mesh,
        in_specs=placed,
        out_specs=(
            P(("samp", "var"), None),
            P(("samp", "var"), None),
            P(("samp", "var"), None),
            P(("var", "samp"), None),
        ),
        check_vma=False,
    )
```

time: 277 us -> 89.8 us (0.32)
  blocking collectives: 118 us -> 0 us
  waiting for transfers between devices: 108 us -> 15.4 us
  starting transfers between devices: 0.08 us -> 37.2 us
  between operations: 14.2 us -> 1.03 us
  matrix products: 12.9 us -> 16.3 us
    psum x3 -> x0, blocking collectives: 103 us -> none  [the longest x1 41.2 us: body(): lax.psum((res_square, jnp.sum(solution_new, axis=0), jnp.sum(solution_new...]
    unnamed x3 -> x0, waiting for transfers between devices: 90.8 us -> none
    ppermute x0 -> x30, starting transfers between devices: none -> 37.2 us  [swap(): return lax.ppermute(values, axis, [(i, i ^ distance) for i in range(size)])]
    reduce_scatter x1 -> x0, waiting for transfers between devices: 16.9 us -> none  [body(): lax.psum_scatter((term / VARIANTS).astype(jnp.bfloat16), 'var', scatter_d...]
    ppermute x0 -> x30, waiting for transfers between devices: none -> 15.4 us  [swap(): return lax.ppermute(values, axis, [(i, i ^ distance) for i in range(size)])]
    all_gather x1 -> x0, blocking collectives: 15 us -> none  [body(): piece = lax.all_gather(direction_b, 'var', axis=0, tiled=True)]
    reduce_sum x5 -> x7, other arithmetic: 15.5 us -> 11.9 us  [the longest x1 10.2 us: body(): called_part = jnp.sum(called, axis=1).astype(F32)]
    dot_general x5, matrix products: 12.9 us -> 16.3 us  [the longest x1 5.15 us: body(): lax.dot_general(piece, called_b, nt, preferred_element_type=F32)]
  transfers between devices with their start and end apart: 2 -> 30, of which waited for: 2 -> 13; matrix products, arithmetic and copies ran while one was open for 2% -> 37% of each run, Pallas kernels for 0% -> 0%
where the time goes in v1:
time: 89.8 us; the launch traced here: 89.4 us
  starting transfers between devices  37.2 us (41%)
  other arithmetic  16.8 us (19%)
  matrix products  16.3 us (18%)
  waiting for transfers between devices  15.4 us (17%)
  local copies, waits for them, and re-layouts  2.68 us (3%)
  between operations  1.03 us (1%)
    ppermute x30, starting transfers between devices, swap(): return lax.ppermute(values, axis, [(i, i ^ distance) for i in range(size)])  37.2 us
    ppermute x30, waiting for transfers between devices, swap(): return lax.ppermute(values, axis, [(i, i ^ distance) for i in range(size)])  15.4 us
    reduce_sum x1, other arithmetic, body(): called_part = jnp.sum(called, axis=1).astype(F32)  10.2 us
    dot_general x1, matrix products, body(): lax.dot_general(piece, called_b, nt, preferred_element_type=F32)  5.15 us
    dot_general x1, matrix products, body(): term = term - jnp.dot(scaled_b, called_b, preferred_element_type=F32)  4.44 us
    dot_general x1, matrix products, body(): term = jnp.dot(scaled_a, coded_b, preferred_element_type=F32)  3.06 us
    dot_general x1, matrix products, body(): cross = jnp.dot(stack, dosage_b, preferred_element_type=F32)  2.32 us
  transfers between devices with their start and end apart: 30, of which 13 were waited for; matrix products, arithmetic and copies ran while one was open for 37% of the time, Pallas kernels for 0%

profile of v1, /device:TPU:0, one launch (start us, length us, event | category | flops | bytes accessed | tf_op | source)
XLA Modules:
  0.0 89.4 jit_solution(3755269375883623713)
XLA Ops:
  0.7 1.0 %fusion.42 = (f32[16]{0:T(128)S(1)}, bf16[16,768]{1,0:T(8,128)(2,1)S(1)}) fusion(f32[768,16]{0,1:T(8,128)} %param.17), kind=kLoop, calls=%fused_computation.109 | loop fusion | flops 24560 | bytes 73792 | tf_op jit(solution)/shard_map/reduce_sum | solution.py:85
  1.6 5.1 %collective-permute-start.2 = (bf16[16,768]{1,0:T(8,128)(2,1)S(1)}, bf16[16,768]{1,0:T(8,128)(2,1)S(1)}, u32[]{:S(2)}, u32[]{:S(2)}) collective-permute-start(bf16[16,768]{1,0:T(8,128)(2,1)S(1)} %get-tuple-element.53), channel_id=1, source_target_pairs={{0,24},{8,16},{16,8},{24,0},{1,25},{9,17},{17,9},{25,1},{2,26},{10... | collective-permute-start | bytes 73736 | tf_op jit(solution)/shard_map/ppermute | solution.py:14
  8.8 0.8 pad_maximum_fusion.3
  9.8 1.6 %gather_fusion = f32[768,32]{1,0:T(8,128)S(1)} fusion(f32[32,768]{0,1:T(8,128)S(1)} %copy.41, s32[1024]{0:T(1024)S(1)} %pad_clamp_fusion), kind=kCustom, calls=%fused_computation | custom fusion | bytes 199680 | tf_op jit(solution)/shard_map/jit(_take)/gather | solution.py:71
  11.6 2.3 %fusion.5 = f32[80,1024]{1,0:T(8,128)S(1)} fusion(s32[768,1024]{1,0:T(8,128)} %param.12, bf16[32,768]{1,0:T(8,128)(2,1)S(1)} %get-tuple-element.43, bf16[32,768]{1,0:T(8,128)(2,1)S(1)} %get-tuple-element.42, bf16[80]{0:T(256)(128)(2,1)S(1)} %pad.9.clone), kind=kOutput, calls=%fused_computation.9 | convolution fusion | flops 126984192 | bytes 3571872 | tf_op jit(solution)/shard_map/dot_general | solution.py:75
  14.3 3.8 %collective-permute-start.25 = (f32[40,256]{1,0:T(8,128)S(1)}, f32[40,256]{1,0:T(8,128)S(1)}, u32[]{:S(2)}, u32[]{:S(2)}) collective-permute-start(f32[40,256]{1,0:T(8,128)S(1)} %bitcast.83), channel_id=1, source_target_pairs={{0,24},{8,16},{16,8},{24,0},{1,25},{9,17},{17,9},{25,1},{2,26},{10... | collective-permute-start | bytes 122888 | tf_op jit(solution)/shard_map/ppermute | solution.py:14
  18.3 10.2 %fusion.39 = (s32[768]{0:T(1024)S(1)}, s32[768]{0:T(1024)S(1)}, bf16[768,3072]{1,0:T(8,128)(2,1)}) fusion(s32[768,3072]{1,0:T(8,128)} %param.11, s32[768,3072]{1,0:T(8,128)} %param.10), kind=kLoop, calls=%fused_computation.108 | loop fusion | flops 9435648 | bytes 23599104 | tf_op jit(solution)/shard_map/reduce_sum | solution.py:67
  29.7 3.3 %collective-permute-done.23 = f32[40,256]{1,0:T(8,128)S(1)} collective-permute-done((f32[40,256]{1,0:T(8,128)S(1)}, f32[40,256]{1,0:T(8,128)S(1)}, u32[]{:S(2)}, u32[]{:S(2)}) %collective-permute-start.23) | collective-permute-done | bytes 40992 | tf_op jit(solution)/shard_map/ppermute | solution.py:14
  33.1 5.2 %fusion.3 = f32[16,768]{1,0:T(8,128)S(1)} fusion(s32[768,3072]{1,0:T(8,128)} %param.11, bf16[16,768]{1,0:T(8,128)(2,1)S(1)} %get-tuple-element.49, bf16[16,768]{1,0:T(8,128)(2,1)S(1)} %get-tuple-element.50, bf16[16,768]{1,0:T(8,128)(2,1)S(1)} %get-tuple-element.51, bf16[16,768]{1,0:T(8,128)(2,1)S(1)} %get-tuple-element.48), kind=kOutput, calls=%fused_computation.7 | convolution fusion | flops 78249984 | bytes 9584640 | tf_op jit(solution)/shard_map/dot_general | solution.py:93
  38.3 2.5 %collective-permute-start.29 = (f32[40,256]{1,0:T(8,128)S(1)}, f32[40,256]{1,0:T(8,128)S(1)}, u32[]{:S(2)}, u32[]{:S(2)}) collective-permute-start(f32[40,256]{1,0:T(8,128)S(1)} %add.224), channel_id=1, source_target_pairs={{0,6},{1,7},{2,4},{3,5},{4,2},{5,3},{6,0},{7,1},{8,14},{9,15},{10,... | collective-permute-start | bytes 122888 | tf_op jit(solution)/shard_map/ppermute | solution.py:14
  41.9 1.3 %fusion.25 = f32[16,768]{1,0:T(8,128)S(1)} fusion(bf16[768,3072]{1,0:T(8,128)(2,1)S(1)} %bitcast.78, bf16[16,768]{1,0:T(8,128)(2,1)S(1)} %get-tuple-element.49, bf16[16,768]{1,0:T(8,128)(2,1)S(1)} %get-tuple-element.50, bf16[16,768]{1,0:T(8,128)(2,1)S(1)} %get-tuple-element.51, bf16[16,768]{1,0:T(8,128)(2,1)S(1)} %get-tuple-element.48), kind=kOutput, calls=%fused_computation.65 | convolution fusion | flops 75890688 | bytes 4866048 | tf_op jit(solution)/shard_map/dot_general | solution.py:92
  43.3 1.5 %collective-permute-done.28 = f32[40,256]{1,0:T(8,128)S(1)} collective-permute-done((f32[40,256]{1,0:T(8,128)S(1)}, f32[40,256]{1,0:T(8,128)S(1)}, u32[]{:S(2)}, u32[]{:S(2)}) %collective-permute-start.28) | collective-permute-done | bytes 40992 | tf_op jit(solution)/shard_map/ppermute | solution.py:14
  45.4 1.7 %collective-permute-start.6 = (f32[40,768]{1,0:T(8,128)S(1)}, f32[40,768]{1,0:T(8,128)S(1)}, u32[]{:S(2)}, u32[]{:S(2)}) collective-permute-start(f32[40,768]{1,0:T(8,128)S(1)} %add.188), channel_id=1, source_target_pairs={{0,6},{1,7},{2,4},{3,5},{4,2},{5,3},{6,0},{7,1},{8,14},{9,15},{10,... | collective-permute-start | bytes 368648 | tf_op jit(solution)/shard_map/ppermute | solution.py:14
  47.7 1.3 %collective-permute-start.4 = (f32[40,768]{1,0:T(8,128)S(1)}, f32[40,768]{1,0:T(8,128)S(1)}, u32[]{:S(2)}, u32[]{:S(2)}) collective-permute-start(f32[40,768]{1,0:T(8,128)S(1)} %add.188), channel_id=1, source_target_pairs={{0,2},{1,3},{2,0},{3,1},{4,6},{5,7},{6,4},{7,5},{8,10},{9,11},{10,... | collective-permute-start | bytes 368648 | tf_op jit(solution)/shard_map/ppermute | solution.py:14
  49.0 2.8 %collective-permute-done.6 = f32[40,768]{1,0:T(8,128)S(1)} collective-permute-done((f32[40,768]{1,0:T(8,128)S(1)}, f32[40,768]{1,0:T(8,128)S(1)}, u32[]{:S(2)}, u32[]{:S(2)}) %collective-permute-start.6) | collective-permute-done | bytes 122912 | tf_op jit(solution)/shard_map/ppermute | solution.py:14
  51.8 1.8 %collective-permute-done.5 = f32[40,768]{1,0:T(8,128)S(1)} collective-permute-done((f32[40,768]{1,0:T(8,128)S(1)}, f32[40,768]{1,0:T(8,128)S(1)}, u32[]{:S(2)}, u32[]{:S(2)}) %collective-permute-start.5) | collective-permute-done | bytes 122912 | tf_op jit(solution)/shard_map/ppermute | solution.py:14
  54.1 2.4 %collective-permute-start.9 = (f32[112]{0:T(128)S(1)}, f32[112]{0:T(128)S(1)}, u32[]{:S(2)}, u32[]{:S(2)}) collective-permute-start(f32[112]{0:T(128)S(1)} %pad_maximum_fusion.6), channel_id=1, source_target_pairs={{0,24},{8,16},{16,8},{24,0},{1,25},{9,17},{17,9},{25,1},{2,26},{10... | collective-permute-start | bytes 1352 | tf_op jit(solution)/shard_map/ppermute | solution.py:14
  57.1 1.4 %collective-permute-start.7 = (f32[112]{0:T(128)S(1)}, f32[112]{0:T(128)S(1)}, u32[]{:S(2)}, u32[]{:S(2)}) collective-permute-start(f32[112]{0:T(128)S(1)} %pad_maximum_fusion.6), channel_id=1, source_target_pairs={{0,8},{8,0},{16,24},{24,16},{1,9},{9,1},{17,25},{25,17},{2,10},{10... | collective-permute-start | bytes 1352 | tf_op jit(solution)/shard_map/ppermute | solution.py:14
  58.5 3.1 %fusion.22 = f32[16,3072]{1,0:T(8,128)S(1)} fusion(bf16[768,3072]{1,0:T(8,128)(2,1)} %get-tuple-element.37, f32[16,768]{1,0:T(8,128)S(1)} %get-tuple-element.36, f32[768]{0:T(1024)S(1)} %multiply.18), kind=kOutput, calls=%fused_computation.53 | convolution fusion | flops 75522048 | bytes 4967424 | tf_op jit(solution)/shard_map/dot_general | solution.py:112
  61.6 4.4 %fusion.1 = bf16[16,3072]{1,0:T(8,128)(2,1)S(1)} fusion(f32[16,3072]{1,0:T(8,128)S(1)} %fusion.22, s32[768,3072]{1,0:T(8,128)} %param.11, f32[768]{0:T(1024)S(1)} %get-tuple-element.30, f32[16,768]{1,0:T(8,128)S(1)} %get-tuple-element.36, f32[768]{0:T(1024)S(1)} %multiply.18), kind=kOutput, calls=%fused_computation.5 | convolution fusion | flops 78041088 | bytes 9787392 | tf_op jit(solution)/shard_map/dot_general | solution.py:113
  66.3 2.4 %collective-permute-start.12 = (bf16[16,768]{1,0:T(8,128)(2,1)S(1)}, bf16[16,768]{1,0:T(8,128)(2,1)S(1)}, u32[]{:S(2)}, u32[]{:S(2)}) collective-permute-start(bf16[16,768]{1,0:T(8,128)(2,1)S(1)} %bitcast.89), channel_id=1, source_target_pairs={{0,24},{8,16},{16,8},{24,0},{1,25},{9,17},{17,9},{25,1},{2,26},{10... | collective-permute-start | bytes 73736 | tf_op jit(solution)/shard_map/ppermute | solution.py:14
  68.7 2.1 %collective-permute-start.10 = (bf16[16,768]{1,0:T(8,128)(2,1)S(1)}, bf16[16,768]{1,0:T(8,128)(2,1)S(1)}, u32[]{:S(2)}, u32[]{:S(2)}) collective-permute-start(bf16[16,768]{1,0:T(8,128)(2,1)S(1)} %bitcast.91), channel_id=1, source_target_pairs={{0,8},{8,0},{16,24},{24,16},{1,9},{9,1},{17,25},{25,17},{2,10},{10... | collective-permute-start | bytes 73736 | tf_op jit(solution)/shard_map/ppermute | solution.py:14
  72.0 1.4 %collective-permute-done.11 = bf16[16,768]{1,0:T(8,128)(2,1)S(1)} collective-permute-done((bf16[16,768]{1,0:T(8,128)(2,1)S(1)}, bf16[16,768]{1,0:T(8,128)(2,1)S(1)}, u32[]{:S(2)}, u32[]{:S(2)}) %collective-permute-start.11) | collective-permute-done | bytes 24608 | tf_op jit(solution)/shard_map/ppermute | solution.py:14
  73.7 1.6 %collective-permute-start.18 = (f32[16]{0:T(128)S(1)}, f32[16]{0:T(128)S(1)}, u32[]{:S(2)}, u32[]{:S(2)}) collective-permute-start(f32[16]{0:T(128)S(1)} %get-tuple-element.33), channel_id=1, source_target_pairs={{0,6},{1,7},{2,4},{3,5},{4,2},{5,3},{6,0},{7,1},{8,14},{9,15},{10,... | collective-permute-start | bytes 200 | tf_op jit(solution)/shard_map/ppermute | solution.py:14
  75.4 2.1 %collective-permute-start.17 = (f32[16]{0:T(128)S(1)}, f32[16]{0:T(128)S(1)}, u32[]{:S(2)}, u32[]{:S(2)}) collective-permute-start(f32[16]{0:T(128)S(1)} %get-tuple-element.33), channel_id=1, source_target_pairs={{0,5},{1,4},{2,7},{3,6},{4,1},{5,0},{6,3},{7,2},{8,13},{9,12},{10,... | collective-permute-start | bytes 200 | tf_op jit(solution)/shard_map/ppermute | solution.py:14
  78.1 1.4 %collective-permute-start.14 = (f32[16]{0:T(128)S(1)}, f32[16]{0:T(128)S(1)}, u32[]{:S(2)}, u32[]{:S(2)}) collective-permute-start(f32[16]{0:T(128)S(1)} %get-tuple-element.33), channel_id=1, source_target_pairs={{0,2},{1,3},{2,0},{3,1},{4,6},{5,7},{6,4},{7,5},{8,10},{9,11},{10,... | collective-permute-start | bytes 200 | tf_op jit(solution)/shard_map/ppermute | solution.py:14
  80.0 1.0 %collective-permute-done.16 = f32[16]{0:T(128)S(1)} collective-permute-done((f32[16]{0:T(128)S(1)}, f32[16]{0:T(128)S(1)}, u32[]{:S(2)}, u32[]{:S(2)}) %collective-permute-start.16) | collective-permute-done | bytes 96 | tf_op jit(solution)/shard_map/ppermute | solution.py:14
  81.7 1.8 %collective-permute-start.22 = (f32[16]{0:T(128)S(1)}, f32[16]{0:T(128)S(1)}, u32[]{:S(2)}, u32[]{:S(2)}) collective-permute-start(f32[16]{0:T(128)S(1)} %add_add_fusion.1), channel_id=1, source_target_pairs={{0,24},{8,16},{16,8},{24,0},{1,25},{9,17},{17,9},{25,1},{2,26},{10... | collective-permute-start | bytes 200 | tf_op jit(solution)/shard_map/ppermute | solution.py:14
  83.5 0.9 %collective-permute-start.21 = (f32[16]{0:T(128)S(1)}, f32[16]{0:T(128)S(1)}, u32[]{:S(2)}, u32[]{:S(2)}) collective-permute-start(f32[16]{0:T(128)S(1)} %add_add_fusion.1), channel_id=1, source_target_pairs={{0,16},{8,24},{16,0},{24,8},{1,17},{9,25},{17,1},{25,9},{2,18},{10... | collective-permute-start | bytes 200 | tf_op jit(solution)/shard_map/ppermute | solution.py:14
  84.4 1.7 %collective-permute-start.20 = (f32[16]{0:T(128)S(1)}, f32[16]{0:T(128)S(1)}, u32[]{:S(2)}, u32[]{:S(2)}) collective-permute-start(f32[16]{0:T(128)S(1)} %add_add_fusion.1), channel_id=1, source_target_pairs={{0,8},{8,0},{16,24},{24,16},{1,9},{9,1},{17,25},{25,17},{2,10},{10... | collective-permute-start | bytes 200 | tf_op jit(solution)/shard_map/ppermute | solution.py:14
  86.1 0.9 %collective-permute-done.22 = f32[16]{0:T(128)S(1)} collective-permute-done((f32[16]{0:T(128)S(1)}, f32[16]{0:T(128)S(1)}, u32[]{:S(2)}, u32[]{:S(2)}) %collective-permute-start.22) | collective-permute-done | bytes 96 | tf_op jit(solution)/shard_map/ppermute | solution.py:14
  87.1 0.9 collective-permute-done.21
  (105 shorter events, 12.5 us)
Async XLA Ops:
  0.6 17.5 %copy-start = (f32[768,16]{0,1:T(8,128)S(1)}, f32[768,16]{0,1:T(8,128)}, u32[]{:S(2)}) copy-start(f32[768,16]{0,1:T(8,128)} %param.17) | copy-start | bytes 147460
  0.6 17.5 %copy-start.1 = (f32[768,16]{0,1:T(8,128)S(1)}, f32[768,16]{0,1:T(8,128)}, u32[]{:S(2)}) copy-start(f32[768,16]{0,1:T(8,128)} %param.15) | copy-start | bytes 147460
  1.6 27.3 %collective-permute-start.2 = (bf16[16,768]{1,0:T(8,128)(2,1)S(1)}, bf16[16,768]{1,0:T(8,128)(2,1)S(1)}, u32[]{:S(2)}, u32[]{:S(2)}) collective-permute-start(bf16[16,768]{1,0:T(8,128)(2,1)S(1)} %get-tuple-element.53), channel_id=1, source_target_pairs={{0,24},{8,16},{16,8},{24,0},{1,25},{9,17},{17,9},{25,1},{2,26},{10... | collective-permute-start | bytes 73736 | tf_op jit(solution)/shard_map/ppermute | solution.py:14
  6.7 22.9 %collective-permute-start.1 = (bf16[16,768]{1,0:T(8,128)(2,1)S(1)}, bf16[16,768]{1,0:T(8,128)(2,1)S(1)}, u32[]{:S(2)}, u32[]{:S(2)}) collective-permute-start(bf16[16,768]{1,0:T(8,128)(2,1)S(1)} %get-tuple-element.53), channel_id=1, source_target_pairs={{0,16},{8,24},{16,0},{24,8},{1,17},{9,25},{17,1},{25,9},{2,18},{10... | collective-permute-start | bytes 73736 | tf_op jit(solution)/shard_map/ppermute | solution.py:14
  6.7 22.9 %collective-permute-start = (bf16[16,768]{1,0:T(8,128)(2,1)S(1)}, bf16[16,768]{1,0:T(8,128)(2,1)S(1)}, u32[]{:S(2)}, u32[]{:S(2)}) collective-permute-start(bf16[16,768]{1,0:T(8,128)(2,1)S(1)} %get-tuple-element.53), channel_id=1, source_target_pairs={{0,8},{8,0},{16,24},{24,16},{1,9},{9,1},{17,25},{25,17},{2,10},{10... | collective-permute-start | bytes 73736 | tf_op jit(solution)/shard_map/ppermute | solution.py:14
  14.3 15.4 %collective-permute-start.25 = (f32[40,256]{1,0:T(8,128)S(1)}, f32[40,256]{1,0:T(8,128)S(1)}, u32[]{:S(2)}, u32[]{:S(2)}) collective-permute-start(f32[40,256]{1,0:T(8,128)S(1)} %bitcast.83), channel_id=1, source_target_pairs={{0,24},{8,16},{16,8},{24,0},{1,25},{9,17},{17,9},{25,1},{2,26},{10... | collective-permute-start | bytes 122888 | tf_op jit(solution)/shard_map/ppermute | solution.py:14
  18.1 11.6 %collective-permute-start.24 = (f32[40,256]{1,0:T(8,128)S(1)}, f32[40,256]{1,0:T(8,128)S(1)}, u32[]{:S(2)}, u32[]{:S(2)}) collective-permute-start(f32[40,256]{1,0:T(8,128)S(1)} %bitcast.84), channel_id=1, source_target_pairs={{0,16},{8,24},{16,0},{24,8},{1,17},{9,25},{17,1},{25,9},{2,18},{10... | collective-permute-start | bytes 122888 | tf_op jit(solution)/shard_map/ppermute | solution.py:14
  28.9 4.1 %collective-permute-start.23 = (f32[40,256]{1,0:T(8,128)S(1)}, f32[40,256]{1,0:T(8,128)S(1)}, u32[]{:S(2)}, u32[]{:S(2)}) collective-permute-start(f32[40,256]{1,0:T(8,128)S(1)} %bitcast.85), channel_id=1, source_target_pairs={{0,8},{8,0},{16,24},{24,16},{1,9},{9,1},{17,25},{25,17},{2,10},{10... | collective-permute-start | bytes 122888 | tf_op jit(solution)/shard_map/ppermute | solution.py:14
  33.0 5.2 %collective-permute-start.26 = (f32[40,256]{1,0:T(8,128)S(1)}, f32[40,256]{1,0:T(8,128)S(1)}, u32[]{:S(2)}, u32[]{:S(2)}) collective-permute-start(f32[40,256]{1,0:T(8,128)S(1)} %fusion.21), channel_id=1, source_target_pairs={{0,1},{1,0},{2,3},{3,2},{4,5},{5,4},{6,7},{7,6},{8,9},{9,8},{10,11... | collective-permute-start | bytes 122888 | tf_op jit(solution)/shard_map/ppermute | solution.py:14
  38.3 5.0 %collective-permute-start.29 = (f32[40,256]{1,0:T(8,128)S(1)}, f32[40,256]{1,0:T(8,128)S(1)}, u32[]{:S(2)}, u32[]{:S(2)}) collective-permute-start(f32[40,256]{1,0:T(8,128)S(1)} %add.224), channel_id=1, source_target_pairs={{0,6},{1,7},{2,4},{3,5},{4,2},{5,3},{6,0},{7,1},{8,14},{9,15},{10,... | collective-permute-start | bytes 122888 | tf_op jit(solution)/shard_map/ppermute | solution.py:14
  40.8 4.0 %collective-permute-start.28 = (f32[40,256]{1,0:T(8,128)S(1)}, f32[40,256]{1,0:T(8,128)S(1)}, u32[]{:S(2)}, u32[]{:S(2)}) collective-permute-start(f32[40,256]{1,0:T(8,128)S(1)} %add.224), channel_id=1, source_target_pairs={{0,4},{1,5},{2,6},{3,7},{4,0},{5,1},{6,2},{7,3},{8,12},{9,13},{10,... | collective-permute-start | bytes 122888 | tf_op jit(solution)/shard_map/ppermute | solution.py:14
  41.3 4.0 %collective-permute-start.27 = (f32[40,256]{1,0:T(8,128)S(1)}, f32[40,256]{1,0:T(8,128)S(1)}, u32[]{:S(2)}, u32[]{:S(2)}) collective-permute-start(f32[40,256]{1,0:T(8,128)S(1)} %add.224), channel_id=1, source_target_pairs={{0,2},{1,3},{2,0},{3,1},{4,6},{5,7},{6,4},{7,5},{8,10},{9,11},{10,... | collective-permute-start | bytes 122888 | tf_op jit(solution)/shard_map/ppermute | solution.py:14
  43.2 2.2 %collective-permute-start.3 = (f32[40,768]{1,0:T(8,128)S(1)}, f32[40,768]{1,0:T(8,128)S(1)}, u32[]{:S(2)}, u32[]{:S(2)}) collective-permute-start(f32[40,768]{1,0:T(8,128)S(1)} %concatenate.25), channel_id=1, source_target_pairs={{0,1},{1,0},{2,3},{3,2},{4,5},{5,4},{6,7},{7,6},{8,9},{9,8},{10,11... | collective-permute-start | bytes 368648 | tf_op jit(solution)/shard_map/ppermute | solution.py:14
  45.4 6.4 %collective-permute-start.6 = (f32[40,768]{1,0:T(8,128)S(1)}, f32[40,768]{1,0:T(8,128)S(1)}, u32[]{:S(2)}, u32[]{:S(2)}) collective-permute-start(f32[40,768]{1,0:T(8,128)S(1)} %add.188), channel_id=1, source_target_pairs={{0,6},{1,7},{2,4},{3,5},{4,2},{5,3},{6,0},{7,1},{8,14},{9,15},{10,... | collective-permute-start | bytes 368648 | tf_op jit(solution)/shard_map/ppermute | solution.py:14
  47.2 6.5 %collective-permute-start.5 = (f32[40,768]{1,0:T(8,128)S(1)}, f32[40,768]{1,0:T(8,128)S(1)}, u32[]{:S(2)}, u32[]{:S(2)}) collective-permute-start(f32[40,768]{1,0:T(8,128)S(1)} %add.188), channel_id=1, source_target_pairs={{0,4},{1,5},{2,6},{3,7},{4,0},{5,1},{6,2},{7,3},{8,12},{9,13},{10,... | collective-permute-start | bytes 368648 | tf_op jit(solution)/shard_map/ppermute | solution.py:14
  47.7 6.1 %collective-permute-start.4 = (f32[40,768]{1,0:T(8,128)S(1)}, f32[40,768]{1,0:T(8,128)S(1)}, u32[]{:S(2)}, u32[]{:S(2)}) collective-permute-start(f32[40,768]{1,0:T(8,128)S(1)} %add.188), channel_id=1, source_target_pairs={{0,2},{1,3},{2,0},{3,1},{4,6},{5,7},{6,4},{7,5},{8,10},{9,11},{10,... | collective-permute-start | bytes 368648 | tf_op jit(solution)/shard_map/ppermute | solution.py:14
  54.1 14.6 %collective-permute-start.9 = (f32[112]{0:T(128)S(1)}, f32[112]{0:T(128)S(1)}, u32[]{:S(2)}, u32[]{:S(2)}) collective-permute-start(f32[112]{0:T(128)S(1)} %pad_maximum_fusion.6), channel_id=1, source_target_pairs={{0,24},{8,16},{16,8},{24,0},{1,25},{9,17},{17,9},{25,1},{2,26},{10... | collective-permute-start | bytes 1352 | tf_op jit(solution)/shard_map/ppermute | solution.py:14
  56.5 14.4 %collective-permute-start.8 = (f32[112]{0:T(128)S(1)}, f32[112]{0:T(128)S(1)}, u32[]{:S(2)}, u32[]{:S(2)}) collective-permute-start(f32[112]{0:T(128)S(1)} %pad_maximum_fusion.6), channel_id=1, source_target_pairs={{0,16},{8,24},{16,0},{24,8},{1,17},{9,25},{17,1},{25,9},{2,18},{10... | collective-permute-start | bytes 1352 | tf_op jit(solution)/shard_map/ppermute | solution.py:14
  57.1 13.7 %collective-permute-start.7 = (f32[112]{0:T(128)S(1)}, f32[112]{0:T(128)S(1)}, u32[]{:S(2)}, u32[]{:S(2)}) collective-permute-start(f32[112]{0:T(128)S(1)} %pad_maximum_fusion.6), channel_id=1, source_target_pairs={{0,8},{8,0},{16,24},{24,16},{1,9},{9,1},{17,25},{25,17},{2,10},{10... | collective-permute-start | bytes 1352 | tf_op jit(solution)/shard_map/ppermute | solution.py:14
  66.3 5.7 %collective-permute-start.12 = (bf16[16,768]{1,0:T(8,128)(2,1)S(1)}, bf16[16,768]{1,0:T(8,128)(2,1)S(1)}, u32[]{:S(2)}, u32[]{:S(2)}) collective-permute-start(bf16[16,768]{1,0:T(8,128)(2,1)S(1)} %bitcast.89), channel_id=1, source_target_pairs={{0,24},{8,16},{16,8},{24,0},{1,25},{9,17},{17,9},{25,1},{2,26},{10... | collective-permute-start | bytes 73736 | tf_op jit(solution)/shard_map/ppermute | solution.py:14
  68.7 4.7 %collective-permute-start.11 = (bf16[16,768]{1,0:T(8,128)(2,1)S(1)}, bf16[16,768]{1,0:T(8,128)(2,1)S(1)}, u32[]{:S(2)}, u32[]{:S(2)}) collective-permute-start(bf16[16,768]{1,0:T(8,128)(2,1)S(1)} %bitcast.90), channel_id=1, source_target_pairs={{0,16},{8,24},{16,0},{24,8},{1,17},{9,25},{17,1},{25,9},{2,18},{10... | collective-permute-start | bytes 73736 | tf_op jit(solution)/shard_map/ppermute | solution.py:14
  68.7 4.7 %collective-permute-start.10 = (bf16[16,768]{1,0:T(8,128)(2,1)S(1)}, bf16[16,768]{1,0:T(8,128)(2,1)S(1)}, u32[]{:S(2)}, u32[]{:S(2)}) collective-permute-start(bf16[16,768]{1,0:T(8,128)(2,1)S(1)} %bitcast.91), channel_id=1, source_target_pairs={{0,8},{8,0},{16,24},{24,16},{1,9},{9,1},{17,25},{25,17},{2,10},{10... | collective-permute-start | bytes 73736 | tf_op jit(solution)/shard_map/ppermute | solution.py:14
  73.6 4.5 %collective-permute-start.19 = (f32[16]{0:T(128)S(1)}, f32[16]{0:T(128)S(1)}, u32[]{:S(2)}, u32[]{:S(2)}) collective-permute-start(f32[16]{0:T(128)S(1)} %get-tuple-element.33), channel_id=1, source_target_pairs={{0,7},{1,6},{2,5},{3,4},{4,3},{5,2},{6,1},{7,0},{8,15},{9,14},{10,... | collective-permute-start | bytes 200 | tf_op jit(solution)/shard_map/ppermute | solution.py:14
  73.7 5.8 %collective-permute-start.18 = (f32[16]{0:T(128)S(1)}, f32[16]{0:T(128)S(1)}, u32[]{:S(2)}, u32[]{:S(2)}) collective-permute-start(f32[16]{0:T(128)S(1)} %get-tuple-element.33), channel_id=1, source_target_pairs={{0,6},{1,7},{2,4},{3,5},{4,2},{5,3},{6,0},{7,1},{8,14},{9,15},{10,... | collective-permute-start | bytes 200 | tf_op jit(solution)/shard_map/ppermute | solution.py:14
  75.4 4.6 %collective-permute-start.17 = (f32[16]{0:T(128)S(1)}, f32[16]{0:T(128)S(1)}, u32[]{:S(2)}, u32[]{:S(2)}) collective-permute-start(f32[16]{0:T(128)S(1)} %get-tuple-element.33), channel_id=1, source_target_pairs={{0,5},{1,4},{2,7},{3,6},{4,1},{5,0},{6,3},{7,2},{8,13},{9,12},{10,... | collective-permute-start | bytes 200 | tf_op jit(solution)/shard_map/ppermute | solution.py:14
  77.4 3.5 %collective-permute-start.16 = (f32[16]{0:T(128)S(1)}, f32[16]{0:T(128)S(1)}, u32[]{:S(2)}, u32[]{:S(2)}) collective-permute-start(f32[16]{0:T(128)S(1)} %get-tuple-element.33), channel_id=1, source_target_pairs={{0,4},{1,5},{2,6},{3,7},{4,0},{5,1},{6,2},{7,3},{8,12},{9,13},{10,... | collective-permute-start | bytes 200 | tf_op jit(solution)/shard_map/ppermute | solution.py:14
  78.1 3.0 %collective-permute-start.15 = (f32[16]{0:T(128)S(1)}, f32[16]{0:T(128)S(1)}, u32[]{:S(2)}, u32[]{:S(2)}) collective-permute-start(f32[16]{0:T(128)S(1)} %get-tuple-element.33), channel_id=1, source_target_pairs={{0,3},{1,2},{2,1},{3,0},{4,7},{5,6},{6,5},{7,4},{8,11},{9,10},{10,... | collective-permute-start | bytes 200 | tf_op jit(solution)/shard_map/ppermute | solution.py:14
  78.1 3.6 %collective-permute-start.14 = (f32[16]{0:T(128)S(1)}, f32[16]{0:T(128)S(1)}, u32[]{:S(2)}, u32[]{:S(2)}) collective-permute-start(f32[16]{0:T(128)S(1)} %get-tuple-element.33), channel_id=1, source_target_pairs={{0,2},{1,3},{2,0},{3,1},{4,6},{5,7},{6,4},{7,5},{8,10},{9,11},{10,... | collective-permute-start | bytes 200 | tf_op jit(solution)/shard_map/ppermute | solution.py:14
  79.5 2.1 %collective-permute-start.13 = (f32[16]{0:T(128)S(1)}, f32[16]{0:T(128)S(1)}, u32[]{:S(2)}, u32[]{:S(2)}) collective-permute-start(f32[16]{0:T(128)S(1)} %get-tuple-element.33), channel_id=1, source_target_pairs={{0,1},{1,0},{2,3},{3,2},{4,5},{5,4},{6,7},{7,6},{8,9},{9,8},{10,11... | collective-permute-start | bytes 200 | tf_op jit(solution)/shard_map/ppermute | solution.py:14
  81.7 5.4 %collective-permute-start.22 = (f32[16]{0:T(128)S(1)}, f32[16]{0:T(128)S(1)}, u32[]{:S(2)}, u32[]{:S(2)}) collective-permute-start(f32[16]{0:T(128)S(1)} %add_add_fusion.1), channel_id=1, source_target_pairs={{0,24},{8,16},{16,8},{24,0},{1,25},{9,17},{17,9},{25,1},{2,26},{10... | collective-permute-start | bytes 200 | tf_op jit(solution)/shard_map/ppermute | solution.py:14
  83.5 4.4 %collective-permute-start.21 = (f32[16]{0:T(128)S(1)}, f32[16]{0:T(128)S(1)}, u32[]{:S(2)}, u32[]{:S(2)}) collective-permute-start(f32[16]{0:T(128)S(1)} %add_add_fusion.1), channel_id=1, source_target_pairs={{0,16},{8,24},{16,0},{24,8},{1,17},{9,25},{17,1},{25,9},{2,18},{10... | collective-permute-start | bytes 200 | tf_op jit(solution)/shard_map/ppermute | solution.py:14
  84.4 3.5 %collective-permute-start.20 = (f32[16]{0:T(128)S(1)}, f32[16]{0:T(128)S(1)}, u32[]{:S(2)}, u32[]{:S(2)}) collective-permute-start(f32[16]{0:T(128)S(1)} %add_add_fusion.1), channel_id=1, source_target_pairs={{0,8},{8,0},{16,24},{24,16},{1,9},{9,1},{17,25},{25,17},{2,10},{10... | collective-permute-start | bytes 200 | tf_op jit(solution)/shard_map/ppermute | solution.py:14
  (5 other events, 53.0 us)

commit v2 on v1

--- a/solution.py
+++ b/solution.py
@@ -36,6 +36,13 @@
 def split2(values):
     high = lax.reduce_precision(values, 8, 7)
     return high.astype(BF16), (values - high).astype(BF16)
+
+
+def split3(values):
+    high = lax.reduce_precision(values, 8, 7)
+    rest = values - high
+    middle = lax.reduce_precision(rest, 8, 7)
+    return high.astype(BF16), middle.astype(BF16), (rest - middle).astype(BF16)
 
 
 def body(genotypes, called, dosage, sample_order, noise_ratio, solution, residual, direction):
@@ -107,16 +114,19 @@
     scaled_b = (2.0 * frequency * scaled).astype(BF16)
 
     small = jnp.concatenate([sums, jnp.sum(loading * loading, axis=1)])
-    small = sum_over(small, "var", [var_all])
+    parts = jnp.zeros((rhs, 128), BF16).at[:3, : small.shape[0]].set(jnp.stack(split3(small)))
 
     term = jnp.dot(scaled_a, coded_b, preferred_element_type=F32)
     term = term - jnp.dot(scaled_b, called_b, preferred_element_type=F32)
     term = (term / variants).astype(BF16)
-    term = term.reshape(rhs, n_var, own)
-    take = lambda p: lax.dynamic_index_in_dim(term, p, axis=1, keepdims=False)
-    back = take(var).astype(F32)
-    for arrived in [swap(take(var ^ k), "var", k) for k in var_all]:
-        back = back + arrived.astype(F32)
+    message = jnp.stack(
+        [jnp.concatenate([term[:, p * own : (p + 1) * own], parts], axis=1) for p in range(n_var)]
+    )
+    message = lax.all_to_all(message, "var", split_axis=0, concat_axis=0)
+    message = jnp.sum(message.astype(F32), axis=0)
+    back = message[:, :own]
+    small = message[0, own:] + message[1, own:] + message[2, own:]
+    small = small[: 7 * rhs]
 
     res_norm, dir_norm, sol_one, sol_two, sol_dir, dir_one, load_square = small.reshape(7, rhs)
     applied = noise_ratio[:, None] * direction_t + back
@@ -125,8 +135,9 @@
     solution_new = solution_t + step_size[:, None] * direction_t
     residual_new = residual_t - step_size[:, None] * applied
     res_new_norm = jnp.sum(residual_new * residual_new, axis=1)
-    res_new_norm = sum_over(res_new_norm, "samp", [list(range(1, n_samp))] if n_samp <= 8 else samp_stages)
-    res_new_norm = sum_over(res_new_norm, "var", [var_all])
+    spread_out = jnp.broadcast_to(jnp.pad(res_new_norm, (0, 128 - rhs)), (n_var * n_samp, 1, 128))
+    spread_out = lax.all_to_all(spread_out, ("var", "samp"), split_axis=0, concat_axis=0)
+    res_new_norm = jnp.sum(spread_out, axis=(0, 1))[:rhs]
     direction_new = residual_new + (res_new_norm / (res_norm + 1e-06))[:, None] * direction_t
 
     wide = imputed // n_var

time: 89.8 us -> 82 us (0.913)
  starting transfers between devices: 37.2 us -> 25.3 us
  waiting for transfers between devices: 15.4 us -> 18.4 us
    ppermute x30 -> x14, starting transfers between devices: 37.2 us -> 17.9 us  [swap(): return lax.ppermute(values, axis, [(i, i ^ distance) for i in range(size)])]
    all_to_all x0 -> x2, waiting for transfers between devices: none -> 12.2 us  [the longest x1 6.38 us: body(): lax.all_to_all(spread_out, ('var', 'samp'), split_axis=0, concat_axis=0)]
    ppermute x30 -> x14, waiting for transfers between devices: 15.4 us -> 6.13 us  [swap(): return lax.ppermute(values, axis, [(i, i ^ distance) for i in range(size)])]
    all_to_all x0 -> x2, starting transfers between devices: none -> 7.41 us  [the longest x1 4.87 us: body(): message = lax.all_to_all(message, 'var', split_axis=0, concat_axis=0)]
  transfers between devices with their start and end apart: 30 -> 16, of which waited for: 13 -> 7; matrix products, arithmetic and copies ran while one was open for 37% -> 31% of each run, Pallas kernels for 0% -> 0%
where the time goes in v2:
time: 82 us; the launch traced here: 81.5 us
  starting transfers between devices  25.3 us (31%)
  waiting for transfers between devices  18.4 us (22%)
  other arithmetic  17.5 us (21%)
  matrix products  16.3 us (20%)
  local copies, waits for them, and re-layouts  3.02 us (4%)
  between operations  1.02 us (1%)
    ppermute x14, starting transfers between devices, swap(): return lax.ppermute(values, axis, [(i, i ^ distance) for i in range(size)])  17.9 us
    reduce_sum x1, other arithmetic, body(): called_part = jnp.sum(called, axis=1).astype(F32)  10.2 us
    all_to_all x1, waiting for transfers between devices, body(): lax.all_to_all(spread_out, ('var', 'samp'), split_axis=0, concat_axis=0)  6.38 us
    ppermute x14, waiting for transfers between devices, swap(): return lax.ppermute(values, axis, [(i, i ^ distance) for i in range(size)])  6.13 us
    all_to_all x1, waiting for transfers between devices, body(): message = lax.all_to_all(message, 'var', split_axis=0, concat_axis=0)  5.87 us
    dot_general x1, matrix products, body(): lax.dot_general(piece, called_b, nt, preferred_element_type=F32)  5.15 us
    all_to_all x1, starting transfers between devices, body(): message = lax.all_to_all(message, 'var', split_axis=0, concat_axis=0)  4.87 us
    dot_general x1, matrix products, body(): term = term - jnp.dot(scaled_b, called_b, preferred_element_type=F32)  4.44 us
  transfers between devices with their start and end apart: 16, of which 7 were waited for; matrix products, arithmetic and copies ran while one was open for 31% of the time, Pallas kernels for 0%

profile of v2, /device:TPU:0, one launch (start us, length us, event | category | flops | bytes accessed | tf_op | source)
XLA Modules:
  0.0 81.5 jit_solution(16871507058579542469)
XLA Ops:
  0.7 1.0 %fusion.60 = (f32[16]{0:T(128)S(1)}, bf16[16,768]{1,0:T(8,128)(2,1)S(1)}) fusion(f32[768,16]{0,1:T(8,128)} %param.19), kind=kLoop, calls=%fused_computation.131 | loop fusion | flops 24560 | bytes 73792 | tf_op jit(solution)/shard_map/reduce_sum | solution.py:92
  1.6 5.1 %collective-permute-start.2 = (bf16[16,768]{1,0:T(8,128)(2,1)S(1)}, bf16[16,768]{1,0:T(8,128)(2,1)S(1)}, u32[]{:S(2)}, u32[]{:S(2)}) collective-permute-start(bf16[16,768]{1,0:T(8,128)(2,1)S(1)} %get-tuple-element.67), channel_id=1, source_target_pairs={{0,24},{8,16},{16,8},{24,0},{1,25},{9,17},{17,9},{25,1},{2,26},{10... | collective-permute-start | bytes 73736 | tf_op jit(solution)/shard_map/ppermute | solution.py:14
  6.7 0.6 collective-permute-start
  7.4 0.7 fusion.41
  8.1 0.7 reduce.8
  8.8 0.8 %pad_maximum_fusion.4 = f32[32,768]{1,0:T(8,128)S(1)} fusion(f32[16,768]{1,0:T(8,128)} %bitcast.111, f32[16,768]{1,0:T(8,128)} %bitcast.112), kind=kLoop, calls=%fused_computation.25 | loop fusion | flops 24576 | bytes 196608 | tf_op jit(solution)/shard_map/concatenate | solution.py:77
  9.8 1.6 %gather_fusion = f32[768,32]{1,0:T(8,128)S(1)} fusion(f32[32,768]{0,1:T(8,128)S(1)} %copy.27, s32[1024]{0:T(1024)S(1)} %pad_clamp_fusion), kind=kCustom, calls=%fused_computation | custom fusion | bytes 199680 | tf_op jit(solution)/shard_map/jit(_take)/gather | solution.py:78
  11.6 2.3 %fusion.5 = f32[80,1024]{1,0:T(8,128)S(1)} fusion(s32[768,1024]{1,0:T(8,128)} %param.14, bf16[32,768]{1,0:T(8,128)(2,1)S(1)} %get-tuple-element.57, bf16[32,768]{1,0:T(8,128)(2,1)S(1)} %get-tuple-element.56, bf16[80]{0:T(256)(128)(2,1)S(1)} %pad.19.clone), kind=kOutput, calls=%fused_computation.9 | convolution fusion | flops 126984192 | bytes 3571872 | tf_op jit(solution)/shard_map/dot_general | solution.py:82
  14.3 3.8 %collective-permute-start.9 = (f32[40,256]{1,0:T(8,128)S(1)}, f32[40,256]{1,0:T(8,128)S(1)}, u32[]{:S(2)}, u32[]{:S(2)}) collective-permute-start(f32[40,256]{1,0:T(8,128)S(1)} %bitcast.116), channel_id=1, source_target_pairs={{0,24},{8,16},{16,8},{24,0},{1,25},{9,17},{17,9},{25,1},{2,26},{10... | collective-permute-start | bytes 122888 | tf_op jit(solution)/shard_map/ppermute | solution.py:14
  18.3 10.2 %fusion.55 = (s32[768]{0:T(1024)S(1)}, s32[768]{0:T(1024)S(1)}, bf16[768,3072]{1,0:T(8,128)(2,1)}) fusion(s32[768,3072]{1,0:T(8,128)} %param.13, s32[768,3072]{1,0:T(8,128)} %param.12), kind=kLoop, calls=%fused_computation.129 | loop fusion | flops 9435648 | bytes 23599104 | tf_op jit(solution)/shard_map/reduce_sum | solution.py:74
  28.9 0.7 collective-permute-start.7
  29.7 5.2 %fusion.3 = f32[16,768]{1,0:T(8,128)S(1)} fusion(s32[768,3072]{1,0:T(8,128)} %param.13, bf16[16,768]{1,0:T(8,128)(2,1)S(1)} %get-tuple-element.63, bf16[16,768]{1,0:T(8,128)(2,1)S(1)} %get-tuple-element.64, bf16[16,768]{1,0:T(8,128)(2,1)S(1)} %get-tuple-element.65, bf16[16,768]{1,0:T(8,128)(2,1)S(1)} %get-tuple-element.62), kind=kOutput, calls=%fused_computation.7 | convolution fusion | flops 78249984 | bytes 9584640 | tf_op jit(solution)/shard_map/dot_general | solution.py:100
  34.8 1.3 %fusion.26 = f32[16,768]{1,0:T(8,128)S(1)} fusion(bf16[768,3072]{1,0:T(8,128)(2,1)S(1)} %bitcast.110, bf16[16,768]{1,0:T(8,128)(2,1)S(1)} %get-tuple-element.63, bf16[16,768]{1,0:T(8,128)(2,1)S(1)} %get-tuple-element.64, bf16[16,768]{1,0:T(8,128)(2,1)S(1)} %get-tuple-element.65, bf16[16,768]{1,0:T(8,128)(2,1)S(1)} %get-tuple-element.62), kind=kOutput, calls=%fused_computation.68 | convolution fusion | flops 75890688 | bytes 4866048 | tf_op jit(solution)/shard_map/dot_general | solution.py:99
  36.3 0.5 collective-permute-start.10
  36.9 0.9 %collective-permute-done.10 = f32[40,256]{1,0:T(8,128)S(1)} collective-permute-done((f32[40,256]{1,0:T(8,128)S(1)}, f32[40,256]{1,0:T(8,128)S(1)}, u32[]{:S(2)}, u32[]{:S(2)}) %collective-permute-start.10) | collective-permute-done | bytes 40992 | tf_op jit(solution)/shard_map/ppermute | solution.py:14
  37.8 2.6 %collective-permute-start.13 = (f32[40,256]{1,0:T(8,128)S(1)}, f32[40,256]{1,0:T(8,128)S(1)}, u32[]{:S(2)}, u32[]{:S(2)}) collective-permute-start(f32[40,256]{1,0:T(8,128)S(1)} %add.171), channel_id=1, source_target_pairs={{0,6},{1,7},{2,4},{3,5},{4,2},{5,3},{6,0},{7,1},{8,14},{9,15},{10,... | collective-permute-start | bytes 122888 | tf_op jit(solution)/shard_map/ppermute | solution.py:14
  40.4 0.5 collective-permute-start.12
  41.3 2.6 %collective-permute-start.6 = (f32[40,768]{1,0:T(8,128)S(1)}, f32[40,768]{1,0:T(8,128)S(1)}, u32[]{:S(2)}, u32[]{:S(2)}) collective-permute-start(f32[40,768]{1,0:T(8,128)S(1)} %add.149), channel_id=1, source_target_pairs={{0,6},{1,7},{2,4},{3,5},{4,2},{5,3},{6,0},{7,1},{8,14},{9,15},{10,... | collective-permute-start | bytes 368648 | tf_op jit(solution)/shard_map/ppermute | solution.py:14
  43.9 0.5 collective-permute-start.5
  45.3 3.1 %collective-permute-done.6 = f32[40,768]{1,0:T(8,128)S(1)} collective-permute-done((f32[40,768]{1,0:T(8,128)S(1)}, f32[40,768]{1,0:T(8,128)S(1)}, u32[]{:S(2)}, u32[]{:S(2)}) %collective-permute-start.6) | collective-permute-done | bytes 122912 | tf_op jit(solution)/shard_map/ppermute | solution.py:14
  48.4 1.7 %collective-permute-done.5 = f32[40,768]{1,0:T(8,128)S(1)} collective-permute-done((f32[40,768]{1,0:T(8,128)S(1)}, f32[40,768]{1,0:T(8,128)S(1)}, u32[]{:S(2)}, u32[]{:S(2)}) %collective-permute-start.5) | collective-permute-done | bytes 122912 | tf_op jit(solution)/shard_map/ppermute | solution.py:14
  50.5 3.1 %fusion.23 = f32[16,3072]{1,0:T(8,128)S(1)} fusion(bf16[768,3072]{1,0:T(8,128)(2,1)} %get-tuple-element.51, f32[16,768]{1,0:T(8,128)S(1)} %get-tuple-element.50, f32[768]{0:T(1024)S(1)} %multiply.19), kind=kOutput, calls=%fused_computation.56 | convolution fusion | flops 75522048 | bytes 4967424 | tf_op jit(solution)/shard_map/dot_general | solution.py:119
  53.6 4.4 %fusion.1 = bf16[16,3072]{1,0:T(8,128)(2,1)S(1)} fusion(f32[16,3072]{1,0:T(8,128)S(1)} %fusion.23, s32[768,3072]{1,0:T(8,128)} %param.13, f32[768]{0:T(1024)S(1)} %get-tuple-element.42, f32[16,768]{1,0:T(8,128)S(1)} %get-tuple-element.50, f32[768]{0:T(1024)S(1)} %multiply.19), kind=kOutput, calls=%fused_computation.5 | convolution fusion | flops 78041088 | bytes 9787392 | tf_op jit(solution)/shard_map/dot_general | solution.py:120
  58.0 0.7 pad_maximum_fusion.1
  58.7 4.9 %all-to-all-start = ((bf16[4,16,896]{2,1,0:T(8,128)(2,1)}), bf16[4,16,896]{2,1,0:T(8,128)(2,1)S(1)}, u32[]{:S(2)}, u32[]{:S(2)}) async-start(bf16[4,16,896]{2,1,0:T(8,128)(2,1)} %pad_maximum_fusion.1), calls=%async_computation | async-start | bytes 229376 | tf_op jit(solution)/shard_map/all_to_all | solution.py:125
  63.6 5.9 %all-to-all-done = bf16[4,16,896]{2,1,0:T(8,128)(2,1)S(1)} async-done(((bf16[4,16,896]{2,1,0:T(8,128)(2,1)}), bf16[4,16,896]{2,1,0:T(8,128)(2,1)S(1)}, u32[]{:S(2)}, u32[]{:S(2)}) %all-to-all-start) | async-done | bytes 114720 | tf_op jit(solution)/shard_map/all_to_all | solution.py:125
  69.8 0.6 broadcast_in_dim.14
  70.4 2.5 %all-to-all-start.1 = ((f32[32,1,128]{2,1,0:T(1,128)}), f32[32,1,128]{2,1,0:T(1,128)S(1)}, u32[]{:S(2)}, u32[]{:S(2)}) async-start(f32[32,1,128]{2,1,0:T(1,128)} %broadcast_in_dim.14), calls=%async_computation.1 | async-start | bytes 32768 | tf_op jit(solution)/shard_map/all_to_all | solution.py:139
  73.0 0.7 multiply_add_fusion
  73.7 6.4 %all-to-all-done.1 = f32[32,1,128]{2,1,0:T(1,128)S(1)} async-done(((f32[32,1,128]{2,1,0:T(1,128)}), f32[32,1,128]{2,1,0:T(1,128)S(1)}, u32[]{:S(2)}, u32[]{:S(2)}) %all-to-all-start.1) | async-done | bytes 16416 | tf_op jit(solution)/shard_map/all_to_all | solution.py:139
  80.1 0.7 add_bitcast_fusion
  80.8 0.7 fusion.31
  (80 shorter events, 3.5 us)
Async XLA Ops:
  0.6 17.5 %copy-start = (f32[768,16]{0,1:T(8,128)S(1)}, f32[768,16]{0,1:T(8,128)}, u32[]{:S(2)}) copy-start(f32[768,16]{0,1:T(8,128)} %param.19) | copy-start | bytes 147460
  0.6 17.5 %copy-start.1 = (f32[768,16]{0,1:T(8,128)S(1)}, f32[768,16]{0,1:T(8,128)}, u32[]{:S(2)}) copy-start(f32[768,16]{0,1:T(8,128)} %param.17) | copy-start | bytes 147460
  1.6 27.3 %collective-permute-start.2 = (bf16[16,768]{1,0:T(8,128)(2,1)S(1)}, bf16[16,768]{1,0:T(8,128)(2,1)S(1)}, u32[]{:S(2)}, u32[]{:S(2)}) collective-permute-start(bf16[16,768]{1,0:T(8,128)(2,1)S(1)} %get-tuple-element.67), channel_id=1, source_target_pairs={{0,24},{8,16},{16,8},{24,0},{1,25},{9,17},{17,9},{25,1},{2,26},{10... | collective-permute-start | bytes 73736 | tf_op jit(solution)/shard_map/ppermute | solution.py:14
  6.7 22.9 %collective-permute-start.1 = (bf16[16,768]{1,0:T(8,128)(2,1)S(1)}, bf16[16,768]{1,0:T(8,128)(2,1)S(1)}, u32[]{:S(2)}, u32[]{:S(2)}) collective-permute-start(bf16[16,768]{1,0:T(8,128)(2,1)S(1)} %get-tuple-element.67), channel_id=1, source_target_pairs={{0,16},{8,24},{16,0},{24,8},{1,17},{9,25},{17,1},{25,9},{2,18},{10... | collective-permute-start | bytes 73736 | tf_op jit(solution)/shard_map/ppermute | solution.py:14
  6.7 22.9 %collective-permute-start = (bf16[16,768]{1,0:T(8,128)(2,1)S(1)}, bf16[16,768]{1,0:T(8,128)(2,1)S(1)}, u32[]{:S(2)}, u32[]{:S(2)}) collective-permute-start(bf16[16,768]{1,0:T(8,128)(2,1)S(1)} %get-tuple-element.67), channel_id=1, source_target_pairs={{0,8},{8,0},{16,24},{24,16},{1,9},{9,1},{17,25},{25,17},{2,10},{10... | collective-permute-start | bytes 73736 | tf_op jit(solution)/shard_map/ppermute | solution.py:14
  14.3 22.0 %collective-permute-start.9 = (f32[40,256]{1,0:T(8,128)S(1)}, f32[40,256]{1,0:T(8,128)S(1)}, u32[]{:S(2)}, u32[]{:S(2)}) collective-permute-start(f32[40,256]{1,0:T(8,128)S(1)} %bitcast.116), channel_id=1, source_target_pairs={{0,24},{8,16},{16,8},{24,0},{1,25},{9,17},{17,9},{25,1},{2,26},{10... | collective-permute-start | bytes 122888 | tf_op jit(solution)/shard_map/ppermute | solution.py:14
  18.1 18.2 %collective-permute-start.8 = (f32[40,256]{1,0:T(8,128)S(1)}, f32[40,256]{1,0:T(8,128)S(1)}, u32[]{:S(2)}, u32[]{:S(2)}) collective-permute-start(f32[40,256]{1,0:T(8,128)S(1)} %bitcast.117), channel_id=1, source_target_pairs={{0,16},{8,24},{16,0},{24,8},{1,17},{9,25},{17,1},{25,9},{2,18},{10... | collective-permute-start | bytes 122888 | tf_op jit(solution)/shard_map/ppermute | solution.py:14
  18.3 10.2 %copy-start.2 = (f32[768,16]{0,1:T(8,128)S(1)}, f32[768,16]{0,1:T(8,128)}, u32[]{:S(2)}) copy-start(f32[768,16]{0,1:T(8,128)} %param.18) | copy-start | bytes 147460
  28.9 7.4 %collective-permute-start.7 = (f32[40,256]{1,0:T(8,128)S(1)}, f32[40,256]{1,0:T(8,128)S(1)}, u32[]{:S(2)}, u32[]{:S(2)}) collective-permute-start(f32[40,256]{1,0:T(8,128)S(1)} %bitcast.118), channel_id=1, source_target_pairs={{0,8},{8,0},{16,24},{24,16},{1,9},{9,1},{17,25},{25,17},{2,10},{10... | collective-permute-start | bytes 122888 | tf_op jit(solution)/shard_map/ppermute | solution.py:14
  29.6 5.2 %slice-start = ((s8[4718592]{0:T(1024)(128)(4,1)}), s8[4194304]{0:T(1024)(128)(4,1)S(1)}, s32[]{:S(2)}) async-start(s8[4718592]{0:T(1024)(128)(4,1)} %bitcast.109), calls=%async_computation.2 | async-start | bytes 8388608
  29.7 5.2 %slice-start.1 = ((s8[4718592]{0:T(1024)(128)(4,1)}), s8[524288]{0:T(1024)(128)(4,1)S(1)}, s32[]{:S(2)}) async-start(s8[4718592]{0:T(1024)(128)(4,1)} %bitcast.109), calls=%async_computation.3 | async-start | bytes 1048576
  36.2 5.0 %collective-permute-start.3 = (f32[40,768]{1,0:T(8,128)S(1)}, f32[40,768]{1,0:T(8,128)S(1)}, u32[]{:S(2)}, u32[]{:S(2)}) collective-permute-start(f32[40,768]{1,0:T(8,128)S(1)} %concatenate.65), channel_id=1, source_target_pairs={{0,1},{1,0},{2,3},{3,2},{4,5},{5,4},{6,7},{7,6},{8,9},{9,8},{10,11... | collective-permute-start | bytes 368648 | tf_op jit(solution)/shard_map/ppermute | solution.py:14
  36.3 1.4 %collective-permute-start.10 = (f32[40,256]{1,0:T(8,128)S(1)}, f32[40,256]{1,0:T(8,128)S(1)}, u32[]{:S(2)}, u32[]{:S(2)}) collective-permute-start(f32[40,256]{1,0:T(8,128)S(1)} %fusion.18), channel_id=1, source_target_pairs={{0,1},{1,0},{2,3},{3,2},{4,5},{5,4},{6,7},{7,6},{8,9},{9,8},{10,11... | collective-permute-start | bytes 122888 | tf_op jit(solution)/shard_map/ppermute | solution.py:14
  37.8 6.7 %collective-permute-start.13 = (f32[40,256]{1,0:T(8,128)S(1)}, f32[40,256]{1,0:T(8,128)S(1)}, u32[]{:S(2)}, u32[]{:S(2)}) collective-permute-start(f32[40,256]{1,0:T(8,128)S(1)} %add.171), channel_id=1, source_target_pairs={{0,6},{1,7},{2,4},{3,5},{4,2},{5,3},{6,0},{7,1},{8,14},{9,15},{10,... | collective-permute-start | bytes 122888 | tf_op jit(solution)/shard_map/ppermute | solution.py:14
  40.4 4.5 %collective-permute-start.12 = (f32[40,256]{1,0:T(8,128)S(1)}, f32[40,256]{1,0:T(8,128)S(1)}, u32[]{:S(2)}, u32[]{:S(2)}) collective-permute-start(f32[40,256]{1,0:T(8,128)S(1)} %add.171), channel_id=1, source_target_pairs={{0,4},{1,5},{2,6},{3,7},{4,0},{5,1},{6,2},{7,3},{8,12},{9,13},{10,... | collective-permute-start | bytes 122888 | tf_op jit(solution)/shard_map/ppermute | solution.py:14
  40.9 4.3 %collective-permute-start.11 = (f32[40,256]{1,0:T(8,128)S(1)}, f32[40,256]{1,0:T(8,128)S(1)}, u32[]{:S(2)}, u32[]{:S(2)}) collective-permute-start(f32[40,256]{1,0:T(8,128)S(1)} %add.171), channel_id=1, source_target_pairs={{0,2},{1,3},{2,0},{3,1},{4,6},{5,7},{6,4},{7,5},{8,10},{9,11},{10,... | collective-permute-start | bytes 122888 | tf_op jit(solution)/shard_map/ppermute | solution.py:14
  41.3 7.1 %collective-permute-start.6 = (f32[40,768]{1,0:T(8,128)S(1)}, f32[40,768]{1,0:T(8,128)S(1)}, u32[]{:S(2)}, u32[]{:S(2)}) collective-permute-start(f32[40,768]{1,0:T(8,128)S(1)} %add.149), channel_id=1, source_target_pairs={{0,6},{1,7},{2,4},{3,5},{4,2},{5,3},{6,0},{7,1},{8,14},{9,15},{10,... | collective-permute-start | bytes 368648 | tf_op jit(solution)/shard_map/ppermute | solution.py:14
  43.9 6.1 %collective-permute-start.5 = (f32[40,768]{1,0:T(8,128)S(1)}, f32[40,768]{1,0:T(8,128)S(1)}, u32[]{:S(2)}, u32[]{:S(2)}) collective-permute-start(f32[40,768]{1,0:T(8,128)S(1)} %add.149), channel_id=1, source_target_pairs={{0,4},{1,5},{2,6},{3,7},{4,0},{5,1},{6,2},{7,3},{8,12},{9,13},{10,... | collective-permute-start | bytes 368648 | tf_op jit(solution)/shard_map/ppermute | solution.py:14
  44.4 5.7 %collective-permute-start.4 = (f32[40,768]{1,0:T(8,128)S(1)}, f32[40,768]{1,0:T(8,128)S(1)}, u32[]{:S(2)}, u32[]{:S(2)}) collective-permute-start(f32[40,768]{1,0:T(8,128)S(1)} %add.149), channel_id=1, source_target_pairs={{0,2},{1,3},{2,0},{3,1},{4,6},{5,7},{6,4},{7,5},{8,10},{9,11},{10,... | collective-permute-start | bytes 368648 | tf_op jit(solution)/shard_map/ppermute | solution.py:14
  53.6 15.9 %copy-start.4 = (f32[16]{0:T(128)S(1)}, f32[16]{0:T(128)}, u32[]{:S(2)}) copy-start(f32[16]{0:T(128)} %param.16) | copy-start | bytes 196
  58.7 10.7 %all-to-all-start = ((bf16[4,16,896]{2,1,0:T(8,128)(2,1)}), bf16[4,16,896]{2,1,0:T(8,128)(2,1)S(1)}, u32[]{:S(2)}, u32[]{:S(2)}) async-start(bf16[4,16,896]{2,1,0:T(8,128)(2,1)} %pad_maximum_fusion.1), calls=%async_computation | async-start | bytes 229376 | tf_op jit(solution)/shard_map/all_to_all | solution.py:125
  69.8 11.7 %copy-start.3 = (f32[16,768]{1,0:T(8,128)}, f32[16,768]{1,0:T(8,128)S(1)}, u32[]{:S(2)}) copy-start(f32[16,768]{1,0:T(8,128)S(1)} %get-tuple-element.46) | copy-start | bytes 147460
  70.4 9.6 %all-to-all-start.1 = ((f32[32,1,128]{2,1,0:T(1,128)}), f32[32,1,128]{2,1,0:T(1,128)S(1)}, u32[]{:S(2)}, u32[]{:S(2)}) async-start(f32[32,1,128]{2,1,0:T(1,128)} %broadcast_in_dim.14), calls=%async_computation.1 | async-start | bytes 32768 | tf_op jit(solution)/shard_map/all_to_all | solution.py:139

commit v3 on v0

v3 whole, which is shorter than its diff:
```python
import functools
import math

import jax
import jax.numpy as jnp
from jax import lax
from jax.experimental import pallas as pl
from jax.experimental.pallas import tpu as pltpu
from jax.sharding import PartitionSpec as P

BF16 = jnp.bfloat16
F32 = jnp.float32
LANES = 128
NT = (((1,), (1,)), ((), ()))
VMEM = pl.BlockSpec(memory_space=pltpu.VMEM)
SMEM = pl.BlockSpec(memory_space=pltpu.SMEM)
ANY = pl.BlockSpec(memory_space=pl.ANY)
MIB = 1 << 20


def swap(values, axis, distance):
    size = lax.axis_size(axis)
    return lax.ppermute(values, axis, [(i, i ^ distance) for i in range(size)])


def halves(values):
    high = values.astype(BF16)
    return high, (values - high.astype(F32)).astype(BF16)


def thirds(values):
    high = values.astype(BF16)
    rest = values - high.astype(F32)
    middle = rest.astype(BF16)
    return high, middle, (rest - middle.astype(F32)).astype(BF16)


def lane_of(shape):
    return lax.broadcasted_iota(jnp.int32, shape, len(shape) - 1)


def columns(values, shape):
    lane = lane_of(shape)
    block = jnp.zeros(shape, F32)
    for q, column in enumerate(values):
        block = jnp.where(lane == q, column, block)
    return block


def to_column(row):
    shape = (16, LANES)
    same = lax.broadcasted_iota(jnp.int32, shape, 0) == lane_of(shape)
    return jnp.sum(jnp.where(same, row, 0.0), axis=1, keepdims=True)


def to_row(column):
    shape = (16, LANES)
    same = lax.broadcasted_iota(jnp.int32, shape, 0) == lane_of(shape)
    return jnp.sum(jnp.where(same, column, 0.0), axis=0, keepdims=True)


def pass_kernel(step_rows, order_ref, sol_ref, dir_ref, res_ref, gen_hbm, call_hbm, dose_hbm,
                coded_ref, called_ref, cross_ref, sums_ref, gbuf, cbuf, dbuf, sems, dsem):
    slots = gbuf.shape[0]
    rows = gen_hbm.shape[0]
    steps = rows // step_rows
    rhs = sol_ref.shape[0]

    def copies(step):
        slot = step % slots
        part = pl.ds(step * step_rows, step_rows)
        return (
            pltpu.make_async_copy(gen_hbm.at[part], gbuf.at[slot], sems.at[0, slot]),
            pltpu.make_async_copy(call_hbm.at[part], cbuf.at[slot], sems.at[1, slot]),
        )

    dose_copy = pltpu.make_async_copy(dose_hbm, dbuf, dsem)
    dose_copy.start()
    for step in range(slots):
        for copy in copies(step):
            copy.start()

    sol, dire, res = sol_ref[...], dir_ref[...], res_ref[...]
    total = lambda x: jnp.sum(x, axis=1, keepdims=True)
    sums_ref[...] = columns(
        [total(res * res), total(dire * dire), total(sol), total(sol * sol), total(sol * dire), total(dire)],
        sums_ref.shape,
    )
    sol_high, sol_low = halves(sol)
    dir_high, dir_low = halves(dire)
    stack = jnp.concatenate([sol_high, dir_high, sol_low, dir_low], axis=0)
    own = sol.shape[1]
    hot = lax.broadcasted_iota(jnp.int32, (own, own), 0) == order_ref[...]
    hot = jnp.where(hot, 1.0, 0.0).astype(BF16)
    picked = jnp.dot(stack, hot, preferred_element_type=F32).astype(BF16)
    picked = jnp.concatenate([picked, jnp.ones((16, own), BF16)], axis=0)
    dose_copy.wait()
    dose = dbuf[...].astype(F32).astype(BF16)
    cross = jnp.dot(picked, dose, preferred_element_type=F32)
    cross_ref[: 2 * rhs] = cross[: 2 * rhs] + cross[2 * rhs : 4 * rhs]
    cross_ref[2 * rhs :] = cross[4 * rhs : 4 * rhs + 8]

    for step in range(steps):
        slot = step % slots
        for copy in copies(step):
            copy.wait()

        def group(i, carry):
            part = pl.ds(pl.multiple_of(i * 16, 16), 16)
            out = pl.ds(pl.multiple_of(step * step_rows + i * 16, 16), 16)
            call = cbuf[slot, part, :]
            coded_ref[out, :] = (gbuf[slot, part, :] * call).astype(F32).astype(BF16)
            called_ref[out, :] = call.astype(F32).astype(BF16)
            return carry

        lax.fori_loop(0, step_rows // 16, group, 0)
        if step + slots < steps:
            for copy in copies(step + slots):
                copy.start()


def forward_kernel(block, place_ref, d0_ref, d1_ref, d2_ref, d3_ref, coded_ref, called_ref, sums_ref,
                   out_ref, w1, w2):
    var = place_ref[0]
    rhs, own = d0_ref.shape
    rows = coded_ref.shape[0]
    samples = coded_ref.shape[1]
    row = lax.broadcasted_iota(jnp.int32, (16, samples), 0)
    zero = jnp.zeros((16, samples), BF16)
    w1[16:32] = zero
    w1[32:48] = jnp.where(row == 0, 1.0, 0.0).astype(BF16)
    w2[0:16] = zero
    w2[32:48] = jnp.where(row == 1, 1.0, 0.0).astype(BF16)
    for k, ref in enumerate((d0_ref, d1_ref, d2_ref, d3_ref)):
        part = pl.ds(pl.multiple_of((var ^ k) * own, LANES), own)
        piece = ref[...].astype(BF16)
        w1[0:16, part] = piece
        w2[16:32, part] = piece
    for i in range(rows // block):
        part = pl.ds(i * block, block)
        got = lax.dot_general(coded_ref[part, :], w1[...], NT, preferred_element_type=F32)
        got = got + lax.dot_general(called_ref[part, :], w2[...], NT, preferred_element_type=F32)
        got = jnp.concatenate([got, jnp.zeros((block, LANES - got.shape[1]), F32)], axis=1)
        out_ref[:, i * block : (i + 1) * block] = got.T[: out_ref.shape[0]]
    out_ref[:, rows:] = jnp.zeros((out_ref.shape[0], LANES), F32)
    out_ref[0:16, rows:] = sums_ref[...]


def chunk_of(cross, start, n_var, width):
    wide = cross.shape[1] // n_var
    lane = lane_of((cross.shape[0], LANES))
    tile = (start // LANES) * LANES
    inside = start - tile
    block = jnp.zeros((cross.shape[0], LANES), F32)
    for v in range(n_var):
        piece = cross[:, pl.ds(pl.multiple_of(v * wide + tile, LANES), LANES)]
        turned = pltpu.roll(piece, (v * width - inside + LANES) % LANES, 1)
        block = jnp.where((lane >= v * width) & (lane < (v + 1) * width), turned, block)
    return block


def chips_kernel(n_var, width, place_ref, own_ref, other_ref, cross_ref, cross_other_ref,
                 total_ref, mine_ref, *rest):
    messages, (both,) = rest[:-1], rest[-1:]
    samp = place_ref[1]
    core = samp % 2
    chip = samp // 2
    rows = own_ref.shape[1] - LANES
    total = own_ref[...] + other_ref[...]
    total_ref[...] = total
    both[...] = cross_ref[...] + cross_other_ref[...]
    mine_ref[...] = chunk_of(both, samp * width, n_var, width)

    main = total[0:32, :rows].astype(BF16)
    counts = total[32:34, :rows]
    pieces = []
    for part in halves(counts):
        part = part.astype(F32)
        for which in range(2):
            for j in range(rows // LANES):
                pieces.append(part[which : which + 1, j * LANES : (j + 1) * LANES])
    while len(pieces) < 32:
        pieces.append(jnp.zeros((1, LANES), F32))
    counts = jnp.concatenate(pieces, axis=0).astype(BF16)
    sums = jnp.zeros((16, LANES), F32)
    for part, values in enumerate(thirds(total[0:16, rows:])):
        values = values.astype(F32)
        sums = sums + (pltpu.roll(values, 16 * part, 1) if part else values)
    for k, message in enumerate(messages):
        chunk = chunk_of(both, ((chip ^ (k + 1)) * 2 + core) * width, n_var, width)
        high, low = halves(chunk[0:32])
        dose = jnp.concatenate([p.astype(F32) for p in thirds(chunk[32:33])] + [jnp.zeros((13, LANES), F32)])
        message[:, :rows] = main
        message[:, rows : rows + LANES] = high
        message[:, rows + LANES : rows + 2 * LANES] = low
        message[:, rows + 2 * LANES : rows + 3 * LANES] = counts
        message[:, rows + 3 * LANES :] = jnp.concatenate([sums, dose], axis=0).astype(BF16)


def back_kernel(variants, width, n_arrived, place_ref, total_ref, mine_ref, coded_ref, called_ref, *rest):
    arrived, own_ref, messages = rest[:n_arrived], rest[n_arrived], rest[n_arrived + 1 :]
    var = place_ref[0]
    rows = total_ref.shape[1] - LANES
    lanes = lane_of((16, LANES))

    main = total_ref[0:32, :rows]
    allele, count = total_ref[32:33, :rows], total_ref[33:34, :rows]
    sums = total_ref[0:16, rows:]
    cross = mine_ref[0:32]
    dose = mine_ref[32:33]
    got_counts = jnp.zeros((32, LANES), F32)
    got_last = jnp.zeros((32, LANES), F32)
    for ref in arrived:
        main = main + ref[:, :rows].astype(F32)
        cross = cross + ref[:, rows : rows + LANES].astype(F32)
        cross = cross + ref[:, rows + LANES : rows + 2 * LANES].astype(F32)
        got_counts = got_counts + ref[:, rows + 2 * LANES : rows + 3 * LANES].astype(F32)
        got_last = got_last + ref[:, rows + 3 * LANES :].astype(F32)
    tiles = rows // LANES
    pick = lambda first: jnp.concatenate(
        [got_counts[first + j : first + j + 1] + got_counts[first + 2 * tiles + j : first + 2 * tiles + j + 1]
         for j in range(tiles)], axis=1
    )
    allele = allele + pick(0)
    count = count + pick(tiles)
    last = got_last[0:16]
    sums = sums + last + pltpu.roll(last, LANES - 16, 1) + pltpu.roll(last, LANES - 32, 1)
    dose = dose + got_last[16:17] + got_last[17:18] + got_last[18:19]

    frequency = (allele + 1.0) / (2.0 * count + 2.0)
    spread = jnp.sqrt(2.0 * frequency * (1.0 - frequency))
    loading = (main[0:16] - 2.0 * frequency * main[16:32]) / spread
    scaled = loading / spread
    scaled_a = scaled.astype(BF16)
    scaled_b = (-2.0 * frequency * scaled).astype(BF16)
    square = jnp.sum(loading * loading, axis=1, keepdims=True)
    sums = jnp.where(lanes < 6, sums, 0.0) + jnp.where(lanes == 6, square, 0.0)

    own = own_ref.shape[1] - 2 * LANES

    def term(p):
        part = pl.ds(pl.multiple_of(p * own, LANES), own)
        got = jnp.dot(scaled_a, coded_ref[:, part], preferred_element_type=F32)
        got = got + jnp.dot(scaled_b, called_ref[:, part], preferred_element_type=F32)
        return got / variants

    def segment(values, p):
        turned = pltpu.roll(values, (LANES - p * width) % LANES, 1)
        return jnp.where(lane_of(values.shape) < width, turned, 0.0)

    def cross_block(p, exact):
        chunk = segment(cross, p)
        sol, dire = chunk[0:16], chunk[16:32]
        if exact:
            return sol + pltpu.roll(dire, 32, 1)
        sol_high, sol_low = [x.astype(F32) for x in halves(sol)]
        dir_high, dir_low = [x.astype(F32) for x in halves(dire)]
        return (
            sol_high + pltpu.roll(dir_high, 32, 1) + pltpu.roll(sol_low, 64, 1) + pltpu.roll(dir_low, 96, 1)
        )

    row = lax.broadcasted_iota(jnp.int32, (16, LANES), 0)

    def sums_block(p, exact):
        own_dose = segment(jnp.broadcast_to(dose, (16, LANES)), p)
        own_dose = pltpu.roll(own_dose, 64, 1)
        if exact:
            return sums + jnp.where(row == 0, own_dose, 0.0)
        block = jnp.zeros((16, LANES), F32)
        for part, values in enumerate(thirds(sums)):
            values = values.astype(F32)
            block = block + (pltpu.roll(values, 16 * part, 1) if part else values)
        for part, values in enumerate(thirds(own_dose)):
            block = block + jnp.where(row == part, values.astype(F32), 0.0)
        return block

    for k, ref in enumerate(messages):
        p = var ^ (k + 1)
        ref[:, :own] = term(p).astype(BF16)
        ref[:, own : own + LANES] = cross_block(p, False).astype(BF16)
        ref[:, own + LANES :] = sums_block(p, False).astype(BF16)
    own_ref[:, :own] = term(var)
    own_ref[:, own : own + LANES] = cross_block(var, True)
    own_ref[:, own + LANES :] = sums_block(var, True)


def step_of(refs, noise_row, variants):
    got = refs[0][...]
    for ref in refs[1:]:
        got = got + ref[...].astype(F32)
    own = got.shape[1] - 2 * LANES
    back, cross, last = got[:, :own], got[:, own : own + LANES], got[:, own + LANES :]
    sums = last + pltpu.roll(last, LANES - 16, 1) + pltpu.roll(last, LANES - 32, 1)
    column = lambda q: sums[:, q : q + 1]
    noise = to_column(noise_row)
    curvature = noise * column(1) + column(6) / variants
    step = column(0) / (curvature + 1e-06)
    return back, cross, last, column, noise, step


def norm_kernel(variants, noise_ref, dir_ref, res_ref, *rest):
    out_ref = rest[-1]
    back, _, _, _, noise, step = step_of(rest[:-1], noise_ref[...], variants)
    new = res_ref[...] - step * (noise * dir_ref[...] + back)
    row = to_row(jnp.sum(new * new, axis=1, keepdims=True))
    out_ref[...] = jnp.broadcast_to(row[None], out_ref.shape)


def new_kernel(variants, samples, width, noise_ref, dir_ref, res_ref, sol_ref, *rest):
    refs, (sol_out, res_out, score_out, norm_out) = rest[:-4], rest[-4:]
    back, cross, last, column, noise, step = step_of(refs, noise_ref[...], variants)
    dire = dir_ref[...]
    sol_out[...] = sol_ref[...] + step * dire
    res_out[...] = res_ref[...] - step * (noise * dire + back)
    norm_out[...] = jnp.broadcast_to(column(0), norm_out.shape)
    cross = cross + pltpu.roll(cross, LANES - 64, 1)
    cross = cross + step * pltpu.roll(cross, LANES - 32, 1)
    dose = pltpu.roll(last, LANES - 64, 1)
    dose = dose[0:1] + dose[1:2] + dose[2:3]
    sol_sum = column(2) + step * column(5)
    sol_square = column(3) + 2.0 * step * column(4) + step * (step * column(1))
    dose_freq = (dose / 100.0 + 1.0) / (2.0 * samples + 2.0)
    dose_spread = jnp.sqrt(2.0 * dose_freq * (1.0 - dose_freq))
    scale = math.sqrt(samples) * jnp.sqrt(sol_square / samples + 1e-06)
    scores = (cross / 100.0 - 2.0 * dose_freq * sol_sum) / (dose_spread * scale)
    score_out[...] = scores[:, :width]


def direction_kernel(norms_ref, norm_ref, res_ref, dir_ref, out_ref):
    new_norm = to_column(jnp.sum(norms_ref[...], axis=0))
    out_ref[...] = res_ref[...] + (new_norm / (norm_ref[:, 0:1] + 1e-06)) * dir_ref[...]


def call(kernel, out, ins, args, scratch=(), limit=16, flops=0, moved=0):
    return pl.pallas_call(
        kernel,
        out_shape=[jax.ShapeDtypeStruct(*o) for o in out],
        in_specs=list(ins),
        out_specs=[VMEM] * len(out),
        scratch_shapes=list(scratch),
        compiler_params=pltpu.CompilerParams(vmem_limit_bytes=limit * MIB),
        cost_estimate=pl.CostEstimate(flops=flops, bytes_accessed=moved, transcendentals=0),
    )(*args)


def body(genotypes, called, dosage, sample_order, noise_ratio, solution, residual, direction):
    var = lax.axis_index("var").astype(jnp.int32)
    samp = lax.axis_index("samp").astype(jnp.int32)
    n_var = lax.axis_size("var")
    n_samp = lax.axis_size("samp")
    own, rhs = direction.shape
    rows, shard = genotypes.shape
    variants = rows * n_var
    samples = own * n_samp * n_var
    imputed = dosage.shape[1]
    width = imputed // (n_var * n_samp)
    place = jnp.stack([var, samp])
    noise = jnp.pad(noise_ratio, (0, LANES - rhs))[None]

    dire, res, sol = direction.T, residual.T, solution.T
    pieces = [dire] + [swap(dire, "var", k) for k in range(1, n_var)]

    step_rows = 128
    slots = 3
    coded, called_b, cross, sums = call(
        functools.partial(pass_kernel, step_rows),
        [((rows, shard), BF16), ((rows, shard), BF16), ((2 * rhs + 8, imputed), F32), ((rhs, LANES), F32)],
        [VMEM] * 4 + [ANY] * 3,
        (sample_order, sol, dire, res, genotypes, called, dosage),
        scratch=[
            pltpu.VMEM((slots, step_rows, shard), jnp.int32),
            pltpu.VMEM((slots, step_rows, shard), jnp.int32),
            pltpu.VMEM((own, imputed), jnp.int32),
            pltpu.SemaphoreType.DMA((2, slots)),
            pltpu.SemaphoreType.DMA,
        ],
        limit=32,
        flops=2 * 80 * own * (own + imputed),
        moved=4 * (2 * rows * shard + own * imputed),
    )
    cross_other = swap(cross, "samp", 1)

    (part,) = call(
        functools.partial(forward_kernel, 128),
        [((2 * rhs + 8, rows + LANES), F32)],
        [SMEM] + [VMEM] * (n_var + 3),
        (place, *pieces, coded, called_b, sums),
        scratch=[pltpu.VMEM((48, shard), BF16), pltpu.VMEM((48, shard), BF16)],
        flops=4 * rows * shard * 256,
        moved=4 * rows * shard,
    )
    part_other = swap(part, "samp", 1)

    n_chips = n_samp // 2
    message = ((2 * rhs, rows + 4 * LANES), BF16)
    total, mine, *messages = call(
        functools.partial(chips_kernel, n_var, width),
        [(part.shape, F32), ((2 * rhs + 8, LANES), F32)] + [message] * (n_chips - 1),
        [SMEM] + [VMEM] * 4,
        (place, part, part_other, cross, cross_other),
        scratch=[pltpu.VMEM(cross.shape, F32)],
        moved=1 * MIB,
    )
    arrived = [swap(m, "samp", 2 * (k + 1)) for k, m in enumerate(messages)]

    wide = own + 2 * LANES
    mine_back, *messages = call(
        functools.partial(back_kernel, variants, width, n_chips - 1),
        [((rhs, wide), F32)] + [((rhs, wide), BF16)] * (n_var - 1),
        [SMEM] + [VMEM] * (4 + n_chips - 1),
        (place, total, mine, coded, called_b, *arrived),
        flops=4 * rows * shard * 256,
        moved=4 * rows * shard,
    )
    backs = [mine_back] + [swap(m, "var", k + 1) for k, m in enumerate(messages)]

    n_all = n_var * n_samp
    (norms,) = call(
        functools.partial(norm_kernel, variants),
        [((n_all, 1, LANES), F32)],
        [VMEM] * (3 + n_var),
        (noise, dire, res, *backs),
        moved=4 * n_all * LANES,
    )
    norms = lax.all_to_all(norms, ("var", "samp"), split_axis=0, concat_axis=0)
    sol_new, res_new, scores, res_norm = call(
        functools.partial(new_kernel, variants, samples, width),
        [((rhs, own), F32), ((rhs, own), F32), ((rhs, width), F32), ((rhs, LANES), F32)],
        [VMEM] * (4 + n_var),
        (noise, dire, res, sol, *backs),
        moved=1 * MIB,
    )
    (dir_new,) = call(
        direction_kernel,
        [((rhs, own), F32)],
        [VMEM] * 4,
        (norms, res_norm, res_new, dire),
    )
    return (sol_new.T, res_new.T, dir_new.T, scores.T)


def solution(mesh):
    placed = (
        P("var", "samp"),
        P("var", "samp"),
        P(("samp", "var"), None),
        P(("samp", "var"), None),
        P(),
        P(("samp", "var"), None),
        P(("samp", "var"), None),
        P(("samp", "var"), None),
    )
    return jax.shard_map(
        body,
        mesh=mesh,
        in_specs=placed,
        out_specs=(
            P(("samp", "var"), None),
            P(("samp", "var"), None),
            P(("samp", "var"), None),
            P(("var", "samp"), None),
        ),
        check_vma=False,
    )
```

time: 277 us -> 66.6 us (0.24)
  blocking collectives: 118 us -> 0 us
  waiting for transfers between devices: 108 us -> 16.2 us
  other arithmetic: 19.2 us -> 0.07 us
  starting transfers between devices: 0.08 us -> 16.9 us
  local copies, waits for them, and re-layouts: 4.75 us -> 18.5 us
  Pallas kernels: 0 us -> 13.7 us
  between operations: 14.2 us -> 0.73 us
  matrix products: 12.9 us -> 0 us
    psum x3 -> x0, blocking collectives: 103 us -> none  [the longest x1 41.2 us: body(): lax.psum((res_square, jnp.sum(solution_new, axis=0), jnp.sum(solution_new...]
    unnamed x3 -> x0, waiting for transfers between devices: 90.8 us -> none
    reduce_scatter x1 -> x0, waiting for transfers between devices: 16.9 us -> none  [body(): lax.psum_scatter((term / VARIANTS).astype(jnp.bfloat16), 'var', scatter_d...]
    unnamed x24 -> x34, local copies, waits for them, and re-layouts: 2.71 us -> 18.5 us
    reduce_sum x5 -> x0, other arithmetic: 15.5 us -> none  [the longest x1 10.1 us: body(): allele_sum = jnp.sum(coded, axis=1).astype(jnp.float32)]
    all_gather x1 -> x0, blocking collectives: 15 us -> none  [body(): piece = lax.all_gather(direction_b, 'var', axis=0, tiled=True)]
    ppermute x0 -> x11, starting transfers between devices: none -> 14.2 us  [swap(): return lax.ppermute(values, axis, [(i, i ^ distance) for i in range(size)])]
    pallas_call x0 -> x7, Pallas kernels: none -> 13.7 us  [call(): pl.pallas_call(kernel, out_shape=[jax.ShapeDtypeStruct(*o) for o in out],...]
  transfers between devices with their start and end apart: 2 -> 12, of which waited for: 2 -> 8; matrix products, arithmetic and copies ran while one was open for 2% -> 0% of each run, Pallas kernels for 0% -> 14%
where the time goes in v3:
time: 66.6 us; the launch traced here: 66 us
  local copies, waits for them, and re-layouts  18.5 us (28%)
  starting transfers between devices  16.9 us (25%)
  waiting for transfers between devices  16.2 us (24%)
  Pallas kernels  13.7 us (21%)
  between operations  0.73 us (1%)
    unnamed x34, local copies, waits for them, and re-layouts  18.5 us
    ppermute x11, starting transfers between devices, swap(): return lax.ppermute(values, axis, [(i, i ^ distance) for i in range(size)])  14.2 us
    pallas_call x7, Pallas kernels, call(): pl.pallas_call(kernel, out_shape=[jax.ShapeDtypeStruct(*o) for o in out],...  13.7 us
    ppermute x11, waiting for transfers between devices, swap(): return lax.ppermute(values, axis, [(i, i ^ distance) for i in range(size)])  10.1 us
    all_to_all x1, waiting for transfers between devices, body(): norms = lax.all_to_all(norms, ('var', 'samp'), split_axis=0, concat_axis=0)  6.04 us
    all_to_all x1, starting transfers between devices, body(): norms = lax.all_to_all(norms, ('var', 'samp'), split_axis=0, concat_axis=0)  2.7 us
  transfers between devices with their start and end apart: 12, of which 8 were waited for; matrix products, arithmetic and copies ran while one was open for 0% of the time, Pallas kernels for 14%

profile of v3, /device:TPU:0, one launch (start us, length us, event | category | flops | bytes accessed | tf_op | source)
XLA Modules:
  0.0 66.0 jit_solution(13509536005665137802)
XLA Ops:
  0.6 3.1 %collective-permute-start = (f32[16,768]{1,0:T(8,128)}, f32[16,768]{1,0:T(8,128)S(1)}, u32[]{:S(2)}, u32[]{:S(2)}) collective-permute-start(f32[16,768]{1,0:T(8,128)} %bitcast.11), channel_id=1, source_target_pairs={{0,8},{8,0},{16,24},{24,16},{1,9},{9,1},{17,25},{25,17},{2,10},{10... | collective-permute-start | bytes 147464 | tf_op jit(solution)/shard_map/ppermute | solution.py:23
  3.7 2.6 %collective-permute-start.1 = (f32[16,768]{1,0:T(8,128)}, f32[16,768]{1,0:T(8,128)S(1)}, u32[]{:S(2)}, u32[]{:S(2)}) collective-permute-start(f32[16,768]{1,0:T(8,128)} %bitcast.12), channel_id=1, source_target_pairs={{0,16},{8,24},{16,0},{24,8},{1,17},{9,25},{17,1},{25,9},{2,18},{10... | collective-permute-start | bytes 147464 | tf_op jit(solution)/shard_map/ppermute | solution.py:23
  6.3 3.7 %copy-done.6 = s32[768,3072]{1,0:T(8,128)S(1)} copy-done((s32[768,3072]{1,0:T(8,128)S(1)}, s32[768,3072]{1,0:T(8,128)}, u32[]{:S(2)}) %copy-start.6) | copy-done | bytes 9437208
  10.0 1.9 %copy-done.7 = s32[768,1024]{1,0:T(8,128)S(1)} copy-done((s32[768,1024]{1,0:T(8,128)S(1)}, s32[768,1024]{1,0:T(8,128)}, u32[]{:S(2)}) %copy-start.7) | copy-done | bytes 3145752
  11.9 0.8 %copy-done.8 = f32[768,16]{0,1:T(8,128)S(1)} copy-done((f32[768,16]{0,1:T(8,128)S(1)}, f32[768,16]{0,1:T(8,128)}, u32[]{:S(2)}) %copy-start.8) | copy-done | bytes 49176
  12.7 0.8 %copy-done.10 = f32[768,16]{0,1:T(8,128)S(1)} copy-done((f32[768,16]{0,1:T(8,128)S(1)}, f32[768,16]{0,1:T(8,128)}, u32[]{:S(2)}) %copy-start.10) | copy-done | bytes 49176
  13.5 0.8 %copy-done.12 = f32[768,16]{0,1:T(8,128)S(1)} copy-done((f32[768,16]{0,1:T(8,128)S(1)}, f32[768,16]{0,1:T(8,128)}, u32[]{:S(2)}) %copy-start.12) | copy-done | bytes 49176
  15.0 5.0 %shard_map.111 = (bf16[768,3072]{1,0:T(8,128)(2,1)S(1)}, bf16[768,3072]{1,0:T(8,128)(2,1)S(1)}, f32[40,1024]{1,0:T(8,128)S(1)}, f32[16,128]{1,0:T(8,128)S(1)}) custom-call(s32[1,768]{1,0:T(1,128)S(1)} %copy-done.15, f32[16,768]{1,0:T(8,128)S(1)} %bitcast.22, f32[16,768]{1,0:T(8,128)S(1)} %bitcast.14, f32[16,768]{1,0:T(8,128)S(1)} %bitcast.19, ...), custom_call_target="tpu_custom_call" | custom-call | flops 220200960 | bytes 22020096 | tf_op jit(solution)/shard_map/pallas_call | solution.py:335
  20.0 2.1 %copy-done = bf16[768,3072]{1,0:T(8,128)(2,1)} copy-done((bf16[768,3072]{1,0:T(8,128)(2,1)}, bf16[768,3072]{1,0:T(8,128)(2,1)S(1)}, u32[]{:S(2)}) %copy-start) | copy-done | bytes 4718616
  22.2 2.2 %copy-done.3 = bf16[768,3072]{1,0:T(8,128)(2,1)} copy-done((bf16[768,3072]{1,0:T(8,128)(2,1)}, bf16[768,3072]{1,0:T(8,128)(2,1)S(1)}, u32[]{:S(2)}) %copy-start.3) | copy-done | bytes 4718616
  24.5 2.3 %copy-done.1 = bf16[768,3072]{1,0:T(8,128)(2,1)S(1)} copy-done((bf16[768,3072]{1,0:T(8,128)(2,1)S(1)}, bf16[768,3072]{1,0:T(8,128)(2,1)}, u32[]{:S(2)}) %copy-start.1) | copy-done | bytes 4718616
  26.8 2.3 %copy-done.4 = bf16[768,3072]{1,0:T(8,128)(2,1)S(1)} copy-done((bf16[768,3072]{1,0:T(8,128)(2,1)S(1)}, bf16[768,3072]{1,0:T(8,128)(2,1)}, u32[]{:S(2)}) %copy-start.4) | copy-done | bytes 4718616
  29.1 3.2 %shard_map.112.own_ref = f32[40,896]{1,0:T(8,128)S(1)} custom-call(s32[2]{0:T(128)S(1)} %pad_add_fusion.place_ref, f32[16,768]{1,0:T(8,128)S(1)} %bitcast.15, f32[16,768]{1,0:T(8,128)S(1)} %collective-permute-done.d1_ref, f32[16,768]{1,0:T(8,128)S(1)} %collective-permute-done.1.d2_ref, f32[16,768]{1,0:T(8,128)S(1)} %collective-permute-done.2.d3_ref, ...), custom_call_target="tpu_custom_call" | custom-call | flops 2415919104 | bytes 9437184 | tf_op jit(solution)/shard_map/pallas_call | solution.py:335
  32.9 1.0 %collective-permute-done.3.other_ref = f32[40,896]{1,0:T(8,128)S(1)} collective-permute-done((f32[40,896]{1,0:T(8,128)S(1)}, f32[40,896]{1,0:T(8,128)S(1)}, u32[]{:S(2)}, u32[]{:S(2)}) %collective-permute-start.3) | collective-permute-done | bytes 143392 | tf_op jit(solution)/shard_map/ppermute | solution.py:23
  33.9 0.8 %shard_map.113 = (f32[40,896]{1,0:T(8,128)S(1)}, f32[40,128]{1,0:T(8,128)S(1)}, bf16[32,1280]{1,0:T(8,128)(2,1)S(1)}, bf16[32,1280]{1,0:T(8,128)(2,1)S(1)}, bf16[32,1280]{1,0:T(8,128)(2,1)S(1)}) custom-call(s32[2]{0:T(128)S(1)} %pad_add_fusion.place_ref, f32[40,896]{1,0:T(8,128)S(1)} %shard_map.112.own_ref, f32[40,896]{1,0:T(8,128)S(1)} %collective-permute-done.3.other_ref, ...), custom_call_target="tpu_custom_call" | custom-call | bytes 1048576 | tf_op jit(solution)/shard_map/pallas_call | solution.py:335
  34.6 1.8 %collective-permute-start.5 = (bf16[32,1280]{1,0:T(8,128)(2,1)S(1)}, bf16[32,1280]{1,0:T(8,128)(2,1)S(1)}, u32[]{:S(2)}, u32[]{:S(2)}) collective-permute-start(bf16[32,1280]{1,0:T(8,128)(2,1)S(1)} %get-tuple-element.27), channel_id=1, source_target_pairs={{0,2},{1,3},{2,0},{3,1},{4,6},{5,7},{6,4},{7,5},{8,10},{9,11},{10,... | collective-permute-start | bytes 245768 | tf_op jit(solution)/shard_map/ppermute | solution.py:23
  36.4 1.5 %collective-permute-start.6 = (bf16[32,1280]{1,0:T(8,128)(2,1)S(1)}, bf16[32,1280]{1,0:T(8,128)(2,1)S(1)}, u32[]{:S(2)}, u32[]{:S(2)}) collective-permute-start(bf16[32,1280]{1,0:T(8,128)(2,1)S(1)} %get-tuple-element.28), channel_id=1, source_target_pairs={{0,4},{1,5},{2,6},{3,7},{4,0},{5,1},{6,2},{7,3},{8,12},{9,13},{10,... | collective-permute-start | bytes 245768 | tf_op jit(solution)/shard_map/ppermute | solution.py:23
  38.2 1.2 %collective-permute-done.5.rest_0_ = bf16[32,1280]{1,0:T(8,128)(2,1)S(1)} collective-permute-done((bf16[32,1280]{1,0:T(8,128)(2,1)S(1)}, bf16[32,1280]{1,0:T(8,128)(2,1)S(1)}, u32[]{:S(2)}, u32[]{:S(2)}) %collective-permute-start.5) | collective-permute-done | bytes 81952 | tf_op jit(solution)/shard_map/ppermute | solution.py:23
  39.4 2.3 %collective-permute-done.6.rest_1_ = bf16[32,1280]{1,0:T(8,128)(2,1)S(1)} collective-permute-done((bf16[32,1280]{1,0:T(8,128)(2,1)S(1)}, bf16[32,1280]{1,0:T(8,128)(2,1)S(1)}, u32[]{:S(2)}, u32[]{:S(2)}) %collective-permute-start.6) | collective-permute-done | bytes 81952 | tf_op jit(solution)/shard_map/ppermute | solution.py:23
  41.7 1.6 %collective-permute-done.7.rest_2_ = bf16[32,1280]{1,0:T(8,128)(2,1)S(1)} collective-permute-done((bf16[32,1280]{1,0:T(8,128)(2,1)S(1)}, bf16[32,1280]{1,0:T(8,128)(2,1)S(1)}, u32[]{:S(2)}, u32[]{:S(2)}) %collective-permute-start.7) | collective-permute-done | bytes 81952 | tf_op jit(solution)/shard_map/ppermute | solution.py:23
  43.3 1.9 %shard_map.114 = (f32[16,1024]{1,0:T(8,128)S(1)}, bf16[16,1024]{1,0:T(8,128)(2,1)S(1)}, bf16[16,1024]{1,0:T(8,128)(2,1)S(1)}, bf16[16,1024]{1,0:T(8,128)(2,1)S(1)}) custom-call(s32[2]{0:T(128)S(1)} %pad_add_fusion.place_ref, f32[40,896]{1,0:T(8,128)S(1)} %get-tuple-element.25.total_ref, f32[40,128]{1,0:T(8,128)S(1)} %get-tuple-element.26.mine_ref, ...), custom_call_target="tpu_custom_call" | custom-call | flops 2415919104 | bytes 9437184 | tf_op jit(solution)/shard_map/pallas_call | solution.py:335
  45.2 3.6 %collective-permute-start.10 = (bf16[16,1024]{1,0:T(8,128)(2,1)S(1)}, bf16[16,1024]{1,0:T(8,128)(2,1)S(1)}, u32[]{:S(2)}, u32[]{:S(2)}) collective-permute-start(bf16[16,1024]{1,0:T(8,128)(2,1)S(1)} %get-tuple-element.33), channel_id=1, source_target_pairs={{0,24},{8,16},{16,8},{24,0},{1,25},{9,17},{17,9},{25,1},{2,26},{10... | collective-permute-start | bytes 98312 | tf_op jit(solution)/shard_map/ppermute | solution.py:23
  48.8 0.8 %collective-permute-start.9 = (bf16[16,1024]{1,0:T(8,128)(2,1)S(1)}, bf16[16,1024]{1,0:T(8,128)(2,1)S(1)}, u32[]{:S(2)}, u32[]{:S(2)}) collective-permute-start(bf16[16,1024]{1,0:T(8,128)(2,1)S(1)} %get-tuple-element.32), channel_id=1, source_target_pairs={{0,16},{8,24},{16,0},{24,8},{1,17},{9,25},{17,1},{25,9},{2,18},{10... | collective-permute-start | bytes 98312 | tf_op jit(solution)/shard_map/ppermute | solution.py:23
  49.6 1.3 %collective-permute-done.10.rest_3_ = bf16[16,1024]{1,0:T(8,128)(2,1)S(1)} collective-permute-done((bf16[16,1024]{1,0:T(8,128)(2,1)S(1)}, bf16[16,1024]{1,0:T(8,128)(2,1)S(1)}, u32[]{:S(2)}, u32[]{:S(2)}) %collective-permute-start.10) | collective-permute-done | bytes 32800 | tf_op jit(solution)/shard_map/ppermute | solution.py:23
  50.9 1.8 %collective-permute-done.8.rest_1_ = bf16[16,1024]{1,0:T(8,128)(2,1)S(1)} collective-permute-done((bf16[16,1024]{1,0:T(8,128)(2,1)S(1)}, bf16[16,1024]{1,0:T(8,128)(2,1)S(1)}, u32[]{:S(2)}, u32[]{:S(2)}) %collective-permute-start.8) | collective-permute-done | bytes 32800 | tf_op jit(solution)/shard_map/ppermute | solution.py:23
  52.7 0.9 %collective-permute-done.9.rest_2_ = bf16[16,1024]{1,0:T(8,128)(2,1)S(1)} collective-permute-done((bf16[16,1024]{1,0:T(8,128)(2,1)S(1)}, bf16[16,1024]{1,0:T(8,128)(2,1)S(1)}, u32[]{:S(2)}, u32[]{:S(2)}) %collective-permute-start.9) | collective-permute-done | bytes 32800 | tf_op jit(solution)/shard_map/ppermute | solution.py:23
  53.6 1.0 %shard_map.116 = f32[32,1,128]{2,1,0:T(1,128)} custom-call(f32[1,128]{1,0:T(1,128)S(1)} %pad_bitcast_fusion.noise_ref, f32[16,768]{1,0:T(8,128)S(1)} %bitcast.16, f32[16,768]{1,0:T(8,128)S(1)} %bitcast.20, f32[16,1024]{1,0:T(8,128)S(1)} %get-tuple-element.30.rest_0_, bf16[16,1024]{1,0:T(8,128)(2,1)S(1)} %collective-permute-done.8.rest_1_, ...), custom_call_target="tpu_custom_call" | custom-call | bytes 16384 | tf_op jit(solution)/shard_map/pallas_call | solution.py:335
  54.6 2.7 %all-to-all-start = ((f32[32,1,128]{2,1,0:T(1,128)}), f32[32,1,128]{2,1,0:T(1,128)S(1)}, u32[]{:S(2)}, u32[]{:S(2)}) async-start(f32[32,1,128]{2,1,0:T(1,128)} %shard_map.116), calls=%async_computation | async-start | bytes 32768 | tf_op jit(solution)/shard_map/all_to_all | solution.py:425
  57.4 1.0 %shard_map.115 = (f32[16,768]{1,0:T(8,128)}, f32[16,768]{1,0:T(8,128)}, f32[16,32]{1,0:T(8,128)}, f32[16,128]{1,0:T(8,128)S(1)}) custom-call(f32[1,128]{1,0:T(1,128)S(1)} %pad_bitcast_fusion.noise_ref, f32[16,768]{1,0:T(8,128)S(1)} %bitcast.17, f32[16,768]{1,0:T(8,128)S(1)} %bitcast.21, f32[16,768]{1,0:T(8,128)S(1)} %bitcast.23, ...), custom_call_target="tpu_custom_call" | custom-call | bytes 1048576 | tf_op jit(solution)/shard_map/pallas_call | solution.py:335
  58.4 6.0 %all-to-all-done.norms_ref = f32[32,1,128]{2,1,0:T(1,128)S(1)} async-done(((f32[32,1,128]{2,1,0:T(1,128)}), f32[32,1,128]{2,1,0:T(1,128)S(1)}, u32[]{:S(2)}, u32[]{:S(2)}) %all-to-all-start) | async-done | bytes 16416 | tf_op jit(solution)/shard_map/all_to_all | solution.py:425
  64.4 0.8 %copy-done.14 = f32[16,768]{1,0:T(8,128)S(1)} copy-done((f32[16,768]{1,0:T(8,128)S(1)}, f32[16,768]{1,0:T(8,128)}, u32[]{:S(2)}) %copy-start.14) | copy-done | bytes 49176
  65.2 0.8 %shard_map.117 = f32[16,768]{1,0:T(8,128)} custom-call(f32[32,1,128]{2,1,0:T(1,128)S(1)} %all-to-all-done.norms_ref, f32[16,128]{1,0:T(8,128)S(1)} %get-tuple-element.36.norm_ref, f32[16,768]{1,0:T(8,128)S(1)} %copy-done.14, f32[16,768]{1,0:T(8,128)S(1)} %bitcast.18), custom_call_target="tpu_custom_call" | custom-call | tf_op jit(solution)/shard_map/pallas_call | solution.py:335
  (35 shorter events, 1.6 us)
Async XLA Ops:
  0.6 23.8 %collective-permute-start = (f32[16,768]{1,0:T(8,128)}, f32[16,768]{1,0:T(8,128)S(1)}, u32[]{:S(2)}, u32[]{:S(2)}) collective-permute-start(f32[16,768]{1,0:T(8,128)} %bitcast.11), channel_id=1, source_target_pairs={{0,8},{8,0},{16,24},{24,16},{1,9},{9,1},{17,25},{25,17},{2,10},{10... | collective-permute-start | bytes 147464 | tf_op jit(solution)/shard_map/ppermute | solution.py:23
  3.7 20.7 %collective-permute-start.1 = (f32[16,768]{1,0:T(8,128)}, f32[16,768]{1,0:T(8,128)S(1)}, u32[]{:S(2)}, u32[]{:S(2)}) collective-permute-start(f32[16,768]{1,0:T(8,128)} %bitcast.12), channel_id=1, source_target_pairs={{0,16},{8,24},{16,0},{24,8},{1,17},{9,25},{17,1},{25,9},{2,18},{10... | collective-permute-start | bytes 147464 | tf_op jit(solution)/shard_map/ppermute | solution.py:23
  6.3 18.1 %collective-permute-start.2 = (f32[16,768]{1,0:T(8,128)}, f32[16,768]{1,0:T(8,128)S(1)}, u32[]{:S(2)}, u32[]{:S(2)}) collective-permute-start(f32[16,768]{1,0:T(8,128)} %bitcast.13), channel_id=1, source_target_pairs={{0,24},{8,16},{16,8},{24,0},{1,25},{9,17},{17,9},{25,1},{2,26},{10... | collective-permute-start | bytes 147464 | tf_op jit(solution)/shard_map/ppermute | solution.py:23
  6.3 3.7 %copy-start.6 = (s32[768,3072]{1,0:T(8,128)S(1)}, s32[768,3072]{1,0:T(8,128)}, u32[]{:S(2)}) copy-start(s32[768,3072]{1,0:T(8,128)} %gen_hbm.1) | copy-start | bytes 28311556
  10.0 1.9 %copy-start.7 = (s32[768,1024]{1,0:T(8,128)S(1)}, s32[768,1024]{1,0:T(8,128)}, u32[]{:S(2)}) copy-start(s32[768,1024]{1,0:T(8,128)} %dose_hbm.1) | copy-start | bytes 9437188
  11.9 0.8 %copy-start.8 = (f32[768,16]{0,1:T(8,128)S(1)}, f32[768,16]{0,1:T(8,128)}, u32[]{:S(2)}) copy-start(f32[768,16]{0,1:T(8,128)} %param.15) | copy-start | bytes 147460
  12.7 0.8 %copy-start.10 = (f32[768,16]{0,1:T(8,128)S(1)}, f32[768,16]{0,1:T(8,128)}, u32[]{:S(2)}) copy-start(f32[768,16]{0,1:T(8,128)} %param.14) | copy-start | bytes 147460
  13.5 0.8 %copy-start.12 = (f32[768,16]{0,1:T(8,128)S(1)}, f32[768,16]{0,1:T(8,128)}, u32[]{:S(2)}) copy-start(f32[768,16]{0,1:T(8,128)} %param.13) | copy-start | bytes 147460
  14.3 0.7 %copy-start.15 = (s32[1,768]{1,0:T(1,128)S(1)}, s32[1,768]{1,0:T(1,128)}, u32[]{:S(2)}) copy-start(s32[1,768]{1,0:T(1,128)} %order_ref.1) | copy-start | bytes 9220
  15.0 9.5 %copy-start.9 = (f32[768,16]{0,1:T(8,128)S(1)}, f32[768,16]{0,1:T(8,128)}, u32[]{:S(2)}) copy-start(f32[768,16]{0,1:T(8,128)} %param.15) | copy-start | bytes 147460
  20.0 2.1 %copy-start = (bf16[768,3072]{1,0:T(8,128)(2,1)}, bf16[768,3072]{1,0:T(8,128)(2,1)S(1)}, u32[]{:S(2)}) copy-start(bf16[768,3072]{1,0:T(8,128)(2,1)S(1)} %get-tuple-element.21.coded_ref) | copy-start | bytes 14155780
  22.2 2.2 %copy-start.3 = (bf16[768,3072]{1,0:T(8,128)(2,1)}, bf16[768,3072]{1,0:T(8,128)(2,1)S(1)}, u32[]{:S(2)}) copy-start(bf16[768,3072]{1,0:T(8,128)(2,1)S(1)} %get-tuple-element.22.called_ref) | copy-start | bytes 14155780
  24.3 8.5 %collective-permute-start.4 = (f32[40,1024]{1,0:T(8,128)S(1)}, f32[40,1024]{1,0:T(8,128)S(1)}, u32[]{:S(2)}, u32[]{:S(2)}) collective-permute-start(f32[40,1024]{1,0:T(8,128)S(1)} %get-tuple-element.24.cross_ref), channel_id=1, source_target_pairs={{0,1},{1,0},{2,3},{3,2},{4,5},{5,4},{6,7},{7,6},{8,9},{9,8},{10,11... | collective-permute-start | bytes 491528 | tf_op jit(solution)/shard_map/ppermute | solution.py:23
  24.4 2.3 %copy-start.1 = (bf16[768,3072]{1,0:T(8,128)(2,1)S(1)}, bf16[768,3072]{1,0:T(8,128)(2,1)}, u32[]{:S(2)}) copy-start(bf16[768,3072]{1,0:T(8,128)(2,1)} %copy-done) | copy-start | bytes 14155780
  26.8 2.3 %copy-start.4 = (bf16[768,3072]{1,0:T(8,128)(2,1)S(1)}, bf16[768,3072]{1,0:T(8,128)(2,1)}, u32[]{:S(2)}) copy-start(bf16[768,3072]{1,0:T(8,128)(2,1)} %copy-done.3) | copy-start | bytes 14155780
  29.1 14.1 %copy-start.2 = (bf16[768,3072]{1,0:T(8,128)(2,1)S(1)}, bf16[768,3072]{1,0:T(8,128)(2,1)}, u32[]{:S(2)}) copy-start(bf16[768,3072]{1,0:T(8,128)(2,1)} %copy-done) | copy-start | bytes 14155780
  29.1 14.1 %copy-start.5 = (bf16[768,3072]{1,0:T(8,128)(2,1)S(1)}, bf16[768,3072]{1,0:T(8,128)(2,1)}, u32[]{:S(2)}) copy-start(bf16[768,3072]{1,0:T(8,128)(2,1)} %copy-done.3) | copy-start | bytes 14155780
  32.3 1.5 %collective-permute-start.3 = (f32[40,896]{1,0:T(8,128)S(1)}, f32[40,896]{1,0:T(8,128)S(1)}, u32[]{:S(2)}, u32[]{:S(2)}) collective-permute-start(f32[40,896]{1,0:T(8,128)S(1)} %shard_map.112.own_ref), channel_id=1, source_target_pairs={{0,1},{1,0},{2,3},{3,2},{4,5},{5,4},{6,7},{7,6},{8,9},{9,8},{10,11... | collective-permute-start | bytes 430088 | tf_op jit(solution)/shard_map/ppermute | solution.py:23
  34.6 4.8 %collective-permute-start.5 = (bf16[32,1280]{1,0:T(8,128)(2,1)S(1)}, bf16[32,1280]{1,0:T(8,128)(2,1)S(1)}, u32[]{:S(2)}, u32[]{:S(2)}) collective-permute-start(bf16[32,1280]{1,0:T(8,128)(2,1)S(1)} %get-tuple-element.27), channel_id=1, source_target_pairs={{0,2},{1,3},{2,0},{3,1},{4,6},{5,7},{6,4},{7,5},{8,10},{9,11},{10,... | collective-permute-start | bytes 245768 | tf_op jit(solution)/shard_map/ppermute | solution.py:23
  36.4 5.3 %collective-permute-start.6 = (bf16[32,1280]{1,0:T(8,128)(2,1)S(1)}, bf16[32,1280]{1,0:T(8,128)(2,1)S(1)}, u32[]{:S(2)}, u32[]{:S(2)}) collective-permute-start(bf16[32,1280]{1,0:T(8,128)(2,1)S(1)} %get-tuple-element.28), channel_id=1, source_target_pairs={{0,4},{1,5},{2,6},{3,7},{4,0},{5,1},{6,2},{7,3},{8,12},{9,13},{10,... | collective-permute-start | bytes 245768 | tf_op jit(solution)/shard_map/ppermute | solution.py:23
  37.9 5.3 %collective-permute-start.7 = (bf16[32,1280]{1,0:T(8,128)(2,1)S(1)}, bf16[32,1280]{1,0:T(8,128)(2,1)S(1)}, u32[]{:S(2)}, u32[]{:S(2)}) collective-permute-start(bf16[32,1280]{1,0:T(8,128)(2,1)S(1)} %get-tuple-element.29), channel_id=1, source_target_pairs={{0,6},{1,7},{2,4},{3,5},{4,2},{5,3},{6,0},{7,1},{8,14},{9,15},{10,... | collective-permute-start | bytes 245768 | tf_op jit(solution)/shard_map/ppermute | solution.py:23
  43.3 6.3 %copy-start.16 = (f32[16]{0:T(128)S(1)}, f32[16]{0:T(128)}, u32[]{:S(2)}) copy-start(f32[16]{0:T(128)} %param.12) | copy-start | bytes 196
  43.3 10.4 %copy-start.11 = (f32[768,16]{0,1:T(8,128)S(1)}, f32[768,16]{0,1:T(8,128)}, u32[]{:S(2)}) copy-start(f32[768,16]{0,1:T(8,128)} %param.14) | copy-start | bytes 147460
  43.3 14.1 %copy-start.13 = (f32[768,16]{0,1:T(8,128)S(1)}, f32[768,16]{0,1:T(8,128)}, u32[]{:S(2)}) copy-start(f32[768,16]{0,1:T(8,128)} %param.13) | copy-start | bytes 147460
  45.2 5.7 %collective-permute-start.10 = (bf16[16,1024]{1,0:T(8,128)(2,1)S(1)}, bf16[16,1024]{1,0:T(8,128)(2,1)S(1)}, u32[]{:S(2)}, u32[]{:S(2)}) collective-permute-start(bf16[16,1024]{1,0:T(8,128)(2,1)S(1)} %get-tuple-element.33), channel_id=1, source_target_pairs={{0,24},{8,16},{16,8},{24,0},{1,25},{9,17},{17,9},{25,1},{2,26},{10... | collective-permute-start | bytes 98312 | tf_op jit(solution)/shard_map/ppermute | solution.py:23
  48.8 3.9 %collective-permute-start.8 = (bf16[16,1024]{1,0:T(8,128)(2,1)S(1)}, bf16[16,1024]{1,0:T(8,128)(2,1)S(1)}, u32[]{:S(2)}, u32[]{:S(2)}) collective-permute-start(bf16[16,1024]{1,0:T(8,128)(2,1)S(1)} %get-tuple-element.31), channel_id=1, source_target_pairs={{0,8},{8,0},{16,24},{24,16},{1,9},{9,1},{17,25},{25,17},{2,10},{10... | collective-permute-start | bytes 98312 | tf_op jit(solution)/shard_map/ppermute | solution.py:23
  48.8 4.8 %collective-permute-start.9 = (bf16[16,1024]{1,0:T(8,128)(2,1)S(1)}, bf16[16,1024]{1,0:T(8,128)(2,1)S(1)}, u32[]{:S(2)}, u32[]{:S(2)}) collective-permute-start(bf16[16,1024]{1,0:T(8,128)(2,1)S(1)} %get-tuple-element.32), channel_id=1, source_target_pairs={{0,16},{8,24},{16,0},{24,8},{1,17},{9,25},{17,1},{25,9},{2,18},{10... | collective-permute-start | bytes 98312 | tf_op jit(solution)/shard_map/ppermute | solution.py:23
  54.6 9.8 %all-to-all-start = ((f32[32,1,128]{2,1,0:T(1,128)}), f32[32,1,128]{2,1,0:T(1,128)S(1)}, u32[]{:S(2)}, u32[]{:S(2)}) async-start(f32[32,1,128]{2,1,0:T(1,128)} %shard_map.116), calls=%async_computation | async-start | bytes 32768 | tf_op jit(solution)/shard_map/all_to_all | solution.py:425
  64.4 0.8 %copy-start.14 = (f32[16,768]{1,0:T(8,128)S(1)}, f32[16,768]{1,0:T(8,128)}, u32[]{:S(2)}) copy-start(f32[16,768]{1,0:T(8,128)} %get-tuple-element.35.res_ref) | copy-start | bytes 147460

commit v4 on v3

--- a/solution.py
+++ b/solution.py
@@ -13,8 +13,7 @@
 LANES = 128
 NT = (((1,), (1,)), ((), ()))
 VMEM = pl.BlockSpec(memory_space=pltpu.VMEM)
-SMEM = pl.BlockSpec(memory_space=pltpu.SMEM)
-ANY = pl.BlockSpec(memory_space=pl.ANY)
+HBM = pl.BlockSpec(memory_space=pltpu.HBM)
 MIB = 1 << 20
 
 
@@ -48,7 +47,7 @@
 
 
 def to_column(row):
-    shape = (16, LANES)
+    shape = (16, row.shape[1])
     same = lax.broadcasted_iota(jnp.int32, shape, 0) == lane_of(shape)
     return jnp.sum(jnp.where(same, row, 0.0), axis=1, keepdims=True)
 
@@ -59,12 +58,13 @@
     return jnp.sum(jnp.where(same, column, 0.0), axis=0, keepdims=True)
 
 
-def pass_kernel(step_rows, order_ref, sol_ref, dir_ref, res_ref, gen_hbm, call_hbm, dose_hbm,
-                coded_ref, called_ref, cross_ref, sums_ref, gbuf, cbuf, dbuf, sems, dsem):
+def pass_kernel(step_rows, order_hbm, sol_hbm, dir_hbm, res_hbm, gen_hbm, call_hbm, dose_hbm,
+                coded_ref, called_ref, cross_ref, sums_ref, gbuf, cbuf, dbuf, order_ref, sol_ref, dir_ref, res_ref,
+                sems, small_sems):
     slots = gbuf.shape[0]
     rows = gen_hbm.shape[0]
     steps = rows // step_rows
-    rhs = sol_ref.shape[0]
+    rhs = sol_hbm.shape[0]
 
     def copies(step):
         slot = step % slots
@@ -74,12 +74,20 @@
             pltpu.make_async_copy(call_hbm.at[part], cbuf.at[slot], sems.at[1, slot]),
         )
 
-    dose_copy = pltpu.make_async_copy(dose_hbm, dbuf, dsem)
-    dose_copy.start()
+    small = [
+        pltpu.make_async_copy(source, target, small_sems.at[i])
+        for i, (source, target) in enumerate(
+            ((order_hbm, order_ref), (sol_hbm, sol_ref), (dir_hbm, dir_ref), (res_hbm, res_ref), (dose_hbm, dbuf))
+        )
+    ]
+    for copy in small:
+        copy.start()
     for step in range(slots):
         for copy in copies(step):
             copy.start()
 
+    for copy in small[:4]:
+        copy.wait()
     sol, dire, res = sol_ref[...], dir_ref[...], res_ref[...]
     total = lambda x: jnp.sum(x, axis=1, keepdims=True)
     sums_ref[...] = columns(
@@ -94,7 +102,7 @@
     hot = jnp.where(hot, 1.0, 0.0).astype(BF16)
     picked = jnp.dot(stack, hot, preferred_element_type=F32).astype(BF16)
     picked = jnp.concatenate([picked, jnp.ones((16, own), BF16)], axis=0)
-    dose_copy.wait()
+    small[4].wait()
     dose = dbuf[...].astype(F32).astype(BF16)
     cross = jnp.dot(picked, dose, preferred_element_type=F32)
     cross_ref[: 2 * rhs] = cross[: 2 * rhs] + cross[2 * rhs : 4 * rhs]
@@ -119,10 +127,10 @@
                 copy.start()
 
 
-def forward_kernel(block, place_ref, d0_ref, d1_ref, d2_ref, d3_ref, coded_ref, called_ref, sums_ref,
+def forward_kernel(block, d0_ref, d1_ref, d2_ref, d3_ref, coded_ref, called_ref, sums_ref,
                    out_ref, w1, w2):
-    var = place_ref[0]
-    rhs, own = d0_ref.shape
+    var = lax.axis_index("var")
+    own = d0_ref.shape[1]
     rows = coded_ref.shape[0]
     samples = coded_ref.shape[1]
     row = lax.broadcasted_iota(jnp.int32, (16, samples), 0)
@@ -159,10 +167,10 @@
     return block
 
 
-def chips_kernel(n_var, width, place_ref, own_ref, other_ref, cross_ref, cross_other_ref,
+def chips_kernel(n_var, width, own_ref, other_ref, cross_ref, cross_other_ref,
                  total_ref, mine_ref, *rest):
     messages, (both,) = rest[:-1], rest[-1:]
-    samp = place_ref[1]
+    samp = lax.axis_index("samp")
     core = samp % 2
     chip = samp // 2
     rows = own_ref.shape[1] - LANES
@@ -197,9 +205,9 @@
         message[:, rows + 3 * LANES :] = jnp.concatenate([sums, dose], axis=0).astype(BF16)
 
 
-def back_kernel(variants, width, n_arrived, place_ref, total_ref, mine_ref, coded_ref, called_ref, *rest):
+def back_kernel(variants, width, n_arrived, total_ref, mine_ref, coded_ref, called_ref, *rest):
     arrived, own_ref, messages = rest[:n_arrived], rest[n_arrived], rest[n_arrived + 1 :]
-    var = place_ref[0]
+    var = lax.axis_index("var")
     rows = total_ref.shape[1] - LANES
     lanes = lane_of((16, LANES))
 
@@ -299,9 +307,10 @@
 
 
 def norm_kernel(variants, noise_ref, dir_ref, res_ref, *rest):
-    out_ref = rest[-1]
-    back, _, _, _, noise, step = step_of(rest[:-1], noise_ref[...], variants)
+    refs, (out_ref, new_ref) = rest[:-2], rest[-2:]
+    back, _, _, _, noise, step = step_of(refs, noise_ref[...], variants)
     new = res_ref[...] - step * (noise * dir_ref[...] + back)
+    new_ref[...] = new
     row = to_row(jnp.sum(new * new, axis=1, keepdims=True))
     out_ref[...] = jnp.broadcast_to(row[None], out_ref.shape)
 
@@ -334,18 +343,16 @@
 def call(kernel, out, ins, args, scratch=(), limit=16, flops=0, moved=0):
     return pl.pallas_call(
         kernel,
-        out_shape=[jax.ShapeDtypeStruct(*o) for o in out],
+        out_shape=[jax.ShapeDtypeStruct(*o) if len(o) == 2 else o[2](*o[:2]) for o in out],
         in_specs=list(ins),
         out_specs=[VMEM] * len(out),
         scratch_shapes=list(scratch),
         compiler_params=pltpu.CompilerParams(vmem_limit_bytes=limit * MIB),
         cost_estimate=pl.CostEstimate(flops=flops, bytes_accessed=moved, transcendentals=0),
-    )(*args)
+    )(*[pltpu.with_memory_space_constraint(x, pltpu.HBM) if spec is HBM else x for spec, x in zip(ins, args)])
 
 
 def body(genotypes, called, dosage, sample_order, noise_ratio, solution, residual, direction):
-    var = lax.axis_index("var").astype(jnp.int32)
-    samp = lax.axis_index("samp").astype(jnp.int32)
     n_var = lax.axis_size("var")
     n_samp = lax.axis_size("samp")
     own, rhs = direction.shape
@@ -354,8 +361,7 @@
     samples = own * n_samp * n_var
     imputed = dosage.shape[1]
     width = imputed // (n_var * n_samp)
-    place = jnp.stack([var, samp])
-    noise = jnp.pad(noise_ratio, (0, LANES - rhs))[None]
+    noise = noise_ratio[None]
 
     dire, res, sol = direction.T, residual.T, solution.T
     pieces = [dire] + [swap(dire, "var", k) for k in range(1, n_var)]
@@ -364,15 +370,19 @@
     slots = 3
     coded, called_b, cross, sums = call(
         functools.partial(pass_kernel, step_rows),
-        [((rows, shard), BF16), ((rows, shard), BF16), ((2 * rhs + 8, imputed), F32), ((rhs, LANES), F32)],
-        [VMEM] * 4 + [ANY] * 3,
+        [((rows, shard), BF16, pltpu.VMEM), ((rows, shard), BF16, pltpu.VMEM), ((2 * rhs + 8, imputed), F32), ((rhs, LANES), F32)],
+        [HBM] * 7,
         (sample_order, sol, dire, res, genotypes, called, dosage),
         scratch=[
             pltpu.VMEM((slots, step_rows, shard), jnp.int32),
             pltpu.VMEM((slots, step_rows, shard), jnp.int32),
             pltpu.VMEM((own, imputed), jnp.int32),
+            pltpu.VMEM((1, own), jnp.int32),
+            pltpu.VMEM((rhs, own), F32),
+            pltpu.VMEM((rhs, own), F32),
+            pltpu.VMEM((rhs, own), F32),
             pltpu.SemaphoreType.DMA((2, slots)),
-            pltpu.SemaphoreType.DMA,
+            pltpu.SemaphoreType.DMA((5,)),
         ],
         limit=32,
         flops=2 * 80 * own * (own + imputed),
@@ -383,8 +393,8 @@
     (part,) = call(
         functools.partial(forward_kernel, 128),
         [((2 * rhs + 8, rows + LANES), F32)],
-        [SMEM] + [VMEM] * (n_var + 3),
-        (place, *pieces, coded, called_b, sums),
+        [VMEM] * (n_var + 3),
+        (*pieces, coded, called_b, sums),
         scratch=[pltpu.VMEM((48, shard), BF16), pltpu.VMEM((48, shard), BF16)],
         flops=4 * rows * shard * 256,
         moved=4 * rows * shard,
@@ -396,8 +406,8 @@
     total, mine, *messages = call(
         functools.partial(chips_kernel, n_var, width),
         [(part.shape, F32), ((2 * rhs + 8, LANES), F32)] + [message] * (n_chips - 1),
-        [SMEM] + [VMEM] * 4,
-        (place, part, part_other, cross, cross_other),
+        [VMEM] * 4,
+        (part, part_other, cross, cross_other),
         scratch=[pltpu.VMEM(cross.shape, F32)],
         moved=1 * MIB,
     )
@@ -407,17 +417,17 @@
     mine_back, *messages = call(
         functools.partial(back_kernel, variants, width, n_chips - 1),
         [((rhs, wide), F32)] + [((rhs, wide), BF16)] * (n_var - 1),
-        [SMEM] + [VMEM] * (4 + n_chips - 1),
-        (place, total, mine, coded, called_b, *arrived),
+        [VMEM] * (4 + n_chips - 1),
+        (total, mine, coded, called_b, *arrived),
         flops=4 * rows * shard * 256,
         moved=4 * rows * shard,
     )
     backs = [mine_back] + [swap(m, "var", k + 1) for k, m in enumerate(messages)]
 
     n_all = n_var * n_samp
-    (norms,) = call(
+    norms, res_keep = call(
         functools.partial(norm_kernel, variants),
-        [((n_all, 1, LANES), F32)],
+        [((n_all, 1, LANES), F32), ((rhs, own), F32)],
         [VMEM] * (3 + n_var),
         (noise, dire, res, *backs),
         moved=4 * n_all * LANES,
@@ -434,7 +444,7 @@
         direction_kernel,
         [((rhs, own), F32)],
         [VMEM] * 4,
-        (norms, res_norm, res_new, dire),
+        (norms, res_norm, res_keep, dire),
     )
     return (sol_new.T, res_new.T, dir_new.T, scores.T)
 

time: 66.6 us -> 51.5 us (0.77)
  local copies, waits for them, and re-layouts: 18.5 us -> 0.01 us
  Pallas kernels: 13.7 us -> 16.2 us
  waiting for transfers between devices: 16.2 us -> 17.6 us
    unnamed x34 -> x8, local copies, waits for them, and re-layouts: 18.5 us -> 0.01 us
    pallas_call x7, Pallas kernels: 13.7 us -> 16.2 us  [call(): pl.pallas_call(kernel, out_shape=[jax.ShapeDtypeStruct(*o) if len(o) == 2...]
    ppermute x11, waiting for transfers between devices: 10.1 us -> 11.5 us  [swap(): return lax.ppermute(values, axis, [(i, i ^ distance) for i in range(size)])]
  transfers between devices with their start and end apart: 12 -> 12, of which waited for: 8 -> 7; matrix products, arithmetic and copies ran while one was open for 0% -> 0% of each run, Pallas kernels for 14% -> 25%
where the time goes in v4:
time: 51.5 us; the launch traced here: 51.3 us
  waiting for transfers between devices  17.6 us (34%)
  starting transfers between devices  16.9 us (33%)
  Pallas kernels  16.2 us (31%)
  between operations  0.71 us (1%)
    pallas_call x7, Pallas kernels, call(): pl.pallas_call(kernel, out_shape=[jax.ShapeDtypeStruct(*o) if len(o) == 2...  16.2 us
    ppermute x11, starting transfers between devices, swap(): return lax.ppermute(values, axis, [(i, i ^ distance) for i in range(size)])  14.3 us
    ppermute x11, waiting for transfers between devices, swap(): return lax.ppermute(values, axis, [(i, i ^ distance) for i in range(size)])  11.5 us
    all_to_all x1, waiting for transfers between devices, body(): norms = lax.all_to_all(norms, ('var', 'samp'), split_axis=0, concat_axis=0)  6.04 us
    all_to_all x1, starting transfers between devices, body(): norms = lax.all_to_all(norms, ('var', 'samp'), split_axis=0, concat_axis=0)  2.54 us
  transfers between devices with their start and end apart: 12, of which 7 were waited for; matrix products, arithmetic and copies ran while one was open for 0% of the time, Pallas kernels for 25%

profile of v4, /device:TPU:0, one launch (start us, length us, event | category | flops | bytes accessed | tf_op | source)
XLA Modules:
  0.0 51.3 jit_solution(1060343838087732925)
XLA Ops:
  0.6 5.1 %collective-permute-start.2 = (f32[16,768]{1,0:T(8,128)}, f32[16,768]{1,0:T(8,128)S(1)}, u32[]{:S(2)}, u32[]{:S(2)}) collective-permute-start(f32[16,768]{1,0:T(8,128)} %bitcast.8), channel_id=1, source_target_pairs={{0,24},{8,16},{16,8},{24,0},{1,25},{9,17},{17,9},{25,1},{2,26},{10... | collective-permute-start | bytes 147464 | tf_op jit(solution)/shard_map/ppermute | solution.py:22
  5.7 0.0 collective-permute-start.1
  5.7 0.6 %collective-permute-start = (f32[16,768]{1,0:T(8,128)}, f32[16,768]{1,0:T(8,128)S(1)}, u32[]{:S(2)}, u32[]{:S(2)}) collective-permute-start(f32[16,768]{1,0:T(8,128)} %bitcast.10), channel_id=1, source_target_pairs={{0,8},{8,0},{16,24},{24,16},{1,9},{9,1},{17,25},{25,17},{2,10},{10... | collective-permute-start | bytes 147464 | tf_op jit(solution)/shard_map/ppermute | solution.py:22
  6.4 9.1 %shard_map.111 = (bf16[768,3072]{1,0:T(8,128)(2,1)S(1)}, bf16[768,3072]{1,0:T(8,128)(2,1)S(1)}, f32[40,1024]{1,0:T(8,128)S(1)}, f32[16,128]{1,0:T(8,128)S(1)}) custom-call(s32[1,768]{1,0:T(1,128)} %order_hbm.1, f32[16,768]{1,0:T(8,128)} %bitcast.19, f32[16,768]{1,0:T(8,128)} %bitcast.11, f32[16,768]{1,0:T(8,128)} %bitcast.16, s32[768,3072]{1,0:T(8,128)} %gen_hbm.1, ...), custom_call_target="tpu_custom_call" | custom-call | flops 220200960 | bytes 22020096 | tf_op jit(solution)/shard_map/pallas_call | solution.py:344
  15.5 0.1 collective-permute-start.4
  15.6 0.0 collective-permute-done.2.d3_ref
  15.6 0.0 collective-permute-done.1.d2_ref
  15.6 0.0 collective-permute-done.d1_ref
  15.6 2.6 %shard_map.112.own_ref = f32[40,896]{1,0:T(8,128)S(1)} custom-call(f32[16,768]{1,0:T(8,128)S(1)} %bitcast.12, f32[16,768]{1,0:T(8,128)S(1)} %collective-permute-done.d1_ref, f32[16,768]{1,0:T(8,128)S(1)} %collective-permute-done.1.d2_ref, f32[16,768]{1,0:T(8,128)S(1)} %collective-permute-done.2.d3_ref, bf16[768,3072]{1,0:T(8,128)(2,1)S(1)} %get-tuple-element.23.coded_ref, ...), custom_call_target="tpu_custom_call" | custom-call | flops 2415919104 | bytes 9437184 | tf_op jit(solution)/shard_map/pallas_call | solution.py:344
  18.3 0.5 collective-permute-start.3
  18.8 0.0 collective-permute-done.4.cross_other_ref
  18.8 1.0 %collective-permute-done.3.other_ref = f32[40,896]{1,0:T(8,128)S(1)} collective-permute-done((f32[40,896]{1,0:T(8,128)S(1)}, f32[40,896]{1,0:T(8,128)S(1)}, u32[]{:S(2)}, u32[]{:S(2)}) %collective-permute-start.3) | collective-permute-done | bytes 143392 | tf_op jit(solution)/shard_map/ppermute | solution.py:22
  19.8 0.2 shard_map.113
  20.0 1.7 %collective-permute-start.5 = (bf16[32,1280]{1,0:T(8,128)(2,1)S(1)}, bf16[32,1280]{1,0:T(8,128)(2,1)S(1)}, u32[]{:S(2)}, u32[]{:S(2)}) collective-permute-start(bf16[32,1280]{1,0:T(8,128)(2,1)S(1)} %get-tuple-element.29), channel_id=1, source_target_pairs={{0,2},{1,3},{2,0},{3,1},{4,6},{5,7},{6,4},{7,5},{8,10},{9,11},{10,... | collective-permute-start | bytes 245768 | tf_op jit(solution)/shard_map/ppermute | solution.py:22
  21.7 1.5 %collective-permute-start.6 = (bf16[32,1280]{1,0:T(8,128)(2,1)S(1)}, bf16[32,1280]{1,0:T(8,128)(2,1)S(1)}, u32[]{:S(2)}, u32[]{:S(2)}) collective-permute-start(bf16[32,1280]{1,0:T(8,128)(2,1)S(1)} %get-tuple-element.30), channel_id=1, source_target_pairs={{0,4},{1,5},{2,6},{3,7},{4,0},{5,1},{6,2},{7,3},{8,12},{9,13},{10,... | collective-permute-start | bytes 245768 | tf_op jit(solution)/shard_map/ppermute | solution.py:22
  23.3 0.3 collective-permute-start.7
  23.6 1.2 %collective-permute-done.5.rest_0_ = bf16[32,1280]{1,0:T(8,128)(2,1)S(1)} collective-permute-done((bf16[32,1280]{1,0:T(8,128)(2,1)S(1)}, bf16[32,1280]{1,0:T(8,128)(2,1)S(1)}, u32[]{:S(2)}, u32[]{:S(2)}) %collective-permute-start.5) | collective-permute-done | bytes 81952 | tf_op jit(solution)/shard_map/ppermute | solution.py:22
  24.8 2.2 %collective-permute-done.6.rest_1_ = bf16[32,1280]{1,0:T(8,128)(2,1)S(1)} collective-permute-done((bf16[32,1280]{1,0:T(8,128)(2,1)S(1)}, bf16[32,1280]{1,0:T(8,128)(2,1)S(1)}, u32[]{:S(2)}, u32[]{:S(2)}) %collective-permute-start.6) | collective-permute-done | bytes 81952 | tf_op jit(solution)/shard_map/ppermute | solution.py:22
  27.0 1.6 %collective-permute-done.7.rest_2_ = bf16[32,1280]{1,0:T(8,128)(2,1)S(1)} collective-permute-done((bf16[32,1280]{1,0:T(8,128)(2,1)S(1)}, bf16[32,1280]{1,0:T(8,128)(2,1)S(1)}, u32[]{:S(2)}, u32[]{:S(2)}) %collective-permute-start.7) | collective-permute-done | bytes 81952 | tf_op jit(solution)/shard_map/ppermute | solution.py:22
  28.6 1.3 %shard_map.114 = (f32[16,1024]{1,0:T(8,128)S(1)}, bf16[16,1024]{1,0:T(8,128)(2,1)S(1)}, bf16[16,1024]{1,0:T(8,128)(2,1)S(1)}, bf16[16,1024]{1,0:T(8,128)(2,1)S(1)}) custom-call(f32[40,896]{1,0:T(8,128)S(1)} %get-tuple-element.27.total_ref, f32[40,128]{1,0:T(8,128)S(1)} %get-tuple-element.28.mine_ref, bf16[768,3072]{1,0:T(8,128)(2,1)S(1)} %get-tuple-element.23.coded_ref, ...), custom_call_target="tpu_custom_call" | custom-call | flops 2415919104 | bytes 9437184 | tf_op jit(solution)/shard_map/pallas_call | solution.py:344
  30.0 1.3 %collective-permute-start.8 = (bf16[16,1024]{1,0:T(8,128)(2,1)S(1)}, bf16[16,1024]{1,0:T(8,128)(2,1)S(1)}, u32[]{:S(2)}, u32[]{:S(2)}) collective-permute-start(bf16[16,1024]{1,0:T(8,128)(2,1)S(1)} %get-tuple-element.33), channel_id=1, source_target_pairs={{0,8},{8,0},{16,24},{24,16},{1,9},{9,1},{17,25},{25,17},{2,10},{10... | collective-permute-start | bytes 98312 | tf_op jit(solution)/shard_map/ppermute | solution.py:22
  31.2 2.9 %collective-permute-start.9 = (bf16[16,1024]{1,0:T(8,128)(2,1)S(1)}, bf16[16,1024]{1,0:T(8,128)(2,1)S(1)}, u32[]{:S(2)}, u32[]{:S(2)}) collective-permute-start(bf16[16,1024]{1,0:T(8,128)(2,1)S(1)} %get-tuple-element.34), channel_id=1, source_target_pairs={{0,16},{8,24},{16,0},{24,8},{1,17},{9,25},{17,1},{25,9},{2,18},{10... | collective-permute-start | bytes 98312 | tf_op jit(solution)/shard_map/ppermute | solution.py:22
  34.2 0.2 collective-permute-start.10
  34.4 0.0 collective-permute-done.8.rest_1_
  34.4 2.0 %collective-permute-done.9.rest_2_ = bf16[16,1024]{1,0:T(8,128)(2,1)S(1)} collective-permute-done((bf16[16,1024]{1,0:T(8,128)(2,1)S(1)}, bf16[16,1024]{1,0:T(8,128)(2,1)S(1)}, u32[]{:S(2)}, u32[]{:S(2)}) %collective-permute-start.9) | collective-permute-done | bytes 32800 | tf_op jit(solution)/shard_map/ppermute | solution.py:22
  36.4 3.5 %collective-permute-done.10.rest_3_ = bf16[16,1024]{1,0:T(8,128)(2,1)S(1)} collective-permute-done((bf16[16,1024]{1,0:T(8,128)(2,1)S(1)}, bf16[16,1024]{1,0:T(8,128)(2,1)S(1)}, u32[]{:S(2)}, u32[]{:S(2)}) %collective-permute-start.10) | collective-permute-done | bytes 32800 | tf_op jit(solution)/shard_map/ppermute | solution.py:22
  39.9 0.0 copy-done.1
  39.9 1.0 %shard_map.116 = (f32[32,1,128]{2,1,0:T(1,128)}, f32[16,768]{1,0:T(8,128)S(1)}) custom-call(f32[1,16]{1,0:T(1,128)S(1)} %bitcast.21, f32[16,768]{1,0:T(8,128)S(1)} %bitcast.13, f32[16,768]{1,0:T(8,128)S(1)} %bitcast.17, f32[16,1024]{1,0:T(8,128)S(1)} %get-tuple-element.32.rest_0_, bf16[16,1024]{1,0:T(8,128)(2,1)S(1)} %collective-permute-done.8.rest_1_, ...), custom_call_target="tpu_custom_call" | custom-call | bytes 16384 | tf_op jit(solution)/shard_map/pallas_call | solution.py:344
  40.9 2.5 %all-to-all-start = ((f32[32,1,128]{2,1,0:T(1,128)}), f32[32,1,128]{2,1,0:T(1,128)S(1)}, u32[]{:S(2)}, u32[]{:S(2)}) async-start(f32[32,1,128]{2,1,0:T(1,128)} %get-tuple-element.38), calls=%async_computation | async-start | bytes 32768 | tf_op jit(solution)/shard_map/all_to_all | solution.py:435
  43.4 1.0 %shard_map.115 = (f32[16,768]{1,0:T(8,128)}, f32[16,768]{1,0:T(8,128)}, f32[16,32]{1,0:T(8,128)}, f32[16,128]{1,0:T(8,128)S(1)}) custom-call(f32[1,16]{1,0:T(1,128)S(1)} %bitcast.22, f32[16,768]{1,0:T(8,128)S(1)} %bitcast.14, f32[16,768]{1,0:T(8,128)S(1)} %bitcast.18, f32[16,768]{1,0:T(8,128)S(1)} %bitcast.20, f32[16,1024]{1,0:T(8,128)S(1)} %get-tuple-element.32.rest_0_, ...), custom_call_target="tpu_custom_call" | custom-call | bytes 1048576 | tf_op jit(solution)/shard_map/pallas_call | solution.py:344
  44.5 6.0 %all-to-all-done.norms_ref = f32[32,1,128]{2,1,0:T(1,128)S(1)} async-done(((f32[32,1,128]{2,1,0:T(1,128)}), f32[32,1,128]{2,1,0:T(1,128)S(1)}, u32[]{:S(2)}, u32[]{:S(2)}) %all-to-all-start) | async-done | bytes 16416 | tf_op jit(solution)/shard_map/all_to_all | solution.py:435
  50.5 0.8 %shard_map.117 = f32[16,768]{1,0:T(8,128)} custom-call(f32[32,1,128]{2,1,0:T(1,128)S(1)} %all-to-all-done.norms_ref, f32[16,128]{1,0:T(8,128)S(1)} %get-tuple-element.39.norm_ref, f32[16,768]{1,0:T(8,128)S(1)} %get-tuple-element.40.res_ref, f32[16,768]{1,0:T(8,128)S(1)} %bitcast.15), custom_call_target="tpu_custom_call" | custom-call | tf_op jit(solution)/shard_map/pallas_call | solution.py:344
  (7 shorter events, 0.0 us)
Async XLA Ops:
  0.6 15.0 %collective-permute-start.2 = (f32[16,768]{1,0:T(8,128)}, f32[16,768]{1,0:T(8,128)S(1)}, u32[]{:S(2)}, u32[]{:S(2)}) collective-permute-start(f32[16,768]{1,0:T(8,128)} %bitcast.8), channel_id=1, source_target_pairs={{0,24},{8,16},{16,8},{24,0},{1,25},{9,17},{17,9},{25,1},{2,26},{10... | collective-permute-start | bytes 147464 | tf_op jit(solution)/shard_map/ppermute | solution.py:22
  5.7 9.9 %collective-permute-start.1 = (f32[16,768]{1,0:T(8,128)}, f32[16,768]{1,0:T(8,128)S(1)}, u32[]{:S(2)}, u32[]{:S(2)}) collective-permute-start(f32[16,768]{1,0:T(8,128)} %bitcast.9), channel_id=1, source_target_pairs={{0,16},{8,24},{16,0},{24,8},{1,17},{9,25},{17,1},{25,9},{2,18},{10... | collective-permute-start | bytes 147464 | tf_op jit(solution)/shard_map/ppermute | solution.py:22
  5.7 9.9 %collective-permute-start = (f32[16,768]{1,0:T(8,128)}, f32[16,768]{1,0:T(8,128)S(1)}, u32[]{:S(2)}, u32[]{:S(2)}) collective-permute-start(f32[16,768]{1,0:T(8,128)} %bitcast.10), channel_id=1, source_target_pairs={{0,8},{8,0},{16,24},{24,16},{1,9},{9,1},{17,25},{25,17},{2,10},{10... | collective-permute-start | bytes 147464 | tf_op jit(solution)/shard_map/ppermute | solution.py:22
  6.4 9.2 %copy-start = (f32[768,16]{0,1:T(8,128)S(1)}, f32[768,16]{0,1:T(8,128)}, u32[]{:S(2)}) copy-start(f32[768,16]{0,1:T(8,128)} %param.15) | copy-start | bytes 147460
  15.5 3.3 %collective-permute-start.4 = (f32[40,1024]{1,0:T(8,128)S(1)}, f32[40,1024]{1,0:T(8,128)S(1)}, u32[]{:S(2)}, u32[]{:S(2)}) collective-permute-start(f32[40,1024]{1,0:T(8,128)S(1)} %get-tuple-element.26.cross_ref), channel_id=1, source_target_pairs={{0,1},{1,0},{2,3},{3,2},{4,5},{5,4},{6,7},{7,6},{8,9},{9,8},{10,11... | collective-permute-start | bytes 491528 | tf_op jit(solution)/shard_map/ppermute | solution.py:22
  18.3 1.5 %collective-permute-start.3 = (f32[40,896]{1,0:T(8,128)S(1)}, f32[40,896]{1,0:T(8,128)S(1)}, u32[]{:S(2)}, u32[]{:S(2)}) collective-permute-start(f32[40,896]{1,0:T(8,128)S(1)} %shard_map.112.own_ref), channel_id=1, source_target_pairs={{0,1},{1,0},{2,3},{3,2},{4,5},{5,4},{6,7},{7,6},{8,9},{9,8},{10,11... | collective-permute-start | bytes 430088 | tf_op jit(solution)/shard_map/ppermute | solution.py:22
  20.0 4.8 %collective-permute-start.5 = (bf16[32,1280]{1,0:T(8,128)(2,1)S(1)}, bf16[32,1280]{1,0:T(8,128)(2,1)S(1)}, u32[]{:S(2)}, u32[]{:S(2)}) collective-permute-start(bf16[32,1280]{1,0:T(8,128)(2,1)S(1)} %get-tuple-element.29), channel_id=1, source_target_pairs={{0,2},{1,3},{2,0},{3,1},{4,6},{5,7},{6,4},{7,5},{8,10},{9,11},{10,... | collective-permute-start | bytes 245768 | tf_op jit(solution)/shard_map/ppermute | solution.py:22
  21.7 5.3 %collective-permute-start.6 = (bf16[32,1280]{1,0:T(8,128)(2,1)S(1)}, bf16[32,1280]{1,0:T(8,128)(2,1)S(1)}, u32[]{:S(2)}, u32[]{:S(2)}) collective-permute-start(bf16[32,1280]{1,0:T(8,128)(2,1)S(1)} %get-tuple-element.30), channel_id=1, source_target_pairs={{0,4},{1,5},{2,6},{3,7},{4,0},{5,1},{6,2},{7,3},{8,12},{9,13},{10,... | collective-permute-start | bytes 245768 | tf_op jit(solution)/shard_map/ppermute | solution.py:22
  23.3 5.3 %collective-permute-start.7 = (bf16[32,1280]{1,0:T(8,128)(2,1)S(1)}, bf16[32,1280]{1,0:T(8,128)(2,1)S(1)}, u32[]{:S(2)}, u32[]{:S(2)}) collective-permute-start(bf16[32,1280]{1,0:T(8,128)(2,1)S(1)} %get-tuple-element.31), channel_id=1, source_target_pairs={{0,6},{1,7},{2,4},{3,5},{4,2},{5,3},{6,0},{7,1},{8,14},{9,15},{10,... | collective-permute-start | bytes 245768 | tf_op jit(solution)/shard_map/ppermute | solution.py:22
  28.6 11.3 %copy-start.1 = (f32[768,16]{0,1:T(8,128)S(1)}, f32[768,16]{0,1:T(8,128)}, u32[]{:S(2)}) copy-start(f32[768,16]{0,1:T(8,128)} %param.14) | copy-start | bytes 147460
  28.6 11.3 %copy-start.3 = (f32[16]{0:T(128)S(1)}, f32[16]{0:T(128)}, u32[]{:S(2)}) copy-start(f32[16]{0:T(128)} %param.12) | copy-start | bytes 196
  28.6 14.8 %copy-start.2 = (f32[768,16]{0,1:T(8,128)S(1)}, f32[768,16]{0,1:T(8,128)}, u32[]{:S(2)}) copy-start(f32[768,16]{0,1:T(8,128)} %param.13) | copy-start | bytes 147460
  30.0 4.4 %collective-permute-start.8 = (bf16[16,1024]{1,0:T(8,128)(2,1)S(1)}, bf16[16,1024]{1,0:T(8,128)(2,1)S(1)}, u32[]{:S(2)}, u32[]{:S(2)}) collective-permute-start(bf16[16,1024]{1,0:T(8,128)(2,1)S(1)} %get-tuple-element.33), channel_id=1, source_target_pairs={{0,8},{8,0},{16,24},{24,16},{1,9},{9,1},{17,25},{25,17},{2,10},{10... | collective-permute-start | bytes 98312 | tf_op jit(solution)/shard_map/ppermute | solution.py:22
  31.2 5.2 %collective-permute-start.9 = (bf16[16,1024]{1,0:T(8,128)(2,1)S(1)}, bf16[16,1024]{1,0:T(8,128)(2,1)S(1)}, u32[]{:S(2)}, u32[]{:S(2)}) collective-permute-start(bf16[16,1024]{1,0:T(8,128)(2,1)S(1)} %get-tuple-element.34), channel_id=1, source_target_pairs={{0,16},{8,24},{16,0},{24,8},{1,17},{9,25},{17,1},{25,9},{2,18},{10... | collective-permute-start | bytes 98312 | tf_op jit(solution)/shard_map/ppermute | solution.py:22
  34.2 5.7 %collective-permute-start.10 = (bf16[16,1024]{1,0:T(8,128)(2,1)S(1)}, bf16[16,1024]{1,0:T(8,128)(2,1)S(1)}, u32[]{:S(2)}, u32[]{:S(2)}) collective-permute-start(bf16[16,1024]{1,0:T(8,128)(2,1)S(1)} %get-tuple-element.35), channel_id=1, source_target_pairs={{0,24},{8,16},{16,8},{24,0},{1,25},{9,17},{17,9},{25,1},{2,26},{10... | collective-permute-start | bytes 98312 | tf_op jit(solution)/shard_map/ppermute | solution.py:22
  40.9 9.6 %all-to-all-start = ((f32[32,1,128]{2,1,0:T(1,128)}), f32[32,1,128]{2,1,0:T(1,128)S(1)}, u32[]{:S(2)}, u32[]{:S(2)}) async-start(f32[32,1,128]{2,1,0:T(1,128)} %get-tuple-element.38), calls=%async_computation | async-start | bytes 32768 | tf_op jit(solution)/shard_map/all_to_all | solution.py:435

commit v5 on v4

--- a/solution.py
+++ b/solution.py
@@ -58,22 +58,34 @@
     return jnp.sum(jnp.where(same, column, 0.0), axis=0, keepdims=True)
 
 
-def pass_kernel(step_rows, order_hbm, sol_hbm, dir_hbm, res_hbm, gen_hbm, call_hbm, dose_hbm,
-                coded_ref, called_ref, cross_ref, sums_ref, gbuf, cbuf, dbuf, order_ref, sol_ref, dir_ref, res_ref,
-                sems, small_sems):
-    slots = gbuf.shape[0]
-    rows = gen_hbm.shape[0]
-    steps = rows // step_rows
+def convert(gen_ref, call_ref, coded_ref, called_ref, first, rows):
+    def group(i, carry):
+        part = pl.ds(pl.multiple_of(first + i * 16, 16), 16)
+        call = call_ref[part, :].astype(F32).astype(BF16)
+        coded_ref[part, :] = gen_ref[part, :].astype(F32).astype(BF16) * call
+        called_ref[part, :] = call
+        return carry
+
+    lax.fori_loop(0, rows // 16, group, 0)
+
+
+def row_copies(first, chunk, rows, pairs, sems):
+    return [
+        [
+            pltpu.make_async_copy(
+                source.at[pl.ds(first + i * chunk, chunk)], target.at[pl.ds(i * chunk, chunk)], sems.at[j, i]
+            )
+            for j, (source, target) in enumerate(pairs)
+        ]
+        for i in range(rows // chunk)
+    ]
+
+
+def first_kernel(chunk, order_hbm, sol_hbm, dir_hbm, res_hbm, gen_hbm, call_hbm, dose_hbm,
+                 coded_ref, called_ref, cross_ref, sums_ref,
+                 order_ref, sol_ref, dir_ref, res_ref, gbuf, cbuf, dbuf, small_sems, sems):
     rhs = sol_hbm.shape[0]
-
-    def copies(step):
-        slot = step % slots
-        part = pl.ds(step * step_rows, step_rows)
-        return (
-            pltpu.make_async_copy(gen_hbm.at[part], gbuf.at[slot], sems.at[0, slot]),
-            pltpu.make_async_copy(call_hbm.at[part], cbuf.at[slot], sems.at[1, slot]),
-        )
-
+    rows = gbuf.shape[0]
     small = [
         pltpu.make_async_copy(source, target, small_sems.at[i])
         for i, (source, target) in enumerate(
@@ -82,10 +94,10 @@
     ]
     for copy in small:
         copy.start()
-    for step in range(slots):
-        for copy in copies(step):
+    parts = row_copies(0, chunk, rows, ((gen_hbm, gbuf), (call_hbm, cbuf)), sems)
+    for part in parts:
+        for copy in part:
             copy.start()
-
     for copy in small[:4]:
         copy.wait()
     sol, dire, res = sol_ref[...], dir_ref[...], res_ref[...]
@@ -107,51 +119,84 @@
     cross = jnp.dot(picked, dose, preferred_element_type=F32)
     cross_ref[: 2 * rhs] = cross[: 2 * rhs] + cross[2 * rhs : 4 * rhs]
     cross_ref[2 * rhs :] = cross[4 * rhs : 4 * rhs + 8]
-
-    for step in range(steps):
-        slot = step % slots
-        for copy in copies(step):
+    for i, part in enumerate(parts):
+        for copy in part:
             copy.wait()
-
-        def group(i, carry):
-            part = pl.ds(pl.multiple_of(i * 16, 16), 16)
-            out = pl.ds(pl.multiple_of(step * step_rows + i * 16, 16), 16)
-            call = cbuf[slot, part, :]
-            coded_ref[out, :] = (gbuf[slot, part, :] * call).astype(F32).astype(BF16)
-            called_ref[out, :] = call.astype(F32).astype(BF16)
-            return carry
-
-        lax.fori_loop(0, step_rows // 16, group, 0)
-        if step + slots < steps:
-            for copy in copies(step + slots):
-                copy.start()
-
-
-def forward_kernel(block, d0_ref, d1_ref, d2_ref, d3_ref, coded_ref, called_ref, sums_ref,
-                   out_ref, w1, w2):
-    var = lax.axis_index("var")
-    own = d0_ref.shape[1]
-    rows = coded_ref.shape[0]
-    samples = coded_ref.shape[1]
-    row = lax.broadcasted_iota(jnp.int32, (16, samples), 0)
-    zero = jnp.zeros((16, samples), BF16)
+        convert(gbuf, cbuf, coded_ref, called_ref, i * chunk, chunk)
+
+
+def pair_kernel(own_ref, other_ref, out_ref):
+    upper = lax.axis_index("var") % 2
+    rhs = own_ref.shape[0]
+    own, other = own_ref[...], other_ref[...]
+    out_ref[:rhs] = jnp.where(upper == 0, own, other).astype(BF16)
+    out_ref[rhs:] = jnp.where(upper == 0, other, own).astype(BF16)
+
+
+def weights(pair_ref, w1, w2):
+    own = pair_ref.shape[1]
+    zero = jnp.zeros((16, 2 * own), BF16)
+    row = lax.broadcasted_iota(jnp.int32, (16, 2 * own), 0)
     w1[16:32] = zero
     w1[32:48] = jnp.where(row == 0, 1.0, 0.0).astype(BF16)
     w2[0:16] = zero
     w2[32:48] = jnp.where(row == 1, 1.0, 0.0).astype(BF16)
-    for k, ref in enumerate((d0_ref, d1_ref, d2_ref, d3_ref)):
-        part = pl.ds(pl.multiple_of((var ^ k) * own, LANES), own)
-        piece = ref[...].astype(BF16)
-        w1[0:16, part] = piece
-        w2[16:32, part] = piece
-    for i in range(rows // block):
-        part = pl.ds(i * block, block)
-        got = lax.dot_general(coded_ref[part, :], w1[...], NT, preferred_element_type=F32)
-        got = got + lax.dot_general(called_ref[part, :], w2[...], NT, preferred_element_type=F32)
-        got = jnp.concatenate([got, jnp.zeros((block, LANES - got.shape[1]), F32)], axis=1)
-        out_ref[:, i * block : (i + 1) * block] = got.T[: out_ref.shape[0]]
-    out_ref[:, rows:] = jnp.zeros((out_ref.shape[0], LANES), F32)
-    out_ref[0:16, rows:] = sums_ref[...]
+    for i in range(2):
+        piece = pair_ref[16 * i : 16 * i + 16]
+        w1[0:16, i * own : (i + 1) * own] = piece
+        w2[16:32, i * own : (i + 1) * own] = piece
+
+
+def product(coded_ref, called_ref, first, rows, samples, w1, w2):
+    part = pl.ds(first, rows)
+    got = lax.dot_general(coded_ref[part, samples], w1[...], NT, preferred_element_type=F32)
+    got = got + lax.dot_general(called_ref[part, samples], w2[...], NT, preferred_element_type=F32)
+    got = jnp.concatenate([got, jnp.zeros((rows, LANES - got.shape[1]), F32)], axis=1)
+    return got.T[:40]
+
+
+def pair_samples(pair, own):
+    return pl.ds(pl.multiple_of(pair * 2 * own, LANES), 2 * own)
+
+
+def second_kernel(chunk, pair_ref, coded_first, called_first, gen_hbm, call_hbm,
+                  coded_ref, called_ref, out_ref, gbuf, cbuf, w1, w2, sems):
+    first, rows = coded_first.shape[0], gbuf.shape[0]
+    own = pair_ref.shape[1]
+    parts = row_copies(first, chunk, rows, ((gen_hbm, gbuf), (call_hbm, cbuf)), sems)
+    for part in parts:
+        for copy in part:
+            copy.start()
+    samples = pair_samples(lax.axis_index("var") // 2, own)
+    weights(pair_ref, w1, w2)
+    for i in range(first // LANES):
+        place = i * LANES
+        out_ref[:, place : place + LANES] = product(coded_first, called_first, place, LANES, samples, w1, w2)
+    for i, part in enumerate(parts):
+        for copy in part:
+            copy.wait()
+        place = i * chunk
+        convert(gbuf, cbuf, coded_ref, called_ref, place, chunk)
+        out_ref[:, first + place : first + place + chunk] = product(
+            coded_ref, called_ref, place, chunk, samples, w1, w2
+        )
+
+
+def third_kernel(pair_ref, coded_first, called_first, coded_ref, called_ref, half_ref, sums_ref, out_ref, w1, w2):
+    own = pair_ref.shape[1]
+    first, rest = coded_first.shape[0], coded_ref.shape[0]
+    samples = pair_samples((lax.axis_index("var") // 2) ^ 1, own)
+    weights(pair_ref, w1, w2)
+    for i in range((first + rest) // LANES):
+        place = i * LANES
+        here = slice(place, place + LANES)
+        if place < first:
+            got = product(coded_first, called_first, place, LANES, samples, w1, w2)
+        else:
+            got = product(coded_ref, called_ref, place - first, LANES, samples, w1, w2)
+        out_ref[:, here] = half_ref[:, here] + got
+    out_ref[:, first + rest :] = jnp.zeros((out_ref.shape[0], LANES), F32)
+    out_ref[0:16, first + rest :] = sums_ref[...]
 
 
 def chunk_of(cross, start, n_var, width):
@@ -205,7 +250,8 @@
         message[:, rows + 3 * LANES :] = jnp.concatenate([sums, dose], axis=0).astype(BF16)
 
 
-def back_kernel(variants, width, n_arrived, total_ref, mine_ref, coded_ref, called_ref, *rest):
+def back_kernel(variants, width, n_arrived, total_ref, mine_ref, coded_first, called_first,
+                coded_ref, called_ref, *rest):
     arrived, own_ref, messages = rest[:n_arrived], rest[n_arrived], rest[n_arrived + 1 :]
     var = lax.axis_index("var")
     rows = total_ref.shape[1] - LANES
@@ -248,8 +294,11 @@
 
     def term(p):
         part = pl.ds(pl.multiple_of(p * own, LANES), own)
-        got = jnp.dot(scaled_a, coded_ref[:, part], preferred_element_type=F32)
-        got = got + jnp.dot(scaled_b, called_ref[:, part], preferred_element_type=F32)
+        first = coded_first.shape[0]
+        got = jnp.dot(scaled_a[:, :first], coded_first[:, part], preferred_element_type=F32)
+        got = got + jnp.dot(scaled_a[:, first:], coded_ref[:, part], preferred_element_type=F32)
+        got = got + jnp.dot(scaled_b[:, :first], called_first[:, part], preferred_element_type=F32)
+        got = got + jnp.dot(scaled_b[:, first:], called_ref[:, part], preferred_element_type=F32)
         return got / variants
 
     def segment(values, p):
@@ -364,40 +413,58 @@
     noise = noise_ratio[None]
 
     dire, res, sol = direction.T, residual.T, solution.T
-    pieces = [dire] + [swap(dire, "var", k) for k in range(1, n_var)]
-
-    step_rows = 128
-    slots = 3
-    coded, called_b, cross, sums = call(
-        functools.partial(pass_kernel, step_rows),
-        [((rows, shard), BF16, pltpu.VMEM), ((rows, shard), BF16, pltpu.VMEM), ((2 * rhs + 8, imputed), F32), ((rhs, LANES), F32)],
+    first, chunk = rows // 3, 128
+    rest = rows - first
+    matrix = lambda n: ((n, shard), BF16, pltpu.VMEM)
+
+    neighbour = swap(dire, "var", 1)
+    coded_a, called_a, cross, sums = call(
+        functools.partial(first_kernel, chunk),
+        [matrix(first), matrix(first), ((2 * rhs + 8, imputed), F32), ((rhs, LANES), F32)],
         [HBM] * 7,
         (sample_order, sol, dire, res, genotypes, called, dosage),
         scratch=[
-            pltpu.VMEM((slots, step_rows, shard), jnp.int32),
-            pltpu.VMEM((slots, step_rows, shard), jnp.int32),
-            pltpu.VMEM((own, imputed), jnp.int32),
             pltpu.VMEM((1, own), jnp.int32),
             pltpu.VMEM((rhs, own), F32),
             pltpu.VMEM((rhs, own), F32),
             pltpu.VMEM((rhs, own), F32),
-            pltpu.SemaphoreType.DMA((2, slots)),
+            pltpu.VMEM((first, shard), jnp.int32),
+            pltpu.VMEM((first, shard), jnp.int32),
+            pltpu.VMEM((own, imputed), jnp.int32),
             pltpu.SemaphoreType.DMA((5,)),
+            pltpu.SemaphoreType.DMA((2, first // chunk)),
         ],
-        limit=32,
+        limit=24,
         flops=2 * 80 * own * (own + imputed),
-        moved=4 * (2 * rows * shard + own * imputed),
-    )
+        moved=4 * (2 * first * shard + own * imputed),
+    )
+    (pair,) = call(pair_kernel, [((2 * rhs, own), BF16)], [VMEM] * 2, (dire, neighbour))
+    pair_other = swap(pair, "var", 2)
     cross_other = swap(cross, "samp", 1)
-
+    both_weights = [pltpu.VMEM((48, 2 * own), BF16), pltpu.VMEM((48, 2 * own), BF16)]
+    coded_b, called_b, half = call(
+        functools.partial(second_kernel, chunk),
+        [matrix(rest), matrix(rest), ((2 * rhs + 8, rows), F32)],
+        [VMEM] * 3 + [HBM] * 2,
+        (pair, coded_a, called_a, genotypes, called),
+        scratch=[
+            pltpu.VMEM((rest, shard), jnp.int32),
+            pltpu.VMEM((rest, shard), jnp.int32),
+            *both_weights,
+            pltpu.SemaphoreType.DMA((2, rest // chunk)),
+        ],
+        limit=24,
+        flops=2 * rows * shard * 256,
+        moved=4 * 2 * rest * shard,
+    )
     (part,) = call(
-        functools.partial(forward_kernel, 128),
+        third_kernel,
         [((2 * rhs + 8, rows + LANES), F32)],
-        [VMEM] * (n_var + 3),
-        (*pieces, coded, called_b, sums),
-        scratch=[pltpu.VMEM((48, shard), BF16), pltpu.VMEM((48, shard), BF16)],
-        flops=4 * rows * shard * 256,
-        moved=4 * rows * shard,
+        [VMEM] * 7,
+        (pair_other, coded_a, called_a, coded_b, called_b, half, sums),
+        scratch=both_weights,
+        flops=2 * rows * shard * 256,
+        moved=2 * rows * shard,
     )
     part_other = swap(part, "samp", 1)
 
@@ -411,18 +478,18 @@
         scratch=[pltpu.VMEM(cross.shape, F32)],
         moved=1 * MIB,
     )
-    arrived = [swap(m, "samp", 2 * (k + 1)) for k, m in enumerate(messages)]
+    arrived = [swap(messages[k], "samp", 2 * (k + 1)) for k in reversed(range(n_chips - 1))]
 
     wide = own + 2 * LANES
     mine_back, *messages = call(
         functools.partial(back_kernel, variants, width, n_chips - 1),
         [((rhs, wide), F32)] + [((rhs, wide), BF16)] * (n_var - 1),
-        [VMEM] * (4 + n_chips - 1),
-        (total, mine, coded, called_b, *arrived),
+        [VMEM] * (6 + n_chips - 1),
+        (total, mine, coded_a, called_a, coded_b, called_b, *arrived),
         flops=4 * rows * shard * 256,
         moved=4 * rows * shard,
     )
-    backs = [mine_back] + [swap(m, "var", k + 1) for k, m in enumerate(messages)]
+    backs = [mine_back] + [swap(messages[k], "var", k + 1) for k in reversed(range(n_var - 1))]
 
     n_all = n_var * n_samp
     norms, res_keep = call(

time: 51.5 us -> 47.7 us (0.926)
  waiting for transfers between devices: 17.6 us -> 13 us
  starting transfers between devices: 16.9 us -> 17.8 us
    ppermute x11 -> x10, waiting for transfers between devices: 11.5 us -> 6.97 us  [swap(): return lax.ppermute(values, axis, [(i, i ^ distance) for i in range(size)])]
    all_to_all x1, starting transfers between devices: 2.54 us -> 3.73 us  [body(): norms = lax.all_to_all(norms, ('var', 'samp'), split_axis=0, concat_axis=0)]
    ppermute x11 -> x10, starting transfers between devices: 14.3 us -> 14 us  [swap(): return lax.ppermute(values, axis, [(i, i ^ distance) for i in range(size)])]
    pallas_call x7 -> x9, Pallas kernels: 16.2 us -> 16 us  [call(): pl.pallas_call(kernel, out_shape=[jax.ShapeDtypeStruct(*o) if len(o) == 2...]
  transfers between devices with their start and end apart: 12 -> 11, of which waited for: 7 -> 7; matrix products, arithmetic and copies ran while one was open for 0% -> 0% of each run, Pallas kernels for 25% -> 27%
where the time goes in v5:
time: 47.7 us; the launch traced here: 47.5 us
  starting transfers between devices  17.8 us (37%)
  Pallas kernels  16 us (34%)
  waiting for transfers between devices  13 us (27%)
  between operations  0.73 us (2%)
    pallas_call x9, Pallas kernels, call(): pl.pallas_call(kernel, out_shape=[jax.ShapeDtypeStruct(*o) if len(o) == 2...  16 us
    ppermute x10, starting transfers between devices, swap(): return lax.ppermute(values, axis, [(i, i ^ distance) for i in range(size)])  14 us
    ppermute x10, waiting for transfers between devices, swap(): return lax.ppermute(values, axis, [(i, i ^ distance) for i in range(size)])  6.97 us
    all_to_all x1, waiting for transfers between devices, body(): norms = lax.all_to_all(norms, ('var', 'samp'), split_axis=0, concat_axis=0)  6.04 us
    all_to_all x1, starting transfers between devices, body(): norms = lax.all_to_all(norms, ('var', 'samp'), split_axis=0, concat_axis=0)  3.73 us
  transfers between devices with their start and end apart: 11, of which 7 were waited for; matrix products, arithmetic and copies ran while one was open for 0% of the time, Pallas kernels for 27%

profile of v5, /device:TPU:0, one launch (start us, length us, event | category | flops | bytes accessed | tf_op | source)
XLA Modules:
  0.0 47.5 jit_solution(240447125893212477)
XLA Ops:
  0.6 3.1 %collective-permute-start = (f32[16,768]{1,0:T(8,128)}, f32[16,768]{1,0:T(8,128)S(1)}, u32[]{:S(2)}, u32[]{:S(2)}) collective-permute-start(f32[16,768]{1,0:T(8,128)} %bitcast.8), channel_id=1, source_target_pairs={{0,8},{8,0},{16,24},{24,16},{1,9},{9,1},{17,25},{25,17},{2,10},{10... | collective-permute-start | bytes 147464 | tf_op jit(solution)/shard_map/ppermute | solution.py:22
  3.7 4.5 %shard_map.112 = (bf16[256,3072]{1,0:T(8,128)(2,1)S(1)}, bf16[256,3072]{1,0:T(8,128)(2,1)S(1)}, f32[40,1024]{1,0:T(8,128)S(1)}, f32[16,128]{1,0:T(8,128)S(1)}) custom-call(s32[1,768]{1,0:T(1,128)} %order_hbm.1, f32[16,768]{1,0:T(8,128)} %bitcast.17, f32[16,768]{1,0:T(8,128)} %bitcast.9, f32[16,768]{1,0:T(8,128)} %bitcast.14, s32[768,3072]{1,0:T(8,128)} %gen_hbm.3, ...), custom_call_target="tpu_custom_call" | custom-call | flops 220200960 | bytes 9437184 | tf_op jit(solution)/shard_map/pallas_call | solution.py:393
  8.2 0.1 collective-permute-start.3
  8.3 0.0 collective-permute-done.other_ref
  8.3 0.0 copy-done
  8.4 2.7 %collective-permute-start.1 = (bf16[32,768]{1,0:T(8,128)(2,1)S(1)}, bf16[32,768]{1,0:T(8,128)(2,1)S(1)}, u32[]{:S(2)}, u32[]{:S(2)}) collective-permute-start(bf16[32,768]{1,0:T(8,128)(2,1)S(1)} %shard_map.111.pair_ref), channel_id=1, source_target_pairs={{0,16},{8,24},{16,0},{24,8},{1,17},{9,25},{17,1},{25,9},{2,18},{10... | collective-permute-start | bytes 147464 | tf_op jit(solution)/shard_map/ppermute | solution.py:22
  11.0 5.6 %shard_map.113 = (bf16[512,3072]{1,0:T(8,128)(2,1)S(1)}, bf16[512,3072]{1,0:T(8,128)(2,1)S(1)}, f32[40,768]{1,0:T(8,128)S(1)}) custom-call(bf16[32,768]{1,0:T(8,128)(2,1)S(1)} %shard_map.111.pair_ref, bf16[256,3072]{1,0:T(8,128)(2,1)S(1)} %get-tuple-element.26.coded_first, bf16[256,3072]{1,0:T(8,128)(2,1)S(1)} %get-tuple-element.27.called_first, ...), custom_call_target="tpu_custom_call" | custom-call | flops 1207959552 | bytes 12582912 | tf_op jit(solution)/shard_map/pallas_call | solution.py:393
  16.7 0.0 collective-permute-done.1.pair_ref
  16.7 1.4 %shard_map.114.own_ref = f32[40,896]{1,0:T(8,128)S(1)} custom-call(bf16[32,768]{1,0:T(8,128)(2,1)S(1)} %collective-permute-done.1.pair_ref, bf16[256,3072]{1,0:T(8,128)(2,1)S(1)} %get-tuple-element.26.coded_first, bf16[256,3072]{1,0:T(8,128)(2,1)S(1)} %get-tuple-element.27.called_first, bf16[512,3072]{1,0:T(8,128)(2,1)S(1)} %get-tuple-element.28.coded_ref, ...), custom_call_target="tpu_custom_call" | custom-call | flops 1207959552 | bytes 4718592 | tf_op jit(solution)/shard_map/pallas_call | solution.py:393
  18.1 0.3 collective-permute-start.2
  18.3 0.0 collective-permute-done.3.cross_other_ref
  18.4 1.2 %collective-permute-done.2.other_ref = f32[40,896]{1,0:T(8,128)S(1)} collective-permute-done((f32[40,896]{1,0:T(8,128)S(1)}, f32[40,896]{1,0:T(8,128)S(1)}, u32[]{:S(2)}, u32[]{:S(2)}) %collective-permute-start.2) | collective-permute-done | bytes 143392 | tf_op jit(solution)/shard_map/ppermute | solution.py:22
  19.5 0.2 shard_map.115
  19.7 2.5 %collective-permute-start.4 = (bf16[32,1280]{1,0:T(8,128)(2,1)S(1)}, bf16[32,1280]{1,0:T(8,128)(2,1)S(1)}, u32[]{:S(2)}, u32[]{:S(2)}) collective-permute-start(bf16[32,1280]{1,0:T(8,128)(2,1)S(1)} %get-tuple-element.35), channel_id=1, source_target_pairs={{0,6},{1,7},{2,4},{3,5},{4,2},{5,3},{6,0},{7,1},{8,14},{9,15},{10,... | collective-permute-start | bytes 245768 | tf_op jit(solution)/shard_map/ppermute | solution.py:22
  22.3 0.5 %collective-permute-start.5 = (bf16[32,1280]{1,0:T(8,128)(2,1)S(1)}, bf16[32,1280]{1,0:T(8,128)(2,1)S(1)}, u32[]{:S(2)}, u32[]{:S(2)}) collective-permute-start(bf16[32,1280]{1,0:T(8,128)(2,1)S(1)} %get-tuple-element.36), channel_id=1, source_target_pairs={{0,4},{1,5},{2,6},{3,7},{4,0},{5,1},{6,2},{7,3},{8,12},{9,13},{10,... | collective-permute-start | bytes 245768 | tf_op jit(solution)/shard_map/ppermute | solution.py:22
  22.8 0.5 %collective-permute-start.6 = (bf16[32,1280]{1,0:T(8,128)(2,1)S(1)}, bf16[32,1280]{1,0:T(8,128)(2,1)S(1)}, u32[]{:S(2)}, u32[]{:S(2)}) collective-permute-start(bf16[32,1280]{1,0:T(8,128)(2,1)S(1)} %get-tuple-element.37), channel_id=1, source_target_pairs={{0,2},{1,3},{2,0},{3,1},{4,6},{5,7},{6,4},{7,5},{8,10},{9,11},{10,... | collective-permute-start | bytes 245768 | tf_op jit(solution)/shard_map/ppermute | solution.py:22
  23.3 2.0 %collective-permute-done.4.rest_0_ = bf16[32,1280]{1,0:T(8,128)(2,1)S(1)} collective-permute-done((bf16[32,1280]{1,0:T(8,128)(2,1)S(1)}, bf16[32,1280]{1,0:T(8,128)(2,1)S(1)}, u32[]{:S(2)}, u32[]{:S(2)}) %collective-permute-start.4) | collective-permute-done | bytes 81952 | tf_op jit(solution)/shard_map/ppermute | solution.py:22
  25.3 1.7 %collective-permute-done.5.rest_1_ = bf16[32,1280]{1,0:T(8,128)(2,1)S(1)} collective-permute-done((bf16[32,1280]{1,0:T(8,128)(2,1)S(1)}, bf16[32,1280]{1,0:T(8,128)(2,1)S(1)}, u32[]{:S(2)}, u32[]{:S(2)}) %collective-permute-start.5) | collective-permute-done | bytes 81952 | tf_op jit(solution)/shard_map/ppermute | solution.py:22
  27.0 0.2 collective-permute-done.6.rest_2_
  27.2 1.4 %shard_map.116 = (f32[16,1024]{1,0:T(8,128)S(1)}, bf16[16,1024]{1,0:T(8,128)(2,1)S(1)}, bf16[16,1024]{1,0:T(8,128)(2,1)S(1)}, bf16[16,1024]{1,0:T(8,128)(2,1)S(1)}) custom-call(f32[40,896]{1,0:T(8,128)S(1)} %get-tuple-element.33.total_ref, f32[40,128]{1,0:T(8,128)S(1)} %get-tuple-element.34.mine_ref, bf16[256,3072]{1,0:T(8,128)(2,1)S(1)} %get-tuple-element.26.coded_first, ...), custom_call_target="tpu_custom_call" | custom-call | flops 2415919104 | bytes 9437184 | tf_op jit(solution)/shard_map/pallas_call | solution.py:393
  28.6 0.2 collective-permute-start.7
  28.8 1.7 %collective-permute-start.8 = (bf16[16,1024]{1,0:T(8,128)(2,1)S(1)}, bf16[16,1024]{1,0:T(8,128)(2,1)S(1)}, u32[]{:S(2)}, u32[]{:S(2)}) collective-permute-start(bf16[16,1024]{1,0:T(8,128)(2,1)S(1)} %get-tuple-element.40), channel_id=1, source_target_pairs={{0,16},{8,24},{16,0},{24,8},{1,17},{9,25},{17,1},{25,9},{2,18},{10... | collective-permute-start | bytes 98312 | tf_op jit(solution)/shard_map/ppermute | solution.py:22
  30.5 2.5 %collective-permute-start.9 = (bf16[16,1024]{1,0:T(8,128)(2,1)S(1)}, bf16[16,1024]{1,0:T(8,128)(2,1)S(1)}, u32[]{:S(2)}, u32[]{:S(2)}) collective-permute-start(bf16[16,1024]{1,0:T(8,128)(2,1)S(1)} %get-tuple-element.41), channel_id=1, source_target_pairs={{0,8},{8,0},{16,24},{24,16},{1,9},{9,1},{17,25},{25,17},{2,10},{10... | collective-permute-start | bytes 98312 | tf_op jit(solution)/shard_map/ppermute | solution.py:22
  33.0 1.3 %collective-permute-done.7.rest_1_ = bf16[16,1024]{1,0:T(8,128)(2,1)S(1)} collective-permute-done((bf16[16,1024]{1,0:T(8,128)(2,1)S(1)}, bf16[16,1024]{1,0:T(8,128)(2,1)S(1)}, u32[]{:S(2)}, u32[]{:S(2)}) %collective-permute-start.7) | collective-permute-done | bytes 32800 | tf_op jit(solution)/shard_map/ppermute | solution.py:22
  34.3 0.0 collective-permute-done.8.rest_2_
  34.3 0.6 %collective-permute-done.9.rest_3_ = bf16[16,1024]{1,0:T(8,128)(2,1)S(1)} collective-permute-done((bf16[16,1024]{1,0:T(8,128)(2,1)S(1)}, bf16[16,1024]{1,0:T(8,128)(2,1)S(1)}, u32[]{:S(2)}, u32[]{:S(2)}) %collective-permute-start.9) | collective-permute-done | bytes 32800 | tf_op jit(solution)/shard_map/ppermute | solution.py:22
  34.9 0.0 copy-done.1
  34.9 1.0 %shard_map.118 = (f32[32,1,128]{2,1,0:T(1,128)}, f32[16,768]{1,0:T(8,128)S(1)}) custom-call(f32[1,16]{1,0:T(1,128)S(1)} %bitcast.19, f32[16,768]{1,0:T(8,128)S(1)} %bitcast.11, f32[16,768]{1,0:T(8,128)S(1)} %bitcast.15, f32[16,1024]{1,0:T(8,128)S(1)} %get-tuple-element.38.rest_0_, bf16[16,1024]{1,0:T(8,128)(2,1)S(1)} %collective-permute-done.7.rest_1_, ...), custom_call_target="tpu_custom_call" | custom-call | bytes 16384 | tf_op jit(solution)/shard_map/pallas_call | solution.py:393
  35.9 3.7 %all-to-all-start = ((f32[32,1,128]{2,1,0:T(1,128)}), f32[32,1,128]{2,1,0:T(1,128)S(1)}, u32[]{:S(2)}, u32[]{:S(2)}) async-start(f32[32,1,128]{2,1,0:T(1,128)} %get-tuple-element.44), calls=%async_computation | async-start | bytes 32768 | tf_op jit(solution)/shard_map/all_to_all | solution.py:502
  39.6 1.0 %shard_map.117 = (f32[16,768]{1,0:T(8,128)}, f32[16,768]{1,0:T(8,128)}, f32[16,32]{1,0:T(8,128)}, f32[16,128]{1,0:T(8,128)S(1)}) custom-call(f32[1,16]{1,0:T(1,128)S(1)} %bitcast.20, f32[16,768]{1,0:T(8,128)S(1)} %bitcast.12, f32[16,768]{1,0:T(8,128)S(1)} %bitcast.16, f32[16,768]{1,0:T(8,128)S(1)} %bitcast.18, f32[16,1024]{1,0:T(8,128)S(1)} %get-tuple-element.38.rest_0_, ...), custom_call_target="tpu_custom_call" | custom-call | bytes 1048576 | tf_op jit(solution)/shard_map/pallas_call | solution.py:393
  40.6 6.0 %all-to-all-done.norms_ref = f32[32,1,128]{2,1,0:T(1,128)S(1)} async-done(((f32[32,1,128]{2,1,0:T(1,128)}), f32[32,1,128]{2,1,0:T(1,128)S(1)}, u32[]{:S(2)}, u32[]{:S(2)}) %all-to-all-start) | async-done | bytes 16416 | tf_op jit(solution)/shard_map/all_to_all | solution.py:502
  46.7 0.8 %shard_map.119 = f32[16,768]{1,0:T(8,128)} custom-call(f32[32,1,128]{2,1,0:T(1,128)S(1)} %all-to-all-done.norms_ref, f32[16,128]{1,0:T(8,128)S(1)} %get-tuple-element.45.norm_ref, f32[16,768]{1,0:T(8,128)S(1)} %get-tuple-element.46.res_ref, f32[16,768]{1,0:T(8,128)S(1)} %bitcast.13), custom_call_target="tpu_custom_call" | custom-call | tf_op jit(solution)/shard_map/pallas_call | solution.py:393
  (7 shorter events, 0.0 us)
Async XLA Ops:
  0.6 7.7 %collective-permute-start = (f32[16,768]{1,0:T(8,128)}, f32[16,768]{1,0:T(8,128)S(1)}, u32[]{:S(2)}, u32[]{:S(2)}) collective-permute-start(f32[16,768]{1,0:T(8,128)} %bitcast.8), channel_id=1, source_target_pairs={{0,8},{8,0},{16,24},{24,16},{1,9},{9,1},{17,25},{25,17},{2,10},{10... | collective-permute-start | bytes 147464 | tf_op jit(solution)/shard_map/ppermute | solution.py:22
  3.7 4.6 %copy-start = (f32[768,16]{0,1:T(8,128)S(1)}, f32[768,16]{0,1:T(8,128)}, u32[]{:S(2)}) copy-start(f32[768,16]{0,1:T(8,128)} %param.15) | copy-start | bytes 147460
  8.2 10.1 %collective-permute-start.3 = (f32[40,1024]{1,0:T(8,128)S(1)}, f32[40,1024]{1,0:T(8,128)S(1)}, u32[]{:S(2)}, u32[]{:S(2)}) collective-permute-start(f32[40,1024]{1,0:T(8,128)S(1)} %get-tuple-element.32.cross_ref), channel_id=1, source_target_pairs={{0,1},{1,0},{2,3},{3,2},{4,5},{5,4},{6,7},{7,6},{8,9},{9,8},{10,11... | collective-permute-start | bytes 491528 | tf_op jit(solution)/shard_map/ppermute | solution.py:22
  8.4 8.3 %collective-permute-start.1 = (bf16[32,768]{1,0:T(8,128)(2,1)S(1)}, bf16[32,768]{1,0:T(8,128)(2,1)S(1)}, u32[]{:S(2)}, u32[]{:S(2)}) collective-permute-start(bf16[32,768]{1,0:T(8,128)(2,1)S(1)} %shard_map.111.pair_ref), channel_id=1, source_target_pairs={{0,16},{8,24},{16,0},{24,8},{1,17},{9,25},{17,1},{25,9},{2,18},{10... | collective-permute-start | bytes 147464 | tf_op jit(solution)/shard_map/ppermute | solution.py:22
  18.1 1.4 %collective-permute-start.2 = (f32[40,896]{1,0:T(8,128)S(1)}, f32[40,896]{1,0:T(8,128)S(1)}, u32[]{:S(2)}, u32[]{:S(2)}) collective-permute-start(f32[40,896]{1,0:T(8,128)S(1)} %shard_map.114.own_ref), channel_id=1, source_target_pairs={{0,1},{1,0},{2,3},{3,2},{4,5},{5,4},{6,7},{7,6},{8,9},{9,8},{10,11... | collective-permute-start | bytes 430088 | tf_op jit(solution)/shard_map/ppermute | solution.py:22
  19.7 5.6 %collective-permute-start.4 = (bf16[32,1280]{1,0:T(8,128)(2,1)S(1)}, bf16[32,1280]{1,0:T(8,128)(2,1)S(1)}, u32[]{:S(2)}, u32[]{:S(2)}) collective-permute-start(bf16[32,1280]{1,0:T(8,128)(2,1)S(1)} %get-tuple-element.35), channel_id=1, source_target_pairs={{0,6},{1,7},{2,4},{3,5},{4,2},{5,3},{6,0},{7,1},{8,14},{9,15},{10,... | collective-permute-start | bytes 245768 | tf_op jit(solution)/shard_map/ppermute | solution.py:22
  22.3 4.8 %collective-permute-start.5 = (bf16[32,1280]{1,0:T(8,128)(2,1)S(1)}, bf16[32,1280]{1,0:T(8,128)(2,1)S(1)}, u32[]{:S(2)}, u32[]{:S(2)}) collective-permute-start(bf16[32,1280]{1,0:T(8,128)(2,1)S(1)} %get-tuple-element.36), channel_id=1, source_target_pairs={{0,4},{1,5},{2,6},{3,7},{4,0},{5,1},{6,2},{7,3},{8,12},{9,13},{10,... | collective-permute-start | bytes 245768 | tf_op jit(solution)/shard_map/ppermute | solution.py:22
  22.8 4.4 %collective-permute-start.6 = (bf16[32,1280]{1,0:T(8,128)(2,1)S(1)}, bf16[32,1280]{1,0:T(8,128)(2,1)S(1)}, u32[]{:S(2)}, u32[]{:S(2)}) collective-permute-start(bf16[32,1280]{1,0:T(8,128)(2,1)S(1)} %get-tuple-element.37), channel_id=1, source_target_pairs={{0,2},{1,3},{2,0},{3,1},{4,6},{5,7},{6,4},{7,5},{8,10},{9,11},{10,... | collective-permute-start | bytes 245768 | tf_op jit(solution)/shard_map/ppermute | solution.py:22
  27.2 7.7 %copy-start.1 = (f32[768,16]{0,1:T(8,128)S(1)}, f32[768,16]{0,1:T(8,128)}, u32[]{:S(2)}) copy-start(f32[768,16]{0,1:T(8,128)} %param.14) | copy-start | bytes 147460
  27.2 7.7 %copy-start.3 = (f32[16]{0:T(128)S(1)}, f32[16]{0:T(128)}, u32[]{:S(2)}) copy-start(f32[16]{0:T(128)} %param.12) | copy-start | bytes 196
  27.2 12.4 %copy-start.2 = (f32[768,16]{0,1:T(8,128)S(1)}, f32[768,16]{0,1:T(8,128)}, u32[]{:S(2)}) copy-start(f32[768,16]{0,1:T(8,128)} %param.13) | copy-start | bytes 147460
  28.6 5.7 %collective-permute-start.7 = (bf16[16,1024]{1,0:T(8,128)(2,1)S(1)}, bf16[16,1024]{1,0:T(8,128)(2,1)S(1)}, u32[]{:S(2)}, u32[]{:S(2)}) collective-permute-start(bf16[16,1024]{1,0:T(8,128)(2,1)S(1)} %get-tuple-element.39), channel_id=1, source_target_pairs={{0,24},{8,16},{16,8},{24,0},{1,25},{9,17},{17,9},{25,1},{2,26},{10... | collective-permute-start | bytes 98312 | tf_op jit(solution)/shard_map/ppermute | solution.py:22
  28.8 5.5 %collective-permute-start.8 = (bf16[16,1024]{1,0:T(8,128)(2,1)S(1)}, bf16[16,1024]{1,0:T(8,128)(2,1)S(1)}, u32[]{:S(2)}, u32[]{:S(2)}) collective-permute-start(bf16[16,1024]{1,0:T(8,128)(2,1)S(1)} %get-tuple-element.40), channel_id=1, source_target_pairs={{0,16},{8,24},{16,0},{24,8},{1,17},{9,25},{17,1},{25,9},{2,18},{10... | collective-permute-start | bytes 98312 | tf_op jit(solution)/shard_map/ppermute | solution.py:22
  30.5 4.4 %collective-permute-start.9 = (bf16[16,1024]{1,0:T(8,128)(2,1)S(1)}, bf16[16,1024]{1,0:T(8,128)(2,1)S(1)}, u32[]{:S(2)}, u32[]{:S(2)}) collective-permute-start(bf16[16,1024]{1,0:T(8,128)(2,1)S(1)} %get-tuple-element.41), channel_id=1, source_target_pairs={{0,8},{8,0},{16,24},{24,16},{1,9},{9,1},{17,25},{25,17},{2,10},{10... | collective-permute-start | bytes 98312 | tf_op jit(solution)/shard_map/ppermute | solution.py:22
  35.9 10.8 %all-to-all-start = ((f32[32,1,128]{2,1,0:T(1,128)}), f32[32,1,128]{2,1,0:T(1,128)S(1)}, u32[]{:S(2)}, u32[]{:S(2)}) async-start(f32[32,1,128]{2,1,0:T(1,128)} %get-tuple-element.44), calls=%async_computation | async-start | bytes 32768 | tf_op jit(solution)/shard_map/all_to_all | solution.py:502

commit v6 on v5

--- a/solution.py
+++ b/solution.py
@@ -66,26 +66,34 @@
         called_ref[part, :] = call
         return carry
 
-    lax.fori_loop(0, rows // 16, group, 0)
-
-
-def row_copies(first, chunk, rows, pairs, sems):
+    lax.fori_loop(0, rows // 16, group, 0, unroll=2)
+
+
+def row_copies(first, chunks, pairs, sems):
+    starts = [sum(chunks[:i]) for i in range(len(chunks))]
     return [
-        [
-            pltpu.make_async_copy(
-                source.at[pl.ds(first + i * chunk, chunk)], target.at[pl.ds(i * chunk, chunk)], sems.at[j, i]
-            )
-            for j, (source, target) in enumerate(pairs)
-        ]
-        for i in range(rows // chunk)
+        (
+            start,
+            rows,
+            [
+                pltpu.make_async_copy(
+                    source.at[pl.ds(first + start, rows)], target.at[pl.ds(start, rows)], sems.at[j, i]
+                )
+                for j, (source, target) in enumerate(pairs)
+            ],
+        )
+        for i, (start, rows) in enumerate(zip(starts, chunks))
     ]
 
 
-def first_kernel(chunk, order_hbm, sol_hbm, dir_hbm, res_hbm, gen_hbm, call_hbm, dose_hbm,
+def chunks_of(rows):
+    return [LANES] * (rows // LANES - 1) + [LANES // 2] * 2
+
+
+def first_kernel(chunks, order_hbm, sol_hbm, dir_hbm, res_hbm, gen_hbm, call_hbm, dose_hbm,
                  coded_ref, called_ref, cross_ref, sums_ref,
                  order_ref, sol_ref, dir_ref, res_ref, gbuf, cbuf, dbuf, small_sems, sems):
     rhs = sol_hbm.shape[0]
-    rows = gbuf.shape[0]
     small = [
         pltpu.make_async_copy(source, target, small_sems.at[i])
         for i, (source, target) in enumerate(
@@ -94,8 +102,8 @@
     ]
     for copy in small:
         copy.start()
-    parts = row_copies(0, chunk, rows, ((gen_hbm, gbuf), (call_hbm, cbuf)), sems)
-    for part in parts:
+    parts = row_copies(0, chunks, ((gen_hbm, gbuf), (call_hbm, cbuf)), sems)
+    for _, _, part in parts:
         for copy in part:
             copy.start()
     for copy in small[:4]:
@@ -119,10 +127,10 @@
     cross = jnp.dot(picked, dose, preferred_element_type=F32)
     cross_ref[: 2 * rhs] = cross[: 2 * rhs] + cross[2 * rhs : 4 * rhs]
     cross_ref[2 * rhs :] = cross[4 * rhs : 4 * rhs + 8]
-    for i, part in enumerate(parts):
+    for start, count, part in parts:
         for copy in part:
             copy.wait()
-        convert(gbuf, cbuf, coded_ref, called_ref, i * chunk, chunk)
+        convert(gbuf, cbuf, coded_ref, called_ref, start, count)
 
 
 def pair_kernel(own_ref, other_ref, out_ref):
@@ -159,12 +167,12 @@
     return pl.ds(pl.multiple_of(pair * 2 * own, LANES), 2 * own)
 
 
-def second_kernel(chunk, pair_ref, coded_first, called_first, gen_hbm, call_hbm,
+def second_kernel(chunks, pair_ref, coded_first, called_first, gen_hbm, call_hbm,
                   coded_ref, called_ref, out_ref, gbuf, cbuf, w1, w2, sems):
-    first, rows = coded_first.shape[0], gbuf.shape[0]
+    first = coded_first.shape[0]
     own = pair_ref.shape[1]
-    parts = row_copies(first, chunk, rows, ((gen_hbm, gbuf), (call_hbm, cbuf)), sems)
-    for part in parts:
+    parts = row_copies(first, chunks, ((gen_hbm, gbuf), (call_hbm, cbuf)), sems)
+    for _, _, part in parts:
         for copy in part:
             copy.start()
     samples = pair_samples(lax.axis_index("var") // 2, own)
@@ -172,14 +180,15 @@
     for i in range(first // LANES):
         place = i * LANES
         out_ref[:, place : place + LANES] = product(coded_first, called_first, place, LANES, samples, w1, w2)
-    for i, part in enumerate(parts):
+    for start, count, part in parts:
         for copy in part:
             copy.wait()
-        place = i * chunk
-        convert(gbuf, cbuf, coded_ref, called_ref, place, chunk)
-        out_ref[:, first + place : first + place + chunk] = product(
-            coded_ref, called_ref, place, chunk, samples, w1, w2
-        )
+        convert(gbuf, cbuf, coded_ref, called_ref, start, count)
+        if (start + count) % LANES == 0:
+            place = start + count - LANES
+            out_ref[:, first + place : first + place + LANES] = product(
+                coded_ref, called_ref, place, LANES, samples, w1, w2
+            )
 
 
 def third_kernel(pair_ref, coded_first, called_first, coded_ref, called_ref, half_ref, sums_ref, out_ref, w1, w2):
@@ -212,9 +221,14 @@
     return block
 
 
-def chips_kernel(n_var, width, own_ref, other_ref, cross_ref, cross_other_ref,
-                 total_ref, mine_ref, *rest):
-    messages, (both,) = rest[:-1], rest[-1:]
+def partners(n_chips):
+    far = list(reversed(range(n_chips // 2, n_chips)))
+    near = list(reversed(range(1, n_chips // 2)))
+    return list(zip(near + [0] * (len(far) - len(near)), far))
+
+
+def chips_kernel(n_var, width, distances, own_ref, other_ref, cross_ref, cross_other_ref, total_ref, mine_ref, *rest):
+    messages, both = rest[:-1], rest[-1]
     samp = lax.axis_index("samp")
     core = samp % 2
     chip = samp // 2
@@ -239,15 +253,19 @@
     for part, values in enumerate(thirds(total[0:16, rows:])):
         values = values.astype(F32)
         sums = sums + (pltpu.roll(values, 16 * part, 1) if part else values)
-    for k, message in enumerate(messages):
-        chunk = chunk_of(both, ((chip ^ (k + 1)) * 2 + core) * width, n_var, width)
-        high, low = halves(chunk[0:32])
-        dose = jnp.concatenate([p.astype(F32) for p in thirds(chunk[32:33])] + [jnp.zeros((13, LANES), F32)])
+    for (zero, one), message in zip(distances, messages):
+        target = chip ^ jnp.where(core == 0, zero, one)
+        dose = []
+        for c in range(2):
+            chunk = chunk_of(both, (target * 2 + c) * width, n_var, width)
+            for i, part in enumerate(halves(chunk[0:32])):
+                at = rows + (2 * c + i) * LANES
+                message[:, at : at + LANES] = part
+            dose += [p.astype(F32) for p in thirds(chunk[32:33])]
+        dose = jnp.concatenate(dose + [jnp.zeros((10, LANES), F32)])
         message[:, :rows] = main
-        message[:, rows : rows + LANES] = high
-        message[:, rows + LANES : rows + 2 * LANES] = low
-        message[:, rows + 2 * LANES : rows + 3 * LANES] = counts
-        message[:, rows + 3 * LANES :] = jnp.concatenate([sums, dose], axis=0).astype(BF16)
+        message[:, rows + 4 * LANES : rows + 5 * LANES] = counts
+        message[:, rows + 5 * LANES :] = jnp.concatenate([sums, dose], axis=0).astype(BF16)
 
 
 def back_kernel(variants, width, n_arrived, total_ref, mine_ref, coded_first, called_first,
@@ -264,12 +282,14 @@
     dose = mine_ref[32:33]
     got_counts = jnp.zeros((32, LANES), F32)
     got_last = jnp.zeros((32, LANES), F32)
+    core = lax.axis_index("samp") % 2
     for ref in arrived:
         main = main + ref[:, :rows].astype(F32)
-        cross = cross + ref[:, rows : rows + LANES].astype(F32)
-        cross = cross + ref[:, rows + LANES : rows + 2 * LANES].astype(F32)
-        got_counts = got_counts + ref[:, rows + 2 * LANES : rows + 3 * LANES].astype(F32)
-        got_last = got_last + ref[:, rows + 3 * LANES :].astype(F32)
+        for i in range(2):
+            at = pl.ds(pl.multiple_of(rows + (2 * core + i) * LANES, LANES), LANES)
+            cross = cross + ref[:, at].astype(F32)
+        got_counts = got_counts + ref[:, rows + 4 * LANES : rows + 5 * LANES].astype(F32)
+        got_last = got_last + ref[:, rows + 5 * LANES :].astype(F32)
     tiles = rows // LANES
     pick = lambda first: jnp.concatenate(
         [got_counts[first + j : first + j + 1] + got_counts[first + 2 * tiles + j : first + 2 * tiles + j + 1]
@@ -279,7 +299,9 @@
     count = count + pick(tiles)
     last = got_last[0:16]
     sums = sums + last + pltpu.roll(last, LANES - 16, 1) + pltpu.roll(last, LANES - 32, 1)
-    dose = dose + got_last[16:17] + got_last[17:18] + got_last[18:19]
+    first_dose = got_last[16:17] + got_last[17:18] + got_last[18:19]
+    second_dose = got_last[19:20] + got_last[20:21] + got_last[21:22]
+    dose = dose + jnp.where(core == 0, first_dose, second_dose)
 
     frequency = (allele + 1.0) / (2.0 * count + 2.0)
     spread = jnp.sqrt(2.0 * frequency * (1.0 - frequency))
@@ -413,13 +435,13 @@
     noise = noise_ratio[None]
 
     dire, res, sol = direction.T, residual.T, solution.T
-    first, chunk = rows // 3, 128
+    first = rows // 3
     rest = rows - first
     matrix = lambda n: ((n, shard), BF16, pltpu.VMEM)
 
     neighbour = swap(dire, "var", 1)
     coded_a, called_a, cross, sums = call(
-        functools.partial(first_kernel, chunk),
+        functools.partial(first_kernel, chunks_of(first)),
         [matrix(first), matrix(first), ((2 * rhs + 8, imputed), F32), ((rhs, LANES), F32)],
         [HBM] * 7,
         (sample_order, sol, dire, res, genotypes, called, dosage),
@@ -432,7 +454,7 @@
             pltpu.VMEM((first, shard), jnp.int32),
             pltpu.VMEM((own, imputed), jnp.int32),
             pltpu.SemaphoreType.DMA((5,)),
-            pltpu.SemaphoreType.DMA((2, first // chunk)),
+            pltpu.SemaphoreType.DMA((2, len(chunks_of(first)))),
         ],
         limit=24,
         flops=2 * 80 * own * (own + imputed),
@@ -443,7 +465,7 @@
     cross_other = swap(cross, "samp", 1)
     both_weights = [pltpu.VMEM((48, 2 * own), BF16), pltpu.VMEM((48, 2 * own), BF16)]
     coded_b, called_b, half = call(
-        functools.partial(second_kernel, chunk),
+        functools.partial(second_kernel, chunks_of(rest)),
         [matrix(rest), matrix(rest), ((2 * rhs + 8, rows), F32)],
         [VMEM] * 3 + [HBM] * 2,
         (pair, coded_a, called_a, genotypes, called),
@@ -451,7 +473,7 @@
             pltpu.VMEM((rest, shard), jnp.int32),
             pltpu.VMEM((rest, shard), jnp.int32),
             *both_weights,
-            pltpu.SemaphoreType.DMA((2, rest // chunk)),
+            pltpu.SemaphoreType.DMA((2, len(chunks_of(rest)))),
         ],
         limit=24,
         flops=2 * rows * shard * 256,
@@ -469,22 +491,29 @@
     part_other = swap(part, "samp", 1)
 
     n_chips = n_samp // 2
-    message = ((2 * rhs, rows + 4 * LANES), BF16)
+    distances = partners(n_chips)
+    message = ((2 * rhs, rows + 6 * LANES), BF16)
     total, mine, *messages = call(
-        functools.partial(chips_kernel, n_var, width),
-        [(part.shape, F32), ((2 * rhs + 8, LANES), F32)] + [message] * (n_chips - 1),
+        functools.partial(chips_kernel, n_var, width, distances),
+        [(part.shape, F32), ((2 * rhs + 8, LANES), F32)] + [message] * len(distances),
         [VMEM] * 4,
         (part, part_other, cross, cross_other),
         scratch=[pltpu.VMEM(cross.shape, F32)],
         moved=1 * MIB,
     )
-    arrived = [swap(messages[k], "samp", 2 * (k + 1)) for k in reversed(range(n_chips - 1))]
+    came, handed = [], []
+    for (zero, one), m in zip(distances, messages):
+        pairs = [(i, i ^ (2 * (one if i % 2 else zero))) for i in range(n_samp) if i % 2 or zero]
+        came.append(lax.ppermute(m, "samp", pairs))
+    for (zero, one), m in zip(distances, came):
+        handed.append(lax.ppermute(m, "samp", [(i, i ^ 1) for i in range(n_samp) if i % 2 or zero]))
+    arrived = came + handed
 
     wide = own + 2 * LANES
     mine_back, *messages = call(
-        functools.partial(back_kernel, variants, width, n_chips - 1),
+        functools.partial(back_kernel, variants, width, len(arrived)),
         [((rhs, wide), F32)] + [((rhs, wide), BF16)] * (n_var - 1),
-        [VMEM] * (6 + n_chips - 1),
+        [VMEM] * (6 + len(arrived)),
         (total, mine, coded_a, called_a, coded_b, called_b, *arrived),
         flops=4 * rows * shard * 256,
         moved=4 * rows * shard,
@@ -494,7 +523,7 @@
     n_all = n_var * n_samp
     norms, res_keep = call(
         functools.partial(norm_kernel, variants),
-        [((n_all, 1, LANES), F32), ((rhs, own), F32)],
+        [((n_all, 1, LANES), F32, pltpu.VMEM), ((rhs, own), F32)],
         [VMEM] * (3 + n_var),
         (noise, dire, res, *backs),
         moved=4 * n_all * LANES,

time: 47.7 us -> 50.1 us (1.050)
  waiting for transfers between devices: 13 us -> 15.4 us
    ppermute x0 -> x4, waiting for transfers between devices: none -> 6.32 us  [the longest x2 3.33 us: body(): came.append(lax.ppermute(m, 'samp', pairs))]
    ppermute x10 -> x7, waiting for transfers between devices: 6.97 us -> 3.08 us  [swap(): return lax.ppermute(values, axis, [(i, i ^ distance) for i in range(size)])]
    ppermute x10 -> x7, starting transfers between devices: 14 us -> 10.5 us  [swap(): return lax.ppermute(values, axis, [(i, i ^ distance) for i in range(size)])]
    ppermute x0 -> x4, starting transfers between devices: none -> 3.49 us  [the longest x2 2.21 us: body(): came.append(lax.ppermute(m, 'samp', pairs))]
  transfers between devices with their start and end apart: 11 -> 12, of which waited for: 7 -> 6; matrix products, arithmetic and copies ran while one was open for 0% -> 0% of each run, Pallas kernels for 27% -> 26%
where the time goes in v6:
time: 50.1 us; the launch traced here: 49.9 us
  starting transfers between devices  17.5 us (35%)
  Pallas kernels  16.2 us (32%)
  waiting for transfers between devices  15.4 us (31%)
  between operations  0.75 us (1%)
    pallas_call x9, Pallas kernels, call(): pl.pallas_call(kernel, out_shape=[jax.ShapeDtypeStruct(*o) if len(o) == 2...  16.2 us
    ppermute x7, starting transfers between devices, swap(): return lax.ppermute(values, axis, [(i, i ^ distance) for i in range(size)])  10.5 us
    all_to_all x1, waiting for transfers between devices, body(): norms = lax.all_to_all(norms, ('var', 'samp'), split_axis=0, concat_axis=0)  6.04 us
    all_to_all x1, starting transfers between devices, body(): norms = lax.all_to_all(norms, ('var', 'samp'), split_axis=0, concat_axis=0)  3.55 us
    ppermute x2, waiting for transfers between devices, body(): came.append(lax.ppermute(m, 'samp', pairs))  3.33 us
    ppermute x7, waiting for transfers between devices, swap(): return lax.ppermute(values, axis, [(i, i ^ distance) for i in range(size)])  3.08 us
    ppermute x2, waiting for transfers between devices, body(): lax.ppermute(m, 'samp', [(i, i ^ 1) for i in range(n_samp) if i % 2 or ze...  2.99 us
    ppermute x2, starting transfers between devices, body(): came.append(lax.ppermute(m, 'samp', pairs))  2.21 us
  transfers between devices with their start and end apart: 12, of which 6 were waited for; matrix products, arithmetic and copies ran while one was open for 0% of the time, Pallas kernels for 26%

profile of v6, /device:TPU:0, one launch (start us, length us, event | category | flops | bytes accessed | tf_op | source)
XLA Modules:
  0.0 49.9 jit_solution(6213734506956077074)
XLA Ops:
  0.6 3.1 %collective-permute-start = (f32[16,768]{1,0:T(8,128)}, f32[16,768]{1,0:T(8,128)S(1)}, u32[]{:S(2)}, u32[]{:S(2)}) collective-permute-start(f32[16,768]{1,0:T(8,128)} %bitcast.8), channel_id=1, source_target_pairs={{0,8},{8,0},{16,24},{24,16},{1,9},{9,1},{17,25},{25,17},{2,10},{10... | collective-permute-start | bytes 147464 | tf_op jit(solution)/shard_map/ppermute | solution.py:22
  3.7 4.7 %shard_map.112 = (bf16[256,3072]{1,0:T(8,128)(2,1)S(1)}, bf16[256,3072]{1,0:T(8,128)(2,1)S(1)}, f32[40,1024]{1,0:T(8,128)S(1)}, f32[16,128]{1,0:T(8,128)S(1)}) custom-call(s32[1,768]{1,0:T(1,128)} %order_hbm.1, f32[16,768]{1,0:T(8,128)} %bitcast.17, f32[16,768]{1,0:T(8,128)} %bitcast.9, f32[16,768]{1,0:T(8,128)} %bitcast.14, s32[768,3072]{1,0:T(8,128)} %gen_hbm.3, ...), custom_call_target="tpu_custom_call" | custom-call | flops 220200960 | bytes 9437184 | tf_op jit(solution)/shard_map/pallas_call | solution.py:415
  8.4 0.1 collective-permute-start.3
  8.5 0.0 collective-permute-done.other_ref
  8.6 2.7 %collective-permute-start.1 = (bf16[32,768]{1,0:T(8,128)(2,1)S(1)}, bf16[32,768]{1,0:T(8,128)(2,1)S(1)}, u32[]{:S(2)}, u32[]{:S(2)}) collective-permute-start(bf16[32,768]{1,0:T(8,128)(2,1)S(1)} %shard_map.111.pair_ref), channel_id=1, source_target_pairs={{0,16},{8,24},{16,0},{24,8},{1,17},{9,25},{17,1},{25,9},{2,18},{10... | collective-permute-start | bytes 147464 | tf_op jit(solution)/shard_map/ppermute | solution.py:22
  11.2 5.6 %shard_map.113 = (bf16[512,3072]{1,0:T(8,128)(2,1)S(1)}, bf16[512,3072]{1,0:T(8,128)(2,1)S(1)}, f32[40,768]{1,0:T(8,128)S(1)}) custom-call(bf16[32,768]{1,0:T(8,128)(2,1)S(1)} %shard_map.111.pair_ref, bf16[256,3072]{1,0:T(8,128)(2,1)S(1)} %get-tuple-element.25.coded_first, bf16[256,3072]{1,0:T(8,128)(2,1)S(1)} %get-tuple-element.26.called_first, ...), custom_call_target="tpu_custom_call" | custom-call | flops 1207959552 | bytes 12582912 | tf_op jit(solution)/shard_map/pallas_call | solution.py:415
  16.8 0.0 collective-permute-done.1.pair_ref
  16.8 1.4 %shard_map.114.own_ref = f32[40,896]{1,0:T(8,128)S(1)} custom-call(bf16[32,768]{1,0:T(8,128)(2,1)S(1)} %collective-permute-done.1.pair_ref, bf16[256,3072]{1,0:T(8,128)(2,1)S(1)} %get-tuple-element.25.coded_first, bf16[256,3072]{1,0:T(8,128)(2,1)S(1)} %get-tuple-element.26.called_first, bf16[512,3072]{1,0:T(8,128)(2,1)S(1)} %get-tuple-element.27.coded_ref, ...), custom_call_target="tpu_custom_call" | custom-call | flops 1207959552 | bytes 4718592 | tf_op jit(solution)/shard_map/pallas_call | solution.py:415
  18.3 0.3 collective-permute-start.2
  18.5 0.0 collective-permute-done.3.cross_other_ref
  18.5 1.2 %collective-permute-done.2.other_ref = f32[40,896]{1,0:T(8,128)S(1)} collective-permute-done((f32[40,896]{1,0:T(8,128)S(1)}, f32[40,896]{1,0:T(8,128)S(1)}, u32[]{:S(2)}, u32[]{:S(2)}) %collective-permute-start.2) | collective-permute-done | bytes 143392 | tf_op jit(solution)/shard_map/ppermute | solution.py:22
  19.7 0.2 shard_map.115
  19.9 1.6 %collective-permute-start.4 = (bf16[32,1536]{1,0:T(8,128)(2,1)S(1)}, bf16[32,1536]{1,0:T(8,128)(2,1)S(1)}, u32[]{:S(2)}, u32[]{:S(2)}) collective-permute-start(bf16[32,1536]{1,0:T(8,128)(2,1)S(1)} %get-tuple-element.34), channel_id=1, source_target_pairs={{0,2},{1,7},{2,0},{3,5},{4,6},{5,3},{6,4},{7,1},{8,10},{9,15},{10,... | collective-permute-start | bytes 294920 | tf_op jit(solution)/shard_map/ppermute | solution.py:507
  21.5 0.7 %collective-permute-start.5 = (bf16[32,1536]{1,0:T(8,128)(2,1)S(1)}, bf16[32,1536]{1,0:T(8,128)(2,1)S(1)}, u32[]{:S(2)}, u32[]{:S(2)}) collective-permute-start(bf16[32,1536]{1,0:T(8,128)(2,1)S(1)} %get-tuple-element.35), channel_id=1, source_target_pairs={{1,5},{3,7},{5,1},{7,3},{9,13},{11,15},{13,9},{15,11},{17,21},{19,... | collective-permute-start | bytes 294920 | tf_op jit(solution)/shard_map/ppermute | solution.py:507
  22.2 3.3 %collective-permute-done.4.rest_0_ = bf16[32,1536]{1,0:T(8,128)(2,1)S(1)} collective-permute-done((bf16[32,1536]{1,0:T(8,128)(2,1)S(1)}, bf16[32,1536]{1,0:T(8,128)(2,1)S(1)}, u32[]{:S(2)}, u32[]{:S(2)}) %collective-permute-start.4) | collective-permute-done | bytes 98336 | tf_op jit(solution)/shard_map/ppermute | solution.py:507
  25.5 0.0 collective-permute-start.6
  25.5 0.0 collective-permute-done.5.rest_1_
  25.5 1.3 %collective-permute-start.7 = (bf16[32,1536]{1,0:T(8,128)(2,1)S(1)}, bf16[32,1536]{1,0:T(8,128)(2,1)S(1)}, u32[]{:S(2)}, u32[]{:S(2)}) collective-permute-start(bf16[32,1536]{1,0:T(8,128)(2,1)S(1)} %collective-permute-done.5.rest_1_), channel_id=1, source_target_pairs={{1,0},{3,2},{5,4},{7,6},{9,8},{11,10},{13,12},{15,14},{17,16},{19,... | collective-permute-start | bytes 294920 | tf_op jit(solution)/shard_map/ppermute | solution.py:509
  26.8 0.0 collective-permute-done.6.rest_2_
  26.8 3.0 %collective-permute-done.7.rest_3_ = bf16[32,1536]{1,0:T(8,128)(2,1)S(1)} collective-permute-done((bf16[32,1536]{1,0:T(8,128)(2,1)S(1)}, bf16[32,1536]{1,0:T(8,128)(2,1)S(1)}, u32[]{:S(2)}, u32[]{:S(2)}) %collective-permute-start.7) | collective-permute-done | bytes 98336 | tf_op jit(solution)/shard_map/ppermute | solution.py:509
  29.8 1.4 %shard_map.116 = (f32[16,1024]{1,0:T(8,128)S(1)}, bf16[16,1024]{1,0:T(8,128)(2,1)S(1)}, bf16[16,1024]{1,0:T(8,128)(2,1)S(1)}, bf16[16,1024]{1,0:T(8,128)(2,1)S(1)}) custom-call(f32[40,896]{1,0:T(8,128)S(1)} %get-tuple-element.32.total_ref, f32[40,128]{1,0:T(8,128)S(1)} %get-tuple-element.33.mine_ref, bf16[256,3072]{1,0:T(8,128)(2,1)S(1)} %get-tuple-element.25.coded_first, ...), custom_call_target="tpu_custom_call" | custom-call | flops 2415919104 | bytes 9437184 | tf_op jit(solution)/shard_map/pallas_call | solution.py:415
  31.2 0.2 collective-permute-start.8
  31.4 1.7 %collective-permute-start.9 = (bf16[16,1024]{1,0:T(8,128)(2,1)S(1)}, bf16[16,1024]{1,0:T(8,128)(2,1)S(1)}, u32[]{:S(2)}, u32[]{:S(2)}) collective-permute-start(bf16[16,1024]{1,0:T(8,128)(2,1)S(1)} %get-tuple-element.38), channel_id=1, source_target_pairs={{0,16},{8,24},{16,0},{24,8},{1,17},{9,25},{17,1},{25,9},{2,18},{10... | collective-permute-start | bytes 98312 | tf_op jit(solution)/shard_map/ppermute | solution.py:22
  33.1 2.5 %collective-permute-start.10 = (bf16[16,1024]{1,0:T(8,128)(2,1)S(1)}, bf16[16,1024]{1,0:T(8,128)(2,1)S(1)}, u32[]{:S(2)}, u32[]{:S(2)}) collective-permute-start(bf16[16,1024]{1,0:T(8,128)(2,1)S(1)} %get-tuple-element.39), channel_id=1, source_target_pairs={{0,8},{8,0},{16,24},{24,16},{1,9},{9,1},{17,25},{25,17},{2,10},{10... | collective-permute-start | bytes 98312 | tf_op jit(solution)/shard_map/ppermute | solution.py:22
  35.6 1.6 %collective-permute-done.8.rest_1_ = bf16[16,1024]{1,0:T(8,128)(2,1)S(1)} collective-permute-done((bf16[16,1024]{1,0:T(8,128)(2,1)S(1)}, bf16[16,1024]{1,0:T(8,128)(2,1)S(1)}, u32[]{:S(2)}, u32[]{:S(2)}) %collective-permute-start.8) | collective-permute-done | bytes 32800 | tf_op jit(solution)/shard_map/ppermute | solution.py:22
  37.1 0.0 collective-permute-done.9.rest_2_
  37.1 0.3 collective-permute-done.10.rest_3_
  37.5 1.0 %shard_map.118 = (f32[32,1,128]{2,1,0:T(1,128)}, f32[16,768]{1,0:T(8,128)S(1)}) custom-call(f32[1,16]{1,0:T(1,128)S(1)} %bitcast.19, f32[16,768]{1,0:T(8,128)S(1)} %bitcast.11, f32[16,768]{1,0:T(8,128)S(1)} %bitcast.15, f32[16,1024]{1,0:T(8,128)S(1)} %get-tuple-element.36.rest_0_, bf16[16,1024]{1,0:T(8,128)(2,1)S(1)} %collective-permute-done.8.rest_1_, ...), custom_call_target="tpu_custom_call" | custom-call | bytes 16384 | tf_op jit(solution)/shard_map/pallas_call | solution.py:415
  38.5 3.5 %all-to-all-start = ((f32[32,1,128]{2,1,0:T(1,128)}), f32[32,1,128]{2,1,0:T(1,128)S(1)}, u32[]{:S(2)}, u32[]{:S(2)}) async-start(f32[32,1,128]{2,1,0:T(1,128)} %get-tuple-element.42), calls=%async_computation | async-start | bytes 32768 | tf_op jit(solution)/shard_map/all_to_all | solution.py:531
  42.0 1.0 %shard_map.117 = (f32[16,768]{1,0:T(8,128)}, f32[16,768]{1,0:T(8,128)}, f32[16,32]{1,0:T(8,128)}, f32[16,128]{1,0:T(8,128)S(1)}) custom-call(f32[1,16]{1,0:T(1,128)S(1)} %bitcast.20, f32[16,768]{1,0:T(8,128)S(1)} %bitcast.12, f32[16,768]{1,0:T(8,128)S(1)} %bitcast.16, f32[16,768]{1,0:T(8,128)S(1)} %bitcast.18, f32[16,1024]{1,0:T(8,128)S(1)} %get-tuple-element.36.rest_0_, ...), custom_call_target="tpu_custom_call" | custom-call | bytes 1048576 | tf_op jit(solution)/shard_map/pallas_call | solution.py:415
  43.1 6.0 %all-to-all-done.norms_ref = f32[32,1,128]{2,1,0:T(1,128)S(1)} async-done(((f32[32,1,128]{2,1,0:T(1,128)}), f32[32,1,128]{2,1,0:T(1,128)S(1)}, u32[]{:S(2)}, u32[]{:S(2)}) %all-to-all-start) | async-done | bytes 16416 | tf_op jit(solution)/shard_map/all_to_all | solution.py:531
  49.1 0.8 %shard_map.119 = f32[16,768]{1,0:T(8,128)} custom-call(f32[32,1,128]{2,1,0:T(1,128)S(1)} %all-to-all-done.norms_ref, f32[16,128]{1,0:T(8,128)S(1)} %get-tuple-element.43.norm_ref, f32[16,768]{1,0:T(8,128)S(1)} %get-tuple-element.44.res_ref, f32[16,768]{1,0:T(8,128)S(1)} %bitcast.13), custom_call_target="tpu_custom_call" | custom-call | tf_op jit(solution)/shard_map/pallas_call | solution.py:415
  (9 shorter events, 0.0 us)
Async XLA Ops:
  0.6 7.9 %collective-permute-start = (f32[16,768]{1,0:T(8,128)}, f32[16,768]{1,0:T(8,128)S(1)}, u32[]{:S(2)}, u32[]{:S(2)}) collective-permute-start(f32[16,768]{1,0:T(8,128)} %bitcast.8), channel_id=1, source_target_pairs={{0,8},{8,0},{16,24},{24,16},{1,9},{9,1},{17,25},{25,17},{2,10},{10... | collective-permute-start | bytes 147464 | tf_op jit(solution)/shard_map/ppermute | solution.py:22
  3.7 4.8 %copy-start = (f32[768,16]{0,1:T(8,128)S(1)}, f32[768,16]{0,1:T(8,128)}, u32[]{:S(2)}) copy-start(f32[768,16]{0,1:T(8,128)} %param.15) | copy-start | bytes 147460
  8.4 10.1 %collective-permute-start.3 = (f32[40,1024]{1,0:T(8,128)S(1)}, f32[40,1024]{1,0:T(8,128)S(1)}, u32[]{:S(2)}, u32[]{:S(2)}) collective-permute-start(f32[40,1024]{1,0:T(8,128)S(1)} %get-tuple-element.31.cross_ref), channel_id=1, source_target_pairs={{0,1},{1,0},{2,3},{3,2},{4,5},{5,4},{6,7},{7,6},{8,9},{9,8},{10,11... | collective-permute-start | bytes 491528 | tf_op jit(solution)/shard_map/ppermute | solution.py:22
  8.6 8.3 %collective-permute-start.1 = (bf16[32,768]{1,0:T(8,128)(2,1)S(1)}, bf16[32,768]{1,0:T(8,128)(2,1)S(1)}, u32[]{:S(2)}, u32[]{:S(2)}) collective-permute-start(bf16[32,768]{1,0:T(8,128)(2,1)S(1)} %shard_map.111.pair_ref), channel_id=1, source_target_pairs={{0,16},{8,24},{16,0},{24,8},{1,17},{9,25},{17,1},{25,9},{2,18},{10... | collective-permute-start | bytes 147464 | tf_op jit(solution)/shard_map/ppermute | solution.py:22
  18.3 1.4 %collective-permute-start.2 = (f32[40,896]{1,0:T(8,128)S(1)}, f32[40,896]{1,0:T(8,128)S(1)}, u32[]{:S(2)}, u32[]{:S(2)}) collective-permute-start(f32[40,896]{1,0:T(8,128)S(1)} %shard_map.114.own_ref), channel_id=1, source_target_pairs={{0,1},{1,0},{2,3},{3,2},{4,5},{5,4},{6,7},{7,6},{8,9},{9,8},{10,11... | collective-permute-start | bytes 430088 | tf_op jit(solution)/shard_map/ppermute | solution.py:22
  19.9 5.5 %collective-permute-start.4 = (bf16[32,1536]{1,0:T(8,128)(2,1)S(1)}, bf16[32,1536]{1,0:T(8,128)(2,1)S(1)}, u32[]{:S(2)}, u32[]{:S(2)}) collective-permute-start(bf16[32,1536]{1,0:T(8,128)(2,1)S(1)} %get-tuple-element.34), channel_id=1, source_target_pairs={{0,2},{1,7},{2,0},{3,5},{4,6},{5,3},{6,4},{7,1},{8,10},{9,15},{10,... | collective-permute-start | bytes 294920 | tf_op jit(solution)/shard_map/ppermute | solution.py:507
  21.5 4.0 %collective-permute-start.5 = (bf16[32,1536]{1,0:T(8,128)(2,1)S(1)}, bf16[32,1536]{1,0:T(8,128)(2,1)S(1)}, u32[]{:S(2)}, u32[]{:S(2)}) collective-permute-start(bf16[32,1536]{1,0:T(8,128)(2,1)S(1)} %get-tuple-element.35), channel_id=1, source_target_pairs={{1,5},{3,7},{5,1},{7,3},{9,13},{11,15},{13,9},{15,11},{17,21},{19,... | collective-permute-start | bytes 294920 | tf_op jit(solution)/shard_map/ppermute | solution.py:507
  25.5 1.3 %collective-permute-start.6 = (bf16[32,1536]{1,0:T(8,128)(2,1)S(1)}, bf16[32,1536]{1,0:T(8,128)(2,1)S(1)}, u32[]{:S(2)}, u32[]{:S(2)}) collective-permute-start(bf16[32,1536]{1,0:T(8,128)(2,1)S(1)} %collective-permute-done.4.rest_0_), channel_id=1, source_target_pairs={{0,1},{1,0},{2,3},{3,2},{4,5},{5,4},{6,7},{7,6},{8,9},{9,8},{10,11... | collective-permute-start | bytes 294920 | tf_op jit(solution)/shard_map/ppermute | solution.py:509
  25.5 4.3 %collective-permute-start.7 = (bf16[32,1536]{1,0:T(8,128)(2,1)S(1)}, bf16[32,1536]{1,0:T(8,128)(2,1)S(1)}, u32[]{:S(2)}, u32[]{:S(2)}) collective-permute-start(bf16[32,1536]{1,0:T(8,128)(2,1)S(1)} %collective-permute-done.5.rest_1_), channel_id=1, source_target_pairs={{1,0},{3,2},{5,4},{7,6},{9,8},{11,10},{13,12},{15,14},{17,16},{19,... | collective-permute-start | bytes 294920 | tf_op jit(solution)/shard_map/ppermute | solution.py:509
  29.8 7.7 %copy-start.1 = (f32[768,16]{0,1:T(8,128)S(1)}, f32[768,16]{0,1:T(8,128)}, u32[]{:S(2)}) copy-start(f32[768,16]{0,1:T(8,128)} %param.14) | copy-start | bytes 147460
  29.8 7.7 %copy-start.3 = (f32[16]{0:T(128)S(1)}, f32[16]{0:T(128)}, u32[]{:S(2)}) copy-start(f32[16]{0:T(128)} %param.12) | copy-start | bytes 196
  29.8 12.3 %copy-start.2 = (f32[768,16]{0,1:T(8,128)S(1)}, f32[768,16]{0,1:T(8,128)}, u32[]{:S(2)}) copy-start(f32[768,16]{0,1:T(8,128)} %param.13) | copy-start | bytes 147460
  31.2 6.0 %collective-permute-start.8 = (bf16[16,1024]{1,0:T(8,128)(2,1)S(1)}, bf16[16,1024]{1,0:T(8,128)(2,1)S(1)}, u32[]{:S(2)}, u32[]{:S(2)}) collective-permute-start(bf16[16,1024]{1,0:T(8,128)(2,1)S(1)} %get-tuple-element.37), channel_id=1, source_target_pairs={{0,24},{8,16},{16,8},{24,0},{1,25},{9,17},{17,9},{25,1},{2,26},{10... | collective-permute-start | bytes 98312 | tf_op jit(solution)/shard_map/ppermute | solution.py:22
  31.4 5.7 %collective-permute-start.9 = (bf16[16,1024]{1,0:T(8,128)(2,1)S(1)}, bf16[16,1024]{1,0:T(8,128)(2,1)S(1)}, u32[]{:S(2)}, u32[]{:S(2)}) collective-permute-start(bf16[16,1024]{1,0:T(8,128)(2,1)S(1)} %get-tuple-element.38), channel_id=1, source_target_pairs={{0,16},{8,24},{16,0},{24,8},{1,17},{9,25},{17,1},{25,9},{2,18},{10... | collective-permute-start | bytes 98312 | tf_op jit(solution)/shard_map/ppermute | solution.py:22
  33.1 4.4 %collective-permute-start.10 = (bf16[16,1024]{1,0:T(8,128)(2,1)S(1)}, bf16[16,1024]{1,0:T(8,128)(2,1)S(1)}, u32[]{:S(2)}, u32[]{:S(2)}) collective-permute-start(bf16[16,1024]{1,0:T(8,128)(2,1)S(1)} %get-tuple-element.39), channel_id=1, source_target_pairs={{0,8},{8,0},{16,24},{24,16},{1,9},{9,1},{17,25},{25,17},{2,10},{10... | collective-permute-start | bytes 98312 | tf_op jit(solution)/shard_map/ppermute | solution.py:22
  38.5 10.6 %all-to-all-start = ((f32[32,1,128]{2,1,0:T(1,128)}), f32[32,1,128]{2,1,0:T(1,128)S(1)}, u32[]{:S(2)}, u32[]{:S(2)}) async-start(f32[32,1,128]{2,1,0:T(1,128)} %get-tuple-element.42), calls=%async_computation | async-start | bytes 32768 | tf_op jit(solution)/shard_map/all_to_all | solution.py:531

commit v7 on v6

--- a/solution.py
+++ b/solution.py
@@ -66,7 +66,7 @@
         called_ref[part, :] = call
         return carry
 
-    lax.fori_loop(0, rows // 16, group, 0, unroll=2)
+    lax.fori_loop(0, rows // 16, group, 0)
 
 
 def row_copies(first, chunks, pairs, sems):
@@ -222,13 +222,13 @@
 
 
 def partners(n_chips):
-    far = list(reversed(range(n_chips // 2, n_chips)))
-    near = list(reversed(range(1, n_chips // 2)))
-    return list(zip(near + [0] * (len(far) - len(near)), far))
-
-
-def chips_kernel(n_var, width, distances, own_ref, other_ref, cross_ref, cross_other_ref, total_ref, mine_ref, *rest):
-    messages, both = rest[:-1], rest[-1]
+    far = list(reversed(range(1, n_chips)))
+    return list(zip(far, far[:-2] + far[-2:][::-1]))
+
+
+def chips_kernel(n_var, width, distances, own_ref, other_ref, cross_ref, cross_other_ref,
+                 total_ref, mine_ref, *rest):
+    messages, (both,) = rest[:-1], rest[-1:]
     samp = lax.axis_index("samp")
     core = samp % 2
     chip = samp // 2
@@ -255,17 +255,14 @@
         sums = sums + (pltpu.roll(values, 16 * part, 1) if part else values)
     for (zero, one), message in zip(distances, messages):
         target = chip ^ jnp.where(core == 0, zero, one)
-        dose = []
-        for c in range(2):
-            chunk = chunk_of(both, (target * 2 + c) * width, n_var, width)
-            for i, part in enumerate(halves(chunk[0:32])):
-                at = rows + (2 * c + i) * LANES
-                message[:, at : at + LANES] = part
-            dose += [p.astype(F32) for p in thirds(chunk[32:33])]
-        dose = jnp.concatenate(dose + [jnp.zeros((10, LANES), F32)])
+        chunk = chunk_of(both, (target * 2 + core) * width, n_var, width)
+        high, low = halves(chunk[0:32])
+        dose = jnp.concatenate([p.astype(F32) for p in thirds(chunk[32:33])] + [jnp.zeros((13, LANES), F32)])
         message[:, :rows] = main
-        message[:, rows + 4 * LANES : rows + 5 * LANES] = counts
-        message[:, rows + 5 * LANES :] = jnp.concatenate([sums, dose], axis=0).astype(BF16)
+        message[:, rows : rows + LANES] = high
+        message[:, rows + LANES : rows + 2 * LANES] = low
+        message[:, rows + 2 * LANES : rows + 3 * LANES] = counts
+        message[:, rows + 3 * LANES :] = jnp.concatenate([sums, dose], axis=0).astype(BF16)
 
 
 def back_kernel(variants, width, n_arrived, total_ref, mine_ref, coded_first, called_first,
@@ -282,14 +279,12 @@
     dose = mine_ref[32:33]
     got_counts = jnp.zeros((32, LANES), F32)
     got_last = jnp.zeros((32, LANES), F32)
-    core = lax.axis_index("samp") % 2
     for ref in arrived:
         main = main + ref[:, :rows].astype(F32)
-        for i in range(2):
-            at = pl.ds(pl.multiple_of(rows + (2 * core + i) * LANES, LANES), LANES)
-            cross = cross + ref[:, at].astype(F32)
-        got_counts = got_counts + ref[:, rows + 4 * LANES : rows + 5 * LANES].astype(F32)
-        got_last = got_last + ref[:, rows + 5 * LANES :].astype(F32)
+        cross = cross + ref[:, rows : rows + LANES].astype(F32)
+        cross = cross + ref[:, rows + LANES : rows + 2 * LANES].astype(F32)
+        got_counts = got_counts + ref[:, rows + 2 * LANES : rows + 3 * LANES].astype(F32)
+        got_last = got_last + ref[:, rows + 3 * LANES :].astype(F32)
     tiles = rows // LANES
     pick = lambda first: jnp.concatenate(
         [got_counts[first + j : first + j + 1] + got_counts[first + 2 * tiles + j : first + 2 * tiles + j + 1]
@@ -299,9 +294,7 @@
     count = count + pick(tiles)
     last = got_last[0:16]
     sums = sums + last + pltpu.roll(last, LANES - 16, 1) + pltpu.roll(last, LANES - 32, 1)
-    first_dose = got_last[16:17] + got_last[17:18] + got_last[18:19]
-    second_dose = got_last[19:20] + got_last[20:21] + got_last[21:22]
-    dose = dose + jnp.where(core == 0, first_dose, second_dose)
+    dose = dose + got_last[16:17] + got_last[17:18] + got_last[18:19]
 
     frequency = (allele + 1.0) / (2.0 * count + 2.0)
     spread = jnp.sqrt(2.0 * frequency * (1.0 - frequency))
@@ -441,7 +434,7 @@
 
     neighbour = swap(dire, "var", 1)
     coded_a, called_a, cross, sums = call(
-        functools.partial(first_kernel, chunks_of(first)),
+        functools.partial(first_kernel, [LANES] * (first // LANES)),
         [matrix(first), matrix(first), ((2 * rhs + 8, imputed), F32), ((rhs, LANES), F32)],
         [HBM] * 7,
         (sample_order, sol, dire, res, genotypes, called, dosage),
@@ -454,7 +447,7 @@
             pltpu.VMEM((first, shard), jnp.int32),
             pltpu.VMEM((own, imputed), jnp.int32),
             pltpu.SemaphoreType.DMA((5,)),
-            pltpu.SemaphoreType.DMA((2, len(chunks_of(first)))),
+            pltpu.SemaphoreType.DMA((2, first // LANES)),
         ],
         limit=24,
         flops=2 * 80 * own * (own + imputed),
@@ -492,7 +485,7 @@
 
     n_chips = n_samp // 2
     distances = partners(n_chips)
-    message = ((2 * rhs, rows + 6 * LANES), BF16)
+    message = ((2 * rhs, rows + 4 * LANES), BF16)
     total, mine, *messages = call(
         functools.partial(chips_kernel, n_var, width, distances),
         [(part.shape, F32), ((2 * rhs + 8, LANES), F32)] + [message] * len(distances),
@@ -501,13 +494,10 @@
         scratch=[pltpu.VMEM(cross.shape, F32)],
         moved=1 * MIB,
     )
-    came, handed = [], []
-    for (zero, one), m in zip(distances, messages):
-        pairs = [(i, i ^ (2 * (one if i % 2 else zero))) for i in range(n_samp) if i % 2 or zero]
-        came.append(lax.ppermute(m, "samp", pairs))
-    for (zero, one), m in zip(distances, came):
-        handed.append(lax.ppermute(m, "samp", [(i, i ^ 1) for i in range(n_samp) if i % 2 or zero]))
-    arrived = came + handed
+    arrived = [
+        lax.ppermute(m, "samp", [(i, i ^ (2 * (one if i % 2 else zero))) for i in range(n_samp)])
+        for (zero, one), m in zip(distances, messages)
+    ]
 
     wide = own + 2 * LANES
     mine_back, *messages = call(
@@ -523,12 +513,14 @@
     n_all = n_var * n_samp
     norms, res_keep = call(
         functools.partial(norm_kernel, variants),
-        [((n_all, 1, LANES), F32, pltpu.VMEM), ((rhs, own), F32)],
+        [((n_all, 1, LANES), F32), ((rhs, own), F32)],
         [VMEM] * (3 + n_var),
         (noise, dire, res, *backs),
         moved=4 * n_all * LANES,
     )
-    norms = lax.all_to_all(norms, ("var", "samp"), split_axis=0, concat_axis=0)
+    middle = (n_var // 2 - 1) * n_samp + 1
+    order = [middle] + [i for i in range(n_all) if i != middle]
+    norms = lax.all_to_all(norms, ("var", "samp"), split_axis=0, concat_axis=0, axis_index_groups=[order])
     sol_new, res_new, scores, res_norm = call(
         functools.partial(new_kernel, variants, samples, width),
         [((rhs, own), F32), ((rhs, own), F32), ((rhs, width), F32), ((rhs, LANES), F32)],

time: 50.1 us -> 48.4 us (0.966)
  waiting for transfers between devices: 15.4 us -> 13.1 us
  starting transfers between devices: 17.5 us -> 18.4 us
    ppermute x4 -> x3, waiting for transfers between devices: 6.32 us -> 3.9 us  [body(): lax.ppermute(m, 'samp', [(i, i ^ 2 * (one if i % 2 else zero)) for i in r...]
    all_to_all x1, starting transfers between devices: 3.55 us -> 4.42 us  [body(): lax.all_to_all(norms, ('var', 'samp'), split_axis=0, concat_axis=0, axis_...]
    ppermute x4 -> x3, starting transfers between devices: 3.49 us -> 3.55 us  [body(): lax.ppermute(m, 'samp', [(i, i ^ 2 * (one if i % 2 else zero)) for i in r...]
  transfers between devices with their start and end apart: 12 -> 11, of which waited for: 6 -> 6; matrix products, arithmetic and copies ran while one was open for 0% -> 0% of each run, Pallas kernels for 26% -> 26%
where the time goes in v7:
time: 48.4 us; the launch traced here: 48.2 us
  starting transfers between devices  18.4 us (38%)
  Pallas kernels  16 us (33%)
  waiting for transfers between devices  13.1 us (27%)
  between operations  0.73 us (2%)
    pallas_call x9, Pallas kernels, call(): pl.pallas_call(kernel, out_shape=[jax.ShapeDtypeStruct(*o) if len(o) == 2...  16 us
    ppermute x7, starting transfers between devices, swap(): return lax.ppermute(values, axis, [(i, i ^ distance) for i in range(size)])  10.5 us
    all_to_all x1, waiting for transfers between devices, body(): lax.all_to_all(norms, ('var', 'samp'), split_axis=0, concat_axis=0, axis_...  6.09 us
    all_to_all x1, starting transfers between devices, body(): lax.all_to_all(norms, ('var', 'samp'), split_axis=0, concat_axis=0, axis_...  4.42 us
    ppermute x3, waiting for transfers between devices, body(): lax.ppermute(m, 'samp', [(i, i ^ 2 * (one if i % 2 else zero)) for i in r...  3.9 us
    ppermute x3, starting transfers between devices, body(): lax.ppermute(m, 'samp', [(i, i ^ 2 * (one if i % 2 else zero)) for i in r...  3.55 us
    ppermute x7, waiting for transfers between devices, swap(): return lax.ppermute(values, axis, [(i, i ^ distance) for i in range(size)])  3.07 us
  transfers between devices with their start and end apart: 11, of which 6 were waited for; matrix products, arithmetic and copies ran while one was open for 0% of the time, Pallas kernels for 26%

profile of v7, /device:TPU:0, one launch (start us, length us, event | category | flops | bytes accessed | tf_op | source)
XLA Modules:
  0.0 48.2 jit_solution(16386833777898986220)
XLA Ops:
  0.6 3.1 %collective-permute-start = (f32[16,768]{1,0:T(8,128)}, f32[16,768]{1,0:T(8,128)S(1)}, u32[]{:S(2)}, u32[]{:S(2)}) collective-permute-start(f32[16,768]{1,0:T(8,128)} %bitcast.8), channel_id=1, source_target_pairs={{0,8},{8,0},{16,24},{24,16},{1,9},{9,1},{17,25},{25,17},{2,10},{10... | collective-permute-start | bytes 147464 | tf_op jit(solution)/shard_map/ppermute | solution.py:22
  3.7 4.5 %shard_map.112 = (bf16[256,3072]{1,0:T(8,128)(2,1)S(1)}, bf16[256,3072]{1,0:T(8,128)(2,1)S(1)}, f32[40,1024]{1,0:T(8,128)S(1)}, f32[16,128]{1,0:T(8,128)S(1)}) custom-call(s32[1,768]{1,0:T(1,128)} %order_hbm.1, f32[16,768]{1,0:T(8,128)} %bitcast.17, f32[16,768]{1,0:T(8,128)} %bitcast.9, f32[16,768]{1,0:T(8,128)} %bitcast.14, s32[768,3072]{1,0:T(8,128)} %gen_hbm.3, ...), custom_call_target="tpu_custom_call" | custom-call | flops 220200960 | bytes 9437184 | tf_op jit(solution)/shard_map/pallas_call | solution.py:408
  8.2 0.1 collective-permute-start.3
  8.3 0.0 collective-permute-done.other_ref
  8.3 0.0 copy-done
  8.4 2.7 %collective-permute-start.1 = (bf16[32,768]{1,0:T(8,128)(2,1)S(1)}, bf16[32,768]{1,0:T(8,128)(2,1)S(1)}, u32[]{:S(2)}, u32[]{:S(2)}) collective-permute-start(bf16[32,768]{1,0:T(8,128)(2,1)S(1)} %shard_map.111.pair_ref), channel_id=1, source_target_pairs={{0,16},{8,24},{16,0},{24,8},{1,17},{9,25},{17,1},{25,9},{2,18},{10... | collective-permute-start | bytes 147464 | tf_op jit(solution)/shard_map/ppermute | solution.py:22
  11.0 5.6 %shard_map.113 = (bf16[512,3072]{1,0:T(8,128)(2,1)S(1)}, bf16[512,3072]{1,0:T(8,128)(2,1)S(1)}, f32[40,768]{1,0:T(8,128)S(1)}) custom-call(bf16[32,768]{1,0:T(8,128)(2,1)S(1)} %shard_map.111.pair_ref, bf16[256,3072]{1,0:T(8,128)(2,1)S(1)} %get-tuple-element.26.coded_first, bf16[256,3072]{1,0:T(8,128)(2,1)S(1)} %get-tuple-element.27.called_first, ...), custom_call_target="tpu_custom_call" | custom-call | flops 1207959552 | bytes 12582912 | tf_op jit(solution)/shard_map/pallas_call | solution.py:408
  16.7 0.0 collective-permute-done.1.pair_ref
  16.7 1.4 %shard_map.114.own_ref = f32[40,896]{1,0:T(8,128)S(1)} custom-call(bf16[32,768]{1,0:T(8,128)(2,1)S(1)} %collective-permute-done.1.pair_ref, bf16[256,3072]{1,0:T(8,128)(2,1)S(1)} %get-tuple-element.26.coded_first, bf16[256,3072]{1,0:T(8,128)(2,1)S(1)} %get-tuple-element.27.called_first, bf16[512,3072]{1,0:T(8,128)(2,1)S(1)} %get-tuple-element.28.coded_ref, ...), custom_call_target="tpu_custom_call" | custom-call | flops 1207959552 | bytes 4718592 | tf_op jit(solution)/shard_map/pallas_call | solution.py:408
  18.1 0.3 collective-permute-start.2
  18.3 0.0 collective-permute-done.3.cross_other_ref
  18.4 1.2 %collective-permute-done.2.other_ref = f32[40,896]{1,0:T(8,128)S(1)} collective-permute-done((f32[40,896]{1,0:T(8,128)S(1)}, f32[40,896]{1,0:T(8,128)S(1)}, u32[]{:S(2)}, u32[]{:S(2)}) %collective-permute-start.2) | collective-permute-done | bytes 143392 | tf_op jit(solution)/shard_map/ppermute | solution.py:22
  19.5 0.2 shard_map.115
  19.7 2.5 %collective-permute-start.4 = (bf16[32,1280]{1,0:T(8,128)(2,1)S(1)}, bf16[32,1280]{1,0:T(8,128)(2,1)S(1)}, u32[]{:S(2)}, u32[]{:S(2)}) collective-permute-start(bf16[32,1280]{1,0:T(8,128)(2,1)S(1)} %get-tuple-element.35), channel_id=1, source_target_pairs={{0,6},{1,7},{2,4},{3,5},{4,2},{5,3},{6,0},{7,1},{8,14},{9,15},{10,... | collective-permute-start | bytes 245768 | tf_op jit(solution)/shard_map/ppermute | solution.py:498
  22.3 0.5 %collective-permute-start.5 = (bf16[32,1280]{1,0:T(8,128)(2,1)S(1)}, bf16[32,1280]{1,0:T(8,128)(2,1)S(1)}, u32[]{:S(2)}, u32[]{:S(2)}) collective-permute-start(bf16[32,1280]{1,0:T(8,128)(2,1)S(1)} %get-tuple-element.36), channel_id=1, source_target_pairs={{0,4},{1,3},{2,6},{3,1},{4,0},{5,7},{6,2},{7,5},{8,12},{9,11},{10,... | collective-permute-start | bytes 245768 | tf_op jit(solution)/shard_map/ppermute | solution.py:498
  22.8 0.5 %collective-permute-start.6 = (bf16[32,1280]{1,0:T(8,128)(2,1)S(1)}, bf16[32,1280]{1,0:T(8,128)(2,1)S(1)}, u32[]{:S(2)}, u32[]{:S(2)}) collective-permute-start(bf16[32,1280]{1,0:T(8,128)(2,1)S(1)} %get-tuple-element.37), channel_id=1, source_target_pairs={{0,2},{1,5},{2,0},{3,7},{4,6},{5,1},{6,4},{7,3},{8,10},{9,13},{10,... | collective-permute-start | bytes 245768 | tf_op jit(solution)/shard_map/ppermute | solution.py:498
  23.3 2.5 %collective-permute-done.4.rest_0_ = bf16[32,1280]{1,0:T(8,128)(2,1)S(1)} collective-permute-done((bf16[32,1280]{1,0:T(8,128)(2,1)S(1)}, bf16[32,1280]{1,0:T(8,128)(2,1)S(1)}, u32[]{:S(2)}, u32[]{:S(2)}) %collective-permute-start.4) | collective-permute-done | bytes 81952 | tf_op jit(solution)/shard_map/ppermute | solution.py:498
  25.8 1.4 %collective-permute-done.5.rest_1_ = bf16[32,1280]{1,0:T(8,128)(2,1)S(1)} collective-permute-done((bf16[32,1280]{1,0:T(8,128)(2,1)S(1)}, bf16[32,1280]{1,0:T(8,128)(2,1)S(1)}, u32[]{:S(2)}, u32[]{:S(2)}) %collective-permute-start.5) | collective-permute-done | bytes 81952 | tf_op jit(solution)/shard_map/ppermute | solution.py:498
  27.2 0.0 collective-permute-done.6.rest_2_
  27.2 1.4 %shard_map.116 = (f32[16,1024]{1,0:T(8,128)S(1)}, bf16[16,1024]{1,0:T(8,128)(2,1)S(1)}, bf16[16,1024]{1,0:T(8,128)(2,1)S(1)}, bf16[16,1024]{1,0:T(8,128)(2,1)S(1)}) custom-call(f32[40,896]{1,0:T(8,128)S(1)} %get-tuple-element.33.total_ref, f32[40,128]{1,0:T(8,128)S(1)} %get-tuple-element.34.mine_ref, bf16[256,3072]{1,0:T(8,128)(2,1)S(1)} %get-tuple-element.26.coded_first, ...), custom_call_target="tpu_custom_call" | custom-call | flops 2415919104 | bytes 9437184 | tf_op jit(solution)/shard_map/pallas_call | solution.py:408
  28.6 0.2 collective-permute-start.7
  28.8 1.7 %collective-permute-start.8 = (bf16[16,1024]{1,0:T(8,128)(2,1)S(1)}, bf16[16,1024]{1,0:T(8,128)(2,1)S(1)}, u32[]{:S(2)}, u32[]{:S(2)}) collective-permute-start(bf16[16,1024]{1,0:T(8,128)(2,1)S(1)} %get-tuple-element.40), channel_id=1, source_target_pairs={{0,16},{8,24},{16,0},{24,8},{1,17},{9,25},{17,1},{25,9},{2,18},{10... | collective-permute-start | bytes 98312 | tf_op jit(solution)/shard_map/ppermute | solution.py:22
  30.5 2.5 %collective-permute-start.9 = (bf16[16,1024]{1,0:T(8,128)(2,1)S(1)}, bf16[16,1024]{1,0:T(8,128)(2,1)S(1)}, u32[]{:S(2)}, u32[]{:S(2)}) collective-permute-start(bf16[16,1024]{1,0:T(8,128)(2,1)S(1)} %get-tuple-element.41), channel_id=1, source_target_pairs={{0,8},{8,0},{16,24},{24,16},{1,9},{9,1},{17,25},{25,17},{2,10},{10... | collective-permute-start | bytes 98312 | tf_op jit(solution)/shard_map/ppermute | solution.py:22
  33.0 1.3 %collective-permute-done.7.rest_1_ = bf16[16,1024]{1,0:T(8,128)(2,1)S(1)} collective-permute-done((bf16[16,1024]{1,0:T(8,128)(2,1)S(1)}, bf16[16,1024]{1,0:T(8,128)(2,1)S(1)}, u32[]{:S(2)}, u32[]{:S(2)}) %collective-permute-start.7) | collective-permute-done | bytes 32800 | tf_op jit(solution)/shard_map/ppermute | solution.py:22
  34.3 0.0 collective-permute-done.8.rest_2_
  34.3 0.6 %collective-permute-done.9.rest_3_ = bf16[16,1024]{1,0:T(8,128)(2,1)S(1)} collective-permute-done((bf16[16,1024]{1,0:T(8,128)(2,1)S(1)}, bf16[16,1024]{1,0:T(8,128)(2,1)S(1)}, u32[]{:S(2)}, u32[]{:S(2)}) %collective-permute-start.9) | collective-permute-done | bytes 32800 | tf_op jit(solution)/shard_map/ppermute | solution.py:22
  34.9 1.0 %shard_map.118 = (f32[32,1,128]{2,1,0:T(1,128)}, f32[16,768]{1,0:T(8,128)S(1)}) custom-call(f32[1,16]{1,0:T(1,128)S(1)} %bitcast.19, f32[16,768]{1,0:T(8,128)S(1)} %bitcast.11, f32[16,768]{1,0:T(8,128)S(1)} %bitcast.15, f32[16,1024]{1,0:T(8,128)S(1)} %get-tuple-element.38.rest_0_, bf16[16,1024]{1,0:T(8,128)(2,1)S(1)} %collective-permute-done.7.rest_1_, ...), custom_call_target="tpu_custom_call" | custom-call | bytes 16384 | tf_op jit(solution)/shard_map/pallas_call | solution.py:408
  35.9 4.4 %all-to-all-start = ((f32[32,1,128]{2,1,0:T(1,128)}), f32[32,1,128]{2,1,0:T(1,128)S(1)}, u32[]{:S(2)}, u32[]{:S(2)}) async-start(f32[32,1,128]{2,1,0:T(1,128)} %get-tuple-element.44), calls=%async_computation | async-start | bytes 32768 | tf_op jit(solution)/shard_map/all_to_all | solution.py:523
  40.3 0.0 copy-done.2
  40.3 1.0 %shard_map.117 = (f32[16,768]{1,0:T(8,128)}, f32[16,768]{1,0:T(8,128)}, f32[16,32]{1,0:T(8,128)}, f32[16,128]{1,0:T(8,128)S(1)}) custom-call(f32[1,16]{1,0:T(1,128)S(1)} %bitcast.20, f32[16,768]{1,0:T(8,128)S(1)} %bitcast.12, f32[16,768]{1,0:T(8,128)S(1)} %bitcast.16, f32[16,768]{1,0:T(8,128)S(1)} %bitcast.18, f32[16,1024]{1,0:T(8,128)S(1)} %get-tuple-element.38.rest_0_, ...), custom_call_target="tpu_custom_call" | custom-call | bytes 1048576 | tf_op jit(solution)/shard_map/pallas_call | solution.py:408
  41.3 6.1 %all-to-all-done.norms_ref = f32[32,1,128]{2,1,0:T(1,128)S(1)} async-done(((f32[32,1,128]{2,1,0:T(1,128)}), f32[32,1,128]{2,1,0:T(1,128)S(1)}, u32[]{:S(2)}, u32[]{:S(2)}) %all-to-all-start) | async-done | bytes 16416 | tf_op jit(solution)/shard_map/all_to_all | solution.py:523
  47.4 0.8 %shard_map.119 = f32[16,768]{1,0:T(8,128)} custom-call(f32[32,1,128]{2,1,0:T(1,128)S(1)} %all-to-all-done.norms_ref, f32[16,128]{1,0:T(8,128)S(1)} %get-tuple-element.45.norm_ref, f32[16,768]{1,0:T(8,128)S(1)} %get-tuple-element.46.res_ref, f32[16,768]{1,0:T(8,128)S(1)} %bitcast.13), custom_call_target="tpu_custom_call" | custom-call | tf_op jit(solution)/shard_map/pallas_call | solution.py:408
  (7 shorter events, 0.0 us)
Async XLA Ops:
  0.6 7.7 %collective-permute-start = (f32[16,768]{1,0:T(8,128)}, f32[16,768]{1,0:T(8,128)S(1)}, u32[]{:S(2)}, u32[]{:S(2)}) collective-permute-start(f32[16,768]{1,0:T(8,128)} %bitcast.8), channel_id=1, source_target_pairs={{0,8},{8,0},{16,24},{24,16},{1,9},{9,1},{17,25},{25,17},{2,10},{10... | collective-permute-start | bytes 147464 | tf_op jit(solution)/shard_map/ppermute | solution.py:22
  3.7 4.6 %copy-start = (f32[768,16]{0,1:T(8,128)S(1)}, f32[768,16]{0,1:T(8,128)}, u32[]{:S(2)}) copy-start(f32[768,16]{0,1:T(8,128)} %param.15) | copy-start | bytes 147460
  8.2 10.1 %collective-permute-start.3 = (f32[40,1024]{1,0:T(8,128)S(1)}, f32[40,1024]{1,0:T(8,128)S(1)}, u32[]{:S(2)}, u32[]{:S(2)}) collective-permute-start(f32[40,1024]{1,0:T(8,128)S(1)} %get-tuple-element.32.cross_ref), channel_id=1, source_target_pairs={{0,1},{1,0},{2,3},{3,2},{4,5},{5,4},{6,7},{7,6},{8,9},{9,8},{10,11... | collective-permute-start | bytes 491528 | tf_op jit(solution)/shard_map/ppermute | solution.py:22
  8.4 8.3 %collective-permute-start.1 = (bf16[32,768]{1,0:T(8,128)(2,1)S(1)}, bf16[32,768]{1,0:T(8,128)(2,1)S(1)}, u32[]{:S(2)}, u32[]{:S(2)}) collective-permute-start(bf16[32,768]{1,0:T(8,128)(2,1)S(1)} %shard_map.111.pair_ref), channel_id=1, source_target_pairs={{0,16},{8,24},{16,0},{24,8},{1,17},{9,25},{17,1},{25,9},{2,18},{10... | collective-permute-start | bytes 147464 | tf_op jit(solution)/shard_map/ppermute | solution.py:22
  18.1 1.4 %collective-permute-start.2 = (f32[40,896]{1,0:T(8,128)S(1)}, f32[40,896]{1,0:T(8,128)S(1)}, u32[]{:S(2)}, u32[]{:S(2)}) collective-permute-start(f32[40,896]{1,0:T(8,128)S(1)} %shard_map.114.own_ref), channel_id=1, source_target_pairs={{0,1},{1,0},{2,3},{3,2},{4,5},{5,4},{6,7},{7,6},{8,9},{9,8},{10,11... | collective-permute-start | bytes 430088 | tf_op jit(solution)/shard_map/ppermute | solution.py:22
  19.7 6.1 %collective-permute-start.4 = (bf16[32,1280]{1,0:T(8,128)(2,1)S(1)}, bf16[32,1280]{1,0:T(8,128)(2,1)S(1)}, u32[]{:S(2)}, u32[]{:S(2)}) collective-permute-start(bf16[32,1280]{1,0:T(8,128)(2,1)S(1)} %get-tuple-element.35), channel_id=1, source_target_pairs={{0,6},{1,7},{2,4},{3,5},{4,2},{5,3},{6,0},{7,1},{8,14},{9,15},{10,... | collective-permute-start | bytes 245768 | tf_op jit(solution)/shard_map/ppermute | solution.py:498
  22.3 4.9 %collective-permute-start.5 = (bf16[32,1280]{1,0:T(8,128)(2,1)S(1)}, bf16[32,1280]{1,0:T(8,128)(2,1)S(1)}, u32[]{:S(2)}, u32[]{:S(2)}) collective-permute-start(bf16[32,1280]{1,0:T(8,128)(2,1)S(1)} %get-tuple-element.36), channel_id=1, source_target_pairs={{0,4},{1,3},{2,6},{3,1},{4,0},{5,7},{6,2},{7,5},{8,12},{9,11},{10,... | collective-permute-start | bytes 245768 | tf_op jit(solution)/shard_map/ppermute | solution.py:498
  22.8 4.4 %collective-permute-start.6 = (bf16[32,1280]{1,0:T(8,128)(2,1)S(1)}, bf16[32,1280]{1,0:T(8,128)(2,1)S(1)}, u32[]{:S(2)}, u32[]{:S(2)}) collective-permute-start(bf16[32,1280]{1,0:T(8,128)(2,1)S(1)} %get-tuple-element.37), channel_id=1, source_target_pairs={{0,2},{1,5},{2,0},{3,7},{4,6},{5,1},{6,4},{7,3},{8,10},{9,13},{10,... | collective-permute-start | bytes 245768 | tf_op jit(solution)/shard_map/ppermute | solution.py:498
  27.2 7.7 %copy-start.1 = (f32[768,16]{0,1:T(8,128)S(1)}, f32[768,16]{0,1:T(8,128)}, u32[]{:S(2)}) copy-start(f32[768,16]{0,1:T(8,128)} %param.14) | copy-start | bytes 147460
  27.2 7.7 %copy-start.3 = (f32[16]{0:T(128)S(1)}, f32[16]{0:T(128)}, u32[]{:S(2)}) copy-start(f32[16]{0:T(128)} %param.12) | copy-start | bytes 196
  27.2 13.1 %copy-start.2 = (f32[768,16]{0,1:T(8,128)S(1)}, f32[768,16]{0,1:T(8,128)}, u32[]{:S(2)}) copy-start(f32[768,16]{0,1:T(8,128)} %param.13) | copy-start | bytes 147460
  28.6 5.7 %collective-permute-start.7 = (bf16[16,1024]{1,0:T(8,128)(2,1)S(1)}, bf16[16,1024]{1,0:T(8,128)(2,1)S(1)}, u32[]{:S(2)}, u32[]{:S(2)}) collective-permute-start(bf16[16,1024]{1,0:T(8,128)(2,1)S(1)} %get-tuple-element.39), channel_id=1, source_target_pairs={{0,24},{8,16},{16,8},{24,0},{1,25},{9,17},{17,9},{25,1},{2,26},{10... | collective-permute-start | bytes 98312 | tf_op jit(solution)/shard_map/ppermute | solution.py:22
  28.8 5.5 %collective-permute-start.8 = (bf16[16,1024]{1,0:T(8,128)(2,1)S(1)}, bf16[16,1024]{1,0:T(8,128)(2,1)S(1)}, u32[]{:S(2)}, u32[]{:S(2)}) collective-permute-start(bf16[16,1024]{1,0:T(8,128)(2,1)S(1)} %get-tuple-element.40), channel_id=1, source_target_pairs={{0,16},{8,24},{16,0},{24,8},{1,17},{9,25},{17,1},{25,9},{2,18},{10... | collective-permute-start | bytes 98312 | tf_op jit(solution)/shard_map/ppermute | solution.py:22
  30.5 4.4 %collective-permute-start.9 = (bf16[16,1024]{1,0:T(8,128)(2,1)S(1)}, bf16[16,1024]{1,0:T(8,128)(2,1)S(1)}, u32[]{:S(2)}, u32[]{:S(2)}) collective-permute-start(bf16[16,1024]{1,0:T(8,128)(2,1)S(1)} %get-tuple-element.41), channel_id=1, source_target_pairs={{0,8},{8,0},{16,24},{24,16},{1,9},{9,1},{17,25},{25,17},{2,10},{10... | collective-permute-start | bytes 98312 | tf_op jit(solution)/shard_map/ppermute | solution.py:22
  35.9 11.5 %all-to-all-start = ((f32[32,1,128]{2,1,0:T(1,128)}), f32[32,1,128]{2,1,0:T(1,128)S(1)}, u32[]{:S(2)}, u32[]{:S(2)}) async-start(f32[32,1,128]{2,1,0:T(1,128)} %get-tuple-element.44), calls=%async_computation | async-start | bytes 32768 | tf_op jit(solution)/shard_map/all_to_all | solution.py:523

commit v8 on v5

v8 whole, which is shorter than its diff:
```python
import functools
import math

import jax
import jax.numpy as jnp
from jax import lax
from jax.experimental import pallas as pl
from jax.experimental.pallas import tpu as pltpu
from jax.sharding import PartitionSpec as P

BF16 = jnp.bfloat16
F32 = jnp.float32
LANES = 128
NT = (((1,), (1,)), ((), ()))
VMEM = pl.BlockSpec(memory_space=pltpu.VMEM)
HBM = pl.BlockSpec(memory_space=pltpu.HBM)
MIB = 1 << 20


def swap(values, axis, distance):
    size = lax.axis_size(axis)
    return lax.ppermute(values, axis, [(i, i ^ distance) for i in range(size)])


def halves(values):
    high = values.astype(BF16)
    return high, (values - high.astype(F32)).astype(BF16)


def thirds(values):
    high = values.astype(BF16)
    rest = values - high.astype(F32)
    middle = rest.astype(BF16)
    return high, middle, (rest - middle.astype(F32)).astype(BF16)


def lane_of(shape):
    return lax.broadcasted_iota(jnp.int32, shape, len(shape) - 1)


def spot(q):
    shape = (16, LANES)
    return lane_of(shape) == 16 * q + lax.broadcasted_iota(jnp.int32, shape, 0)


def as_row(values):
    block = jnp.zeros((16, LANES), F32)
    for q, column in values.items():
        block = jnp.where(spot(q), column, block)
    return jnp.sum(block, axis=0, keepdims=True)


def as_column(row, q):
    return jnp.sum(jnp.where(spot(q), row, 0.0), axis=1, keepdims=True)


def to_column(row):
    shape = (16, row.shape[1])
    same = lax.broadcasted_iota(jnp.int32, shape, 0) == lane_of(shape)
    return jnp.sum(jnp.where(same, row, 0.0), axis=1, keepdims=True)


def convert(gen_ref, call_ref, coded_ref, called_ref, first, rows):
    def group(i, carry):
        part = pl.ds(pl.multiple_of(first + i * 16, 16), 16)
        call = call_ref[part, :].astype(F32).astype(BF16)
        coded_ref[part, :] = gen_ref[part, :].astype(F32).astype(BF16) * call
        called_ref[part, :] = call
        return carry

    lax.fori_loop(0, rows // 16, group, 0)


def row_copies(first, chunk, rows, pairs, sems):
    return [
        [
            pltpu.make_async_copy(
                source.at[pl.ds(first + i * chunk, chunk)], target.at[pl.ds(i * chunk, chunk)], sems.at[j, i]
            )
            for j, (source, target) in enumerate(pairs)
        ]
        for i in range(rows // chunk)
    ]


def first_kernel(chunk, sol_hbm, dir_hbm, res_hbm, gen_hbm, call_hbm, coded_ref, called_ref, sums_ref,
                 sol_ref, dir_ref, res_ref, gbuf, cbuf, small_sems, sems):
    rows = gbuf.shape[0]
    small = [
        pltpu.make_async_copy(source, target, small_sems.at[i])
        for i, (source, target) in enumerate(((sol_hbm, sol_ref), (dir_hbm, dir_ref), (res_hbm, res_ref)))
    ]
    for copy in small:
        copy.start()
    parts = row_copies(0, chunk, rows, ((gen_hbm, gbuf), (call_hbm, cbuf)), sems)
    for part in parts:
        for copy in part:
            copy.start()
    for copy in small:
        copy.wait()
    sol, dire, res = sol_ref[...], dir_ref[...], res_ref[...]
    products = (res * res, dire * dire, sol, sol * sol, sol * dire, dire)
    row = as_row({q: jnp.sum(x, axis=1, keepdims=True) for q, x in enumerate(products)})
    sums_ref[...] = jnp.broadcast_to(row, sums_ref.shape)
    for i, part in enumerate(parts):
        for copy in part:
            copy.wait()
        convert(gbuf, cbuf, coded_ref, called_ref, i * chunk, chunk)


def pair_kernel(own_ref, other_ref, out_ref):
    upper = lax.axis_index("var") % 2
    rhs = own_ref.shape[0]
    own, other = own_ref[...], other_ref[...]
    out_ref[:rhs] = jnp.where(upper == 0, own, other).astype(BF16)
    out_ref[rhs:] = jnp.where(upper == 0, other, own).astype(BF16)


def weights(pair_ref, w1, w2):
    own = pair_ref.shape[1]
    zero = jnp.zeros((16, 2 * own), BF16)
    row = lax.broadcasted_iota(jnp.int32, (16, 2 * own), 0)
    w1[16:32] = zero
    w1[32:48] = jnp.where(row == 0, 1.0, 0.0).astype(BF16)
    w2[0:16] = zero
    w2[32:48] = jnp.where(row == 1, 1.0, 0.0).astype(BF16)
    for i in range(2):
        piece = pair_ref[16 * i : 16 * i + 16]
        w1[0:16, i * own : (i + 1) * own] = piece
        w2[16:32, i * own : (i + 1) * own] = piece


def product(coded_ref, called_ref, first, rows, samples, w1, w2):
    part = pl.ds(first, rows)
    got = lax.dot_general(coded_ref[part, samples], w1[...], NT, preferred_element_type=F32)
    got = got + lax.dot_general(called_ref[part, samples], w2[...], NT, preferred_element_type=F32)
    got = jnp.concatenate([got, jnp.zeros((rows, LANES - got.shape[1]), F32)], axis=1)
    return got.T[:40]


def pair_samples(pair, own):
    return pl.ds(pl.multiple_of(pair * 2 * own, LANES), 2 * own)


def second_kernel(chunk, pair_ref, coded_first, called_first, gen_hbm, call_hbm,
                  coded_ref, called_ref, out_ref, gbuf, cbuf, w1, w2, sems):
    first, rows = coded_first.shape[0], gbuf.shape[0]
    own = pair_ref.shape[1]
    parts = row_copies(first, chunk, rows, ((gen_hbm, gbuf), (call_hbm, cbuf)), sems)
    for part in parts:
        for copy in part:
            copy.start()
    samples = pair_samples(lax.axis_index("var") // 2, own)
    weights(pair_ref, w1, w2)
    for i in range(first // LANES):
        place = i * LANES
        out_ref[:, place : place + LANES] = product(coded_first, called_first, place, LANES, samples, w1, w2)
    for i, part in enumerate(parts):
        for copy in part:
            copy.wait()
        place = i * chunk
        convert(gbuf, cbuf, coded_ref, called_ref, place, chunk)
        out_ref[:, first + place : first + place + chunk] = product(
            coded_ref, called_ref, place, chunk, samples, w1, w2
        )


def third_kernel(pair_ref, coded_first, called_first, coded_ref, called_ref, half_ref, sums_ref, out_ref, w1, w2):
    own = pair_ref.shape[1]
    first, rest = coded_first.shape[0], coded_ref.shape[0]
    samples = pair_samples((lax.axis_index("var") // 2) ^ 1, own)
    weights(pair_ref, w1, w2)
    for i in range((first + rest) // LANES):
        place = i * LANES
        here = slice(place, place + LANES)
        if place < first:
            got = product(coded_first, called_first, place, LANES, samples, w1, w2)
        else:
            got = product(coded_ref, called_ref, place - first, LANES, samples, w1, w2)
        out_ref[:, here] = half_ref[:, here] + got
    out_ref[:, first + rest :] = jnp.zeros((out_ref.shape[0], LANES), F32)
    out_ref[0:8, first + rest :] = sums_ref[...]


def chips_kernel(own_ref, other_ref, total_ref, message):
    rows = own_ref.shape[1] - LANES
    total = own_ref[...] + other_ref[...]
    total_ref[...] = total
    pieces = []
    for part in halves(total[32:34, :rows]):
        part = part.astype(F32)
        for which in range(2):
            for j in range(rows // LANES):
                pieces.append(part[which : which + 1, j * LANES : (j + 1) * LANES])
    pieces += [part.astype(F32) for part in thirds(total[0:1, rows:])]
    pieces.append(jnp.zeros((32 - len(pieces), LANES), F32))
    message[:, :rows] = total[0:32, :rows].astype(BF16)
    message[:, rows:] = jnp.concatenate(pieces, axis=0).astype(BF16)


def dosage_kernel(order_hbm, sol_hbm, dir_hbm, dose_hbm, after_ref, cross_ref,
                  order_ref, sol_ref, dir_ref, dbuf, sems):
    rhs = sol_hbm.shape[0]
    copies = [
        pltpu.make_async_copy(source, target, sems.at[i])
        for i, (source, target) in enumerate(
            ((order_hbm, order_ref), (sol_hbm, sol_ref), (dir_hbm, dir_ref), (dose_hbm, dbuf))
        )
    ]
    for copy in copies:
        copy.start()
    for copy in copies[:3]:
        copy.wait()
    sol_high, sol_low = halves(sol_ref[...])
    dir_high, dir_low = halves(dir_ref[...])
    stack = jnp.concatenate([sol_high, dir_high, sol_low, dir_low], axis=0)
    own = stack.shape[1]
    hot = lax.broadcasted_iota(jnp.int32, (own, own), 0) == order_ref[...]
    hot = jnp.where(hot, 1.0, 0.0).astype(BF16)
    picked = jnp.dot(stack, hot, preferred_element_type=F32).astype(BF16)
    picked = jnp.concatenate([picked, jnp.ones((16, own), BF16)], axis=0)
    copies[3].wait()
    dose = dbuf[...].astype(F32).astype(BF16)
    cross = jnp.dot(picked, dose, preferred_element_type=F32)
    cross_ref[: 2 * rhs] = cross[: 2 * rhs] + cross[2 * rhs : 4 * rhs]
    cross_ref[2 * rhs :] = cross[4 * rhs : 4 * rhs + 8]


def back_kernel(variants, n_arrived, total_ref, coded_first, called_first, coded_ref, called_ref, *rest):
    arrived, own_ref, messages = rest[:n_arrived], rest[n_arrived], rest[n_arrived + 1 :]
    var = lax.axis_index("var")
    rows = total_ref.shape[1] - LANES

    main = total_ref[0:32, :rows]
    allele, count = total_ref[32:33, :rows], total_ref[33:34, :rows]
    extra = jnp.zeros((32, LANES), F32)
    for ref in arrived:
        main = main + ref[:, :rows].astype(F32)
        extra = extra + ref[:, rows:].astype(F32)
    tiles = rows // LANES
    pick = lambda first: jnp.concatenate(
        [extra[first + j : first + j + 1] + extra[first + 2 * tiles + j : first + 2 * tiles + j + 1]
         for j in range(tiles)], axis=1
    )
    allele = allele + pick(0)
    count = count + pick(tiles)
    last = 4 * tiles
    sums = total_ref[0:1, rows:] + extra[last : last + 1] + extra[last + 1 : last + 2] + extra[last + 2 : last + 3]

    frequency = (allele + 1.0) / (2.0 * count + 2.0)
    spread = jnp.sqrt(2.0 * frequency * (1.0 - frequency))
    loading = (main[0:16] - 2.0 * frequency * main[16:32]) / spread
    scaled = loading / spread
    scaled_a = scaled.astype(BF16)
    scaled_b = (-2.0 * frequency * scaled).astype(BF16)
    square = as_row({6: jnp.sum(loading * loading, axis=1, keepdims=True)})
    sums = jnp.where(lane_of((1, LANES)) < 96, sums, square)

    own = own_ref.shape[1] - LANES
    first = coded_first.shape[0]

    def term(p):
        part = pl.ds(pl.multiple_of(p * own, LANES), own)
        got = jnp.dot(scaled_a[:, :first], coded_first[:, part], preferred_element_type=F32)
        got = got + jnp.dot(scaled_a[:, first:], coded_ref[:, part], preferred_element_type=F32)
        got = got + jnp.dot(scaled_b[:, :first], called_first[:, part], preferred_element_type=F32)
        got = got + jnp.dot(scaled_b[:, first:], called_ref[:, part], preferred_element_type=F32)
        return got / variants

    parts = [part.astype(F32) for part in thirds(sums)]
    block = jnp.concatenate(parts + [jnp.zeros((13, LANES), F32)], axis=0).astype(BF16)
    for k, ref in enumerate(messages):
        ref[:, :own] = term(var ^ (k + 1)).astype(BF16)
        ref[:, own:] = block
    own_ref[:, :own] = term(var)
    own_ref[:, own:] = jnp.concatenate([sums, jnp.zeros((15, LANES), F32)], axis=0)


def step_of(refs, noise_row, variants):
    got = refs[0][...]
    for ref in refs[1:]:
        got = got + ref[...].astype(F32)
    own = got.shape[1] - LANES
    back, last = got[:, :own], got[:, own:]
    sums = last[0:1] + last[1:2] + last[2:3]
    column = functools.partial(as_column, sums)
    noise = to_column(noise_row)
    curvature = noise * column(1) + column(6) / variants
    step = column(0) / (curvature + 1e-06)
    return back, column, noise, step


def norm_kernel(variants, width, noise_ref, dir_ref, res_ref, cross_ref, *rest):
    refs, (out_ref, new_ref) = rest[:-2], rest[-2:]
    back, _, noise, step = step_of(refs, noise_ref[...], variants)
    new = res_ref[...] - step * (noise * dir_ref[...] + back)
    new_ref[...] = new
    norm = as_row({6: jnp.sum(new * new, axis=1, keepdims=True)})
    cross = cross_ref[0:16] + step * cross_ref[16:32]
    lane = lane_of((8, LANES))
    top = lax.broadcasted_iota(jnp.int32, (8, LANES), 0) == 0
    norm = jnp.where(top, norm, 0.0)
    for j in range(out_ref.shape[0]):
        tile, inside = (j * width) // LANES * LANES, (j * width) % LANES
        turn = lambda x, to: pltpu.roll(x, (to - inside) % LANES, 1) if (to - inside) % LANES else x
        here = slice(tile, tile + LANES)
        block = jnp.where(lane < width, turn(cross[0:8, here], 0), norm)
        block = jnp.where((lane >= 32) & (lane < 32 + width), turn(cross[8:16, here], 32), block)
        dose = turn(cross_ref[32:40, here], 64)
        out_ref[j] = jnp.where((lane >= 64) & (lane < 64 + width) & top, dose, block)


def new_kernel(variants, noise_ref, dir_ref, res_ref, sol_ref, *rest):
    refs, (sol_out, res_out, stats_out) = rest[:-3], rest[-3:]
    back, column, noise, step = step_of(refs, noise_ref[...], variants)
    dire = dir_ref[...]
    sol_out[...] = sol_ref[...] + step * dire
    res_out[...] = res_ref[...] - step * (noise * dire + back)
    sol_sum = column(2) + step * column(5)
    sol_square = column(3) + 2.0 * step * column(4) + step * (step * column(1))
    lane = lane_of(stats_out.shape)
    stats_out[...] = jnp.where(lane == 0, column(0), jnp.where(lane == 1, sol_sum, sol_square))


def last_kernel(samples, width, came_ref, stats_ref, res_ref, dir_ref, out_ref, score_out):
    total = jnp.sum(came_ref[...], axis=0)
    new_norm = as_column(total[0:1], 6)
    out_ref[...] = res_ref[...] + (new_norm / (stats_ref[:, 0:1] + 1e-06)) * dir_ref[...]
    cross = jnp.concatenate([total, pltpu.roll(total, LANES - 32, 1)], axis=0)
    dose = pltpu.roll(total, LANES - 64, 1)[0:1]
    sol_sum, sol_square = stats_ref[:, 1:2], stats_ref[:, 2:3]
    dose_freq = (dose / 100.0 + 1.0) / (2.0 * samples + 2.0)
    dose_spread = jnp.sqrt(2.0 * dose_freq * (1.0 - dose_freq))
    scale = math.sqrt(samples) * jnp.sqrt(sol_square / samples + 1e-06)
    scores = (cross / 100.0 - 2.0 * dose_freq * sol_sum) / (dose_spread * scale)
    score_out[...] = scores[:, :width]


def call(kernel, out, ins, args, scratch=(), limit=16, flops=0, moved=0):
    return pl.pallas_call(
        kernel,
        out_shape=[jax.ShapeDtypeStruct(*o) if len(o) == 2 else o[2](*o[:2]) for o in out],
        in_specs=list(ins),
        out_specs=[VMEM] * len(out),
        scratch_shapes=list(scratch),
        compiler_params=pltpu.CompilerParams(vmem_limit_bytes=limit * MIB),
        cost_estimate=pl.CostEstimate(flops=flops, bytes_accessed=moved, transcendentals=0),
    )(*[pltpu.with_memory_space_constraint(x, pltpu.HBM) if spec is HBM else x for spec, x in zip(ins, args)])


def body(genotypes, called, dosage, sample_order, noise_ratio, solution, residual, direction):
    n_var = lax.axis_size("var")
    n_samp = lax.axis_size("samp")
    own, rhs = direction.shape
    rows, shard = genotypes.shape
    variants = rows * n_var
    samples = own * n_samp * n_var
    imputed = dosage.shape[1]
    width = imputed // (n_var * n_samp)
    noise = noise_ratio[None]

    dire, res, sol = direction.T, residual.T, solution.T
    first, chunk = rows // 3, 128
    rest = rows - first
    matrix = lambda n: ((n, shard), BF16, pltpu.VMEM)

    neighbour = swap(dire, "var", 1)
    coded_a, called_a, sums = call(
        functools.partial(first_kernel, chunk),
        [matrix(first), matrix(first), ((8, LANES), F32)],
        [HBM] * 5,
        (sol, dire, res, genotypes, called),
        scratch=[
            pltpu.VMEM((rhs, own), F32),
            pltpu.VMEM((rhs, own), F32),
            pltpu.VMEM((rhs, own), F32),
            pltpu.VMEM((first, shard), jnp.int32),
            pltpu.VMEM((first, shard), jnp.int32),
            pltpu.SemaphoreType.DMA((3,)),
            pltpu.SemaphoreType.DMA((2, first // chunk)),
        ],
        limit=24,
        moved=4 * 2 * first * shard,
    )
    (pair,) = call(pair_kernel, [((2 * rhs, own), BF16)], [VMEM] * 2, (dire, neighbour))
    pair_other = swap(pair, "var", 2)
    both_weights = [pltpu.VMEM((48, 2 * own), BF16), pltpu.VMEM((48, 2 * own), BF16)]
    coded_b, called_b, half = call(
        functools.partial(second_kernel, chunk),
        [matrix(rest), matrix(rest), ((2 * rhs + 8, rows), F32)],
        [VMEM] * 3 + [HBM] * 2,
        (pair, coded_a, called_a, genotypes, called),
        scratch=[
            pltpu.VMEM((rest, shard), jnp.int32),
            pltpu.VMEM((rest, shard), jnp.int32),
            *both_weights,
            pltpu.SemaphoreType.DMA((2, rest // chunk)),
        ],
        limit=24,
        flops=2 * rows * shard * 256,
        moved=4 * 2 * rest * shard,
    )
    (part,) = call(
        third_kernel,
        [((2 * rhs + 8, rows + LANES), F32)],
        [VMEM] * 7,
        (pair_other, coded_a, called_a, coded_b, called_b, half, sums),
        scratch=both_weights,
        flops=2 * rows * shard * 256,
        moved=2 * rows * shard,
    )
    part_other = swap(part, "samp", 1)

    n_chips = n_samp // 2
    total, message = call(
        chips_kernel,
        [(part.shape, F32), ((2 * rhs, rows + LANES), BF16)],
        [VMEM] * 2,
        (part, part_other),
        moved=1 * MIB,
    )
    arrived = [swap(message, "samp", 2 * k) for k in range(1, n_chips)]
    (cross,) = call(
        dosage_kernel,
        [((2 * rhs + 8, imputed), F32)],
        [HBM] * 4 + [VMEM],
        (sample_order, sol, dire, dosage, total),
        scratch=[
            pltpu.VMEM((1, own), jnp.int32),
            pltpu.VMEM((rhs, own), F32),
            pltpu.VMEM((rhs, own), F32),
            pltpu.VMEM((own, imputed), jnp.int32),
            pltpu.SemaphoreType.DMA((4,)),
        ],
        flops=2 * 80 * own * (own + imputed),
        moved=4 * own * imputed,
    )

    wide = own + LANES
    mine_back, *messages = call(
        functools.partial(back_kernel, variants, len(arrived)),
        [((rhs, wide), F32)] + [((rhs, wide), BF16)] * (n_var - 1),
        [VMEM] * (5 + len(arrived)),
        (total, coded_a, called_a, coded_b, called_b, *arrived),
        flops=4 * rows * shard * 256,
        moved=4 * rows * shard,
    )
    backs = [mine_back] + [swap(messages[k], "var", k + 1) for k in reversed(range(n_var - 1))]

    n_all = n_var * n_samp
    outgoing, res_keep = call(
        functools.partial(norm_kernel, variants, width),
        [((n_all, 8, LANES), F32), ((rhs, own), F32)],
        [VMEM] * (4 + n_var),
        (noise, dire, res, cross, *backs),
        moved=4 * 8 * n_all * LANES,
    )
    came = lax.all_to_all(outgoing, ("var", "samp"), split_axis=0, concat_axis=0)
    sol_new, res_new, stats = call(
        functools.partial(new_kernel, variants),
        [((rhs, own), F32), ((rhs, own), F32), ((rhs, LANES), F32)],
        [VMEM] * (4 + n_var),
        (noise, dire, res, sol, *backs),
        moved=1 * MIB,
    )
    dir_new, scores = call(
        functools.partial(last_kernel, samples, width),
        [((rhs, own), F32), ((rhs, width), F32)],
        [VMEM] * 4,
        (came, stats, res_keep, dire),
    )
    return (sol_new.T, res_new.T, dir_new.T, scores.T)


def solution(mesh):
    placed = (
        P("var", "samp"),
        P("var", "samp"),
        P(("samp", "var"), None),
        P(("samp", "var"), None),
        P(),
        P(("samp", "var"), None),
        P(("samp", "var"), None),
        P(("samp", "var"), None),
    )
    return jax.shard_map(
        body,
        mesh=mesh,
        in_specs=placed,
        out_specs=(
            P(("samp", "var"), None),
            P(("samp", "var"), None),
            P(("samp", "var"), None),
            P(("var", "samp"), None),
        ),
        check_vma=False,
    )
```

time: 47.7 us -> 47.1 us (0.987)
  starting transfers between devices: 17.8 us -> 16.9 us
  Pallas kernels: 16 us -> 16.7 us
  waiting for transfers between devices: 13 us -> 12.5 us
    ppermute x10 -> x9, waiting for transfers between devices: 6.97 us -> 5.01 us  [swap(): return lax.ppermute(values, axis, [(i, i ^ distance) for i in range(size)])]
    all_to_all x1, waiting for transfers between devices: 6.04 us -> 7.47 us  [body(): lax.all_to_all(outgoing, ('var', 'samp'), split_axis=0, concat_axis=0)]
    pallas_call x9 -> x10, Pallas kernels: 16 us -> 16.7 us  [call(): pl.pallas_call(kernel, out_shape=[jax.ShapeDtypeStruct(*o) if len(o) == 2...]
    all_to_all x1, starting transfers between devices: 3.73 us -> 3.06 us  [body(): lax.all_to_all(outgoing, ('var', 'samp'), split_axis=0, concat_axis=0)]
    ppermute x10 -> x9, starting transfers between devices: 14 us -> 13.8 us  [swap(): return lax.ppermute(values, axis, [(i, i ^ distance) for i in range(size)])]
  transfers between devices with their start and end apart: 11 -> 10, of which waited for: 7 -> 5; matrix products, arithmetic and copies ran while one was open for 0% -> 0% of each run, Pallas kernels for 27% -> 26%
where the time goes in v8:
time: 47.1 us; the launch traced here: 46.9 us
  starting transfers between devices  16.9 us (36%)
  Pallas kernels  16.7 us (35%)
  waiting for transfers between devices  12.5 us (27%)
  between operations  0.79 us (2%)
    pallas_call x10, Pallas kernels, call(): pl.pallas_call(kernel, out_shape=[jax.ShapeDtypeStruct(*o) if len(o) == 2...  16.7 us
    ppermute x9, starting transfers between devices, swap(): return lax.ppermute(values, axis, [(i, i ^ distance) for i in range(size)])  13.8 us
    all_to_all x1, waiting for transfers between devices, body(): lax.all_to_all(outgoing, ('var', 'samp'), split_axis=0, concat_axis=0)  7.47 us
    ppermute x9, waiting for transfers between devices, swap(): return lax.ppermute(values, axis, [(i, i ^ distance) for i in range(size)])  5.01 us
    all_to_all x1, starting transfers between devices, body(): lax.all_to_all(outgoing, ('var', 'samp'), split_axis=0, concat_axis=0)  3.06 us
  transfers between devices with their start and end apart: 10, of which 5 were waited for; matrix products, arithmetic and copies ran while one was open for 0% of the time, Pallas kernels for 26%

profile of v8, /device:TPU:0, one launch (start us, length us, event | category | flops | bytes accessed | tf_op | source)
XLA Modules:
  0.0 46.9 jit_solution(10529520613538624513)
XLA Ops:
  0.6 3.1 %collective-permute-start = (f32[16,768]{1,0:T(8,128)}, f32[16,768]{1,0:T(8,128)S(1)}, u32[]{:S(2)}, u32[]{:S(2)}) collective-permute-start(f32[16,768]{1,0:T(8,128)} %bitcast.8), channel_id=1, source_target_pairs={{0,8},{8,0},{16,24},{24,16},{1,9},{9,1},{17,25},{25,17},{2,10},{10... | collective-permute-start | bytes 147464 | tf_op jit(solution)/shard_map/ppermute | solution.py:22
  3.7 3.4 %shard_map.112 = (bf16[256,3072]{1,0:T(8,128)(2,1)S(1)}, bf16[256,3072]{1,0:T(8,128)(2,1)S(1)}, f32[8,128]{1,0:T(8,128)S(1)}) custom-call(f32[16,768]{1,0:T(8,128)} %bitcast.15, f32[16,768]{1,0:T(8,128)} %bitcast.9, f32[16,768]{1,0:T(8,128)} %bitcast.18, s32[768,3072]{1,0:T(8,128)} %gen_hbm.3, s32[768,3072]{1,0:T(8,128)} %call_hbm.3), custom_call_target="tpu_custom_call" | custom-call | bytes 6291456 | tf_op jit(solution)/shard_map/pallas_call | solution.py:340
  7.1 0.0 collective-permute-done.other_ref
  7.1 0.0 copy-done
  7.2 2.7 %collective-permute-start.1 = (bf16[32,768]{1,0:T(8,128)(2,1)S(1)}, bf16[32,768]{1,0:T(8,128)(2,1)S(1)}, u32[]{:S(2)}, u32[]{:S(2)}) collective-permute-start(bf16[32,768]{1,0:T(8,128)(2,1)S(1)} %shard_map.111.pair_ref), channel_id=1, source_target_pairs={{0,16},{8,24},{16,0},{24,8},{1,17},{9,25},{17,1},{25,9},{2,18},{10... | collective-permute-start | bytes 147464 | tf_op jit(solution)/shard_map/ppermute | solution.py:22
  9.8 5.6 %shard_map.113 = (bf16[512,3072]{1,0:T(8,128)(2,1)S(1)}, bf16[512,3072]{1,0:T(8,128)(2,1)S(1)}, f32[40,768]{1,0:T(8,128)S(1)}) custom-call(bf16[32,768]{1,0:T(8,128)(2,1)S(1)} %shard_map.111.pair_ref, bf16[256,3072]{1,0:T(8,128)(2,1)S(1)} %get-tuple-element.23.coded_first, bf16[256,3072]{1,0:T(8,128)(2,1)S(1)} %get-tuple-element.24.called_first, ...), custom_call_target="tpu_custom_call" | custom-call | flops 1207959552 | bytes 12582912 | tf_op jit(solution)/shard_map/pallas_call | solution.py:340
  15.5 0.0 collective-permute-done.1.pair_ref
  15.5 1.4 %shard_map.114.own_ref = f32[40,896]{1,0:T(8,128)S(1)} custom-call(bf16[32,768]{1,0:T(8,128)(2,1)S(1)} %collective-permute-done.1.pair_ref, bf16[256,3072]{1,0:T(8,128)(2,1)S(1)} %get-tuple-element.23.coded_first, bf16[256,3072]{1,0:T(8,128)(2,1)S(1)} %get-tuple-element.24.called_first, bf16[512,3072]{1,0:T(8,128)(2,1)S(1)} %get-tuple-element.25.coded_ref, ...), custom_call_target="tpu_custom_call" | custom-call | flops 1207959552 | bytes 4718592 | tf_op jit(solution)/shard_map/pallas_call | solution.py:340
  16.9 0.1 collective-permute-start.2
  17.0 1.4 %collective-permute-done.2.other_ref = f32[40,896]{1,0:T(8,128)S(1)} collective-permute-done((f32[40,896]{1,0:T(8,128)S(1)}, f32[40,896]{1,0:T(8,128)S(1)}, u32[]{:S(2)}, u32[]{:S(2)}) %collective-permute-start.2) | collective-permute-done | bytes 143392 | tf_op jit(solution)/shard_map/ppermute | solution.py:22
  18.4 2.5 %collective-permute-start.5 = (bf16[32,896]{1,0:T(8,128)(2,1)S(1)}, bf16[32,896]{1,0:T(8,128)(2,1)S(1)}, u32[]{:S(2)}, u32[]{:S(2)}) collective-permute-start(bf16[32,896]{1,0:T(8,128)(2,1)S(1)} %get-tuple-element.30), channel_id=1, source_target_pairs={{0,6},{1,7},{2,4},{3,5},{4,2},{5,3},{6,0},{7,1},{8,14},{9,15},{10,... | collective-permute-start | bytes 172040 | tf_op jit(solution)/shard_map/ppermute | solution.py:22
  20.9 0.5 %collective-permute-start.4 = (bf16[32,896]{1,0:T(8,128)(2,1)S(1)}, bf16[32,896]{1,0:T(8,128)(2,1)S(1)}, u32[]{:S(2)}, u32[]{:S(2)}) collective-permute-start(bf16[32,896]{1,0:T(8,128)(2,1)S(1)} %get-tuple-element.30), channel_id=1, source_target_pairs={{0,4},{1,5},{2,6},{3,7},{4,0},{5,1},{6,2},{7,3},{8,12},{9,13},{10,... | collective-permute-start | bytes 172040 | tf_op jit(solution)/shard_map/ppermute | solution.py:22
  21.4 0.5 %collective-permute-start.3 = (bf16[32,896]{1,0:T(8,128)(2,1)S(1)}, bf16[32,896]{1,0:T(8,128)(2,1)S(1)}, u32[]{:S(2)}, u32[]{:S(2)}) collective-permute-start(bf16[32,896]{1,0:T(8,128)(2,1)S(1)} %get-tuple-element.30), channel_id=1, source_target_pairs={{0,2},{1,3},{2,0},{3,1},{4,6},{5,7},{6,4},{7,5},{8,10},{9,11},{10,... | collective-permute-start | bytes 172040 | tf_op jit(solution)/shard_map/ppermute | solution.py:22
  21.9 1.6 %collective-permute-done.5.rest_2_ = bf16[32,896]{1,0:T(8,128)(2,1)S(1)} collective-permute-done((bf16[32,896]{1,0:T(8,128)(2,1)S(1)}, bf16[32,896]{1,0:T(8,128)(2,1)S(1)}, u32[]{:S(2)}, u32[]{:S(2)}) %collective-permute-start.5) | collective-permute-done | bytes 57376 | tf_op jit(solution)/shard_map/ppermute | solution.py:22
  23.5 1.5 %collective-permute-done.4.rest_1_ = bf16[32,896]{1,0:T(8,128)(2,1)S(1)} collective-permute-done((bf16[32,896]{1,0:T(8,128)(2,1)S(1)}, bf16[32,896]{1,0:T(8,128)(2,1)S(1)}, u32[]{:S(2)}, u32[]{:S(2)}) %collective-permute-start.4) | collective-permute-done | bytes 57376 | tf_op jit(solution)/shard_map/ppermute | solution.py:22
  25.0 0.5 %collective-permute-done.3.rest_0_ = bf16[32,896]{1,0:T(8,128)(2,1)S(1)} collective-permute-done((bf16[32,896]{1,0:T(8,128)(2,1)S(1)}, bf16[32,896]{1,0:T(8,128)(2,1)S(1)}, u32[]{:S(2)}, u32[]{:S(2)}) %collective-permute-start.3) | collective-permute-done | bytes 57376 | tf_op jit(solution)/shard_map/ppermute | solution.py:22
  25.6 1.4 %shard_map.116 = (f32[16,896]{1,0:T(8,128)S(1)}, bf16[16,896]{1,0:T(8,128)(2,1)S(1)}, bf16[16,896]{1,0:T(8,128)(2,1)S(1)}, bf16[16,896]{1,0:T(8,128)(2,1)S(1)}) custom-call(f32[40,896]{1,0:T(8,128)S(1)} %get-tuple-element.29.total_ref.after_ref, bf16[256,3072]{1,0:T(8,128)(2,1)S(1)} %get-tuple-element.23.coded_first, ...), custom_call_target="tpu_custom_call" | custom-call | flops 2415919104 | bytes 9437184 | tf_op jit(solution)/shard_map/pallas_call | solution.py:340
  26.9 0.0 copy-start.4
  26.9 0.0 copy-start.2
  27.0 0.7 %collective-permute-start.6 = (bf16[16,896]{1,0:T(8,128)(2,1)S(1)}, bf16[16,896]{1,0:T(8,128)(2,1)S(1)}, u32[]{:S(2)}, u32[]{:S(2)}) collective-permute-start(bf16[16,896]{1,0:T(8,128)(2,1)S(1)} %get-tuple-element.32), channel_id=1, source_target_pairs={{0,24},{8,16},{16,8},{24,0},{1,25},{9,17},{17,9},{25,1},{2,26},{10... | collective-permute-start | bytes 86024 | tf_op jit(solution)/shard_map/ppermute | solution.py:22
  27.7 1.7 %collective-permute-start.7 = (bf16[16,896]{1,0:T(8,128)(2,1)S(1)}, bf16[16,896]{1,0:T(8,128)(2,1)S(1)}, u32[]{:S(2)}, u32[]{:S(2)}) collective-permute-start(bf16[16,896]{1,0:T(8,128)(2,1)S(1)} %get-tuple-element.33), channel_id=1, source_target_pairs={{0,16},{8,24},{16,0},{24,8},{1,17},{9,25},{17,1},{25,9},{2,18},{10... | collective-permute-start | bytes 86024 | tf_op jit(solution)/shard_map/ppermute | solution.py:22
  29.4 2.0 %collective-permute-start.8 = (bf16[16,896]{1,0:T(8,128)(2,1)S(1)}, bf16[16,896]{1,0:T(8,128)(2,1)S(1)}, u32[]{:S(2)}, u32[]{:S(2)}) collective-permute-start(bf16[16,896]{1,0:T(8,128)(2,1)S(1)} %get-tuple-element.34), channel_id=1, source_target_pairs={{0,8},{8,0},{16,24},{24,16},{1,9},{9,1},{17,25},{25,17},{2,10},{10... | collective-permute-start | bytes 86024 | tf_op jit(solution)/shard_map/ppermute | solution.py:22
  31.4 2.4 %shard_map.118.cross_ref = f32[40,1024]{1,0:T(8,128)S(1)} custom-call(s32[1,768]{1,0:T(1,128)} %order_hbm.1, f32[16,768]{1,0:T(8,128)} %bitcast.16, f32[16,768]{1,0:T(8,128)} %bitcast.10, s32[768,1024]{1,0:T(8,128)} %dose_hbm.1, f32[40,896]{1,0:T(8,128)S(1)} %get-tuple-element.29.total_ref.after_ref), custom_call_target="tpu_custom_call" | custom-call | flops 220200960 | bytes 3145728 | tf_op jit(solution)/shard_map/pallas_call | solution.py:340
  33.8 0.0 collective-permute-done.6.rest_1_
  33.9 0.0 collective-permute-done.7.rest_2_
  33.9 0.0 collective-permute-done.8.rest_3_
  33.9 0.9 %shard_map.119 = (f32[32,8,128]{2,1,0:T(8,128)}, f32[16,768]{1,0:T(8,128)S(1)}) custom-call(f32[1,16]{1,0:T(1,128)S(1)} %bitcast.21, f32[16,768]{1,0:T(8,128)S(1)} %bitcast.12, f32[16,768]{1,0:T(8,128)S(1)} %bitcast.19, f32[40,1024]{1,0:T(8,128)S(1)} %shard_map.118.cross_ref, f32[16,896]{1,0:T(8,128)S(1)} %get-tuple-element.31.rest_0_, ...), custom_call_target="tpu_custom_call" | custom-call | bytes 131072 | tf_op jit(solution)/shard_map/pallas_call | solution.py:340
  34.8 3.1 %all-to-all-start = ((f32[32,8,128]{2,1,0:T(8,128)}), f32[32,8,128]{2,1,0:T(8,128)S(1)}, u32[]{:S(2)}, u32[]{:S(2)}) async-start(f32[32,8,128]{2,1,0:T(8,128)} %get-tuple-element.37), calls=%async_computation | async-start | bytes 262144 | tf_op jit(solution)/shard_map/all_to_all | solution.py:458
  37.9 0.0 copy-done.2
  37.9 0.7 %shard_map.117 = (f32[16,768]{1,0:T(8,128)}, f32[16,768]{1,0:T(8,128)}, f32[16,128]{1,0:T(8,128)S(1)}) custom-call(f32[1,16]{1,0:T(1,128)S(1)} %bitcast.22, f32[16,768]{1,0:T(8,128)S(1)} %bitcast.13, f32[16,768]{1,0:T(8,128)S(1)} %bitcast.20, f32[16,768]{1,0:T(8,128)S(1)} %bitcast.17, f32[16,896]{1,0:T(8,128)S(1)} %get-tuple-element.31.rest_0_, ...), custom_call_target="tpu_custom_call" | custom-call | bytes 1048576 | tf_op jit(solution)/shard_map/pallas_call | solution.py:340
  38.6 7.5 %all-to-all-done.came_ref = f32[32,8,128]{2,1,0:T(8,128)S(1)} async-done(((f32[32,8,128]{2,1,0:T(8,128)}), f32[32,8,128]{2,1,0:T(8,128)S(1)}, u32[]{:S(2)}, u32[]{:S(2)}) %all-to-all-start) | async-done | bytes 131104 | tf_op jit(solution)/shard_map/all_to_all | solution.py:458
  46.1 0.8 %shard_map.120 = (f32[16,768]{1,0:T(8,128)}, f32[16,32]{1,0:T(8,128)}) custom-call(f32[32,8,128]{2,1,0:T(8,128)S(1)} %all-to-all-done.came_ref, f32[16,128]{1,0:T(8,128)S(1)} %get-tuple-element.38.stats_ref, f32[16,768]{1,0:T(8,128)S(1)} %get-tuple-element.39.res_ref, f32[16,768]{1,0:T(8,128)S(1)} %bitcast.14), custom_call_target="tpu_custom_call" | custom-call | tf_op jit(solution)/shard_map/pallas_call | solution.py:340
  (8 shorter events, 0.1 us)
Async XLA Ops:
  0.6 6.5 %collective-permute-start = (f32[16,768]{1,0:T(8,128)}, f32[16,768]{1,0:T(8,128)S(1)}, u32[]{:S(2)}, u32[]{:S(2)}) collective-permute-start(f32[16,768]{1,0:T(8,128)} %bitcast.8), channel_id=1, source_target_pairs={{0,8},{8,0},{16,24},{24,16},{1,9},{9,1},{17,25},{25,17},{2,10},{10... | collective-permute-start | bytes 147464 | tf_op jit(solution)/shard_map/ppermute | solution.py:22
  3.7 3.4 %copy-start = (f32[768,16]{0,1:T(8,128)S(1)}, f32[768,16]{0,1:T(8,128)}, u32[]{:S(2)}) copy-start(f32[768,16]{0,1:T(8,128)} %param.15) | copy-start | bytes 147460
  7.2 8.3 %collective-permute-start.1 = (bf16[32,768]{1,0:T(8,128)(2,1)S(1)}, bf16[32,768]{1,0:T(8,128)(2,1)S(1)}, u32[]{:S(2)}, u32[]{:S(2)}) collective-permute-start(bf16[32,768]{1,0:T(8,128)(2,1)S(1)} %shard_map.111.pair_ref), channel_id=1, source_target_pairs={{0,16},{8,24},{16,0},{24,8},{1,17},{9,25},{17,1},{25,9},{2,18},{10... | collective-permute-start | bytes 147464 | tf_op jit(solution)/shard_map/ppermute | solution.py:22
  16.9 1.4 %collective-permute-start.2 = (f32[40,896]{1,0:T(8,128)S(1)}, f32[40,896]{1,0:T(8,128)S(1)}, u32[]{:S(2)}, u32[]{:S(2)}) collective-permute-start(f32[40,896]{1,0:T(8,128)S(1)} %shard_map.114.own_ref), channel_id=1, source_target_pairs={{0,1},{1,0},{2,3},{3,2},{4,5},{5,4},{6,7},{7,6},{8,9},{9,8},{10,11... | collective-permute-start | bytes 430088 | tf_op jit(solution)/shard_map/ppermute | solution.py:22
  18.4 5.2 %collective-permute-start.5 = (bf16[32,896]{1,0:T(8,128)(2,1)S(1)}, bf16[32,896]{1,0:T(8,128)(2,1)S(1)}, u32[]{:S(2)}, u32[]{:S(2)}) collective-permute-start(bf16[32,896]{1,0:T(8,128)(2,1)S(1)} %get-tuple-element.30), channel_id=1, source_target_pairs={{0,6},{1,7},{2,4},{3,5},{4,2},{5,3},{6,0},{7,1},{8,14},{9,15},{10,... | collective-permute-start | bytes 172040 | tf_op jit(solution)/shard_map/ppermute | solution.py:22
  20.9 4.2 %collective-permute-start.4 = (bf16[32,896]{1,0:T(8,128)(2,1)S(1)}, bf16[32,896]{1,0:T(8,128)(2,1)S(1)}, u32[]{:S(2)}, u32[]{:S(2)}) collective-permute-start(bf16[32,896]{1,0:T(8,128)(2,1)S(1)} %get-tuple-element.30), channel_id=1, source_target_pairs={{0,4},{1,5},{2,6},{3,7},{4,0},{5,1},{6,2},{7,3},{8,12},{9,13},{10,... | collective-permute-start | bytes 172040 | tf_op jit(solution)/shard_map/ppermute | solution.py:22
  21.4 4.2 %collective-permute-start.3 = (bf16[32,896]{1,0:T(8,128)(2,1)S(1)}, bf16[32,896]{1,0:T(8,128)(2,1)S(1)}, u32[]{:S(2)}, u32[]{:S(2)}) collective-permute-start(bf16[32,896]{1,0:T(8,128)(2,1)S(1)} %get-tuple-element.30), channel_id=1, source_target_pairs={{0,2},{1,3},{2,0},{3,1},{4,6},{5,7},{6,4},{7,5},{8,10},{9,11},{10,... | collective-permute-start | bytes 172040 | tf_op jit(solution)/shard_map/ppermute | solution.py:22
  26.9 6.9 %copy-start.1 = (f32[768,16]{0,1:T(8,128)S(1)}, f32[768,16]{0,1:T(8,128)}, u32[]{:S(2)}) copy-start(f32[768,16]{0,1:T(8,128)} %param.15) | copy-start | bytes 147460
  26.9 7.0 %copy-start.3 = (f32[768,16]{0,1:T(8,128)S(1)}, f32[768,16]{0,1:T(8,128)}, u32[]{:S(2)}) copy-start(f32[768,16]{0,1:T(8,128)} %param.14) | copy-start | bytes 147460
  26.9 7.0 %copy-start.4 = (f32[16]{0:T(128)S(1)}, f32[16]{0:T(128)}, u32[]{:S(2)}) copy-start(f32[16]{0:T(128)} %param.12) | copy-start | bytes 196
  26.9 10.9 %copy-start.2 = (f32[768,16]{0,1:T(8,128)S(1)}, f32[768,16]{0,1:T(8,128)}, u32[]{:S(2)}) copy-start(f32[768,16]{0,1:T(8,128)} %param.13) | copy-start | bytes 147460
  27.0 6.9 %collective-permute-start.6 = (bf16[16,896]{1,0:T(8,128)(2,1)S(1)}, bf16[16,896]{1,0:T(8,128)(2,1)S(1)}, u32[]{:S(2)}, u32[]{:S(2)}) collective-permute-start(bf16[16,896]{1,0:T(8,128)(2,1)S(1)} %get-tuple-element.32), channel_id=1, source_target_pairs={{0,24},{8,16},{16,8},{24,0},{1,25},{9,17},{17,9},{25,1},{2,26},{10... | collective-permute-start | bytes 86024 | tf_op jit(solution)/shard_map/ppermute | solution.py:22
  27.7 6.2 %collective-permute-start.7 = (bf16[16,896]{1,0:T(8,128)(2,1)S(1)}, bf16[16,896]{1,0:T(8,128)(2,1)S(1)}, u32[]{:S(2)}, u32[]{:S(2)}) collective-permute-start(bf16[16,896]{1,0:T(8,128)(2,1)S(1)} %get-tuple-element.33), channel_id=1, source_target_pairs={{0,16},{8,24},{16,0},{24,8},{1,17},{9,25},{17,1},{25,9},{2,18},{10... | collective-permute-start | bytes 86024 | tf_op jit(solution)/shard_map/ppermute | solution.py:22
  29.4 4.5 %collective-permute-start.8 = (bf16[16,896]{1,0:T(8,128)(2,1)S(1)}, bf16[16,896]{1,0:T(8,128)(2,1)S(1)}, u32[]{:S(2)}, u32[]{:S(2)}) collective-permute-start(bf16[16,896]{1,0:T(8,128)(2,1)S(1)} %get-tuple-element.34), channel_id=1, source_target_pairs={{0,8},{8,0},{16,24},{24,16},{1,9},{9,1},{17,25},{25,17},{2,10},{10... | collective-permute-start | bytes 86024 | tf_op jit(solution)/shard_map/ppermute | solution.py:22
  34.8 11.3 %all-to-all-start = ((f32[32,8,128]{2,1,0:T(8,128)}), f32[32,8,128]{2,1,0:T(8,128)S(1)}, u32[]{:S(2)}, u32[]{:S(2)}) async-start(f32[32,8,128]{2,1,0:T(8,128)} %get-tuple-element.37), calls=%async_computation | async-start | bytes 262144 | tf_op jit(solution)/shard_map/all_to_all | solution.py:458

commit v9 on v8

--- a/solution.py
+++ b/solution.py
@@ -60,52 +60,46 @@
     return jnp.sum(jnp.where(same, row, 0.0), axis=1, keepdims=True)
 
 
-def convert(gen_ref, call_ref, coded_ref, called_ref, first, rows):
+def rows_of_16(count, step):
     def group(i, carry):
-        part = pl.ds(pl.multiple_of(first + i * 16, 16), 16)
-        call = call_ref[part, :].astype(F32).astype(BF16)
-        coded_ref[part, :] = gen_ref[part, :].astype(F32).astype(BF16) * call
-        called_ref[part, :] = call
+        step(pl.ds(pl.multiple_of(i * 16, 16), 16))
         return carry
 
-    lax.fori_loop(0, rows // 16, group, 0)
-
-
-def row_copies(first, chunk, rows, pairs, sems):
+    lax.fori_loop(0, count // 16, group, 0)
+
+
+def row_copies(source, target, first, chunk, sems):
     return [
-        [
-            pltpu.make_async_copy(
-                source.at[pl.ds(first + i * chunk, chunk)], target.at[pl.ds(i * chunk, chunk)], sems.at[j, i]
-            )
-            for j, (source, target) in enumerate(pairs)
-        ]
-        for i in range(rows // chunk)
+        pltpu.make_async_copy(source.at[pl.ds(first + i, chunk)], target.at[pl.ds(i, chunk)], sems.at[i // chunk])
+        for i in range(0, target.shape[0], chunk)
     ]
 
 
-def first_kernel(chunk, sol_hbm, dir_hbm, res_hbm, gen_hbm, call_hbm, coded_ref, called_ref, sums_ref,
-                 sol_ref, dir_ref, res_ref, gbuf, cbuf, small_sems, sems):
-    rows = gbuf.shape[0]
+def genotype_kernel(chunk, sol_hbm, dir_hbm, res_hbm, gen_hbm, out_ref, sums_ref,
+                    sol_ref, dir_ref, res_ref, gbuf, small_sems, sems):
     small = [
         pltpu.make_async_copy(source, target, small_sems.at[i])
         for i, (source, target) in enumerate(((sol_hbm, sol_ref), (dir_hbm, dir_ref), (res_hbm, res_ref)))
     ]
     for copy in small:
         copy.start()
-    parts = row_copies(0, chunk, rows, ((gen_hbm, gbuf), (call_hbm, cbuf)), sems)
-    for part in parts:
-        for copy in part:
-            copy.start()
+    parts = row_copies(gen_hbm, gbuf, 0, chunk, sems)
+    for copy in parts:
+        copy.start()
     for copy in small:
         copy.wait()
     sol, dire, res = sol_ref[...], dir_ref[...], res_ref[...]
     products = (res * res, dire * dire, sol, sol * sol, sol * dire, dire)
     row = as_row({q: jnp.sum(x, axis=1, keepdims=True) for q, x in enumerate(products)})
     sums_ref[...] = jnp.broadcast_to(row, sums_ref.shape)
-    for i, part in enumerate(parts):
-        for copy in part:
-            copy.wait()
-        convert(gbuf, cbuf, coded_ref, called_ref, i * chunk, chunk)
+    for i, copy in enumerate(parts):
+        copy.wait()
+        source, target = gbuf.at[pl.ds(i * chunk, chunk)], out_ref.at[pl.ds(i * chunk, chunk)]
+
+        def step(part):
+            target[part, :] = source[part, :].astype(F32).astype(BF16)
+
+        rows_of_16(chunk, step)
 
 
 def pair_kernel(own_ref, other_ref, out_ref):
@@ -142,47 +136,45 @@
     return pl.ds(pl.multiple_of(pair * 2 * own, LANES), 2 * own)
 
 
-def second_kernel(chunk, pair_ref, coded_first, called_first, gen_hbm, call_hbm,
-                  coded_ref, called_ref, out_ref, gbuf, cbuf, w1, w2, sems):
-    first, rows = coded_first.shape[0], gbuf.shape[0]
+def mask_kernel(pair_ref, first_ref, call_ref, gen_hbm, coded_ref, called_ref, out_ref, gbuf, w1, w2, sems):
     own = pair_ref.shape[1]
-    parts = row_copies(first, chunk, rows, ((gen_hbm, gbuf), (call_hbm, cbuf)), sems)
-    for part in parts:
-        for copy in part:
-            copy.start()
+    first = first_ref.shape[0]
+    copies = row_copies(gen_hbm, gbuf, first, LANES, sems)
+    for copy in copies:
+        copy.start()
     samples = pair_samples(lax.axis_index("var") // 2, own)
     weights(pair_ref, w1, w2)
-    for i in range(first // LANES):
-        place = i * LANES
-        out_ref[:, place : place + LANES] = product(coded_first, called_first, place, LANES, samples, w1, w2)
-    for i, part in enumerate(parts):
-        for copy in part:
-            copy.wait()
-        place = i * chunk
-        convert(gbuf, cbuf, coded_ref, called_ref, place, chunk)
-        out_ref[:, first + place : first + place + chunk] = product(
-            coded_ref, called_ref, place, chunk, samples, w1, w2
-        )
-
-
-def third_kernel(pair_ref, coded_first, called_first, coded_ref, called_ref, half_ref, sums_ref, out_ref, w1, w2):
+    for place in range(0, call_ref.shape[0], LANES):
+        here = pl.ds(place, LANES)
+        if place < first:
+            gen = first_ref.at[here]
+        else:
+            gen = gbuf.at[pl.ds(place - first, LANES)]
+            copies[(place - first) // LANES].wait()
+        call, coded, called = call_ref.at[here], coded_ref.at[here], called_ref.at[here]
+
+        def step(part):
+            mask = call[part, :].astype(F32).astype(BF16)
+            coded[part, :] = gen[part, :].astype(F32).astype(BF16) * mask
+            called[part, :] = mask
+
+        rows_of_16(LANES, step)
+        out_ref[:, place : place + LANES] = product(coded_ref, called_ref, place, LANES, samples, w1, w2)
+
+
+def forward_kernel(pair_ref, coded_ref, called_ref, half_ref, sums_ref, out_ref, w1, w2):
     own = pair_ref.shape[1]
-    first, rest = coded_first.shape[0], coded_ref.shape[0]
+    rows = coded_ref.shape[0]
     samples = pair_samples((lax.axis_index("var") // 2) ^ 1, own)
     weights(pair_ref, w1, w2)
-    for i in range((first + rest) // LANES):
-        place = i * LANES
+    for place in range(0, rows, LANES):
         here = slice(place, place + LANES)
-        if place < first:
-            got = product(coded_first, called_first, place, LANES, samples, w1, w2)
-        else:
-            got = product(coded_ref, called_ref, place - first, LANES, samples, w1, w2)
-        out_ref[:, here] = half_ref[:, here] + got
-    out_ref[:, first + rest :] = jnp.zeros((out_ref.shape[0], LANES), F32)
-    out_ref[0:8, first + rest :] = sums_ref[...]
-
-
-def chips_kernel(own_ref, other_ref, total_ref, message):
+        out_ref[:, here] = half_ref[:, here] + product(coded_ref, called_ref, place, LANES, samples, w1, w2)
+    out_ref[:, rows:] = jnp.zeros((out_ref.shape[0], LANES), F32)
+    out_ref[0:8, rows:] = sums_ref[...]
+
+
+def chips_kernel(own_ref, other_ref, total_ref, *messages):
     rows = own_ref.shape[1] - LANES
     total = own_ref[...] + other_ref[...]
     total_ref[...] = total
@@ -194,23 +186,14 @@
                 pieces.append(part[which : which + 1, j * LANES : (j + 1) * LANES])
     pieces += [part.astype(F32) for part in thirds(total[0:1, rows:])]
     pieces.append(jnp.zeros((32 - len(pieces), LANES), F32))
-    message[:, :rows] = total[0:32, :rows].astype(BF16)
-    message[:, rows:] = jnp.concatenate(pieces, axis=0).astype(BF16)
-
-
-def dosage_kernel(order_hbm, sol_hbm, dir_hbm, dose_hbm, after_ref, cross_ref,
-                  order_ref, sol_ref, dir_ref, dbuf, sems):
-    rhs = sol_hbm.shape[0]
-    copies = [
-        pltpu.make_async_copy(source, target, sems.at[i])
-        for i, (source, target) in enumerate(
-            ((order_hbm, order_ref), (sol_hbm, sol_ref), (dir_hbm, dir_ref), (dose_hbm, dbuf))
-        )
-    ]
-    for copy in copies:
-        copy.start()
-    for copy in copies[:3]:
-        copy.wait()
+    extra = jnp.concatenate(pieces, axis=0).astype(BF16)
+    for message in messages:
+        message[:, :rows] = total[0:32, :rows].astype(BF16)
+        message[:, rows:] = extra
+
+
+def dosage_kernel(order_ref, sol_ref, dir_ref, dose_ref, after_ref, cross_ref):
+    rhs = sol_ref.shape[0]
     sol_high, sol_low = halves(sol_ref[...])
     dir_high, dir_low = halves(dir_ref[...])
     stack = jnp.concatenate([sol_high, dir_high, sol_low, dir_low], axis=0)
@@ -219,14 +202,13 @@
     hot = jnp.where(hot, 1.0, 0.0).astype(BF16)
     picked = jnp.dot(stack, hot, preferred_element_type=F32).astype(BF16)
     picked = jnp.concatenate([picked, jnp.ones((16, own), BF16)], axis=0)
-    copies[3].wait()
-    dose = dbuf[...].astype(F32).astype(BF16)
+    dose = dose_ref[...].astype(F32).astype(BF16)
     cross = jnp.dot(picked, dose, preferred_element_type=F32)
     cross_ref[: 2 * rhs] = cross[: 2 * rhs] + cross[2 * rhs : 4 * rhs]
     cross_ref[2 * rhs :] = cross[4 * rhs : 4 * rhs + 8]
 
 
-def back_kernel(variants, n_arrived, total_ref, coded_first, called_first, coded_ref, called_ref, *rest):
+def back_kernel(variants, n_arrived, total_ref, coded_ref, called_ref, *rest):
     arrived, own_ref, messages = rest[:n_arrived], rest[n_arrived], rest[n_arrived + 1 :]
     var = lax.axis_index("var")
     rows = total_ref.shape[1] - LANES
@@ -257,14 +239,11 @@
     sums = jnp.where(lane_of((1, LANES)) < 96, sums, square)
 
     own = own_ref.shape[1] - LANES
-    first = coded_first.shape[0]
 
     def term(p):
         part = pl.ds(pl.multiple_of(p * own, LANES), own)
-        got = jnp.dot(scaled_a[:, :first], coded_first[:, part], preferred_element_type=F32)
-        got = got + jnp.dot(scaled_a[:, first:], coded_ref[:, part], preferred_element_type=F32)
-        got = got + jnp.dot(scaled_b[:, :first], called_first[:, part], preferred_element_type=F32)
-        got = got + jnp.dot(scaled_b[:, first:], called_ref[:, part], preferred_element_type=F32)
+        got = jnp.dot(scaled_a, coded_ref[:, part], preferred_element_type=F32)
+        got = got + jnp.dot(scaled_b, called_ref[:, part], preferred_element_type=F32)
         return got / variants
 
     parts = [part.astype(F32) for part in thirds(sums)]
@@ -297,17 +276,29 @@
     new_ref[...] = new
     norm = as_row({6: jnp.sum(new * new, axis=1, keepdims=True)})
     cross = cross_ref[0:16] + step * cross_ref[16:32]
-    lane = lane_of((8, LANES))
-    top = lax.broadcasted_iota(jnp.int32, (8, LANES), 0) == 0
-    norm = jnp.where(top, norm, 0.0)
+    dose = cross_ref[32:40]
+    lane = lane_of((16, LANES))
+    row = lax.broadcasted_iota(jnp.int32, (16, LANES), 0)
+    turned = {}
+
+    def turn(values, name, tile, by):
+        if (name, tile, by) not in turned:
+            piece = values[:, tile : tile + LANES]
+            turned[name, tile, by] = pltpu.roll(piece, by, 1) if by else piece
+        return turned[name, tile, by]
+
     for j in range(out_ref.shape[0]):
         tile, inside = (j * width) // LANES * LANES, (j * width) % LANES
-        turn = lambda x, to: pltpu.roll(x, (to - inside) % LANES, 1) if (to - inside) % LANES else x
-        here = slice(tile, tile + LANES)
-        block = jnp.where(lane < width, turn(cross[0:8, here], 0), norm)
-        block = jnp.where((lane >= 32) & (lane < 32 + width), turn(cross[8:16, here], 32), block)
-        dose = turn(cross_ref[32:40, here], 64)
-        out_ref[j] = jnp.where((lane >= 64) & (lane < 64 + width) & top, dose, block)
+        block = jnp.zeros((16, LANES), F32)
+        for m in range(4):
+            here = (row // 4 == m) & (lane >= 32 * m) & (lane < 32 * m + width)
+            block = jnp.where(here, turn(cross, "cross", tile, (32 * m - inside) % LANES), block)
+        block = block[0:8] + block[8:16]
+        block = block[0:4] + block[4:8]
+        last = jnp.where(lane[0:1] < width, turn(dose, "dose", tile, -inside % LANES)[0:1], norm)
+        for k in range(4):
+            out_ref[j, :, k * LANES : (k + 1) * LANES] = block[k : k + 1]
+        out_ref[j, :, 4 * LANES :] = last
 
 
 def new_kernel(variants, noise_ref, dir_ref, res_ref, sol_ref, *rest):
@@ -324,10 +315,16 @@
 
 def last_kernel(samples, width, came_ref, stats_ref, res_ref, dir_ref, out_ref, score_out):
     total = jnp.sum(came_ref[...], axis=0)
-    new_norm = as_column(total[0:1], 6)
-    out_ref[...] = res_ref[...] + (new_norm / (stats_ref[:, 0:1] + 1e-06)) * dir_ref[...]
-    cross = jnp.concatenate([total, pltpu.roll(total, LANES - 32, 1)], axis=0)
-    dose = pltpu.roll(total, LANES - 64, 1)[0:1]
+    last = total[:, 4 * LANES :]
+    out_ref[...] = res_ref[...] + (as_column(last, 6) / (stats_ref[:, 0:1] + 1e-06)) * dir_ref[...]
+    row = lax.broadcasted_iota(jnp.int32, (16, LANES), 0)
+    spread = jnp.zeros((16, LANES), F32)
+    for k in range(4):
+        spread = jnp.where(row % 4 == k, total[:, k * LANES : (k + 1) * LANES], spread)
+    cross = spread
+    for m in range(1, 4):
+        cross = jnp.where(row // 4 == m, pltpu.roll(spread, LANES - 32 * m, 1), cross)
+    dose = last
     sol_sum, sol_square = stats_ref[:, 1:2], stats_ref[:, 2:3]
     dose_freq = (dose / 100.0 + 1.0) / (2.0 * samples + 2.0)
     dose_spread = jnp.sqrt(2.0 * dose_freq * (1.0 - dose_freq))
@@ -361,50 +358,47 @@
 
     dire, res, sol = direction.T, residual.T, solution.T
     first, chunk = rows // 3, 128
-    rest = rows - first
     matrix = lambda n: ((n, shard), BF16, pltpu.VMEM)
 
     neighbour = swap(dire, "var", 1)
-    coded_a, called_a, sums = call(
-        functools.partial(first_kernel, chunk),
-        [matrix(first), matrix(first), ((8, LANES), F32)],
-        [HBM] * 5,
-        (sol, dire, res, genotypes, called),
+    coarse, sums = call(
+        functools.partial(genotype_kernel, chunk),
+        [matrix(first), ((8, LANES), F32)],
+        [HBM] * 4,
+        (sol, dire, res, genotypes),
         scratch=[
             pltpu.VMEM((rhs, own), F32),
             pltpu.VMEM((rhs, own), F32),
             pltpu.VMEM((rhs, own), F32),
             pltpu.VMEM((first, shard), jnp.int32),
-            pltpu.VMEM((first, shard), jnp.int32),
             pltpu.SemaphoreType.DMA((3,)),
-            pltpu.SemaphoreType.DMA((2, first // chunk)),
+            pltpu.SemaphoreType.DMA((first // chunk,)),
         ],
-        limit=24,
-        moved=4 * 2 * first * shard,
-    )
-    (pair,) = call(pair_kernel, [((2 * rhs, own), BF16)], [VMEM] * 2, (dire, neighbour))
+        limit=6,
+        moved=4 * first * shard,
+    )
+    (pair,) = call(pair_kernel, [((2 * rhs, own), BF16)], [VMEM] * 2, (dire, neighbour), limit=4)
     pair_other = swap(pair, "var", 2)
     both_weights = [pltpu.VMEM((48, 2 * own), BF16), pltpu.VMEM((48, 2 * own), BF16)]
-    coded_b, called_b, half = call(
-        functools.partial(second_kernel, chunk),
-        [matrix(rest), matrix(rest), ((2 * rhs + 8, rows), F32)],
-        [VMEM] * 3 + [HBM] * 2,
-        (pair, coded_a, called_a, genotypes, called),
+    coded, called_b, half = call(
+        mask_kernel,
+        [matrix(rows), matrix(rows), ((2 * rhs + 8, rows), F32)],
+        [VMEM] * 3 + [HBM],
+        (pair, coarse, called, genotypes),
         scratch=[
-            pltpu.VMEM((rest, shard), jnp.int32),
-            pltpu.VMEM((rest, shard), jnp.int32),
+            pltpu.VMEM((rows - first, shard), jnp.int32),
             *both_weights,
-            pltpu.SemaphoreType.DMA((2, rest // chunk)),
+            pltpu.SemaphoreType.DMA(((rows - first) // LANES,)),
         ],
-        limit=24,
+        limit=12,
         flops=2 * rows * shard * 256,
-        moved=4 * 2 * rest * shard,
+        moved=4 * rows * shard,
     )
     (part,) = call(
-        third_kernel,
+        forward_kernel,
         [((2 * rhs + 8, rows + LANES), F32)],
-        [VMEM] * 7,
-        (pair_other, coded_a, called_a, coded_b, called_b, half, sums),
+        [VMEM] * 5,
+        (pair_other, coded, called_b, half, sums),
         scratch=both_weights,
         flops=2 * rows * shard * 256,
         moved=2 * rows * shard,
@@ -412,26 +406,19 @@
     part_other = swap(part, "samp", 1)
 
     n_chips = n_samp // 2
-    total, message = call(
+    total, *messages = call(
         chips_kernel,
-        [(part.shape, F32), ((2 * rhs, rows + LANES), BF16)],
+        [(part.shape, F32)] + [((2 * rhs, rows + LANES), BF16)] * (n_chips - 1),
         [VMEM] * 2,
         (part, part_other),
         moved=1 * MIB,
     )
-    arrived = [swap(message, "samp", 2 * k) for k in range(1, n_chips)]
+    arrived = [swap(messages[k], "samp", 2 * (k + 1)) for k in reversed(range(n_chips - 1))]
     (cross,) = call(
         dosage_kernel,
         [((2 * rhs + 8, imputed), F32)],
-        [HBM] * 4 + [VMEM],
+        [VMEM] * 5,
         (sample_order, sol, dire, dosage, total),
-        scratch=[
-            pltpu.VMEM((1, own), jnp.int32),
-            pltpu.VMEM((rhs, own), F32),
-            pltpu.VMEM((rhs, own), F32),
-            pltpu.VMEM((own, imputed), jnp.int32),
-            pltpu.SemaphoreType.DMA((4,)),
-        ],
         flops=2 * 80 * own * (own + imputed),
         moved=4 * own * imputed,
     )
@@ -440,8 +427,8 @@
     mine_back, *messages = call(
         functools.partial(back_kernel, variants, len(arrived)),
         [((rhs, wide), F32)] + [((rhs, wide), BF16)] * (n_var - 1),
-        [VMEM] * (5 + len(arrived)),
-        (total, coded_a, called_a, coded_b, called_b, *arrived),
+        [VMEM] * (3 + len(arrived)),
+        (total, coded, called_b, *arrived),
         flops=4 * rows * shard * 256,
         moved=4 * rows * shard,
     )
@@ -450,10 +437,10 @@
     n_all = n_var * n_samp
     outgoing, res_keep = call(
         functools.partial(norm_kernel, variants, width),
-        [((n_all, 8, LANES), F32), ((rhs, own), F32)],
+        [((n_all, 1, 5 * LANES), F32), ((rhs, own), F32)],
         [VMEM] * (4 + n_var),
         (noise, dire, res, cross, *backs),
-        moved=4 * 8 * n_all * LANES,
+        moved=4 * 5 * n_all * LANES,
     )
     came = lax.all_to_all(outgoing, ("var", "samp"), split_axis=0, concat_axis=0)
     sol_new, res_new, stats = call(

time: 47.1 us -> 45.7 us (0.970)
  Pallas kernels: 16.7 us -> 13.4 us
  waiting for transfers between devices: 12.5 us -> 13.8 us
  starting transfers between devices: 16.9 us -> 17.5 us
    pallas_call x10, Pallas kernels: 16.7 us -> 13.4 us  [call(): pl.pallas_call(kernel, out_shape=[jax.ShapeDtypeStruct(*o) if len(o) == 2...]
    ppermute x9, waiting for transfers between devices: 5.01 us -> 6.95 us  [swap(): return lax.ppermute(values, axis, [(i, i ^ distance) for i in range(size)])]
    all_to_all x1, waiting for transfers between devices: 7.47 us -> 6.86 us  [body(): lax.all_to_all(outgoing, ('var', 'samp'), split_axis=0, concat_axis=0)]
  transfers between devices with their start and end apart: 10 -> 10, of which waited for: 5 -> 7; matrix products, arithmetic and copies ran while one was open for 0% -> 0% of each run, Pallas kernels for 26% -> 19%
where the time goes in v9:
time: 45.7 us; the launch traced here: 45.5 us
  starting transfers between devices  17.5 us (38%)
  waiting for transfers between devices  13.8 us (30%)
  Pallas kernels  13.4 us (29%)
  between operations  0.72 us (2%)
    ppermute x9, starting transfers between devices, swap(): return lax.ppermute(values, axis, [(i, i ^ distance) for i in range(size)])  14.2 us
    pallas_call x10, Pallas kernels, call(): pl.pallas_call(kernel, out_shape=[jax.ShapeDtypeStruct(*o) if len(o) == 2...  13.4 us
    ppermute x9, waiting for transfers between devices, swap(): return lax.ppermute(values, axis, [(i, i ^ distance) for i in range(size)])  6.95 us
    all_to_all x1, waiting for transfers between devices, body(): lax.all_to_all(outgoing, ('var', 'samp'), split_axis=0, concat_axis=0)  6.86 us
    all_to_all x1, starting transfers between devices, body(): lax.all_to_all(outgoing, ('var', 'samp'), split_axis=0, concat_axis=0)  3.27 us
  transfers between devices with their start and end apart: 10, of which 7 were waited for; matrix products, arithmetic and copies ran while one was open for 0% of the time, Pallas kernels for 19%

profile of v9, /device:TPU:0, one launch (start us, length us, event | category | flops | bytes accessed | tf_op | source)
XLA Modules:
  0.0 45.5 jit_solution(1925813462170003304)
XLA Ops:
  0.6 3.1 %collective-permute-start = (f32[16,768]{1,0:T(8,128)}, f32[16,768]{1,0:T(8,128)S(1)}, u32[]{:S(2)}, u32[]{:S(2)}) collective-permute-start(f32[16,768]{1,0:T(8,128)} %bitcast.8), channel_id=1, source_target_pairs={{0,8},{8,0},{16,24},{24,16},{1,9},{9,1},{17,25},{25,17},{2,10},{10... | collective-permute-start | bytes 147464 | tf_op jit(solution)/shard_map/ppermute | solution.py:22
  3.7 2.2 %shard_map.112 = (bf16[256,3072]{1,0:T(8,128)(2,1)S(1)}, f32[8,128]{1,0:T(8,128)S(1)}) custom-call(f32[16,768]{1,0:T(8,128)} %bitcast.15, f32[16,768]{1,0:T(8,128)} %bitcast.9, f32[16,768]{1,0:T(8,128)} %bitcast.18, s32[768,3072]{1,0:T(8,128)} %gen_hbm.3), custom_call_target="tpu_custom_call" | custom-call | bytes 3145728 | tf_op jit(solution)/shard_map/pallas_call | solution.py:337
  6.0 0.0 collective-permute-done.other_ref
  6.0 0.0 copy-done.2
  6.0 3.1 %collective-permute-start.1 = (bf16[32,768]{1,0:T(8,128)(2,1)S(1)}, bf16[32,768]{1,0:T(8,128)(2,1)S(1)}, u32[]{:S(2)}, u32[]{:S(2)}) collective-permute-start(bf16[32,768]{1,0:T(8,128)(2,1)S(1)} %shard_map.111.pair_ref), channel_id=1, source_target_pairs={{0,16},{8,24},{16,0},{24,8},{1,17},{9,25},{17,1},{25,9},{2,18},{10... | collective-permute-start | bytes 147464 | tf_op jit(solution)/shard_map/ppermute | solution.py:22
  9.1 0.0 copy-done
  9.1 5.2 %shard_map.113 = (bf16[768,3072]{1,0:T(8,128)(2,1)S(1)}, bf16[768,3072]{1,0:T(8,128)(2,1)S(1)}, f32[40,768]{1,0:T(8,128)S(1)}) custom-call(bf16[32,768]{1,0:T(8,128)(2,1)S(1)} %shard_map.111.pair_ref, bf16[256,3072]{1,0:T(8,128)(2,1)S(1)} %get-tuple-element.24.first_ref, s32[768,3072]{1,0:T(8,128)S(1)} %copy-done, s32[768,3072]{1,0:T(8,128)} %gen_hbm.3), custom_call_target="tpu_custom_call" | custom-call | flops 1207959552 | bytes 9437184 | tf_op jit(solution)/shard_map/pallas_call | solution.py:337
  14.4 0.0 collective-permute-done.1.pair_ref
  14.4 1.4 %shard_map.114.own_ref = f32[40,896]{1,0:T(8,128)S(1)} custom-call(bf16[32,768]{1,0:T(8,128)(2,1)S(1)} %collective-permute-done.1.pair_ref, bf16[768,3072]{1,0:T(8,128)(2,1)S(1)} %get-tuple-element.25.coded_ref, bf16[768,3072]{1,0:T(8,128)(2,1)S(1)} %get-tuple-element.26.called_ref, f32[40,768]{1,0:T(8,128)S(1)} %get-tuple-element.27.half_ref, ...), custom_call_target="tpu_custom_call" | custom-call | flops 1207959552 | bytes 4718592 | tf_op jit(solution)/shard_map/pallas_call | solution.py:337
  15.8 0.1 collective-permute-start.2
  15.9 1.4 %collective-permute-done.2.other_ref = f32[40,896]{1,0:T(8,128)S(1)} collective-permute-done((f32[40,896]{1,0:T(8,128)S(1)}, f32[40,896]{1,0:T(8,128)S(1)}, u32[]{:S(2)}, u32[]{:S(2)}) %collective-permute-start.2) | collective-permute-done | bytes 143392 | tf_op jit(solution)/shard_map/ppermute | solution.py:22
  17.3 2.5 %collective-permute-start.3 = (bf16[32,896]{1,0:T(8,128)(2,1)S(1)}, bf16[32,896]{1,0:T(8,128)(2,1)S(1)}, u32[]{:S(2)}, u32[]{:S(2)}) collective-permute-start(bf16[32,896]{1,0:T(8,128)(2,1)S(1)} %get-tuple-element.30), channel_id=1, source_target_pairs={{0,6},{1,7},{2,4},{3,5},{4,2},{5,3},{6,0},{7,1},{8,14},{9,15},{10,... | collective-permute-start | bytes 172040 | tf_op jit(solution)/shard_map/ppermute | solution.py:22
  19.8 0.5 %collective-permute-start.4 = (bf16[32,896]{1,0:T(8,128)(2,1)S(1)}, bf16[32,896]{1,0:T(8,128)(2,1)S(1)}, u32[]{:S(2)}, u32[]{:S(2)}) collective-permute-start(bf16[32,896]{1,0:T(8,128)(2,1)S(1)} %get-tuple-element.31), channel_id=1, source_target_pairs={{0,4},{1,5},{2,6},{3,7},{4,0},{5,1},{6,2},{7,3},{8,12},{9,13},{10,... | collective-permute-start | bytes 172040 | tf_op jit(solution)/shard_map/ppermute | solution.py:22
  20.3 0.5 %collective-permute-start.5 = (bf16[32,896]{1,0:T(8,128)(2,1)S(1)}, bf16[32,896]{1,0:T(8,128)(2,1)S(1)}, u32[]{:S(2)}, u32[]{:S(2)}) collective-permute-start(bf16[32,896]{1,0:T(8,128)(2,1)S(1)} %get-tuple-element.32), channel_id=1, source_target_pairs={{0,2},{1,3},{2,0},{3,1},{4,6},{5,7},{6,4},{7,5},{8,10},{9,11},{10,... | collective-permute-start | bytes 172040 | tf_op jit(solution)/shard_map/ppermute | solution.py:22
  20.8 1.6 %collective-permute-done.3.rest_0_ = bf16[32,896]{1,0:T(8,128)(2,1)S(1)} collective-permute-done((bf16[32,896]{1,0:T(8,128)(2,1)S(1)}, bf16[32,896]{1,0:T(8,128)(2,1)S(1)}, u32[]{:S(2)}, u32[]{:S(2)}) %collective-permute-start.3) | collective-permute-done | bytes 57376 | tf_op jit(solution)/shard_map/ppermute | solution.py:22
  22.4 1.5 %collective-permute-done.4.rest_1_ = bf16[32,896]{1,0:T(8,128)(2,1)S(1)} collective-permute-done((bf16[32,896]{1,0:T(8,128)(2,1)S(1)}, bf16[32,896]{1,0:T(8,128)(2,1)S(1)}, u32[]{:S(2)}, u32[]{:S(2)}) %collective-permute-start.4) | collective-permute-done | bytes 57376 | tf_op jit(solution)/shard_map/ppermute | solution.py:22
  24.0 0.5 %collective-permute-done.5.rest_2_ = bf16[32,896]{1,0:T(8,128)(2,1)S(1)} collective-permute-done((bf16[32,896]{1,0:T(8,128)(2,1)S(1)}, bf16[32,896]{1,0:T(8,128)(2,1)S(1)}, u32[]{:S(2)}, u32[]{:S(2)}) %collective-permute-start.5) | collective-permute-done | bytes 57376 | tf_op jit(solution)/shard_map/ppermute | solution.py:22
  24.5 0.0 copy-start.6
  24.5 1.4 %shard_map.116 = (f32[16,896]{1,0:T(8,128)S(1)}, bf16[16,896]{1,0:T(8,128)(2,1)S(1)}, bf16[16,896]{1,0:T(8,128)(2,1)S(1)}, bf16[16,896]{1,0:T(8,128)(2,1)S(1)}) custom-call(f32[40,896]{1,0:T(8,128)S(1)} %get-tuple-element.29.total_ref.after_ref, bf16[768,3072]{1,0:T(8,128)(2,1)S(1)} %get-tuple-element.25.coded_ref, ...), custom_call_target="tpu_custom_call" | custom-call | flops 2415919104 | bytes 9437184 | tf_op jit(solution)/shard_map/pallas_call | solution.py:337
  25.9 1.8 %collective-permute-start.6 = (bf16[16,896]{1,0:T(8,128)(2,1)S(1)}, bf16[16,896]{1,0:T(8,128)(2,1)S(1)}, u32[]{:S(2)}, u32[]{:S(2)}) collective-permute-start(bf16[16,896]{1,0:T(8,128)(2,1)S(1)} %get-tuple-element.34), channel_id=1, source_target_pairs={{0,24},{8,16},{16,8},{24,0},{1,25},{9,17},{17,9},{25,1},{2,26},{10... | collective-permute-start | bytes 86024 | tf_op jit(solution)/shard_map/ppermute | solution.py:22
  27.7 1.3 %collective-permute-start.7 = (bf16[16,896]{1,0:T(8,128)(2,1)S(1)}, bf16[16,896]{1,0:T(8,128)(2,1)S(1)}, u32[]{:S(2)}, u32[]{:S(2)}) collective-permute-start(bf16[16,896]{1,0:T(8,128)(2,1)S(1)} %get-tuple-element.35), channel_id=1, source_target_pairs={{0,16},{8,24},{16,0},{24,8},{1,17},{9,25},{17,1},{25,9},{2,18},{10... | collective-permute-start | bytes 86024 | tf_op jit(solution)/shard_map/ppermute | solution.py:22
  28.9 1.4 %collective-permute-start.8 = (bf16[16,896]{1,0:T(8,128)(2,1)S(1)}, bf16[16,896]{1,0:T(8,128)(2,1)S(1)}, u32[]{:S(2)}, u32[]{:S(2)}) collective-permute-start(bf16[16,896]{1,0:T(8,128)(2,1)S(1)} %get-tuple-element.36), channel_id=1, source_target_pairs={{0,8},{8,0},{16,24},{24,16},{1,9},{9,1},{17,25},{25,17},{2,10},{10... | collective-permute-start | bytes 86024 | tf_op jit(solution)/shard_map/ppermute | solution.py:22
  30.3 0.0 copy-done.3
  30.3 0.6 %shard_map.118.cross_ref = f32[40,1024]{1,0:T(8,128)S(1)} custom-call(s32[1,768]{1,0:T(1,128)S(1)} %copy-done.5, f32[16,768]{1,0:T(8,128)S(1)} %bitcast.16, f32[16,768]{1,0:T(8,128)S(1)} %bitcast.11, s32[768,1024]{1,0:T(8,128)S(1)} %copy-done.1, f32[40,896]{1,0:T(8,128)S(1)} %get-tuple-element.29.total_ref.after_ref), custom_call_target="tpu_custom_call" | custom-call | flops 220200960 | bytes 3145728 | tf_op jit(solution)/shard_map/pallas_call | solution.py:337
  30.9 0.6 %collective-permute-done.6.rest_1_ = bf16[16,896]{1,0:T(8,128)(2,1)S(1)} collective-permute-done((bf16[16,896]{1,0:T(8,128)(2,1)S(1)}, bf16[16,896]{1,0:T(8,128)(2,1)S(1)}, u32[]{:S(2)}, u32[]{:S(2)}) %collective-permute-start.6) | collective-permute-done | bytes 28704 | tf_op jit(solution)/shard_map/ppermute | solution.py:22
  31.6 1.3 %collective-permute-done.7.rest_2_ = bf16[16,896]{1,0:T(8,128)(2,1)S(1)} collective-permute-done((bf16[16,896]{1,0:T(8,128)(2,1)S(1)}, bf16[16,896]{1,0:T(8,128)(2,1)S(1)}, u32[]{:S(2)}, u32[]{:S(2)}) %collective-permute-start.7) | collective-permute-done | bytes 28704 | tf_op jit(solution)/shard_map/ppermute | solution.py:22
  32.9 0.0 collective-permute-done.8.rest_3_
  32.9 0.9 %shard_map.119 = (f32[32,1,640]{2,1,0:T(1,128)}, f32[16,768]{1,0:T(8,128)S(1)}) custom-call(f32[1,16]{1,0:T(1,128)S(1)} %bitcast.21, f32[16,768]{1,0:T(8,128)S(1)} %bitcast.12, f32[16,768]{1,0:T(8,128)S(1)} %bitcast.19, f32[40,1024]{1,0:T(8,128)S(1)} %shard_map.118.cross_ref, f32[16,896]{1,0:T(8,128)S(1)} %get-tuple-element.33.rest_0_, ...), custom_call_target="tpu_custom_call" | custom-call | bytes 81920 | tf_op jit(solution)/shard_map/pallas_call | solution.py:337
  33.8 3.3 %all-to-all-start = ((f32[32,1,640]{2,1,0:T(1,128)}), f32[32,1,640]{2,1,0:T(1,128)S(1)}, u32[]{:S(2)}, u32[]{:S(2)}) async-start(f32[32,1,640]{2,1,0:T(1,128)} %get-tuple-element.39), calls=%async_computation | async-start | bytes 163840 | tf_op jit(solution)/shard_map/all_to_all | solution.py:445
  37.1 0.7 %shard_map.117 = (f32[16,768]{1,0:T(8,128)}, f32[16,768]{1,0:T(8,128)}, f32[16,128]{1,0:T(8,128)S(1)}) custom-call(f32[1,16]{1,0:T(1,128)S(1)} %bitcast.22, f32[16,768]{1,0:T(8,128)S(1)} %bitcast.13, f32[16,768]{1,0:T(8,128)S(1)} %bitcast.20, f32[16,768]{1,0:T(8,128)S(1)} %bitcast.17, f32[16,896]{1,0:T(8,128)S(1)} %get-tuple-element.33.rest_0_, ...), custom_call_target="tpu_custom_call" | custom-call | bytes 1048576 | tf_op jit(solution)/shard_map/pallas_call | solution.py:337
  37.8 6.9 %all-to-all-done.came_ref = f32[32,1,640]{2,1,0:T(1,128)S(1)} async-done(((f32[32,1,640]{2,1,0:T(1,128)}), f32[32,1,640]{2,1,0:T(1,128)S(1)}, u32[]{:S(2)}, u32[]{:S(2)}) %all-to-all-start) | async-done | bytes 81952 | tf_op jit(solution)/shard_map/all_to_all | solution.py:445
  44.7 0.8 %shard_map.120 = (f32[16,768]{1,0:T(8,128)}, f32[16,32]{1,0:T(8,128)}) custom-call(f32[32,1,640]{2,1,0:T(1,128)S(1)} %all-to-all-done.came_ref, f32[16,128]{1,0:T(8,128)S(1)} %get-tuple-element.40.stats_ref, f32[16,768]{1,0:T(8,128)S(1)} %get-tuple-element.41.res_ref, f32[16,768]{1,0:T(8,128)S(1)} %bitcast.14), custom_call_target="tpu_custom_call" | custom-call | tf_op jit(solution)/shard_map/pallas_call | solution.py:337
  (12 shorter events, 0.1 us)
Async XLA Ops:
  0.6 5.4 %collective-permute-start = (f32[16,768]{1,0:T(8,128)}, f32[16,768]{1,0:T(8,128)S(1)}, u32[]{:S(2)}, u32[]{:S(2)}) collective-permute-start(f32[16,768]{1,0:T(8,128)} %bitcast.8), channel_id=1, source_target_pairs={{0,8},{8,0},{16,24},{24,16},{1,9},{9,1},{17,25},{25,17},{2,10},{10... | collective-permute-start | bytes 147464 | tf_op jit(solution)/shard_map/ppermute | solution.py:22
  3.7 2.3 %copy-start.2 = (f32[768,16]{0,1:T(8,128)S(1)}, f32[768,16]{0,1:T(8,128)}, u32[]{:S(2)}) copy-start(f32[768,16]{0,1:T(8,128)} %param.15) | copy-start | bytes 147460
  3.7 5.4 %copy-start = (s32[768,3072]{1,0:T(8,128)S(1)}, s32[768,3072]{1,0:T(8,128)}, u32[]{:S(2)}) copy-start(s32[768,3072]{1,0:T(8,128)} %call_ref.1) | copy-start | bytes 28311556
  6.0 8.4 %collective-permute-start.1 = (bf16[32,768]{1,0:T(8,128)(2,1)S(1)}, bf16[32,768]{1,0:T(8,128)(2,1)S(1)}, u32[]{:S(2)}, u32[]{:S(2)}) collective-permute-start(bf16[32,768]{1,0:T(8,128)(2,1)S(1)} %shard_map.111.pair_ref), channel_id=1, source_target_pairs={{0,16},{8,24},{16,0},{24,8},{1,17},{9,25},{17,1},{25,9},{2,18},{10... | collective-permute-start | bytes 147464 | tf_op jit(solution)/shard_map/ppermute | solution.py:22
  15.8 1.4 %collective-permute-start.2 = (f32[40,896]{1,0:T(8,128)S(1)}, f32[40,896]{1,0:T(8,128)S(1)}, u32[]{:S(2)}, u32[]{:S(2)}) collective-permute-start(f32[40,896]{1,0:T(8,128)S(1)} %shard_map.114.own_ref), channel_id=1, source_target_pairs={{0,1},{1,0},{2,3},{3,2},{4,5},{5,4},{6,7},{7,6},{8,9},{9,8},{10,11... | collective-permute-start | bytes 430088 | tf_op jit(solution)/shard_map/ppermute | solution.py:22
  17.3 5.2 %collective-permute-start.3 = (bf16[32,896]{1,0:T(8,128)(2,1)S(1)}, bf16[32,896]{1,0:T(8,128)(2,1)S(1)}, u32[]{:S(2)}, u32[]{:S(2)}) collective-permute-start(bf16[32,896]{1,0:T(8,128)(2,1)S(1)} %get-tuple-element.30), channel_id=1, source_target_pairs={{0,6},{1,7},{2,4},{3,5},{4,2},{5,3},{6,0},{7,1},{8,14},{9,15},{10,... | collective-permute-start | bytes 172040 | tf_op jit(solution)/shard_map/ppermute | solution.py:22
  19.8 4.2 %collective-permute-start.4 = (bf16[32,896]{1,0:T(8,128)(2,1)S(1)}, bf16[32,896]{1,0:T(8,128)(2,1)S(1)}, u32[]{:S(2)}, u32[]{:S(2)}) collective-permute-start(bf16[32,896]{1,0:T(8,128)(2,1)S(1)} %get-tuple-element.31), channel_id=1, source_target_pairs={{0,4},{1,5},{2,6},{3,7},{4,0},{5,1},{6,2},{7,3},{8,12},{9,13},{10,... | collective-permute-start | bytes 172040 | tf_op jit(solution)/shard_map/ppermute | solution.py:22
  20.3 4.2 %collective-permute-start.5 = (bf16[32,896]{1,0:T(8,128)(2,1)S(1)}, bf16[32,896]{1,0:T(8,128)(2,1)S(1)}, u32[]{:S(2)}, u32[]{:S(2)}) collective-permute-start(bf16[32,896]{1,0:T(8,128)(2,1)S(1)} %get-tuple-element.32), channel_id=1, source_target_pairs={{0,2},{1,3},{2,0},{3,1},{4,6},{5,7},{6,4},{7,5},{8,10},{9,11},{10,... | collective-permute-start | bytes 172040 | tf_op jit(solution)/shard_map/ppermute | solution.py:22
  24.5 5.8 %copy-start.1 = (s32[768,1024]{1,0:T(8,128)S(1)}, s32[768,1024]{1,0:T(8,128)}, u32[]{:S(2)}) copy-start(s32[768,1024]{1,0:T(8,128)} %dose_ref.1) | copy-start | bytes 9437188
  24.5 5.8 %copy-start.3 = (f32[768,16]{0,1:T(8,128)S(1)}, f32[768,16]{0,1:T(8,128)}, u32[]{:S(2)}) copy-start(f32[768,16]{0,1:T(8,128)} %param.13) | copy-start | bytes 147460
  24.5 5.8 %copy-start.5 = (s32[1,768]{1,0:T(1,128)S(1)}, s32[1,768]{1,0:T(1,128)}, u32[]{:S(2)}) copy-start(s32[1,768]{1,0:T(1,128)} %order_ref.1) | copy-start | bytes 9220
  24.5 8.4 %copy-start.4 = (f32[768,16]{0,1:T(8,128)S(1)}, f32[768,16]{0,1:T(8,128)}, u32[]{:S(2)}) copy-start(f32[768,16]{0,1:T(8,128)} %param.14) | copy-start | bytes 147460
  24.5 8.4 %copy-start.6 = (f32[16]{0:T(128)S(1)}, f32[16]{0:T(128)}, u32[]{:S(2)}) copy-start(f32[16]{0:T(128)} %param.12) | copy-start | bytes 196
  25.9 5.7 %collective-permute-start.6 = (bf16[16,896]{1,0:T(8,128)(2,1)S(1)}, bf16[16,896]{1,0:T(8,128)(2,1)S(1)}, u32[]{:S(2)}, u32[]{:S(2)}) collective-permute-start(bf16[16,896]{1,0:T(8,128)(2,1)S(1)} %get-tuple-element.34), channel_id=1, source_target_pairs={{0,24},{8,16},{16,8},{24,0},{1,25},{9,17},{17,9},{25,1},{2,26},{10... | collective-permute-start | bytes 86024 | tf_op jit(solution)/shard_map/ppermute | solution.py:22
  27.7 5.2 %collective-permute-start.7 = (bf16[16,896]{1,0:T(8,128)(2,1)S(1)}, bf16[16,896]{1,0:T(8,128)(2,1)S(1)}, u32[]{:S(2)}, u32[]{:S(2)}) collective-permute-start(bf16[16,896]{1,0:T(8,128)(2,1)S(1)} %get-tuple-element.35), channel_id=1, source_target_pairs={{0,16},{8,24},{16,0},{24,8},{1,17},{9,25},{17,1},{25,9},{2,18},{10... | collective-permute-start | bytes 86024 | tf_op jit(solution)/shard_map/ppermute | solution.py:22
  28.9 3.9 %collective-permute-start.8 = (bf16[16,896]{1,0:T(8,128)(2,1)S(1)}, bf16[16,896]{1,0:T(8,128)(2,1)S(1)}, u32[]{:S(2)}, u32[]{:S(2)}) collective-permute-start(bf16[16,896]{1,0:T(8,128)(2,1)S(1)} %get-tuple-element.36), channel_id=1, source_target_pairs={{0,8},{8,0},{16,24},{24,16},{1,9},{9,1},{17,25},{25,17},{2,10},{10... | collective-permute-start | bytes 86024 | tf_op jit(solution)/shard_map/ppermute | solution.py:22
  33.8 10.9 %all-to-all-start = ((f32[32,1,640]{2,1,0:T(1,128)}), f32[32,1,640]{2,1,0:T(1,128)S(1)}, u32[]{:S(2)}, u32[]{:S(2)}) async-start(f32[32,1,640]{2,1,0:T(1,128)} %get-tuple-element.39), calls=%async_computation | async-start | bytes 163840 | tf_op jit(solution)/shard_map/all_to_all | solution.py:445

commit v10 on v9

--- a/solution.py
+++ b/solution.py
@@ -60,12 +60,13 @@
     return jnp.sum(jnp.where(same, row, 0.0), axis=1, keepdims=True)
 
 
-def rows_of_16(count, step):
-    def group(i, carry):
-        step(pl.ds(pl.multiple_of(i * 16, 16), 16))
-        return carry
-
-    lax.fori_loop(0, count // 16, group, 0)
+BLOCK = 512
+
+
+def blocks(rows, samples):
+    return [
+        (pl.ds(row, 16), pl.ds(sample, BLOCK)) for row in range(0, rows, 16) for sample in range(0, samples, BLOCK)
+    ]
 
 
 def row_copies(source, target, first, chunk, sems):
@@ -95,11 +96,8 @@
     for i, copy in enumerate(parts):
         copy.wait()
         source, target = gbuf.at[pl.ds(i * chunk, chunk)], out_ref.at[pl.ds(i * chunk, chunk)]
-
-        def step(part):
-            target[part, :] = source[part, :].astype(F32).astype(BF16)
-
-        rows_of_16(chunk, step)
+        for here in blocks(chunk, source.shape[1]):
+            target[here] = source[here].astype(F32).astype(BF16)
 
 
 def pair_kernel(own_ref, other_ref, out_ref):
@@ -144,22 +142,26 @@
         copy.start()
     samples = pair_samples(lax.axis_index("var") // 2, own)
     weights(pair_ref, w1, w2)
-    for place in range(0, call_ref.shape[0], LANES):
+    rows, shard = call_ref.shape
+
+    def convert(place):
         here = pl.ds(place, LANES)
-        if place < first:
-            gen = first_ref.at[here]
-        else:
-            gen = gbuf.at[pl.ds(place - first, LANES)]
+        gen = first_ref.at[here] if place < first else gbuf.at[pl.ds(place - first, LANES)]
+        call, coded, called = call_ref.at[here], coded_ref.at[here], called_ref.at[here]
+        for block in blocks(LANES, shard):
+            mask = call[block].astype(F32).astype(BF16)
+            value = gen[block] if place < first else gen[block].astype(F32).astype(BF16)
+            coded[block] = value * mask
+            called[block] = mask
+
+    for place in range(0, rows + LANES, LANES):
+        if first <= place < rows:
             copies[(place - first) // LANES].wait()
-        call, coded, called = call_ref.at[here], coded_ref.at[here], called_ref.at[here]
-
-        def step(part):
-            mask = call[part, :].astype(F32).astype(BF16)
-            coded[part, :] = gen[part, :].astype(F32).astype(BF16) * mask
-            called[part, :] = mask
-
-        rows_of_16(LANES, step)
-        out_ref[:, place : place + LANES] = product(coded_ref, called_ref, place, LANES, samples, w1, w2)
+        if place < rows:
+            convert(place)
+        if place:
+            before = place - LANES
+            out_ref[:, before:place] = product(coded_ref, called_ref, before, LANES, samples, w1, w2)
 
 
 def forward_kernel(pair_ref, coded_ref, called_ref, half_ref, sums_ref, out_ref, w1, w2):
@@ -357,7 +359,7 @@
     noise = noise_ratio[None]
 
     dire, res, sol = direction.T, residual.T, solution.T
-    first, chunk = rows // 3, 128
+    first, chunk = rows // 2, 128
     matrix = lambda n: ((n, shard), BF16, pltpu.VMEM)
 
     neighbour = swap(dire, "var", 1)

time: 45.7 us -> 45.2 us (0.989)
  starting transfers between devices: 17.5 us -> 17 us
where the time goes in v10:
time: 45.2 us; the launch traced here: 45 us
  starting transfers between devices  17 us (38%)
  waiting for transfers between devices  14.1 us (31%)
  Pallas kernels  13.1 us (29%)
  between operations  0.73 us (2%)
    ppermute x9, starting transfers between devices, swap(): return lax.ppermute(values, axis, [(i, i ^ distance) for i in range(size)])  13.8 us
    pallas_call x10, Pallas kernels, call(): pl.pallas_call(kernel, out_shape=[jax.ShapeDtypeStruct(*o) if len(o) == 2...  13.1 us
    ppermute x9, waiting for transfers between devices, swap(): return lax.ppermute(values, axis, [(i, i ^ distance) for i in range(size)])  7.28 us
    all_to_all x1, waiting for transfers between devices, body(): lax.all_to_all(outgoing, ('var', 'samp'), split_axis=0, concat_axis=0)  6.86 us
    all_to_all x1, starting transfers between devices, body(): lax.all_to_all(outgoing, ('var', 'samp'), split_axis=0, concat_axis=0)  3.21 us
  transfers between devices with their start and end apart: 10, of which 7 were waited for; matrix products, arithmetic and copies ran while one was open for 0% of the time, Pallas kernels for 19%

profile of v10, /device:TPU:0, one launch (start us, length us, event | category | flops | bytes accessed | tf_op | source)
XLA Modules:
  0.0 45.0 jit_solution(2404034615535994652)
XLA Ops:
  0.6 3.1 %collective-permute-start = (f32[16,768]{1,0:T(8,128)}, f32[16,768]{1,0:T(8,128)S(1)}, u32[]{:S(2)}, u32[]{:S(2)}) collective-permute-start(f32[16,768]{1,0:T(8,128)} %bitcast.8), channel_id=1, source_target_pairs={{0,8},{8,0},{16,24},{24,16},{1,9},{9,1},{17,25},{25,17},{2,10},{10... | collective-permute-start | bytes 147464 | tf_op jit(solution)/shard_map/ppermute | solution.py:22
  3.7 2.7 %shard_map.112 = (bf16[384,3072]{1,0:T(8,128)(2,1)S(1)}, f32[8,128]{1,0:T(8,128)S(1)}) custom-call(f32[16,768]{1,0:T(8,128)} %bitcast.15, f32[16,768]{1,0:T(8,128)} %bitcast.9, f32[16,768]{1,0:T(8,128)} %bitcast.18, s32[768,3072]{1,0:T(8,128)} %gen_hbm.3), custom_call_target="tpu_custom_call" | custom-call | bytes 4718592 | tf_op jit(solution)/shard_map/pallas_call | solution.py:339
  6.4 0.0 collective-permute-done.other_ref
  6.4 0.0 copy-done.2
  6.5 2.7 %collective-permute-start.1 = (bf16[32,768]{1,0:T(8,128)(2,1)S(1)}, bf16[32,768]{1,0:T(8,128)(2,1)S(1)}, u32[]{:S(2)}, u32[]{:S(2)}) collective-permute-start(bf16[32,768]{1,0:T(8,128)(2,1)S(1)} %shard_map.111.pair_ref), channel_id=1, source_target_pairs={{0,16},{8,24},{16,0},{24,8},{1,17},{9,25},{17,1},{25,9},{2,18},{10... | collective-permute-start | bytes 147464 | tf_op jit(solution)/shard_map/ppermute | solution.py:22
  9.1 0.0 copy-done
  9.1 4.5 %shard_map.113 = (bf16[768,3072]{1,0:T(8,128)(2,1)S(1)}, bf16[768,3072]{1,0:T(8,128)(2,1)S(1)}, f32[40,768]{1,0:T(8,128)S(1)}) custom-call(bf16[32,768]{1,0:T(8,128)(2,1)S(1)} %shard_map.111.pair_ref, bf16[384,3072]{1,0:T(8,128)(2,1)S(1)} %get-tuple-element.24.first_ref, s32[768,3072]{1,0:T(8,128)S(1)} %copy-done, s32[768,3072]{1,0:T(8,128)} %gen_hbm.3), custom_call_target="tpu_custom_call" | custom-call | flops 1207959552 | bytes 9437184 | tf_op jit(solution)/shard_map/pallas_call | solution.py:339
  13.6 0.0 collective-permute-done.1.pair_ref
  13.6 1.4 %shard_map.114.own_ref = f32[40,896]{1,0:T(8,128)S(1)} custom-call(bf16[32,768]{1,0:T(8,128)(2,1)S(1)} %collective-permute-done.1.pair_ref, bf16[768,3072]{1,0:T(8,128)(2,1)S(1)} %get-tuple-element.25.coded_ref, bf16[768,3072]{1,0:T(8,128)(2,1)S(1)} %get-tuple-element.26.called_ref, f32[40,768]{1,0:T(8,128)S(1)} %get-tuple-element.27.half_ref, ...), custom_call_target="tpu_custom_call" | custom-call | flops 1207959552 | bytes 4718592 | tf_op jit(solution)/shard_map/pallas_call | solution.py:339
  15.1 0.1 collective-permute-start.2
  15.1 1.4 %collective-permute-done.2.other_ref = f32[40,896]{1,0:T(8,128)S(1)} collective-permute-done((f32[40,896]{1,0:T(8,128)S(1)}, f32[40,896]{1,0:T(8,128)S(1)}, u32[]{:S(2)}, u32[]{:S(2)}) %collective-permute-start.2) | collective-permute-done | bytes 143392 | tf_op jit(solution)/shard_map/ppermute | solution.py:22
  16.5 2.5 %collective-permute-start.3 = (bf16[32,896]{1,0:T(8,128)(2,1)S(1)}, bf16[32,896]{1,0:T(8,128)(2,1)S(1)}, u32[]{:S(2)}, u32[]{:S(2)}) collective-permute-start(bf16[32,896]{1,0:T(8,128)(2,1)S(1)} %get-tuple-element.30), channel_id=1, source_target_pairs={{0,6},{1,7},{2,4},{3,5},{4,2},{5,3},{6,0},{7,1},{8,14},{9,15},{10,... | collective-permute-start | bytes 172040 | tf_op jit(solution)/shard_map/ppermute | solution.py:22
  19.0 0.5 %collective-permute-start.4 = (bf16[32,896]{1,0:T(8,128)(2,1)S(1)}, bf16[32,896]{1,0:T(8,128)(2,1)S(1)}, u32[]{:S(2)}, u32[]{:S(2)}) collective-permute-start(bf16[32,896]{1,0:T(8,128)(2,1)S(1)} %get-tuple-element.31), channel_id=1, source_target_pairs={{0,4},{1,5},{2,6},{3,7},{4,0},{5,1},{6,2},{7,3},{8,12},{9,13},{10,... | collective-permute-start | bytes 172040 | tf_op jit(solution)/shard_map/ppermute | solution.py:22
  19.5 0.5 %collective-permute-start.5 = (bf16[32,896]{1,0:T(8,128)(2,1)S(1)}, bf16[32,896]{1,0:T(8,128)(2,1)S(1)}, u32[]{:S(2)}, u32[]{:S(2)}) collective-permute-start(bf16[32,896]{1,0:T(8,128)(2,1)S(1)} %get-tuple-element.32), channel_id=1, source_target_pairs={{0,2},{1,3},{2,0},{3,1},{4,6},{5,7},{6,4},{7,5},{8,10},{9,11},{10,... | collective-permute-start | bytes 172040 | tf_op jit(solution)/shard_map/ppermute | solution.py:22
  20.1 1.6 %collective-permute-done.3.rest_0_ = bf16[32,896]{1,0:T(8,128)(2,1)S(1)} collective-permute-done((bf16[32,896]{1,0:T(8,128)(2,1)S(1)}, bf16[32,896]{1,0:T(8,128)(2,1)S(1)}, u32[]{:S(2)}, u32[]{:S(2)}) %collective-permute-start.3) | collective-permute-done | bytes 57376 | tf_op jit(solution)/shard_map/ppermute | solution.py:22
  21.7 1.5 %collective-permute-done.4.rest_1_ = bf16[32,896]{1,0:T(8,128)(2,1)S(1)} collective-permute-done((bf16[32,896]{1,0:T(8,128)(2,1)S(1)}, bf16[32,896]{1,0:T(8,128)(2,1)S(1)}, u32[]{:S(2)}, u32[]{:S(2)}) %collective-permute-start.4) | collective-permute-done | bytes 57376 | tf_op jit(solution)/shard_map/ppermute | solution.py:22
  23.2 0.5 %collective-permute-done.5.rest_2_ = bf16[32,896]{1,0:T(8,128)(2,1)S(1)} collective-permute-done((bf16[32,896]{1,0:T(8,128)(2,1)S(1)}, bf16[32,896]{1,0:T(8,128)(2,1)S(1)}, u32[]{:S(2)}, u32[]{:S(2)}) %collective-permute-start.5) | collective-permute-done | bytes 57376 | tf_op jit(solution)/shard_map/ppermute | solution.py:22
  23.7 0.0 copy-start.6
  23.7 1.4 %shard_map.116 = (f32[16,896]{1,0:T(8,128)S(1)}, bf16[16,896]{1,0:T(8,128)(2,1)S(1)}, bf16[16,896]{1,0:T(8,128)(2,1)S(1)}, bf16[16,896]{1,0:T(8,128)(2,1)S(1)}) custom-call(f32[40,896]{1,0:T(8,128)S(1)} %get-tuple-element.29.total_ref.after_ref, bf16[768,3072]{1,0:T(8,128)(2,1)S(1)} %get-tuple-element.25.coded_ref, ...), custom_call_target="tpu_custom_call" | custom-call | flops 2415919104 | bytes 9437184 | tf_op jit(solution)/shard_map/pallas_call | solution.py:339
  25.1 2.2 %collective-permute-start.6 = (bf16[16,896]{1,0:T(8,128)(2,1)S(1)}, bf16[16,896]{1,0:T(8,128)(2,1)S(1)}, u32[]{:S(2)}, u32[]{:S(2)}) collective-permute-start(bf16[16,896]{1,0:T(8,128)(2,1)S(1)} %get-tuple-element.34), channel_id=1, source_target_pairs={{0,24},{8,16},{16,8},{24,0},{1,25},{9,17},{17,9},{25,1},{2,26},{10... | collective-permute-start | bytes 86024 | tf_op jit(solution)/shard_map/ppermute | solution.py:22
  27.4 0.8 %collective-permute-start.7 = (bf16[16,896]{1,0:T(8,128)(2,1)S(1)}, bf16[16,896]{1,0:T(8,128)(2,1)S(1)}, u32[]{:S(2)}, u32[]{:S(2)}) collective-permute-start(bf16[16,896]{1,0:T(8,128)(2,1)S(1)} %get-tuple-element.35), channel_id=1, source_target_pairs={{0,16},{8,24},{16,0},{24,8},{1,17},{9,25},{17,1},{25,9},{2,18},{10... | collective-permute-start | bytes 86024 | tf_op jit(solution)/shard_map/ppermute | solution.py:22
  28.2 1.4 %collective-permute-start.8 = (bf16[16,896]{1,0:T(8,128)(2,1)S(1)}, bf16[16,896]{1,0:T(8,128)(2,1)S(1)}, u32[]{:S(2)}, u32[]{:S(2)}) collective-permute-start(bf16[16,896]{1,0:T(8,128)(2,1)S(1)} %get-tuple-element.36), channel_id=1, source_target_pairs={{0,8},{8,0},{16,24},{24,16},{1,9},{9,1},{17,25},{25,17},{2,10},{10... | collective-permute-start | bytes 86024 | tf_op jit(solution)/shard_map/ppermute | solution.py:22
  29.5 0.6 %shard_map.118.cross_ref = f32[40,1024]{1,0:T(8,128)S(1)} custom-call(s32[1,768]{1,0:T(1,128)S(1)} %copy-done.5, f32[16,768]{1,0:T(8,128)S(1)} %bitcast.16, f32[16,768]{1,0:T(8,128)S(1)} %bitcast.11, s32[768,1024]{1,0:T(8,128)S(1)} %copy-done.1, f32[40,896]{1,0:T(8,128)S(1)} %get-tuple-element.29.total_ref.after_ref), custom_call_target="tpu_custom_call" | custom-call | flops 220200960 | bytes 3145728 | tf_op jit(solution)/shard_map/pallas_call | solution.py:339
  30.2 0.7 %collective-permute-done.6.rest_1_ = bf16[16,896]{1,0:T(8,128)(2,1)S(1)} collective-permute-done((bf16[16,896]{1,0:T(8,128)(2,1)S(1)}, bf16[16,896]{1,0:T(8,128)(2,1)S(1)}, u32[]{:S(2)}, u32[]{:S(2)}) %collective-permute-start.6) | collective-permute-done | bytes 28704 | tf_op jit(solution)/shard_map/ppermute | solution.py:22
  30.8 1.6 %collective-permute-done.7.rest_2_ = bf16[16,896]{1,0:T(8,128)(2,1)S(1)} collective-permute-done((bf16[16,896]{1,0:T(8,128)(2,1)S(1)}, bf16[16,896]{1,0:T(8,128)(2,1)S(1)}, u32[]{:S(2)}, u32[]{:S(2)}) %collective-permute-start.7) | collective-permute-done | bytes 28704 | tf_op jit(solution)/shard_map/ppermute | solution.py:22
  32.5 0.0 collective-permute-done.8.rest_3_
  32.5 0.0 copy-done.6
  32.5 0.9 %shard_map.119 = (f32[32,1,640]{2,1,0:T(1,128)}, f32[16,768]{1,0:T(8,128)S(1)}) custom-call(f32[1,16]{1,0:T(1,128)S(1)} %bitcast.21, f32[16,768]{1,0:T(8,128)S(1)} %bitcast.12, f32[16,768]{1,0:T(8,128)S(1)} %bitcast.19, f32[40,1024]{1,0:T(8,128)S(1)} %shard_map.118.cross_ref, f32[16,896]{1,0:T(8,128)S(1)} %get-tuple-element.33.rest_0_, ...), custom_call_target="tpu_custom_call" | custom-call | bytes 81920 | tf_op jit(solution)/shard_map/pallas_call | solution.py:339
  33.4 3.2 %all-to-all-start = ((f32[32,1,640]{2,1,0:T(1,128)}), f32[32,1,640]{2,1,0:T(1,128)S(1)}, u32[]{:S(2)}, u32[]{:S(2)}) async-start(f32[32,1,640]{2,1,0:T(1,128)} %get-tuple-element.39), calls=%async_computation | async-start | bytes 163840 | tf_op jit(solution)/shard_map/all_to_all | solution.py:447
  36.6 0.7 %shard_map.117 = (f32[16,768]{1,0:T(8,128)}, f32[16,768]{1,0:T(8,128)}, f32[16,128]{1,0:T(8,128)S(1)}) custom-call(f32[1,16]{1,0:T(1,128)S(1)} %bitcast.22, f32[16,768]{1,0:T(8,128)S(1)} %bitcast.13, f32[16,768]{1,0:T(8,128)S(1)} %bitcast.20, f32[16,768]{1,0:T(8,128)S(1)} %bitcast.17, f32[16,896]{1,0:T(8,128)S(1)} %get-tuple-element.33.rest_0_, ...), custom_call_target="tpu_custom_call" | custom-call | bytes 1048576 | tf_op jit(solution)/shard_map/pallas_call | solution.py:339
  37.3 6.9 %all-to-all-done.came_ref = f32[32,1,640]{2,1,0:T(1,128)S(1)} async-done(((f32[32,1,640]{2,1,0:T(1,128)}), f32[32,1,640]{2,1,0:T(1,128)S(1)}, u32[]{:S(2)}, u32[]{:S(2)}) %all-to-all-start) | async-done | bytes 81952 | tf_op jit(solution)/shard_map/all_to_all | solution.py:447
  44.2 0.8 %shard_map.120 = (f32[16,768]{1,0:T(8,128)}, f32[16,32]{1,0:T(8,128)}) custom-call(f32[32,1,640]{2,1,0:T(1,128)S(1)} %all-to-all-done.came_ref, f32[16,128]{1,0:T(8,128)S(1)} %get-tuple-element.40.stats_ref, f32[16,768]{1,0:T(8,128)S(1)} %get-tuple-element.41.res_ref, f32[16,768]{1,0:T(8,128)S(1)} %bitcast.14), custom_call_target="tpu_custom_call" | custom-call | tf_op jit(solution)/shard_map/pallas_call | solution.py:339
  (12 shorter events, 0.1 us)
Async XLA Ops:
  0.6 5.8 %collective-permute-start = (f32[16,768]{1,0:T(8,128)}, f32[16,768]{1,0:T(8,128)S(1)}, u32[]{:S(2)}, u32[]{:S(2)}) collective-permute-start(f32[16,768]{1,0:T(8,128)} %bitcast.8), channel_id=1, source_target_pairs={{0,8},{8,0},{16,24},{24,16},{1,9},{9,1},{17,25},{25,17},{2,10},{10... | collective-permute-start | bytes 147464 | tf_op jit(solution)/shard_map/ppermute | solution.py:22
  3.7 2.7 %copy-start.2 = (f32[768,16]{0,1:T(8,128)S(1)}, f32[768,16]{0,1:T(8,128)}, u32[]{:S(2)}) copy-start(f32[768,16]{0,1:T(8,128)} %param.15) | copy-start | bytes 147460
  3.7 5.4 %copy-start = (s32[768,3072]{1,0:T(8,128)S(1)}, s32[768,3072]{1,0:T(8,128)}, u32[]{:S(2)}) copy-start(s32[768,3072]{1,0:T(8,128)} %call_ref.1) | copy-start | bytes 28311556
  6.5 7.1 %collective-permute-start.1 = (bf16[32,768]{1,0:T(8,128)(2,1)S(1)}, bf16[32,768]{1,0:T(8,128)(2,1)S(1)}, u32[]{:S(2)}, u32[]{:S(2)}) collective-permute-start(bf16[32,768]{1,0:T(8,128)(2,1)S(1)} %shard_map.111.pair_ref), channel_id=1, source_target_pairs={{0,16},{8,24},{16,0},{24,8},{1,17},{9,25},{17,1},{25,9},{2,18},{10... | collective-permute-start | bytes 147464 | tf_op jit(solution)/shard_map/ppermute | solution.py:22
  15.1 1.4 %collective-permute-start.2 = (f32[40,896]{1,0:T(8,128)S(1)}, f32[40,896]{1,0:T(8,128)S(1)}, u32[]{:S(2)}, u32[]{:S(2)}) collective-permute-start(f32[40,896]{1,0:T(8,128)S(1)} %shard_map.114.own_ref), channel_id=1, source_target_pairs={{0,1},{1,0},{2,3},{3,2},{4,5},{5,4},{6,7},{7,6},{8,9},{9,8},{10,11... | collective-permute-start | bytes 430088 | tf_op jit(solution)/shard_map/ppermute | solution.py:22
  16.5 5.2 %collective-permute-start.3 = (bf16[32,896]{1,0:T(8,128)(2,1)S(1)}, bf16[32,896]{1,0:T(8,128)(2,1)S(1)}, u32[]{:S(2)}, u32[]{:S(2)}) collective-permute-start(bf16[32,896]{1,0:T(8,128)(2,1)S(1)} %get-tuple-element.30), channel_id=1, source_target_pairs={{0,6},{1,7},{2,4},{3,5},{4,2},{5,3},{6,0},{7,1},{8,14},{9,15},{10,... | collective-permute-start | bytes 172040 | tf_op jit(solution)/shard_map/ppermute | solution.py:22
  19.0 4.2 %collective-permute-start.4 = (bf16[32,896]{1,0:T(8,128)(2,1)S(1)}, bf16[32,896]{1,0:T(8,128)(2,1)S(1)}, u32[]{:S(2)}, u32[]{:S(2)}) collective-permute-start(bf16[32,896]{1,0:T(8,128)(2,1)S(1)} %get-tuple-element.31), channel_id=1, source_target_pairs={{0,4},{1,5},{2,6},{3,7},{4,0},{5,1},{6,2},{7,3},{8,12},{9,13},{10,... | collective-permute-start | bytes 172040 | tf_op jit(solution)/shard_map/ppermute | solution.py:22
  19.5 4.2 %collective-permute-start.5 = (bf16[32,896]{1,0:T(8,128)(2,1)S(1)}, bf16[32,896]{1,0:T(8,128)(2,1)S(1)}, u32[]{:S(2)}, u32[]{:S(2)}) collective-permute-start(bf16[32,896]{1,0:T(8,128)(2,1)S(1)} %get-tuple-element.32), channel_id=1, source_target_pairs={{0,2},{1,3},{2,0},{3,1},{4,6},{5,7},{6,4},{7,5},{8,10},{9,11},{10,... | collective-permute-start | bytes 172040 | tf_op jit(solution)/shard_map/ppermute | solution.py:22
  23.7 5.8 %copy-start.1 = (s32[768,1024]{1,0:T(8,128)S(1)}, s32[768,1024]{1,0:T(8,128)}, u32[]{:S(2)}) copy-start(s32[768,1024]{1,0:T(8,128)} %dose_ref.1) | copy-start | bytes 9437188
  23.7 5.8 %copy-start.3 = (f32[768,16]{0,1:T(8,128)S(1)}, f32[768,16]{0,1:T(8,128)}, u32[]{:S(2)}) copy-start(f32[768,16]{0,1:T(8,128)} %param.13) | copy-start | bytes 147460
  23.7 5.8 %copy-start.5 = (s32[1,768]{1,0:T(1,128)S(1)}, s32[1,768]{1,0:T(1,128)}, u32[]{:S(2)}) copy-start(s32[1,768]{1,0:T(1,128)} %order_ref.1) | copy-start | bytes 9220
  23.7 8.7 %copy-start.4 = (f32[768,16]{0,1:T(8,128)S(1)}, f32[768,16]{0,1:T(8,128)}, u32[]{:S(2)}) copy-start(f32[768,16]{0,1:T(8,128)} %param.14) | copy-start | bytes 147460
  23.7 8.7 %copy-start.6 = (f32[16]{0:T(128)S(1)}, f32[16]{0:T(128)}, u32[]{:S(2)}) copy-start(f32[16]{0:T(128)} %param.12) | copy-start | bytes 196
  25.1 5.7 %collective-permute-start.6 = (bf16[16,896]{1,0:T(8,128)(2,1)S(1)}, bf16[16,896]{1,0:T(8,128)(2,1)S(1)}, u32[]{:S(2)}, u32[]{:S(2)}) collective-permute-start(bf16[16,896]{1,0:T(8,128)(2,1)S(1)} %get-tuple-element.34), channel_id=1, source_target_pairs={{0,24},{8,16},{16,8},{24,0},{1,25},{9,17},{17,9},{25,1},{2,26},{10... | collective-permute-start | bytes 86024 | tf_op jit(solution)/shard_map/ppermute | solution.py:22
  27.4 5.1 %collective-permute-start.7 = (bf16[16,896]{1,0:T(8,128)(2,1)S(1)}, bf16[16,896]{1,0:T(8,128)(2,1)S(1)}, u32[]{:S(2)}, u32[]{:S(2)}) collective-permute-start(bf16[16,896]{1,0:T(8,128)(2,1)S(1)} %get-tuple-element.35), channel_id=1, source_target_pairs={{0,16},{8,24},{16,0},{24,8},{1,17},{9,25},{17,1},{25,9},{2,18},{10... | collective-permute-start | bytes 86024 | tf_op jit(solution)/shard_map/ppermute | solution.py:22
  28.2 4.3 %collective-permute-start.8 = (bf16[16,896]{1,0:T(8,128)(2,1)S(1)}, bf16[16,896]{1,0:T(8,128)(2,1)S(1)}, u32[]{:S(2)}, u32[]{:S(2)}) collective-permute-start(bf16[16,896]{1,0:T(8,128)(2,1)S(1)} %get-tuple-element.36), channel_id=1, source_target_pairs={{0,8},{8,0},{16,24},{24,16},{1,9},{9,1},{17,25},{25,17},{2,10},{10... | collective-permute-start | bytes 86024 | tf_op jit(solution)/shard_map/ppermute | solution.py:22
  33.4 10.8 %all-to-all-start = ((f32[32,1,640]{2,1,0:T(1,128)}), f32[32,1,640]{2,1,0:T(1,128)S(1)}, u32[]{:S(2)}, u32[]{:S(2)}) async-start(f32[32,1,640]{2,1,0:T(1,128)} %get-tuple-element.39), calls=%async_computation | async-start | bytes 163840 | tf_op jit(solution)/shard_map/all_to_all | solution.py:447

commit v11 on v10

--- a/solution.py
+++ b/solution.py
@@ -60,7 +60,7 @@
     return jnp.sum(jnp.where(same, row, 0.0), axis=1, keepdims=True)
 
 
-BLOCK = 512
+BLOCK = 1024
 
 
 def blocks(rows, samples):
@@ -108,40 +108,34 @@
     out_ref[rhs:] = jnp.where(upper == 0, other, own).astype(BF16)
 
 
-def weights(pair_ref, w1, w2):
+def weights(pair_ref, w):
     own = pair_ref.shape[1]
-    zero = jnp.zeros((16, 2 * own), BF16)
     row = lax.broadcasted_iota(jnp.int32, (16, 2 * own), 0)
-    w1[16:32] = zero
-    w1[32:48] = jnp.where(row == 0, 1.0, 0.0).astype(BF16)
-    w2[0:16] = zero
-    w2[32:48] = jnp.where(row == 1, 1.0, 0.0).astype(BF16)
+    w[16:32] = jnp.where(row == 0, 1.0, 0.0).astype(BF16)
     for i in range(2):
-        piece = pair_ref[16 * i : 16 * i + 16]
-        w1[0:16, i * own : (i + 1) * own] = piece
-        w2[16:32, i * own : (i + 1) * own] = piece
-
-
-def product(coded_ref, called_ref, first, rows, samples, w1, w2):
+        w[0:16, i * own : (i + 1) * own] = pair_ref[16 * i : 16 * i + 16]
+
+
+def product(coded_ref, called_ref, first, rows, samples, w):
     part = pl.ds(first, rows)
-    got = lax.dot_general(coded_ref[part, samples], w1[...], NT, preferred_element_type=F32)
-    got = got + lax.dot_general(called_ref[part, samples], w2[...], NT, preferred_element_type=F32)
-    got = jnp.concatenate([got, jnp.zeros((rows, LANES - got.shape[1]), F32)], axis=1)
-    return got.T[:40]
+    coded = lax.dot_general(w[...], coded_ref[part, samples], NT, preferred_element_type=F32)
+    called = lax.dot_general(w[...], called_ref[part, samples], NT, preferred_element_type=F32)
+    counts = jnp.concatenate([coded[16:17], called[16:17], jnp.zeros((6, rows), F32)], axis=0)
+    return jnp.concatenate([coded[0:16], called[0:16], counts], axis=0)
 
 
 def pair_samples(pair, own):
     return pl.ds(pl.multiple_of(pair * 2 * own, LANES), 2 * own)
 
 
-def mask_kernel(pair_ref, first_ref, call_ref, gen_hbm, coded_ref, called_ref, out_ref, gbuf, w1, w2, sems):
+def mask_kernel(pair_ref, first_ref, call_ref, gen_hbm, coded_ref, called_ref, out_ref, gbuf, w, sems):
     own = pair_ref.shape[1]
     first = first_ref.shape[0]
     copies = row_copies(gen_hbm, gbuf, first, LANES, sems)
     for copy in copies:
         copy.start()
     samples = pair_samples(lax.axis_index("var") // 2, own)
-    weights(pair_ref, w1, w2)
+    weights(pair_ref, w)
     rows, shard = call_ref.shape
 
     def convert(place):
@@ -154,24 +148,25 @@
             coded[block] = value * mask
             called[block] = mask
 
-    for place in range(0, rows + LANES, LANES):
-        if first <= place < rows:
-            copies[(place - first) // LANES].wait()
-        if place < rows:
-            convert(place)
+    chunk = 2 * LANES
+    for place in range(0, rows + chunk, chunk):
+        for part in range(place, min(place + chunk, rows), LANES):
+            if part >= first:
+                copies[(part - first) // LANES].wait()
+            convert(part)
         if place:
-            before = place - LANES
-            out_ref[:, before:place] = product(coded_ref, called_ref, before, LANES, samples, w1, w2)
-
-
-def forward_kernel(pair_ref, coded_ref, called_ref, half_ref, sums_ref, out_ref, w1, w2):
+            before = place - chunk
+            out_ref[:, before:place] = product(coded_ref, called_ref, before, chunk, samples, w)
+
+
+def forward_kernel(pair_ref, coded_ref, called_ref, half_ref, sums_ref, out_ref, w):
     own = pair_ref.shape[1]
     rows = coded_ref.shape[0]
     samples = pair_samples((lax.axis_index("var") // 2) ^ 1, own)
-    weights(pair_ref, w1, w2)
-    for place in range(0, rows, LANES):
-        here = slice(place, place + LANES)
-        out_ref[:, here] = half_ref[:, here] + product(coded_ref, called_ref, place, LANES, samples, w1, w2)
+    weights(pair_ref, w)
+    for place in range(0, rows, 2 * LANES):
+        here = slice(place, place + 2 * LANES)
+        out_ref[:, here] = half_ref[:, here] + product(coded_ref, called_ref, place, 2 * LANES, samples, w)
     out_ref[:, rows:] = jnp.zeros((out_ref.shape[0], LANES), F32)
     out_ref[0:8, rows:] = sums_ref[...]
 
@@ -381,7 +376,7 @@
     )
     (pair,) = call(pair_kernel, [((2 * rhs, own), BF16)], [VMEM] * 2, (dire, neighbour), limit=4)
     pair_other = swap(pair, "var", 2)
-    both_weights = [pltpu.VMEM((48, 2 * own), BF16), pltpu.VMEM((48, 2 * own), BF16)]
+    row_weights = pltpu.VMEM((2 * rhs, 2 * own), BF16)
     coded, called_b, half = call(
         mask_kernel,
         [matrix(rows), matrix(rows), ((2 * rhs + 8, rows), F32)],
@@ -389,7 +384,7 @@
         (pair, coarse, called, genotypes),
         scratch=[
             pltpu.VMEM((rows - first, shard), jnp.int32),
-            *both_weights,
+            row_weights,
             pltpu.SemaphoreType.DMA(((rows - first) // LANES,)),
         ],
         limit=12,
@@ -401,7 +396,7 @@
         [((2 * rhs + 8, rows + LANES), F32)],
         [VMEM] * 5,
         (pair_other, coded, called_b, half, sums),
-        scratch=both_weights,
+        scratch=[row_weights],
         flops=2 * rows * shard * 256,
         moved=2 * rows * shard,
     )

time: 45.2 us -> 44.8 us (level)
  Pallas kernels: 13.1 us -> 12.6 us
    pallas_call x10, Pallas kernels: 13.1 us -> 12.6 us  [call(): pl.pallas_call(kernel, out_shape=[jax.ShapeDtypeStruct(*o) if len(o) == 2...]
  transfers between devices with their start and end apart: 10 -> 10, of which waited for: 7 -> 7; matrix products, arithmetic and copies ran while one was open for 0% -> 0% of each run, Pallas kernels for 19% -> 18%
where the time goes in v11:
time: 44.8 us; the launch traced here: 44.6 us
  starting transfers between devices  16.9 us (38%)
  waiting for transfers between devices  14.3 us (32%)
  Pallas kernels  12.6 us (28%)
  between operations  0.74 us (2%)
    ppermute x9, starting transfers between devices, swap(): return lax.ppermute(values, axis, [(i, i ^ distance) for i in range(size)])  13.8 us
    pallas_call x10, Pallas kernels, call(): pl.pallas_call(kernel, out_shape=[jax.ShapeDtypeStruct(*o) if len(o) == 2...  12.6 us
    ppermute x9, waiting for transfers between devices, swap(): return lax.ppermute(values, axis, [(i, i ^ distance) for i in range(size)])  7.41 us
    all_to_all x1, waiting for transfers between devices, body(): lax.all_to_all(outgoing, ('var', 'samp'), split_axis=0, concat_axis=0)  6.86 us
    all_to_all x1, starting transfers between devices, body(): lax.all_to_all(outgoing, ('var', 'samp'), split_axis=0, concat_axis=0)  3.17 us
  transfers between devices with their start and end apart: 10, of which 7 were waited for; matrix products, arithmetic and copies ran while one was open for 0% of the time, Pallas kernels for 18%

profile of v11, /device:TPU:0, one launch (start us, length us, event | category | flops | bytes accessed | tf_op | source)
XLA Modules:
  0.0 44.6 jit_solution(2561380079039341856)
XLA Ops:
  0.6 3.1 %collective-permute-start = (f32[16,768]{1,0:T(8,128)}, f32[16,768]{1,0:T(8,128)S(1)}, u32[]{:S(2)}, u32[]{:S(2)}) collective-permute-start(f32[16,768]{1,0:T(8,128)} %bitcast.8), channel_id=1, source_target_pairs={{0,8},{8,0},{16,24},{24,16},{1,9},{9,1},{17,25},{25,17},{2,10},{10... | collective-permute-start | bytes 147464 | tf_op jit(solution)/shard_map/ppermute | solution.py:22
  3.7 2.7 %shard_map.112 = (bf16[384,3072]{1,0:T(8,128)(2,1)S(1)}, f32[8,128]{1,0:T(8,128)S(1)}) custom-call(f32[16,768]{1,0:T(8,128)} %bitcast.15, f32[16,768]{1,0:T(8,128)} %bitcast.9, f32[16,768]{1,0:T(8,128)} %bitcast.18, s32[768,3072]{1,0:T(8,128)} %gen_hbm.3), custom_call_target="tpu_custom_call" | custom-call | bytes 4718592 | tf_op jit(solution)/shard_map/pallas_call | solution.py:334
  6.4 0.0 collective-permute-done.other_ref
  6.4 0.0 copy-done.2
  6.5 2.7 %collective-permute-start.1 = (bf16[32,768]{1,0:T(8,128)(2,1)S(1)}, bf16[32,768]{1,0:T(8,128)(2,1)S(1)}, u32[]{:S(2)}, u32[]{:S(2)}) collective-permute-start(bf16[32,768]{1,0:T(8,128)(2,1)S(1)} %shard_map.111.pair_ref), channel_id=1, source_target_pairs={{0,16},{8,24},{16,0},{24,8},{1,17},{9,25},{17,1},{25,9},{2,18},{10... | collective-permute-start | bytes 147464 | tf_op jit(solution)/shard_map/ppermute | solution.py:22
  9.1 0.0 copy-done
  9.1 3.9 %shard_map.113 = (bf16[768,3072]{1,0:T(8,128)(2,1)S(1)}, bf16[768,3072]{1,0:T(8,128)(2,1)S(1)}, f32[40,768]{1,0:T(8,128)S(1)}) custom-call(bf16[32,768]{1,0:T(8,128)(2,1)S(1)} %shard_map.111.pair_ref, bf16[384,3072]{1,0:T(8,128)(2,1)S(1)} %get-tuple-element.24.first_ref, s32[768,3072]{1,0:T(8,128)S(1)} %copy-done, s32[768,3072]{1,0:T(8,128)} %gen_hbm.3), custom_call_target="tpu_custom_call" | custom-call | flops 1207959552 | bytes 9437184 | tf_op jit(solution)/shard_map/pallas_call | solution.py:334
  13.0 0.0 collective-permute-done.1.pair_ref
  13.0 1.5 %shard_map.114.own_ref = f32[40,896]{1,0:T(8,128)S(1)} custom-call(bf16[32,768]{1,0:T(8,128)(2,1)S(1)} %collective-permute-done.1.pair_ref, bf16[768,3072]{1,0:T(8,128)(2,1)S(1)} %get-tuple-element.25.coded_ref, bf16[768,3072]{1,0:T(8,128)(2,1)S(1)} %get-tuple-element.26.called_ref, f32[40,768]{1,0:T(8,128)S(1)} %get-tuple-element.27.half_ref, ...), custom_call_target="tpu_custom_call" | custom-call | flops 1207959552 | bytes 4718592 | tf_op jit(solution)/shard_map/pallas_call | solution.py:334
  14.5 0.1 collective-permute-start.2
  14.6 1.4 %collective-permute-done.2.other_ref = f32[40,896]{1,0:T(8,128)S(1)} collective-permute-done((f32[40,896]{1,0:T(8,128)S(1)}, f32[40,896]{1,0:T(8,128)S(1)}, u32[]{:S(2)}, u32[]{:S(2)}) %collective-permute-start.2) | collective-permute-done | bytes 143392 | tf_op jit(solution)/shard_map/ppermute | solution.py:22
  16.0 2.5 %collective-permute-start.3 = (bf16[32,896]{1,0:T(8,128)(2,1)S(1)}, bf16[32,896]{1,0:T(8,128)(2,1)S(1)}, u32[]{:S(2)}, u32[]{:S(2)}) collective-permute-start(bf16[32,896]{1,0:T(8,128)(2,1)S(1)} %get-tuple-element.30), channel_id=1, source_target_pairs={{0,6},{1,7},{2,4},{3,5},{4,2},{5,3},{6,0},{7,1},{8,14},{9,15},{10,... | collective-permute-start | bytes 172040 | tf_op jit(solution)/shard_map/ppermute | solution.py:22
  18.5 0.5 %collective-permute-start.4 = (bf16[32,896]{1,0:T(8,128)(2,1)S(1)}, bf16[32,896]{1,0:T(8,128)(2,1)S(1)}, u32[]{:S(2)}, u32[]{:S(2)}) collective-permute-start(bf16[32,896]{1,0:T(8,128)(2,1)S(1)} %get-tuple-element.31), channel_id=1, source_target_pairs={{0,4},{1,5},{2,6},{3,7},{4,0},{5,1},{6,2},{7,3},{8,12},{9,13},{10,... | collective-permute-start | bytes 172040 | tf_op jit(solution)/shard_map/ppermute | solution.py:22
  19.0 0.5 %collective-permute-start.5 = (bf16[32,896]{1,0:T(8,128)(2,1)S(1)}, bf16[32,896]{1,0:T(8,128)(2,1)S(1)}, u32[]{:S(2)}, u32[]{:S(2)}) collective-permute-start(bf16[32,896]{1,0:T(8,128)(2,1)S(1)} %get-tuple-element.32), channel_id=1, source_target_pairs={{0,2},{1,3},{2,0},{3,1},{4,6},{5,7},{6,4},{7,5},{8,10},{9,11},{10,... | collective-permute-start | bytes 172040 | tf_op jit(solution)/shard_map/ppermute | solution.py:22
  19.6 1.6 %collective-permute-done.3.rest_0_ = bf16[32,896]{1,0:T(8,128)(2,1)S(1)} collective-permute-done((bf16[32,896]{1,0:T(8,128)(2,1)S(1)}, bf16[32,896]{1,0:T(8,128)(2,1)S(1)}, u32[]{:S(2)}, u32[]{:S(2)}) %collective-permute-start.3) | collective-permute-done | bytes 57376 | tf_op jit(solution)/shard_map/ppermute | solution.py:22
  21.2 1.5 %collective-permute-done.4.rest_1_ = bf16[32,896]{1,0:T(8,128)(2,1)S(1)} collective-permute-done((bf16[32,896]{1,0:T(8,128)(2,1)S(1)}, bf16[32,896]{1,0:T(8,128)(2,1)S(1)}, u32[]{:S(2)}, u32[]{:S(2)}) %collective-permute-start.4) | collective-permute-done | bytes 57376 | tf_op jit(solution)/shard_map/ppermute | solution.py:22
  22.7 0.5 %collective-permute-done.5.rest_2_ = bf16[32,896]{1,0:T(8,128)(2,1)S(1)} collective-permute-done((bf16[32,896]{1,0:T(8,128)(2,1)S(1)}, bf16[32,896]{1,0:T(8,128)(2,1)S(1)}, u32[]{:S(2)}, u32[]{:S(2)}) %collective-permute-start.5) | collective-permute-done | bytes 57376 | tf_op jit(solution)/shard_map/ppermute | solution.py:22
  23.2 0.0 copy-start.6
  23.2 1.4 %shard_map.116 = (f32[16,896]{1,0:T(8,128)S(1)}, bf16[16,896]{1,0:T(8,128)(2,1)S(1)}, bf16[16,896]{1,0:T(8,128)(2,1)S(1)}, bf16[16,896]{1,0:T(8,128)(2,1)S(1)}) custom-call(f32[40,896]{1,0:T(8,128)S(1)} %get-tuple-element.29.total_ref.after_ref, bf16[768,3072]{1,0:T(8,128)(2,1)S(1)} %get-tuple-element.25.coded_ref, ...), custom_call_target="tpu_custom_call" | custom-call | flops 2415919104 | bytes 9437184 | tf_op jit(solution)/shard_map/pallas_call | solution.py:334
  24.6 2.5 %collective-permute-start.6 = (bf16[16,896]{1,0:T(8,128)(2,1)S(1)}, bf16[16,896]{1,0:T(8,128)(2,1)S(1)}, u32[]{:S(2)}, u32[]{:S(2)}) collective-permute-start(bf16[16,896]{1,0:T(8,128)(2,1)S(1)} %get-tuple-element.34), channel_id=1, source_target_pairs={{0,24},{8,16},{16,8},{24,0},{1,25},{9,17},{17,9},{25,1},{2,26},{10... | collective-permute-start | bytes 86024 | tf_op jit(solution)/shard_map/ppermute | solution.py:22
  27.1 0.5 %collective-permute-start.7 = (bf16[16,896]{1,0:T(8,128)(2,1)S(1)}, bf16[16,896]{1,0:T(8,128)(2,1)S(1)}, u32[]{:S(2)}, u32[]{:S(2)}) collective-permute-start(bf16[16,896]{1,0:T(8,128)(2,1)S(1)} %get-tuple-element.35), channel_id=1, source_target_pairs={{0,16},{8,24},{16,0},{24,8},{1,17},{9,25},{17,1},{25,9},{2,18},{10... | collective-permute-start | bytes 86024 | tf_op jit(solution)/shard_map/ppermute | solution.py:22
  27.6 1.4 %collective-permute-start.8 = (bf16[16,896]{1,0:T(8,128)(2,1)S(1)}, bf16[16,896]{1,0:T(8,128)(2,1)S(1)}, u32[]{:S(2)}, u32[]{:S(2)}) collective-permute-start(bf16[16,896]{1,0:T(8,128)(2,1)S(1)} %get-tuple-element.36), channel_id=1, source_target_pairs={{0,8},{8,0},{16,24},{24,16},{1,9},{9,1},{17,25},{25,17},{2,10},{10... | collective-permute-start | bytes 86024 | tf_op jit(solution)/shard_map/ppermute | solution.py:22
  29.0 0.0 copy-done.3
  29.0 0.6 %shard_map.118.cross_ref = f32[40,1024]{1,0:T(8,128)S(1)} custom-call(s32[1,768]{1,0:T(1,128)S(1)} %copy-done.5, f32[16,768]{1,0:T(8,128)S(1)} %bitcast.16, f32[16,768]{1,0:T(8,128)S(1)} %bitcast.11, s32[768,1024]{1,0:T(8,128)S(1)} %copy-done.1, f32[40,896]{1,0:T(8,128)S(1)} %get-tuple-element.29.total_ref.after_ref), custom_call_target="tpu_custom_call" | custom-call | flops 220200960 | bytes 3145728 | tf_op jit(solution)/shard_map/pallas_call | solution.py:334
  29.7 0.9 %collective-permute-done.6.rest_1_ = bf16[16,896]{1,0:T(8,128)(2,1)S(1)} collective-permute-done((bf16[16,896]{1,0:T(8,128)(2,1)S(1)}, bf16[16,896]{1,0:T(8,128)(2,1)S(1)}, u32[]{:S(2)}, u32[]{:S(2)}) %collective-permute-start.6) | collective-permute-done | bytes 28704 | tf_op jit(solution)/shard_map/ppermute | solution.py:22
  30.6 1.5 %collective-permute-done.7.rest_2_ = bf16[16,896]{1,0:T(8,128)(2,1)S(1)} collective-permute-done((bf16[16,896]{1,0:T(8,128)(2,1)S(1)}, bf16[16,896]{1,0:T(8,128)(2,1)S(1)}, u32[]{:S(2)}, u32[]{:S(2)}) %collective-permute-start.7) | collective-permute-done | bytes 28704 | tf_op jit(solution)/shard_map/ppermute | solution.py:22
  32.1 0.0 collective-permute-done.8.rest_3_
  32.1 0.9 %shard_map.119 = (f32[32,1,640]{2,1,0:T(1,128)}, f32[16,768]{1,0:T(8,128)S(1)}) custom-call(f32[1,16]{1,0:T(1,128)S(1)} %bitcast.21, f32[16,768]{1,0:T(8,128)S(1)} %bitcast.12, f32[16,768]{1,0:T(8,128)S(1)} %bitcast.19, f32[40,1024]{1,0:T(8,128)S(1)} %shard_map.118.cross_ref, f32[16,896]{1,0:T(8,128)S(1)} %get-tuple-element.33.rest_0_, ...), custom_call_target="tpu_custom_call" | custom-call | bytes 81920 | tf_op jit(solution)/shard_map/pallas_call | solution.py:334
  33.0 3.2 %all-to-all-start = ((f32[32,1,640]{2,1,0:T(1,128)}), f32[32,1,640]{2,1,0:T(1,128)S(1)}, u32[]{:S(2)}, u32[]{:S(2)}) async-start(f32[32,1,640]{2,1,0:T(1,128)} %get-tuple-element.39), calls=%async_computation | async-start | bytes 163840 | tf_op jit(solution)/shard_map/all_to_all | solution.py:442
  36.1 0.7 %shard_map.117 = (f32[16,768]{1,0:T(8,128)}, f32[16,768]{1,0:T(8,128)}, f32[16,128]{1,0:T(8,128)S(1)}) custom-call(f32[1,16]{1,0:T(1,128)S(1)} %bitcast.22, f32[16,768]{1,0:T(8,128)S(1)} %bitcast.13, f32[16,768]{1,0:T(8,128)S(1)} %bitcast.20, f32[16,768]{1,0:T(8,128)S(1)} %bitcast.17, f32[16,896]{1,0:T(8,128)S(1)} %get-tuple-element.33.rest_0_, ...), custom_call_target="tpu_custom_call" | custom-call | bytes 1048576 | tf_op jit(solution)/shard_map/pallas_call | solution.py:334
  36.9 6.9 %all-to-all-done.came_ref = f32[32,1,640]{2,1,0:T(1,128)S(1)} async-done(((f32[32,1,640]{2,1,0:T(1,128)}), f32[32,1,640]{2,1,0:T(1,128)S(1)}, u32[]{:S(2)}, u32[]{:S(2)}) %all-to-all-start) | async-done | bytes 81952 | tf_op jit(solution)/shard_map/all_to_all | solution.py:442
  43.8 0.8 %shard_map.120 = (f32[16,768]{1,0:T(8,128)}, f32[16,32]{1,0:T(8,128)}) custom-call(f32[32,1,640]{2,1,0:T(1,128)S(1)} %all-to-all-done.came_ref, f32[16,128]{1,0:T(8,128)S(1)} %get-tuple-element.40.stats_ref, f32[16,768]{1,0:T(8,128)S(1)} %get-tuple-element.41.res_ref, f32[16,768]{1,0:T(8,128)S(1)} %bitcast.14), custom_call_target="tpu_custom_call" | custom-call | tf_op jit(solution)/shard_map/pallas_call | solution.py:334
  (12 shorter events, 0.1 us)
Async XLA Ops:
  0.6 5.8 %collective-permute-start = (f32[16,768]{1,0:T(8,128)}, f32[16,768]{1,0:T(8,128)S(1)}, u32[]{:S(2)}, u32[]{:S(2)}) collective-permute-start(f32[16,768]{1,0:T(8,128)} %bitcast.8), channel_id=1, source_target_pairs={{0,8},{8,0},{16,24},{24,16},{1,9},{9,1},{17,25},{25,17},{2,10},{10... | collective-permute-start | bytes 147464 | tf_op jit(solution)/shard_map/ppermute | solution.py:22
  3.7 2.7 %copy-start.2 = (f32[768,16]{0,1:T(8,128)S(1)}, f32[768,16]{0,1:T(8,128)}, u32[]{:S(2)}) copy-start(f32[768,16]{0,1:T(8,128)} %param.15) | copy-start | bytes 147460
  3.7 5.4 %copy-start = (s32[768,3072]{1,0:T(8,128)S(1)}, s32[768,3072]{1,0:T(8,128)}, u32[]{:S(2)}) copy-start(s32[768,3072]{1,0:T(8,128)} %call_ref.1) | copy-start | bytes 28311556
  6.5 6.5 %collective-permute-start.1 = (bf16[32,768]{1,0:T(8,128)(2,1)S(1)}, bf16[32,768]{1,0:T(8,128)(2,1)S(1)}, u32[]{:S(2)}, u32[]{:S(2)}) collective-permute-start(bf16[32,768]{1,0:T(8,128)(2,1)S(1)} %shard_map.111.pair_ref), channel_id=1, source_target_pairs={{0,16},{8,24},{16,0},{24,8},{1,17},{9,25},{17,1},{25,9},{2,18},{10... | collective-permute-start | bytes 147464 | tf_op jit(solution)/shard_map/ppermute | solution.py:22
  14.5 1.4 %collective-permute-start.2 = (f32[40,896]{1,0:T(8,128)S(1)}, f32[40,896]{1,0:T(8,128)S(1)}, u32[]{:S(2)}, u32[]{:S(2)}) collective-permute-start(f32[40,896]{1,0:T(8,128)S(1)} %shard_map.114.own_ref), channel_id=1, source_target_pairs={{0,1},{1,0},{2,3},{3,2},{4,5},{5,4},{6,7},{7,6},{8,9},{9,8},{10,11... | collective-permute-start | bytes 430088 | tf_op jit(solution)/shard_map/ppermute | solution.py:22
  16.0 5.2 %collective-permute-start.3 = (bf16[32,896]{1,0:T(8,128)(2,1)S(1)}, bf16[32,896]{1,0:T(8,128)(2,1)S(1)}, u32[]{:S(2)}, u32[]{:S(2)}) collective-permute-start(bf16[32,896]{1,0:T(8,128)(2,1)S(1)} %get-tuple-element.30), channel_id=1, source_target_pairs={{0,6},{1,7},{2,4},{3,5},{4,2},{5,3},{6,0},{7,1},{8,14},{9,15},{10,... | collective-permute-start | bytes 172040 | tf_op jit(solution)/shard_map/ppermute | solution.py:22
  18.5 4.2 %collective-permute-start.4 = (bf16[32,896]{1,0:T(8,128)(2,1)S(1)}, bf16[32,896]{1,0:T(8,128)(2,1)S(1)}, u32[]{:S(2)}, u32[]{:S(2)}) collective-permute-start(bf16[32,896]{1,0:T(8,128)(2,1)S(1)} %get-tuple-element.31), channel_id=1, source_target_pairs={{0,4},{1,5},{2,6},{3,7},{4,0},{5,1},{6,2},{7,3},{8,12},{9,13},{10,... | collective-permute-start | bytes 172040 | tf_op jit(solution)/shard_map/ppermute | solution.py:22
  19.0 4.2 %collective-permute-start.5 = (bf16[32,896]{1,0:T(8,128)(2,1)S(1)}, bf16[32,896]{1,0:T(8,128)(2,1)S(1)}, u32[]{:S(2)}, u32[]{:S(2)}) collective-permute-start(bf16[32,896]{1,0:T(8,128)(2,1)S(1)} %get-tuple-element.32), channel_id=1, source_target_pairs={{0,2},{1,3},{2,0},{3,1},{4,6},{5,7},{6,4},{7,5},{8,10},{9,11},{10,... | collective-permute-start | bytes 172040 | tf_op jit(solution)/shard_map/ppermute | solution.py:22
  23.2 5.8 %copy-start.1 = (s32[768,1024]{1,0:T(8,128)S(1)}, s32[768,1024]{1,0:T(8,128)}, u32[]{:S(2)}) copy-start(s32[768,1024]{1,0:T(8,128)} %dose_ref.1) | copy-start | bytes 9437188
  23.2 5.8 %copy-start.3 = (f32[768,16]{0,1:T(8,128)S(1)}, f32[768,16]{0,1:T(8,128)}, u32[]{:S(2)}) copy-start(f32[768,16]{0,1:T(8,128)} %param.13) | copy-start | bytes 147460
  23.2 5.8 %copy-start.5 = (s32[1,768]{1,0:T(1,128)S(1)}, s32[1,768]{1,0:T(1,128)}, u32[]{:S(2)}) copy-start(s32[1,768]{1,0:T(1,128)} %order_ref.1) | copy-start | bytes 9220
  23.2 8.9 %copy-start.4 = (f32[768,16]{0,1:T(8,128)S(1)}, f32[768,16]{0,1:T(8,128)}, u32[]{:S(2)}) copy-start(f32[768,16]{0,1:T(8,128)} %param.14) | copy-start | bytes 147460
  23.2 8.9 %copy-start.6 = (f32[16]{0:T(128)S(1)}, f32[16]{0:T(128)}, u32[]{:S(2)}) copy-start(f32[16]{0:T(128)} %param.12) | copy-start | bytes 196
  24.6 5.9 %collective-permute-start.6 = (bf16[16,896]{1,0:T(8,128)(2,1)S(1)}, bf16[16,896]{1,0:T(8,128)(2,1)S(1)}, u32[]{:S(2)}, u32[]{:S(2)}) collective-permute-start(bf16[16,896]{1,0:T(8,128)(2,1)S(1)} %get-tuple-element.34), channel_id=1, source_target_pairs={{0,24},{8,16},{16,8},{24,0},{1,25},{9,17},{17,9},{25,1},{2,26},{10... | collective-permute-start | bytes 86024 | tf_op jit(solution)/shard_map/ppermute | solution.py:22
  27.1 4.9 %collective-permute-start.7 = (bf16[16,896]{1,0:T(8,128)(2,1)S(1)}, bf16[16,896]{1,0:T(8,128)(2,1)S(1)}, u32[]{:S(2)}, u32[]{:S(2)}) collective-permute-start(bf16[16,896]{1,0:T(8,128)(2,1)S(1)} %get-tuple-element.35), channel_id=1, source_target_pairs={{0,16},{8,24},{16,0},{24,8},{1,17},{9,25},{17,1},{25,9},{2,18},{10... | collective-permute-start | bytes 86024 | tf_op jit(solution)/shard_map/ppermute | solution.py:22
  27.6 4.4 %collective-permute-start.8 = (bf16[16,896]{1,0:T(8,128)(2,1)S(1)}, bf16[16,896]{1,0:T(8,128)(2,1)S(1)}, u32[]{:S(2)}, u32[]{:S(2)}) collective-permute-start(bf16[16,896]{1,0:T(8,128)(2,1)S(1)} %get-tuple-element.36), channel_id=1, source_target_pairs={{0,8},{8,0},{16,24},{24,16},{1,9},{9,1},{17,25},{25,17},{2,10},{10... | collective-permute-start | bytes 86024 | tf_op jit(solution)/shard_map/ppermute | solution.py:22
  33.0 10.8 %all-to-all-start = ((f32[32,1,640]{2,1,0:T(1,128)}), f32[32,1,640]{2,1,0:T(1,128)S(1)}, u32[]{:S(2)}, u32[]{:S(2)}) async-start(f32[32,1,640]{2,1,0:T(1,128)} %get-tuple-element.39), calls=%async_computation | async-start | bytes 163840 | tf_op jit(solution)/shard_map/all_to_all | solution.py:442

commit v12 on v11

--- a/solution.py
+++ b/solution.py
@@ -142,11 +142,19 @@
         here = pl.ds(place, LANES)
         gen = first_ref.at[here] if place < first else gbuf.at[pl.ds(place - first, LANES)]
         call, coded, called = call_ref.at[here], coded_ref.at[here], called_ref.at[here]
+
+        def store(block, value, mask):
+            coded[block] = value
+            called[block] = mask
+
+        held = None
         for block in blocks(LANES, shard):
             mask = call[block].astype(F32).astype(BF16)
             value = gen[block] if place < first else gen[block].astype(F32).astype(BF16)
-            coded[block] = value * mask
-            called[block] = mask
+            if held:
+                store(*held)
+            held = (block, value * mask, mask)
+        store(*held)
 
     chunk = 2 * LANES
     for place in range(0, rows + chunk, chunk):
@@ -354,7 +362,7 @@
     noise = noise_ratio[None]
 
     dire, res, sol = direction.T, residual.T, solution.T
-    first, chunk = rows // 2, 128
+    first, chunk = rows // 3 * 2, 128
     matrix = lambda n: ((n, shard), BF16, pltpu.VMEM)
 
     neighbour = swap(dire, "var", 1)
@@ -371,7 +379,7 @@
             pltpu.SemaphoreType.DMA((3,)),
             pltpu.SemaphoreType.DMA((first // chunk,)),
         ],
-        limit=6,
+        limit=10,
         moved=4 * first * shard,
     )
     (pair,) = call(pair_kernel, [((2 * rhs, own), BF16)], [VMEM] * 2, (dire, neighbour), limit=4)
@@ -410,7 +418,7 @@
         (part, part_other),
         moved=1 * MIB,
     )
-    arrived = [swap(messages[k], "samp", 2 * (k + 1)) for k in reversed(range(n_chips - 1))]
+    arrived = [swap(messages[k], "samp", 2 * (k + 1) + 1) for k in reversed(range(n_chips - 1))]
     (cross,) = call(
         dosage_kernel,
         [((2 * rhs + 8, imputed), F32)],

time: 44.8 us -> 44.3 us (0.989)
    ppermute x9, starting transfers between devices: 13.8 us -> 13.3 us  [swap(): return lax.ppermute(values, axis, [(i, i ^ distance) for i in range(size)])]
where the time goes in v12:
time: 44.3 us; the launch traced here: 44.1 us
  starting transfers between devices  16.6 us (37%)
  waiting for transfers between devices  14.3 us (32%)
  Pallas kernels  12.4 us (28%)
  between operations  0.74 us (2%)
    ppermute x9, starting transfers between devices, swap(): return lax.ppermute(values, axis, [(i, i ^ distance) for i in range(size)])  13.3 us
    pallas_call x10, Pallas kernels, call(): pl.pallas_call(kernel, out_shape=[jax.ShapeDtypeStruct(*o) if len(o) == 2...  12.4 us
    ppermute x9, waiting for transfers between devices, swap(): return lax.ppermute(values, axis, [(i, i ^ distance) for i in range(size)])  7.46 us
    all_to_all x1, waiting for transfers between devices, body(): lax.all_to_all(outgoing, ('var', 'samp'), split_axis=0, concat_axis=0)  6.86 us
    all_to_all x1, starting transfers between devices, body(): lax.all_to_all(outgoing, ('var', 'samp'), split_axis=0, concat_axis=0)  3.34 us
  transfers between devices with their start and end apart: 10, of which 7 were waited for; matrix products, arithmetic and copies ran while one was open for 0% of the time, Pallas kernels for 18%

profile of v12, /device:TPU:0, one launch (start us, length us, event | category | flops | bytes accessed | tf_op | source)
XLA Modules:
  0.0 44.1 jit_solution(2582518336964434115)
XLA Ops:
  0.6 3.1 %collective-permute-start = (f32[16,768]{1,0:T(8,128)}, f32[16,768]{1,0:T(8,128)S(1)}, u32[]{:S(2)}, u32[]{:S(2)}) collective-permute-start(f32[16,768]{1,0:T(8,128)} %bitcast.8), channel_id=1, source_target_pairs={{0,8},{8,0},{16,24},{24,16},{1,9},{9,1},{17,25},{25,17},{2,10},{10... | collective-permute-start | bytes 147464 | tf_op jit(solution)/shard_map/ppermute | solution.py:22
  3.7 3.2 %shard_map.112 = (bf16[512,3072]{1,0:T(8,128)(2,1)S(1)}, f32[8,128]{1,0:T(8,128)S(1)}) custom-call(f32[16,768]{1,0:T(8,128)} %bitcast.15, f32[16,768]{1,0:T(8,128)} %bitcast.9, f32[16,768]{1,0:T(8,128)} %bitcast.18, s32[768,3072]{1,0:T(8,128)} %gen_hbm.3), custom_call_target="tpu_custom_call" | custom-call | bytes 6291456 | tf_op jit(solution)/shard_map/pallas_call | solution.py:342
  6.9 0.0 collective-permute-done.other_ref
  6.9 2.7 %collective-permute-start.1 = (bf16[32,768]{1,0:T(8,128)(2,1)S(1)}, bf16[32,768]{1,0:T(8,128)(2,1)S(1)}, u32[]{:S(2)}, u32[]{:S(2)}) collective-permute-start(bf16[32,768]{1,0:T(8,128)(2,1)S(1)} %shard_map.111.pair_ref), channel_id=1, source_target_pairs={{0,16},{8,24},{16,0},{24,8},{1,17},{9,25},{17,1},{25,9},{2,18},{10... | collective-permute-start | bytes 147464 | tf_op jit(solution)/shard_map/ppermute | solution.py:22
  9.6 3.2 %shard_map.113 = (bf16[768,3072]{1,0:T(8,128)(2,1)S(1)}, bf16[768,3072]{1,0:T(8,128)(2,1)S(1)}, f32[40,768]{1,0:T(8,128)S(1)}) custom-call(bf16[32,768]{1,0:T(8,128)(2,1)S(1)} %shard_map.111.pair_ref, bf16[512,3072]{1,0:T(8,128)(2,1)S(1)} %get-tuple-element.24.first_ref, s32[768,3072]{1,0:T(8,128)S(1)} %copy-done, s32[768,3072]{1,0:T(8,128)} %gen_hbm.3), custom_call_target="tpu_custom_call" | custom-call | flops 1207959552 | bytes 9437184 | tf_op jit(solution)/shard_map/pallas_call | solution.py:342
  12.8 0.0 collective-permute-done.1.pair_ref
  12.8 1.5 %shard_map.114.own_ref = f32[40,896]{1,0:T(8,128)S(1)} custom-call(bf16[32,768]{1,0:T(8,128)(2,1)S(1)} %collective-permute-done.1.pair_ref, bf16[768,3072]{1,0:T(8,128)(2,1)S(1)} %get-tuple-element.25.coded_ref, bf16[768,3072]{1,0:T(8,128)(2,1)S(1)} %get-tuple-element.26.called_ref, f32[40,768]{1,0:T(8,128)S(1)} %get-tuple-element.27.half_ref, ...), custom_call_target="tpu_custom_call" | custom-call | flops 1207959552 | bytes 4718592 | tf_op jit(solution)/shard_map/pallas_call | solution.py:342
  14.4 0.1 collective-permute-start.2
  14.4 1.4 %collective-permute-done.2.other_ref = f32[40,896]{1,0:T(8,128)S(1)} collective-permute-done((f32[40,896]{1,0:T(8,128)S(1)}, f32[40,896]{1,0:T(8,128)S(1)}, u32[]{:S(2)}, u32[]{:S(2)}) %collective-permute-start.2) | collective-permute-done | bytes 143392 | tf_op jit(solution)/shard_map/ppermute | solution.py:22
  15.8 2.3 %collective-permute-start.3 = (bf16[32,896]{1,0:T(8,128)(2,1)S(1)}, bf16[32,896]{1,0:T(8,128)(2,1)S(1)}, u32[]{:S(2)}, u32[]{:S(2)}) collective-permute-start(bf16[32,896]{1,0:T(8,128)(2,1)S(1)} %get-tuple-element.30), channel_id=1, source_target_pairs={{0,7},{1,6},{2,5},{3,4},{4,3},{5,2},{6,1},{7,0},{8,15},{9,14},{10,... | collective-permute-start | bytes 172040 | tf_op jit(solution)/shard_map/ppermute | solution.py:22
  18.1 0.5 %collective-permute-start.4 = (bf16[32,896]{1,0:T(8,128)(2,1)S(1)}, bf16[32,896]{1,0:T(8,128)(2,1)S(1)}, u32[]{:S(2)}, u32[]{:S(2)}) collective-permute-start(bf16[32,896]{1,0:T(8,128)(2,1)S(1)} %get-tuple-element.31), channel_id=1, source_target_pairs={{0,5},{1,4},{2,7},{3,6},{4,1},{5,0},{6,3},{7,2},{8,13},{9,12},{10,... | collective-permute-start | bytes 172040 | tf_op jit(solution)/shard_map/ppermute | solution.py:22
  18.6 0.3 collective-permute-start.5
  18.9 1.8 %collective-permute-done.3.rest_0_ = bf16[32,896]{1,0:T(8,128)(2,1)S(1)} collective-permute-done((bf16[32,896]{1,0:T(8,128)(2,1)S(1)}, bf16[32,896]{1,0:T(8,128)(2,1)S(1)}, u32[]{:S(2)}, u32[]{:S(2)}) %collective-permute-start.3) | collective-permute-done | bytes 57376 | tf_op jit(solution)/shard_map/ppermute | solution.py:22
  20.7 1.2 %collective-permute-done.4.rest_1_ = bf16[32,896]{1,0:T(8,128)(2,1)S(1)} collective-permute-done((bf16[32,896]{1,0:T(8,128)(2,1)S(1)}, bf16[32,896]{1,0:T(8,128)(2,1)S(1)}, u32[]{:S(2)}, u32[]{:S(2)}) %collective-permute-start.4) | collective-permute-done | bytes 57376 | tf_op jit(solution)/shard_map/ppermute | solution.py:22
  21.8 0.6 %collective-permute-done.5.rest_2_ = bf16[32,896]{1,0:T(8,128)(2,1)S(1)} collective-permute-done((bf16[32,896]{1,0:T(8,128)(2,1)S(1)}, bf16[32,896]{1,0:T(8,128)(2,1)S(1)}, u32[]{:S(2)}, u32[]{:S(2)}) %collective-permute-start.5) | collective-permute-done | bytes 57376 | tf_op jit(solution)/shard_map/ppermute | solution.py:22
  22.4 0.0 copy-start.6
  22.5 1.4 %shard_map.116 = (f32[16,896]{1,0:T(8,128)S(1)}, bf16[16,896]{1,0:T(8,128)(2,1)S(1)}, bf16[16,896]{1,0:T(8,128)(2,1)S(1)}, bf16[16,896]{1,0:T(8,128)(2,1)S(1)}) custom-call(f32[40,896]{1,0:T(8,128)S(1)} %get-tuple-element.29.total_ref.after_ref, bf16[768,3072]{1,0:T(8,128)(2,1)S(1)} %get-tuple-element.25.coded_ref, ...), custom_call_target="tpu_custom_call" | custom-call | flops 2415919104 | bytes 9437184 | tf_op jit(solution)/shard_map/pallas_call | solution.py:342
  23.9 2.8 %collective-permute-start.6 = (bf16[16,896]{1,0:T(8,128)(2,1)S(1)}, bf16[16,896]{1,0:T(8,128)(2,1)S(1)}, u32[]{:S(2)}, u32[]{:S(2)}) collective-permute-start(bf16[16,896]{1,0:T(8,128)(2,1)S(1)} %get-tuple-element.34), channel_id=1, source_target_pairs={{0,24},{8,16},{16,8},{24,0},{1,25},{9,17},{17,9},{25,1},{2,26},{10... | collective-permute-start | bytes 86024 | tf_op jit(solution)/shard_map/ppermute | solution.py:22
  26.7 0.0 collective-permute-start.7
  26.7 1.6 %collective-permute-start.8 = (bf16[16,896]{1,0:T(8,128)(2,1)S(1)}, bf16[16,896]{1,0:T(8,128)(2,1)S(1)}, u32[]{:S(2)}, u32[]{:S(2)}) collective-permute-start(bf16[16,896]{1,0:T(8,128)(2,1)S(1)} %get-tuple-element.36), channel_id=1, source_target_pairs={{0,8},{8,0},{16,24},{24,16},{1,9},{9,1},{17,25},{25,17},{2,10},{10... | collective-permute-start | bytes 86024 | tf_op jit(solution)/shard_map/ppermute | solution.py:22
  28.3 0.0 copy-done.1
  28.3 0.0 copy-done.5
  28.3 0.6 %shard_map.118.cross_ref = f32[40,1024]{1,0:T(8,128)S(1)} custom-call(s32[1,768]{1,0:T(1,128)S(1)} %copy-done.5, f32[16,768]{1,0:T(8,128)S(1)} %bitcast.16, f32[16,768]{1,0:T(8,128)S(1)} %bitcast.11, s32[768,1024]{1,0:T(8,128)S(1)} %copy-done.1, f32[40,896]{1,0:T(8,128)S(1)} %get-tuple-element.29.total_ref.after_ref), custom_call_target="tpu_custom_call" | custom-call | flops 220200960 | bytes 3145728 | tf_op jit(solution)/shard_map/pallas_call | solution.py:342
  28.9 0.8 %collective-permute-done.6.rest_1_ = bf16[16,896]{1,0:T(8,128)(2,1)S(1)} collective-permute-done((bf16[16,896]{1,0:T(8,128)(2,1)S(1)}, bf16[16,896]{1,0:T(8,128)(2,1)S(1)}, u32[]{:S(2)}, u32[]{:S(2)}) %collective-permute-start.6) | collective-permute-done | bytes 28704 | tf_op jit(solution)/shard_map/ppermute | solution.py:22
  29.6 1.8 %collective-permute-done.7.rest_2_ = bf16[16,896]{1,0:T(8,128)(2,1)S(1)} collective-permute-done((bf16[16,896]{1,0:T(8,128)(2,1)S(1)}, bf16[16,896]{1,0:T(8,128)(2,1)S(1)}, u32[]{:S(2)}, u32[]{:S(2)}) %collective-permute-start.7) | collective-permute-done | bytes 28704 | tf_op jit(solution)/shard_map/ppermute | solution.py:22
  31.4 0.0 collective-permute-done.8.rest_3_
  31.4 0.0 copy-done.4
  31.4 0.9 %shard_map.119 = (f32[32,1,640]{2,1,0:T(1,128)}, f32[16,768]{1,0:T(8,128)S(1)}) custom-call(f32[1,16]{1,0:T(1,128)S(1)} %bitcast.21, f32[16,768]{1,0:T(8,128)S(1)} %bitcast.12, f32[16,768]{1,0:T(8,128)S(1)} %bitcast.19, f32[40,1024]{1,0:T(8,128)S(1)} %shard_map.118.cross_ref, f32[16,896]{1,0:T(8,128)S(1)} %get-tuple-element.33.rest_0_, ...), custom_call_target="tpu_custom_call" | custom-call | bytes 81920 | tf_op jit(solution)/shard_map/pallas_call | solution.py:342
  32.3 3.3 %all-to-all-start = ((f32[32,1,640]{2,1,0:T(1,128)}), f32[32,1,640]{2,1,0:T(1,128)S(1)}, u32[]{:S(2)}, u32[]{:S(2)}) async-start(f32[32,1,640]{2,1,0:T(1,128)} %get-tuple-element.39), calls=%async_computation | async-start | bytes 163840 | tf_op jit(solution)/shard_map/all_to_all | solution.py:450
  35.7 0.7 %shard_map.117 = (f32[16,768]{1,0:T(8,128)}, f32[16,768]{1,0:T(8,128)}, f32[16,128]{1,0:T(8,128)S(1)}) custom-call(f32[1,16]{1,0:T(1,128)S(1)} %bitcast.22, f32[16,768]{1,0:T(8,128)S(1)} %bitcast.13, f32[16,768]{1,0:T(8,128)S(1)} %bitcast.20, f32[16,768]{1,0:T(8,128)S(1)} %bitcast.17, f32[16,896]{1,0:T(8,128)S(1)} %get-tuple-element.33.rest_0_, ...), custom_call_target="tpu_custom_call" | custom-call | bytes 1048576 | tf_op jit(solution)/shard_map/pallas_call | solution.py:342
  36.4 6.9 %all-to-all-done.came_ref = f32[32,1,640]{2,1,0:T(1,128)S(1)} async-done(((f32[32,1,640]{2,1,0:T(1,128)}), f32[32,1,640]{2,1,0:T(1,128)S(1)}, u32[]{:S(2)}, u32[]{:S(2)}) %all-to-all-start) | async-done | bytes 81952 | tf_op jit(solution)/shard_map/all_to_all | solution.py:450
  43.3 0.8 %shard_map.120 = (f32[16,768]{1,0:T(8,128)}, f32[16,32]{1,0:T(8,128)}) custom-call(f32[32,1,640]{2,1,0:T(1,128)S(1)} %all-to-all-done.came_ref, f32[16,128]{1,0:T(8,128)S(1)} %get-tuple-element.40.stats_ref, f32[16,768]{1,0:T(8,128)S(1)} %get-tuple-element.41.res_ref, f32[16,768]{1,0:T(8,128)S(1)} %bitcast.14), custom_call_target="tpu_custom_call" | custom-call | tf_op jit(solution)/shard_map/pallas_call | solution.py:342
  (12 shorter events, 0.1 us)
Async XLA Ops:
  0.6 6.3 %collective-permute-start = (f32[16,768]{1,0:T(8,128)}, f32[16,768]{1,0:T(8,128)S(1)}, u32[]{:S(2)}, u32[]{:S(2)}) collective-permute-start(f32[16,768]{1,0:T(8,128)} %bitcast.8), channel_id=1, source_target_pairs={{0,8},{8,0},{16,24},{24,16},{1,9},{9,1},{17,25},{25,17},{2,10},{10... | collective-permute-start | bytes 147464 | tf_op jit(solution)/shard_map/ppermute | solution.py:22
  3.7 3.2 %copy-start.2 = (f32[768,16]{0,1:T(8,128)S(1)}, f32[768,16]{0,1:T(8,128)}, u32[]{:S(2)}) copy-start(f32[768,16]{0,1:T(8,128)} %param.15) | copy-start | bytes 147460
  3.7 5.9 %copy-start = (s32[768,3072]{1,0:T(8,128)S(1)}, s32[768,3072]{1,0:T(8,128)}, u32[]{:S(2)}) copy-start(s32[768,3072]{1,0:T(8,128)} %call_ref.1) | copy-start | bytes 28311556
  6.9 5.9 %collective-permute-start.1 = (bf16[32,768]{1,0:T(8,128)(2,1)S(1)}, bf16[32,768]{1,0:T(8,128)(2,1)S(1)}, u32[]{:S(2)}, u32[]{:S(2)}) collective-permute-start(bf16[32,768]{1,0:T(8,128)(2,1)S(1)} %shard_map.111.pair_ref), channel_id=1, source_target_pairs={{0,16},{8,24},{16,0},{24,8},{1,17},{9,25},{17,1},{25,9},{2,18},{10... | collective-permute-start | bytes 147464 | tf_op jit(solution)/shard_map/ppermute | solution.py:22
  14.4 1.4 %collective-permute-start.2 = (f32[40,896]{1,0:T(8,128)S(1)}, f32[40,896]{1,0:T(8,128)S(1)}, u32[]{:S(2)}, u32[]{:S(2)}) collective-permute-start(f32[40,896]{1,0:T(8,128)S(1)} %shard_map.114.own_ref), channel_id=1, source_target_pairs={{0,1},{1,0},{2,3},{3,2},{4,5},{5,4},{6,7},{7,6},{8,9},{9,8},{10,11... | collective-permute-start | bytes 430088 | tf_op jit(solution)/shard_map/ppermute | solution.py:22
  15.8 4.9 %collective-permute-start.3 = (bf16[32,896]{1,0:T(8,128)(2,1)S(1)}, bf16[32,896]{1,0:T(8,128)(2,1)S(1)}, u32[]{:S(2)}, u32[]{:S(2)}) collective-permute-start(bf16[32,896]{1,0:T(8,128)(2,1)S(1)} %get-tuple-element.30), channel_id=1, source_target_pairs={{0,7},{1,6},{2,5},{3,4},{4,3},{5,2},{6,1},{7,0},{8,15},{9,14},{10,... | collective-permute-start | bytes 172040 | tf_op jit(solution)/shard_map/ppermute | solution.py:22
  18.1 3.8 %collective-permute-start.4 = (bf16[32,896]{1,0:T(8,128)(2,1)S(1)}, bf16[32,896]{1,0:T(8,128)(2,1)S(1)}, u32[]{:S(2)}, u32[]{:S(2)}) collective-permute-start(bf16[32,896]{1,0:T(8,128)(2,1)S(1)} %get-tuple-element.31), channel_id=1, source_target_pairs={{0,5},{1,4},{2,7},{3,6},{4,1},{5,0},{6,3},{7,2},{8,13},{9,12},{10,... | collective-permute-start | bytes 172040 | tf_op jit(solution)/shard_map/ppermute | solution.py:22
  18.6 3.9 %collective-permute-start.5 = (bf16[32,896]{1,0:T(8,128)(2,1)S(1)}, bf16[32,896]{1,0:T(8,128)(2,1)S(1)}, u32[]{:S(2)}, u32[]{:S(2)}) collective-permute-start(bf16[32,896]{1,0:T(8,128)(2,1)S(1)} %get-tuple-element.32), channel_id=1, source_target_pairs={{0,3},{1,2},{2,1},{3,0},{4,7},{5,6},{6,5},{7,4},{8,11},{9,10},{10,... | collective-permute-start | bytes 172040 | tf_op jit(solution)/shard_map/ppermute | solution.py:22
  22.4 5.8 %copy-start.1 = (s32[768,1024]{1,0:T(8,128)S(1)}, s32[768,1024]{1,0:T(8,128)}, u32[]{:S(2)}) copy-start(s32[768,1024]{1,0:T(8,128)} %dose_ref.1) | copy-start | bytes 9437188
  22.4 5.8 %copy-start.3 = (f32[768,16]{0,1:T(8,128)S(1)}, f32[768,16]{0,1:T(8,128)}, u32[]{:S(2)}) copy-start(f32[768,16]{0,1:T(8,128)} %param.13) | copy-start | bytes 147460
  22.4 5.8 %copy-start.5 = (s32[1,768]{1,0:T(1,128)S(1)}, s32[1,768]{1,0:T(1,128)}, u32[]{:S(2)}) copy-start(s32[1,768]{1,0:T(1,128)} %order_ref.1) | copy-start | bytes 9220
  22.4 9.0 %copy-start.4 = (f32[768,16]{0,1:T(8,128)S(1)}, f32[768,16]{0,1:T(8,128)}, u32[]{:S(2)}) copy-start(f32[768,16]{0,1:T(8,128)} %param.14) | copy-start | bytes 147460
  22.4 9.0 %copy-start.6 = (f32[16]{0:T(128)S(1)}, f32[16]{0:T(128)}, u32[]{:S(2)}) copy-start(f32[16]{0:T(128)} %param.12) | copy-start | bytes 196
  23.9 5.8 %collective-permute-start.6 = (bf16[16,896]{1,0:T(8,128)(2,1)S(1)}, bf16[16,896]{1,0:T(8,128)(2,1)S(1)}, u32[]{:S(2)}, u32[]{:S(2)}) collective-permute-start(bf16[16,896]{1,0:T(8,128)(2,1)S(1)} %get-tuple-element.34), channel_id=1, source_target_pairs={{0,24},{8,16},{16,8},{24,0},{1,25},{9,17},{17,9},{25,1},{2,26},{10... | collective-permute-start | bytes 86024 | tf_op jit(solution)/shard_map/ppermute | solution.py:22
  26.7 4.8 %collective-permute-start.7 = (bf16[16,896]{1,0:T(8,128)(2,1)S(1)}, bf16[16,896]{1,0:T(8,128)(2,1)S(1)}, u32[]{:S(2)}, u32[]{:S(2)}) collective-permute-start(bf16[16,896]{1,0:T(8,128)(2,1)S(1)} %get-tuple-element.35), channel_id=1, source_target_pairs={{0,16},{8,24},{16,0},{24,8},{1,17},{9,25},{17,1},{25,9},{2,18},{10... | collective-permute-start | bytes 86024 | tf_op jit(solution)/shard_map/ppermute | solution.py:22
  26.7 4.8 %collective-permute-start.8 = (bf16[16,896]{1,0:T(8,128)(2,1)S(1)}, bf16[16,896]{1,0:T(8,128)(2,1)S(1)}, u32[]{:S(2)}, u32[]{:S(2)}) collective-permute-start(bf16[16,896]{1,0:T(8,128)(2,1)S(1)} %get-tuple-element.36), channel_id=1, source_target_pairs={{0,8},{8,0},{16,24},{24,16},{1,9},{9,1},{17,25},{25,17},{2,10},{10... | collective-permute-start | bytes 86024 | tf_op jit(solution)/shard_map/ppermute | solution.py:22
  32.3 11.0 %all-to-all-start = ((f32[32,1,640]{2,1,0:T(1,128)}), f32[32,1,640]{2,1,0:T(1,128)S(1)}, u32[]{:S(2)}, u32[]{:S(2)}) async-start(f32[32,1,640]{2,1,0:T(1,128)} %get-tuple-element.39), calls=%async_computation | async-start | bytes 163840 | tf_op jit(solution)/shard_map/all_to_all | solution.py:450

commit v13 on v12

--- a/solution.py
+++ b/solution.py
@@ -116,12 +116,16 @@
         w[0:16, i * own : (i + 1) * own] = pair_ref[16 * i : 16 * i + 16]
 
 
+def rows_of(coded, called):
+    counts = jnp.concatenate([coded[16:17], called[16:17], jnp.zeros((6, coded.shape[1]), F32)], axis=0)
+    return jnp.concatenate([coded[0:16], called[0:16], counts], axis=0)
+
+
 def product(coded_ref, called_ref, first, rows, samples, w):
     part = pl.ds(first, rows)
     coded = lax.dot_general(w[...], coded_ref[part, samples], NT, preferred_element_type=F32)
     called = lax.dot_general(w[...], called_ref[part, samples], NT, preferred_element_type=F32)
-    counts = jnp.concatenate([coded[16:17], called[16:17], jnp.zeros((6, rows), F32)], axis=0)
-    return jnp.concatenate([coded[0:16], called[0:16], counts], axis=0)
+    return rows_of(coded, called)
 
 
 def pair_samples(pair, own):
@@ -134,37 +138,52 @@
     copies = row_copies(gen_hbm, gbuf, first, LANES, sems)
     for copy in copies:
         copy.start()
-    samples = pair_samples(lax.axis_index("var") // 2, own)
     weights(pair_ref, w)
     rows, shard = call_ref.shape
+    chunk = 2 * LANES
+    depth = 2 * LANES
+    start = pl.multiple_of((lax.axis_index("var") // 2) * 2 * own, LANES)
 
     def convert(place):
-        here = pl.ds(place, LANES)
-        gen = first_ref.at[here] if place < first else gbuf.at[pl.ds(place - first, LANES)]
-        call, coded, called = call_ref.at[here], coded_ref.at[here], called_ref.at[here]
-
-        def store(block, value, mask):
-            coded[block] = value
-            called[block] = mask
-
         held = None
-        for block in blocks(LANES, shard):
-            mask = call[block].astype(F32).astype(BF16)
-            value = gen[block] if place < first else gen[block].astype(F32).astype(BF16)
-            if held:
-                store(*held)
-            held = (block, value * mask, mask)
-        store(*held)
-
-    chunk = 2 * LANES
-    for place in range(0, rows + chunk, chunk):
-        for part in range(place, min(place + chunk, rows), LANES):
+        for part in range(place, place + chunk, LANES):
+            here = pl.ds(part, LANES)
             if part >= first:
                 copies[(part - first) // LANES].wait()
-            convert(part)
+            gen = first_ref.at[here] if part < first else gbuf.at[pl.ds(part - first, LANES)]
+            call, coded, called = call_ref.at[here], coded_ref.at[here], called_ref.at[here]
+            for block in blocks(LANES, shard):
+                mask = call[block].astype(F32).astype(BF16)
+                value = gen[block] if part < first else gen[block].astype(F32).astype(BF16)
+                if held:
+                    held[0][held[2]], held[1][held[2]] = held[3], held[4]
+                held = (coded, called, block, value * mask, mask)
+                yield
+        held[0][held[2]], held[1][held[2]] = held[3], held[4]
+
+    def multiply(place):
+        part = pl.ds(place, chunk)
+        coded = called = jnp.zeros((w.shape[0], chunk), F32)
+        for at in range(0, 2 * own, depth):
+            here = pl.ds(pl.multiple_of(start + at, LANES), depth)
+            piece = w[:, at : at + depth]
+            coded = coded + lax.dot_general(piece, coded_ref[part, here], NT, preferred_element_type=F32)
+            yield
+            called = called + lax.dot_general(piece, called_ref[part, here], NT, preferred_element_type=F32)
+            yield
+        out_ref[:, place : place + chunk] = rows_of(coded, called)
+
+    for place in range(0, rows + chunk, chunk):
+        steps = convert(place) if place < rows else iter(())
+        n_steps = chunk // 16 * (shard // BLOCK)
         if place:
-            before = place - chunk
-            out_ref[:, before:place] = product(coded_ref, called_ref, before, chunk, samples, w)
+            products = multiply(place - chunk)
+            n_products = 2 * (2 * own // depth)
+            for _ in products:
+                for _ in range(-(-n_steps // n_products)):
+                    next(steps, None)
+        for _ in steps:
+            pass
 
 
 def forward_kernel(pair_ref, coded_ref, called_ref, half_ref, sums_ref, out_ref, w):

time: 44.3 us -> 44.5 us (level)
  Pallas kernels: 12.4 us -> 12.9 us
    pallas_call x10, Pallas kernels: 12.4 us -> 12.9 us  [call(): pl.pallas_call(kernel, out_shape=[jax.ShapeDtypeStruct(*o) if len(o) == 2...]
  transfers between devices with their start and end apart: 10 -> 10, of which waited for: 7 -> 7; matrix products, arithmetic and copies ran while one was open for 0% -> 0% of each run, Pallas kernels for 18% -> 19%
where the time goes in v13:
time: 44.5 us; the launch traced here: 44.3 us
  starting transfers between devices  16.5 us (37%)
  waiting for transfers between devices  14 us (31%)
  Pallas kernels  12.9 us (29%)
  between operations  0.74 us (2%)
    ppermute x9, starting transfers between devices, swap(): return lax.ppermute(values, axis, [(i, i ^ distance) for i in range(size)])  13.3 us
    pallas_call x10, Pallas kernels, call(): pl.pallas_call(kernel, out_shape=[jax.ShapeDtypeStruct(*o) if len(o) == 2...  12.9 us
    ppermute x9, waiting for transfers between devices, swap(): return lax.ppermute(values, axis, [(i, i ^ distance) for i in range(size)])  7.18 us
    all_to_all x1, waiting for transfers between devices, body(): lax.all_to_all(outgoing, ('var', 'samp'), split_axis=0, concat_axis=0)  6.86 us
    all_to_all x1, starting transfers between devices, body(): lax.all_to_all(outgoing, ('var', 'samp'), split_axis=0, concat_axis=0)  3.29 us
  transfers between devices with their start and end apart: 10, of which 7 were waited for; matrix products, arithmetic and copies ran while one was open for 0% of the time, Pallas kernels for 19%

profile of v13, /device:TPU:0, one launch (start us, length us, event | category | flops | bytes accessed | tf_op | source)
XLA Modules:
  0.0 44.3 jit_solution(2044722314427982385)
XLA Ops:
  0.6 3.1 %collective-permute-start = (f32[16,768]{1,0:T(8,128)}, f32[16,768]{1,0:T(8,128)S(1)}, u32[]{:S(2)}, u32[]{:S(2)}) collective-permute-start(f32[16,768]{1,0:T(8,128)} %bitcast.8), channel_id=1, source_target_pairs={{0,8},{8,0},{16,24},{24,16},{1,9},{9,1},{17,25},{25,17},{2,10},{10... | collective-permute-start | bytes 147464 | tf_op jit(solution)/shard_map/ppermute | solution.py:22
  3.7 3.2 %shard_map.112 = (bf16[512,3072]{1,0:T(8,128)(2,1)S(1)}, f32[8,128]{1,0:T(8,128)S(1)}) custom-call(f32[16,768]{1,0:T(8,128)} %bitcast.15, f32[16,768]{1,0:T(8,128)} %bitcast.9, f32[16,768]{1,0:T(8,128)} %bitcast.18, s32[768,3072]{1,0:T(8,128)} %gen_hbm.3), custom_call_target="tpu_custom_call" | custom-call | bytes 6291456 | tf_op jit(solution)/shard_map/pallas_call | solution.py:361
  6.9 0.0 collective-permute-done.other_ref
  6.9 2.7 %collective-permute-start.1 = (bf16[32,768]{1,0:T(8,128)(2,1)S(1)}, bf16[32,768]{1,0:T(8,128)(2,1)S(1)}, u32[]{:S(2)}, u32[]{:S(2)}) collective-permute-start(bf16[32,768]{1,0:T(8,128)(2,1)S(1)} %shard_map.111.pair_ref), channel_id=1, source_target_pairs={{0,16},{8,24},{16,0},{24,8},{1,17},{9,25},{17,1},{25,9},{2,18},{10... | collective-permute-start | bytes 147464 | tf_op jit(solution)/shard_map/ppermute | solution.py:22
  9.6 3.7 %shard_map.113 = (bf16[768,3072]{1,0:T(8,128)(2,1)S(1)}, bf16[768,3072]{1,0:T(8,128)(2,1)S(1)}, f32[40,768]{1,0:T(8,128)S(1)}) custom-call(bf16[32,768]{1,0:T(8,128)(2,1)S(1)} %shard_map.111.pair_ref, bf16[512,3072]{1,0:T(8,128)(2,1)S(1)} %get-tuple-element.24.first_ref, s32[768,3072]{1,0:T(8,128)S(1)} %copy-done, s32[768,3072]{1,0:T(8,128)} %gen_hbm.3), custom_call_target="tpu_custom_call" | custom-call | flops 1207959552 | bytes 9437184 | tf_op jit(solution)/shard_map/pallas_call | solution.py:361
  13.4 0.0 collective-permute-done.1.pair_ref
  13.4 1.5 %shard_map.114.own_ref = f32[40,896]{1,0:T(8,128)S(1)} custom-call(bf16[32,768]{1,0:T(8,128)(2,1)S(1)} %collective-permute-done.1.pair_ref, bf16[768,3072]{1,0:T(8,128)(2,1)S(1)} %get-tuple-element.25.coded_ref, bf16[768,3072]{1,0:T(8,128)(2,1)S(1)} %get-tuple-element.26.called_ref, f32[40,768]{1,0:T(8,128)S(1)} %get-tuple-element.27.half_ref, ...), custom_call_target="tpu_custom_call" | custom-call | flops 1207959552 | bytes 4718592 | tf_op jit(solution)/shard_map/pallas_call | solution.py:361
  14.9 0.1 collective-permute-start.2
  15.0 1.4 %collective-permute-done.2.other_ref = f32[40,896]{1,0:T(8,128)S(1)} collective-permute-done((f32[40,896]{1,0:T(8,128)S(1)}, f32[40,896]{1,0:T(8,128)S(1)}, u32[]{:S(2)}, u32[]{:S(2)}) %collective-permute-start.2) | collective-permute-done | bytes 143392 | tf_op jit(solution)/shard_map/ppermute | solution.py:22
  16.4 2.3 %collective-permute-start.3 = (bf16[32,896]{1,0:T(8,128)(2,1)S(1)}, bf16[32,896]{1,0:T(8,128)(2,1)S(1)}, u32[]{:S(2)}, u32[]{:S(2)}) collective-permute-start(bf16[32,896]{1,0:T(8,128)(2,1)S(1)} %get-tuple-element.30), channel_id=1, source_target_pairs={{0,7},{1,6},{2,5},{3,4},{4,3},{5,2},{6,1},{7,0},{8,15},{9,14},{10,... | collective-permute-start | bytes 172040 | tf_op jit(solution)/shard_map/ppermute | solution.py:22
  18.6 0.5 %collective-permute-start.4 = (bf16[32,896]{1,0:T(8,128)(2,1)S(1)}, bf16[32,896]{1,0:T(8,128)(2,1)S(1)}, u32[]{:S(2)}, u32[]{:S(2)}) collective-permute-start(bf16[32,896]{1,0:T(8,128)(2,1)S(1)} %get-tuple-element.31), channel_id=1, source_target_pairs={{0,5},{1,4},{2,7},{3,6},{4,1},{5,0},{6,3},{7,2},{8,13},{9,12},{10,... | collective-permute-start | bytes 172040 | tf_op jit(solution)/shard_map/ppermute | solution.py:22
  19.1 0.3 collective-permute-start.5
  19.4 1.8 %collective-permute-done.3.rest_0_ = bf16[32,896]{1,0:T(8,128)(2,1)S(1)} collective-permute-done((bf16[32,896]{1,0:T(8,128)(2,1)S(1)}, bf16[32,896]{1,0:T(8,128)(2,1)S(1)}, u32[]{:S(2)}, u32[]{:S(2)}) %collective-permute-start.3) | collective-permute-done | bytes 57376 | tf_op jit(solution)/shard_map/ppermute | solution.py:22
  21.2 1.2 %collective-permute-done.4.rest_1_ = bf16[32,896]{1,0:T(8,128)(2,1)S(1)} collective-permute-done((bf16[32,896]{1,0:T(8,128)(2,1)S(1)}, bf16[32,896]{1,0:T(8,128)(2,1)S(1)}, u32[]{:S(2)}, u32[]{:S(2)}) %collective-permute-start.4) | collective-permute-done | bytes 57376 | tf_op jit(solution)/shard_map/ppermute | solution.py:22
  22.4 0.6 %collective-permute-done.5.rest_2_ = bf16[32,896]{1,0:T(8,128)(2,1)S(1)} collective-permute-done((bf16[32,896]{1,0:T(8,128)(2,1)S(1)}, bf16[32,896]{1,0:T(8,128)(2,1)S(1)}, u32[]{:S(2)}, u32[]{:S(2)}) %collective-permute-start.5) | collective-permute-done | bytes 57376 | tf_op jit(solution)/shard_map/ppermute | solution.py:22
  23.0 0.0 copy-start.6
  23.0 1.4 %shard_map.116 = (f32[16,896]{1,0:T(8,128)S(1)}, bf16[16,896]{1,0:T(8,128)(2,1)S(1)}, bf16[16,896]{1,0:T(8,128)(2,1)S(1)}, bf16[16,896]{1,0:T(8,128)(2,1)S(1)}) custom-call(f32[40,896]{1,0:T(8,128)S(1)} %get-tuple-element.29.total_ref.after_ref, bf16[768,3072]{1,0:T(8,128)(2,1)S(1)} %get-tuple-element.25.coded_ref, ...), custom_call_target="tpu_custom_call" | custom-call | flops 2415919104 | bytes 9437184 | tf_op jit(solution)/shard_map/pallas_call | solution.py:361
  24.4 2.3 %collective-permute-start.6 = (bf16[16,896]{1,0:T(8,128)(2,1)S(1)}, bf16[16,896]{1,0:T(8,128)(2,1)S(1)}, u32[]{:S(2)}, u32[]{:S(2)}) collective-permute-start(bf16[16,896]{1,0:T(8,128)(2,1)S(1)} %get-tuple-element.34), channel_id=1, source_target_pairs={{0,24},{8,16},{16,8},{24,0},{1,25},{9,17},{17,9},{25,1},{2,26},{10... | collective-permute-start | bytes 86024 | tf_op jit(solution)/shard_map/ppermute | solution.py:22
  26.7 0.3 collective-permute-start.7
  26.9 1.8 %collective-permute-start.8 = (bf16[16,896]{1,0:T(8,128)(2,1)S(1)}, bf16[16,896]{1,0:T(8,128)(2,1)S(1)}, u32[]{:S(2)}, u32[]{:S(2)}) collective-permute-start(bf16[16,896]{1,0:T(8,128)(2,1)S(1)} %get-tuple-element.36), channel_id=1, source_target_pairs={{0,8},{8,0},{16,24},{24,16},{1,9},{9,1},{17,25},{25,17},{2,10},{10... | collective-permute-start | bytes 86024 | tf_op jit(solution)/shard_map/ppermute | solution.py:22
  28.8 0.0 copy-done.1
  28.8 0.0 copy-done.5
  28.8 0.6 %shard_map.118.cross_ref = f32[40,1024]{1,0:T(8,128)S(1)} custom-call(s32[1,768]{1,0:T(1,128)S(1)} %copy-done.5, f32[16,768]{1,0:T(8,128)S(1)} %bitcast.16, f32[16,768]{1,0:T(8,128)S(1)} %bitcast.11, s32[768,1024]{1,0:T(8,128)S(1)} %copy-done.1, f32[40,896]{1,0:T(8,128)S(1)} %get-tuple-element.29.total_ref.after_ref), custom_call_target="tpu_custom_call" | custom-call | flops 220200960 | bytes 3145728 | tf_op jit(solution)/shard_map/pallas_call | solution.py:361
  29.4 0.6 %collective-permute-done.6.rest_1_ = bf16[16,896]{1,0:T(8,128)(2,1)S(1)} collective-permute-done((bf16[16,896]{1,0:T(8,128)(2,1)S(1)}, bf16[16,896]{1,0:T(8,128)(2,1)S(1)}, u32[]{:S(2)}, u32[]{:S(2)}) %collective-permute-start.6) | collective-permute-done | bytes 28704 | tf_op jit(solution)/shard_map/ppermute | solution.py:22
  30.1 1.6 %collective-permute-done.7.rest_2_ = bf16[16,896]{1,0:T(8,128)(2,1)S(1)} collective-permute-done((bf16[16,896]{1,0:T(8,128)(2,1)S(1)}, bf16[16,896]{1,0:T(8,128)(2,1)S(1)}, u32[]{:S(2)}, u32[]{:S(2)}) %collective-permute-start.7) | collective-permute-done | bytes 28704 | tf_op jit(solution)/shard_map/ppermute | solution.py:22
  31.7 0.0 collective-permute-done.8.rest_3_
  31.7 0.0 copy-done.4
  31.7 0.9 %shard_map.119 = (f32[32,1,640]{2,1,0:T(1,128)}, f32[16,768]{1,0:T(8,128)S(1)}) custom-call(f32[1,16]{1,0:T(1,128)S(1)} %bitcast.21, f32[16,768]{1,0:T(8,128)S(1)} %bitcast.12, f32[16,768]{1,0:T(8,128)S(1)} %bitcast.19, f32[40,1024]{1,0:T(8,128)S(1)} %shard_map.118.cross_ref, f32[16,896]{1,0:T(8,128)S(1)} %get-tuple-element.33.rest_0_, ...), custom_call_target="tpu_custom_call" | custom-call | bytes 81920 | tf_op jit(solution)/shard_map/pallas_call | solution.py:361
  32.6 3.3 %all-to-all-start = ((f32[32,1,640]{2,1,0:T(1,128)}), f32[32,1,640]{2,1,0:T(1,128)S(1)}, u32[]{:S(2)}, u32[]{:S(2)}) async-start(f32[32,1,640]{2,1,0:T(1,128)} %get-tuple-element.39), calls=%async_computation | async-start | bytes 163840 | tf_op jit(solution)/shard_map/all_to_all | solution.py:469
  35.9 0.7 %shard_map.117 = (f32[16,768]{1,0:T(8,128)}, f32[16,768]{1,0:T(8,128)}, f32[16,128]{1,0:T(8,128)S(1)}) custom-call(f32[1,16]{1,0:T(1,128)S(1)} %bitcast.22, f32[16,768]{1,0:T(8,128)S(1)} %bitcast.13, f32[16,768]{1,0:T(8,128)S(1)} %bitcast.20, f32[16,768]{1,0:T(8,128)S(1)} %bitcast.17, f32[16,896]{1,0:T(8,128)S(1)} %get-tuple-element.33.rest_0_, ...), custom_call_target="tpu_custom_call" | custom-call | bytes 1048576 | tf_op jit(solution)/shard_map/pallas_call | solution.py:361
  36.6 6.9 %all-to-all-done.came_ref = f32[32,1,640]{2,1,0:T(1,128)S(1)} async-done(((f32[32,1,640]{2,1,0:T(1,128)}), f32[32,1,640]{2,1,0:T(1,128)S(1)}, u32[]{:S(2)}, u32[]{:S(2)}) %all-to-all-start) | async-done | bytes 81952 | tf_op jit(solution)/shard_map/all_to_all | solution.py:469
  43.5 0.8 %shard_map.120 = (f32[16,768]{1,0:T(8,128)}, f32[16,32]{1,0:T(8,128)}) custom-call(f32[32,1,640]{2,1,0:T(1,128)S(1)} %all-to-all-done.came_ref, f32[16,128]{1,0:T(8,128)S(1)} %get-tuple-element.40.stats_ref, f32[16,768]{1,0:T(8,128)S(1)} %get-tuple-element.41.res_ref, f32[16,768]{1,0:T(8,128)S(1)} %bitcast.14), custom_call_target="tpu_custom_call" | custom-call | tf_op jit(solution)/shard_map/pallas_call | solution.py:361
  (12 shorter events, 0.1 us)
Async XLA Ops:
  0.6 6.3 %collective-permute-start = (f32[16,768]{1,0:T(8,128)}, f32[16,768]{1,0:T(8,128)S(1)}, u32[]{:S(2)}, u32[]{:S(2)}) collective-permute-start(f32[16,768]{1,0:T(8,128)} %bitcast.8), channel_id=1, source_target_pairs={{0,8},{8,0},{16,24},{24,16},{1,9},{9,1},{17,25},{25,17},{2,10},{10... | collective-permute-start | bytes 147464 | tf_op jit(solution)/shard_map/ppermute | solution.py:22
  3.7 3.2 %copy-start.2 = (f32[768,16]{0,1:T(8,128)S(1)}, f32[768,16]{0,1:T(8,128)}, u32[]{:S(2)}) copy-start(f32[768,16]{0,1:T(8,128)} %param.15) | copy-start | bytes 147460
  3.7 5.9 %copy-start = (s32[768,3072]{1,0:T(8,128)S(1)}, s32[768,3072]{1,0:T(8,128)}, u32[]{:S(2)}) copy-start(s32[768,3072]{1,0:T(8,128)} %call_ref.1) | copy-start | bytes 28311556
  6.9 6.4 %collective-permute-start.1 = (bf16[32,768]{1,0:T(8,128)(2,1)S(1)}, bf16[32,768]{1,0:T(8,128)(2,1)S(1)}, u32[]{:S(2)}, u32[]{:S(2)}) collective-permute-start(bf16[32,768]{1,0:T(8,128)(2,1)S(1)} %shard_map.111.pair_ref), channel_id=1, source_target_pairs={{0,16},{8,24},{16,0},{24,8},{1,17},{9,25},{17,1},{25,9},{2,18},{10... | collective-permute-start | bytes 147464 | tf_op jit(solution)/shard_map/ppermute | solution.py:22
  14.9 1.4 %collective-permute-start.2 = (f32[40,896]{1,0:T(8,128)S(1)}, f32[40,896]{1,0:T(8,128)S(1)}, u32[]{:S(2)}, u32[]{:S(2)}) collective-permute-start(f32[40,896]{1,0:T(8,128)S(1)} %shard_map.114.own_ref), channel_id=1, source_target_pairs={{0,1},{1,0},{2,3},{3,2},{4,5},{5,4},{6,7},{7,6},{8,9},{9,8},{10,11... | collective-permute-start | bytes 430088 | tf_op jit(solution)/shard_map/ppermute | solution.py:22
  16.4 4.9 %collective-permute-start.3 = (bf16[32,896]{1,0:T(8,128)(2,1)S(1)}, bf16[32,896]{1,0:T(8,128)(2,1)S(1)}, u32[]{:S(2)}, u32[]{:S(2)}) collective-permute-start(bf16[32,896]{1,0:T(8,128)(2,1)S(1)} %get-tuple-element.30), channel_id=1, source_target_pairs={{0,7},{1,6},{2,5},{3,4},{4,3},{5,2},{6,1},{7,0},{8,15},{9,14},{10,... | collective-permute-start | bytes 172040 | tf_op jit(solution)/shard_map/ppermute | solution.py:22
  18.6 3.8 %collective-permute-start.4 = (bf16[32,896]{1,0:T(8,128)(2,1)S(1)}, bf16[32,896]{1,0:T(8,128)(2,1)S(1)}, u32[]{:S(2)}, u32[]{:S(2)}) collective-permute-start(bf16[32,896]{1,0:T(8,128)(2,1)S(1)} %get-tuple-element.31), channel_id=1, source_target_pairs={{0,5},{1,4},{2,7},{3,6},{4,1},{5,0},{6,3},{7,2},{8,13},{9,12},{10,... | collective-permute-start | bytes 172040 | tf_op jit(solution)/shard_map/ppermute | solution.py:22
  19.1 3.9 %collective-permute-start.5 = (bf16[32,896]{1,0:T(8,128)(2,1)S(1)}, bf16[32,896]{1,0:T(8,128)(2,1)S(1)}, u32[]{:S(2)}, u32[]{:S(2)}) collective-permute-start(bf16[32,896]{1,0:T(8,128)(2,1)S(1)} %get-tuple-element.32), channel_id=1, source_target_pairs={{0,3},{1,2},{2,1},{3,0},{4,7},{5,6},{6,5},{7,4},{8,11},{9,10},{10,... | collective-permute-start | bytes 172040 | tf_op jit(solution)/shard_map/ppermute | solution.py:22
  23.0 5.8 %copy-start.1 = (s32[768,1024]{1,0:T(8,128)S(1)}, s32[768,1024]{1,0:T(8,128)}, u32[]{:S(2)}) copy-start(s32[768,1024]{1,0:T(8,128)} %dose_ref.1) | copy-start | bytes 9437188
  23.0 5.8 %copy-start.3 = (f32[768,16]{0,1:T(8,128)S(1)}, f32[768,16]{0,1:T(8,128)}, u32[]{:S(2)}) copy-start(f32[768,16]{0,1:T(8,128)} %param.13) | copy-start | bytes 147460
  23.0 5.8 %copy-start.5 = (s32[1,768]{1,0:T(1,128)S(1)}, s32[1,768]{1,0:T(1,128)}, u32[]{:S(2)}) copy-start(s32[1,768]{1,0:T(1,128)} %order_ref.1) | copy-start | bytes 9220
  23.0 8.7 %copy-start.4 = (f32[768,16]{0,1:T(8,128)S(1)}, f32[768,16]{0,1:T(8,128)}, u32[]{:S(2)}) copy-start(f32[768,16]{0,1:T(8,128)} %param.14) | copy-start | bytes 147460
  23.0 8.7 %copy-start.6 = (f32[16]{0:T(128)S(1)}, f32[16]{0:T(128)}, u32[]{:S(2)}) copy-start(f32[16]{0:T(128)} %param.12) | copy-start | bytes 196
  24.4 5.7 %collective-permute-start.6 = (bf16[16,896]{1,0:T(8,128)(2,1)S(1)}, bf16[16,896]{1,0:T(8,128)(2,1)S(1)}, u32[]{:S(2)}, u32[]{:S(2)}) collective-permute-start(bf16[16,896]{1,0:T(8,128)(2,1)S(1)} %get-tuple-element.34), channel_id=1, source_target_pairs={{0,24},{8,16},{16,8},{24,0},{1,25},{9,17},{17,9},{25,1},{2,26},{10... | collective-permute-start | bytes 86024 | tf_op jit(solution)/shard_map/ppermute | solution.py:22
  26.7 5.0 %collective-permute-start.7 = (bf16[16,896]{1,0:T(8,128)(2,1)S(1)}, bf16[16,896]{1,0:T(8,128)(2,1)S(1)}, u32[]{:S(2)}, u32[]{:S(2)}) collective-permute-start(bf16[16,896]{1,0:T(8,128)(2,1)S(1)} %get-tuple-element.35), channel_id=1, source_target_pairs={{0,16},{8,24},{16,0},{24,8},{1,17},{9,25},{17,1},{25,9},{2,18},{10... | collective-permute-start | bytes 86024 | tf_op jit(solution)/shard_map/ppermute | solution.py:22
  26.9 4.7 %collective-permute-start.8 = (bf16[16,896]{1,0:T(8,128)(2,1)S(1)}, bf16[16,896]{1,0:T(8,128)(2,1)S(1)}, u32[]{:S(2)}, u32[]{:S(2)}) collective-permute-start(bf16[16,896]{1,0:T(8,128)(2,1)S(1)} %get-tuple-element.36), channel_id=1, source_target_pairs={{0,8},{8,0},{16,24},{24,16},{1,9},{9,1},{17,25},{25,17},{2,10},{10... | collective-permute-start | bytes 86024 | tf_op jit(solution)/shard_map/ppermute | solution.py:22
  32.6 10.9 %all-to-all-start = ((f32[32,1,640]{2,1,0:T(1,128)}), f32[32,1,640]{2,1,0:T(1,128)S(1)}, u32[]{:S(2)}, u32[]{:S(2)}) async-start(f32[32,1,640]{2,1,0:T(1,128)} %get-tuple-element.39), calls=%async_computation | async-start | bytes 163840 | tf_op jit(solution)/shard_map/all_to_all | solution.py:469

commit v14 on v12

--- a/solution.py
+++ b/solution.py
@@ -61,6 +61,7 @@
 
 
 BLOCK = 1024
+CHUNK = 256
 
 
 def blocks(rows, samples):
@@ -76,15 +77,15 @@
     ]
 
 
-def genotype_kernel(chunk, sol_hbm, dir_hbm, res_hbm, gen_hbm, out_ref, sums_ref,
-                    sol_ref, dir_ref, res_ref, gbuf, small_sems, sems):
+def called_kernel(chunk, sol_hbm, dir_hbm, res_hbm, call_hbm, out_ref, sums_ref,
+                  sol_ref, dir_ref, res_ref, cbuf, small_sems, sems):
     small = [
         pltpu.make_async_copy(source, target, small_sems.at[i])
         for i, (source, target) in enumerate(((sol_hbm, sol_ref), (dir_hbm, dir_ref), (res_hbm, res_ref)))
     ]
     for copy in small:
         copy.start()
-    parts = row_copies(gen_hbm, gbuf, 0, chunk, sems)
+    parts = row_copies(call_hbm, cbuf, 0, chunk, sems)
     for copy in parts:
         copy.start()
     for copy in small:
@@ -95,7 +96,7 @@
     sums_ref[...] = jnp.broadcast_to(row, sums_ref.shape)
     for i, copy in enumerate(parts):
         copy.wait()
-        source, target = gbuf.at[pl.ds(i * chunk, chunk)], out_ref.at[pl.ds(i * chunk, chunk)]
+        source, target = cbuf.at[pl.ds(i * chunk, chunk)], out_ref.at[pl.ds(i * chunk, chunk)]
         for here in blocks(chunk, source.shape[1]):
             target[here] = source[here].astype(F32).astype(BF16)
 
@@ -116,11 +117,18 @@
         w[0:16, i * own : (i + 1) * own] = pair_ref[16 * i : 16 * i + 16]
 
 
-def product(coded_ref, called_ref, first, rows, samples, w):
-    part = pl.ds(first, rows)
-    coded = lax.dot_general(w[...], coded_ref[part, samples], NT, preferred_element_type=F32)
-    called = lax.dot_general(w[...], called_ref[part, samples], NT, preferred_element_type=F32)
-    counts = jnp.concatenate([coded[16:17], called[16:17], jnp.zeros((6, rows), F32)], axis=0)
+def product(w, matrix, first, rows, samples):
+    return lax.dot_general(w[...], matrix[pl.ds(first, rows), samples], NT, preferred_element_type=F32)
+
+
+def split_product(w, head, tail, first, rows, samples):
+    if first < head.shape[0]:
+        return product(w, head, first, rows, samples)
+    return product(w, tail, first - head.shape[0], rows, samples)
+
+
+def rows_of(coded, called):
+    counts = jnp.concatenate([coded[16:17], called[16:17], jnp.zeros((6, coded.shape[1]), F32)], axis=0)
     return jnp.concatenate([coded[0:16], called[0:16], counts], axis=0)
 
 
@@ -128,53 +136,70 @@
     return pl.ds(pl.multiple_of(pair * 2 * own, LANES), 2 * own)
 
 
-def mask_kernel(pair_ref, first_ref, call_ref, gen_hbm, coded_ref, called_ref, out_ref, gbuf, w, sems):
+def called_product_kernel(pair_ref, called_first, out_ref, w):
     own = pair_ref.shape[1]
-    first = first_ref.shape[0]
-    copies = row_copies(gen_hbm, gbuf, first, LANES, sems)
+    samples = pair_samples(lax.axis_index("var") // 2, own)
+    weights(pair_ref, w)
+    for place in range(0, called_first.shape[0], CHUNK):
+        out_ref[:, place : place + CHUNK] = product(w, called_first, place, CHUNK, samples)
+
+
+def mask_kernel(pair_ref, called_first, done_ref, gen_ref, call_hbm, coded_ref, called_ref, out_ref, cbuf, w, sems):
+    own = pair_ref.shape[1]
+    rows, shard = gen_ref.shape
+    first = called_first.shape[0]
+    copies = row_copies(call_hbm, cbuf, first, LANES, sems)
     for copy in copies:
         copy.start()
     samples = pair_samples(lax.axis_index("var") // 2, own)
     weights(pair_ref, w)
-    rows, shard = call_ref.shape
 
     def convert(place):
-        here = pl.ds(place, LANES)
-        gen = first_ref.at[here] if place < first else gbuf.at[pl.ds(place - first, LANES)]
-        call, coded, called = call_ref.at[here], coded_ref.at[here], called_ref.at[here]
+        here, after = pl.ds(place, LANES), place - first
+        gen, coded = gen_ref.at[here], coded_ref.at[here]
+        if after >= 0:
+            copies[after // LANES].wait()
+            call, called = cbuf.at[pl.ds(after, LANES)], called_ref.at[pl.ds(after, LANES)]
+        else:
+            mask_ref = called_first.at[here]
 
         def store(block, value, mask):
             coded[block] = value
-            called[block] = mask
+            if after >= 0:
+                called[block] = mask
 
         held = None
         for block in blocks(LANES, shard):
-            mask = call[block].astype(F32).astype(BF16)
-            value = gen[block] if place < first else gen[block].astype(F32).astype(BF16)
+            mask = call[block].astype(F32).astype(BF16) if after >= 0 else mask_ref[block]
+            value = gen[block].astype(F32).astype(BF16) * mask
             if held:
                 store(*held)
-            held = (block, value * mask, mask)
+            held = (block, value, mask)
         store(*held)
 
-    chunk = 2 * LANES
-    for place in range(0, rows + chunk, chunk):
-        for part in range(place, min(place + chunk, rows), LANES):
-            if part >= first:
-                copies[(part - first) // LANES].wait()
+    for place in range(0, rows + CHUNK, CHUNK):
+        for part in range(place, min(place + CHUNK, rows), LANES):
             convert(part)
         if place:
-            before = place - chunk
-            out_ref[:, before:place] = product(coded_ref, called_ref, before, chunk, samples, w)
-
-
-def forward_kernel(pair_ref, coded_ref, called_ref, half_ref, sums_ref, out_ref, w):
+            before = place - CHUNK
+            coded = product(w, coded_ref, before, CHUNK, samples)
+            if before < first:
+                called = done_ref[:, before:place]
+            else:
+                called = product(w, called_ref, before - first, CHUNK, samples)
+            out_ref[:, before:place] = rows_of(coded, called)
+
+
+def forward_kernel(pair_ref, coded_ref, called_first, called_ref, half_ref, sums_ref, out_ref, w):
     own = pair_ref.shape[1]
     rows = coded_ref.shape[0]
     samples = pair_samples((lax.axis_index("var") // 2) ^ 1, own)
     weights(pair_ref, w)
-    for place in range(0, rows, 2 * LANES):
-        here = slice(place, place + 2 * LANES)
-        out_ref[:, here] = half_ref[:, here] + product(coded_ref, called_ref, place, 2 * LANES, samples, w)
+    for place in range(0, rows, CHUNK):
+        here = slice(place, place + CHUNK)
+        coded = product(w, coded_ref, place, CHUNK, samples)
+        called = split_product(w, called_first, called_ref, place, CHUNK, samples)
+        out_ref[:, here] = half_ref[:, here] + rows_of(coded, called)
     out_ref[:, rows:] = jnp.zeros((out_ref.shape[0], LANES), F32)
     out_ref[0:8, rows:] = sums_ref[...]
 
@@ -213,7 +238,7 @@
     cross_ref[2 * rhs :] = cross[4 * rhs : 4 * rhs + 8]
 
 
-def back_kernel(variants, n_arrived, total_ref, coded_ref, called_ref, *rest):
+def back_kernel(variants, n_arrived, total_ref, coded_ref, called_first, called_ref, *rest):
     arrived, own_ref, messages = rest[:n_arrived], rest[n_arrived], rest[n_arrived + 1 :]
     var = lax.axis_index("var")
     rows = total_ref.shape[1] - LANES
@@ -248,7 +273,9 @@
     def term(p):
         part = pl.ds(pl.multiple_of(p * own, LANES), own)
         got = jnp.dot(scaled_a, coded_ref[:, part], preferred_element_type=F32)
-        got = got + jnp.dot(scaled_b, called_ref[:, part], preferred_element_type=F32)
+        first = called_first.shape[0]
+        got = got + jnp.dot(scaled_b[:, :first], called_first[:, part], preferred_element_type=F32)
+        got = got + jnp.dot(scaled_b[:, first:], called_ref[:, part], preferred_element_type=F32)
         return got / variants
 
     parts = [part.astype(F32) for part in thirds(sums)]
@@ -366,11 +393,11 @@
     matrix = lambda n: ((n, shard), BF16, pltpu.VMEM)
 
     neighbour = swap(dire, "var", 1)
-    coarse, sums = call(
-        functools.partial(genotype_kernel, chunk),
+    called_a, sums = call(
+        functools.partial(called_kernel, chunk),
         [matrix(first), ((8, LANES), F32)],
         [HBM] * 4,
-        (sol, dire, res, genotypes),
+        (sol, dire, res, called),
         scratch=[
             pltpu.VMEM((rhs, own), F32),
             pltpu.VMEM((rhs, own), F32),
@@ -385,11 +412,21 @@
     (pair,) = call(pair_kernel, [((2 * rhs, own), BF16)], [VMEM] * 2, (dire, neighbour), limit=4)
     pair_other = swap(pair, "var", 2)
     row_weights = pltpu.VMEM((2 * rhs, 2 * own), BF16)
+    (done,) = call(
+        called_product_kernel,
+        [((2 * rhs, first), F32)],
+        [VMEM] * 2,
+        (pair, called_a),
+        scratch=[row_weights],
+        limit=4,
+        flops=first * shard * 256,
+        moved=first * shard,
+    )
     coded, called_b, half = call(
         mask_kernel,
-        [matrix(rows), matrix(rows), ((2 * rhs + 8, rows), F32)],
-        [VMEM] * 3 + [HBM],
-        (pair, coarse, called, genotypes),
+        [matrix(rows), matrix(rows - first), ((2 * rhs + 8, rows), F32)],
+        [VMEM] * 4 + [HBM],
+        (pair, called_a, done, genotypes, called),
         scratch=[
             pltpu.VMEM((rows - first, shard), jnp.int32),
             row_weights,
@@ -402,8 +439,8 @@
     (part,) = call(
         forward_kernel,
         [((2 * rhs + 8, rows + LANES), F32)],
-        [VMEM] * 5,
-        (pair_other, coded, called_b, half, sums),
+        [VMEM] * 6,
+        (pair_other, coded, called_a, called_b, half, sums),
         scratch=[row_weights],
         flops=2 * rows * shard * 256,
         moved=2 * rows * shard,
@@ -432,8 +469,8 @@
     mine_back, *messages = call(
         functools.partial(back_kernel, variants, len(arrived)),
         [((rhs, wide), F32)] + [((rhs, wide), BF16)] * (n_var - 1),
-        [VMEM] * (3 + len(arrived)),
-        (total, coded, called_b, *arrived),
+        [VMEM] * (4 + len(arrived)),
+        (total, coded, called_a, called_b, *arrived),
         flops=4 * rows * shard * 256,
         moved=4 * rows * shard,
     )

time: 44.3 us -> 44.3 us (level)
  Pallas kernels: 12.4 us -> 12.9 us
  waiting for transfers between devices: 14.3 us -> 13.8 us
    ppermute x9, waiting for transfers between devices: 7.46 us -> 6.94 us  [swap(): return lax.ppermute(values, axis, [(i, i ^ distance) for i in range(size)])]
    pallas_call x10 -> x11, Pallas kernels: 12.4 us -> 12.9 us  [call(): pl.pallas_call(kernel, out_shape=[jax.ShapeDtypeStruct(*o) if len(o) == 2...]
  transfers between devices with their start and end apart: 10 -> 10, of which waited for: 7 -> 7; matrix products, arithmetic and copies ran while one was open for 0% -> 0% of each run, Pallas kernels for 18% -> 19%
where the time goes in v14:
time: 44.3 us; the launch traced here: 44.1 us
  starting transfers between devices  16.6 us (37%)
  waiting for transfers between devices  13.8 us (31%)
  Pallas kernels  12.9 us (29%)
  between operations  0.74 us (2%)
    ppermute x9, starting transfers between devices, swap(): return lax.ppermute(values, axis, [(i, i ^ distance) for i in range(size)])  13.3 us
    pallas_call x11, Pallas kernels, call(): pl.pallas_call(kernel, out_shape=[jax.ShapeDtypeStruct(*o) if len(o) == 2...  12.9 us
    ppermute x9, waiting for transfers between devices, swap(): return lax.ppermute(values, axis, [(i, i ^ distance) for i in range(size)])  6.94 us
    all_to_all x1, waiting for transfers between devices, body(): lax.all_to_all(outgoing, ('var', 'samp'), split_axis=0, concat_axis=0)  6.86 us
    all_to_all x1, starting transfers between devices, body(): lax.all_to_all(outgoing, ('var', 'samp'), split_axis=0, concat_axis=0)  3.34 us
  transfers between devices with their start and end apart: 10, of which 7 were waited for; matrix products, arithmetic and copies ran while one was open for 0% of the time, Pallas kernels for 19%

profile of v14, /device:TPU:0, one launch (start us, length us, event | category | flops | bytes accessed | tf_op | source)
XLA Modules:
  0.0 44.1 jit_solution(11857175954894124001)
XLA Ops:
  0.6 3.1 %collective-permute-start = (f32[16,768]{1,0:T(8,128)}, f32[16,768]{1,0:T(8,128)S(1)}, u32[]{:S(2)}, u32[]{:S(2)}) collective-permute-start(f32[16,768]{1,0:T(8,128)} %bitcast.8), channel_id=1, source_target_pairs={{0,8},{8,0},{16,24},{24,16},{1,9},{9,1},{17,25},{25,17},{2,10},{10... | collective-permute-start | bytes 147464 | tf_op jit(solution)/shard_map/ppermute | solution.py:22
  3.7 3.2 %shard_map.112 = (bf16[512,3072]{1,0:T(8,128)(2,1)S(1)}, f32[8,128]{1,0:T(8,128)S(1)}) custom-call(f32[16,768]{1,0:T(8,128)} %bitcast.15, f32[16,768]{1,0:T(8,128)} %bitcast.9, f32[16,768]{1,0:T(8,128)} %bitcast.18, s32[768,3072]{1,0:T(8,128)} %call_hbm.3), custom_call_target="tpu_custom_call" | custom-call | bytes 6291456 | tf_op jit(solution)/shard_map/pallas_call | solution.py:369
  6.9 0.0 collective-permute-done.other_ref
  7.0 2.7 %collective-permute-start.1 = (bf16[32,768]{1,0:T(8,128)(2,1)S(1)}, bf16[32,768]{1,0:T(8,128)(2,1)S(1)}, u32[]{:S(2)}, u32[]{:S(2)}) collective-permute-start(bf16[32,768]{1,0:T(8,128)(2,1)S(1)} %shard_map.111.pair_ref), channel_id=1, source_target_pairs={{0,16},{8,24},{16,0},{24,8},{1,17},{9,25},{17,1},{25,9},{2,18},{10... | collective-permute-start | bytes 147464 | tf_op jit(solution)/shard_map/ppermute | solution.py:22
  9.6 0.6 %shard_map.113.done_ref = f32[32,512]{1,0:T(8,128)S(1)} custom-call(bf16[32,768]{1,0:T(8,128)(2,1)S(1)} %shard_map.111.pair_ref, bf16[512,3072]{1,0:T(8,128)(2,1)S(1)} %get-tuple-element.24.called_first), custom_call_target="tpu_custom_call" | custom-call | flops 402653184 | bytes 1572864 | tf_op jit(solution)/shard_map/pallas_call | solution.py:369
  10.2 0.0 copy-done
  10.2 3.1 %shard_map.114 = (bf16[768,3072]{1,0:T(8,128)(2,1)S(1)}, bf16[256,3072]{1,0:T(8,128)(2,1)S(1)}, f32[40,768]{1,0:T(8,128)S(1)}) custom-call(bf16[32,768]{1,0:T(8,128)(2,1)S(1)} %shard_map.111.pair_ref, bf16[512,3072]{1,0:T(8,128)(2,1)S(1)} %get-tuple-element.24.called_first, f32[32,512]{1,0:T(8,128)S(1)} %shard_map.113.done_ref, s32[768,3072]{1,0:T(8,128)S(1)} %copy-done, ...), custom_call_target="tpu_custom_call" | custom-call | flops 1207959552 | bytes 9437184 | tf_op jit(solution)/shard_map/pallas_call | solution.py:369
  13.4 0.0 collective-permute-done.1.pair_ref
  13.4 1.5 %shard_map.115.own_ref = f32[40,896]{1,0:T(8,128)S(1)} custom-call(bf16[32,768]{1,0:T(8,128)(2,1)S(1)} %collective-permute-done.1.pair_ref, bf16[768,3072]{1,0:T(8,128)(2,1)S(1)} %get-tuple-element.25.coded_ref, bf16[512,3072]{1,0:T(8,128)(2,1)S(1)} %get-tuple-element.24.called_first, bf16[256,3072]{1,0:T(8,128)(2,1)S(1)} %get-tuple-element.26.called_ref, ...), custom_call_target="tpu_custom_call" | custom-call | flops 1207959552 | bytes 4718592 | tf_op jit(solution)/shard_map/pallas_call | solution.py:369
  14.9 0.1 collective-permute-start.2
  15.0 1.4 %collective-permute-done.2.other_ref = f32[40,896]{1,0:T(8,128)S(1)} collective-permute-done((f32[40,896]{1,0:T(8,128)S(1)}, f32[40,896]{1,0:T(8,128)S(1)}, u32[]{:S(2)}, u32[]{:S(2)}) %collective-permute-start.2) | collective-permute-done | bytes 143392 | tf_op jit(solution)/shard_map/ppermute | solution.py:22
  16.4 2.3 %collective-permute-start.3 = (bf16[32,896]{1,0:T(8,128)(2,1)S(1)}, bf16[32,896]{1,0:T(8,128)(2,1)S(1)}, u32[]{:S(2)}, u32[]{:S(2)}) collective-permute-start(bf16[32,896]{1,0:T(8,128)(2,1)S(1)} %get-tuple-element.30), channel_id=1, source_target_pairs={{0,7},{1,6},{2,5},{3,4},{4,3},{5,2},{6,1},{7,0},{8,15},{9,14},{10,... | collective-permute-start | bytes 172040 | tf_op jit(solution)/shard_map/ppermute | solution.py:22
  18.6 0.5 %collective-permute-start.4 = (bf16[32,896]{1,0:T(8,128)(2,1)S(1)}, bf16[32,896]{1,0:T(8,128)(2,1)S(1)}, u32[]{:S(2)}, u32[]{:S(2)}) collective-permute-start(bf16[32,896]{1,0:T(8,128)(2,1)S(1)} %get-tuple-element.31), channel_id=1, source_target_pairs={{0,5},{1,4},{2,7},{3,6},{4,1},{5,0},{6,3},{7,2},{8,13},{9,12},{10,... | collective-permute-start | bytes 172040 | tf_op jit(solution)/shard_map/ppermute | solution.py:22
  19.1 0.3 collective-permute-start.5
  19.4 1.8 %collective-permute-done.3.rest_0_ = bf16[32,896]{1,0:T(8,128)(2,1)S(1)} collective-permute-done((bf16[32,896]{1,0:T(8,128)(2,1)S(1)}, bf16[32,896]{1,0:T(8,128)(2,1)S(1)}, u32[]{:S(2)}, u32[]{:S(2)}) %collective-permute-start.3) | collective-permute-done | bytes 57376 | tf_op jit(solution)/shard_map/ppermute | solution.py:22
  21.2 1.2 %collective-permute-done.4.rest_1_ = bf16[32,896]{1,0:T(8,128)(2,1)S(1)} collective-permute-done((bf16[32,896]{1,0:T(8,128)(2,1)S(1)}, bf16[32,896]{1,0:T(8,128)(2,1)S(1)}, u32[]{:S(2)}, u32[]{:S(2)}) %collective-permute-start.4) | collective-permute-done | bytes 57376 | tf_op jit(solution)/shard_map/ppermute | solution.py:22
  22.4 0.6 %collective-permute-done.5.rest_2_ = bf16[32,896]{1,0:T(8,128)(2,1)S(1)} collective-permute-done((bf16[32,896]{1,0:T(8,128)(2,1)S(1)}, bf16[32,896]{1,0:T(8,128)(2,1)S(1)}, u32[]{:S(2)}, u32[]{:S(2)}) %collective-permute-start.5) | collective-permute-done | bytes 57376 | tf_op jit(solution)/shard_map/ppermute | solution.py:22
  23.0 0.0 copy-start.6
  23.0 1.4 %shard_map.117 = (f32[16,896]{1,0:T(8,128)S(1)}, bf16[16,896]{1,0:T(8,128)(2,1)S(1)}, bf16[16,896]{1,0:T(8,128)(2,1)S(1)}, bf16[16,896]{1,0:T(8,128)(2,1)S(1)}) custom-call(f32[40,896]{1,0:T(8,128)S(1)} %get-tuple-element.29.total_ref.after_ref, bf16[768,3072]{1,0:T(8,128)(2,1)S(1)} %get-tuple-element.25.coded_ref, ...), custom_call_target="tpu_custom_call" | custom-call | flops 2415919104 | bytes 9437184 | tf_op jit(solution)/shard_map/pallas_call | solution.py:369
  24.4 2.3 %collective-permute-start.6 = (bf16[16,896]{1,0:T(8,128)(2,1)S(1)}, bf16[16,896]{1,0:T(8,128)(2,1)S(1)}, u32[]{:S(2)}, u32[]{:S(2)}) collective-permute-start(bf16[16,896]{1,0:T(8,128)(2,1)S(1)} %get-tuple-element.34), channel_id=1, source_target_pairs={{0,24},{8,16},{16,8},{24,0},{1,25},{9,17},{17,9},{25,1},{2,26},{10... | collective-permute-start | bytes 86024 | tf_op jit(solution)/shard_map/ppermute | solution.py:22
  26.7 0.3 collective-permute-start.7
  26.9 1.9 %collective-permute-start.8 = (bf16[16,896]{1,0:T(8,128)(2,1)S(1)}, bf16[16,896]{1,0:T(8,128)(2,1)S(1)}, u32[]{:S(2)}, u32[]{:S(2)}) collective-permute-start(bf16[16,896]{1,0:T(8,128)(2,1)S(1)} %get-tuple-element.36), channel_id=1, source_target_pairs={{0,8},{8,0},{16,24},{24,16},{1,9},{9,1},{17,25},{25,17},{2,10},{10... | collective-permute-start | bytes 86024 | tf_op jit(solution)/shard_map/ppermute | solution.py:22
  28.8 0.0 copy-done.3
  28.8 0.6 %shard_map.119.cross_ref = f32[40,1024]{1,0:T(8,128)S(1)} custom-call(s32[1,768]{1,0:T(1,128)S(1)} %copy-done.5, f32[16,768]{1,0:T(8,128)S(1)} %bitcast.16, f32[16,768]{1,0:T(8,128)S(1)} %bitcast.11, s32[768,1024]{1,0:T(8,128)S(1)} %copy-done.1, f32[40,896]{1,0:T(8,128)S(1)} %get-tuple-element.29.total_ref.after_ref), custom_call_target="tpu_custom_call" | custom-call | flops 220200960 | bytes 3145728 | tf_op jit(solution)/shard_map/pallas_call | solution.py:369
  29.4 0.7 %collective-permute-done.6.rest_1_ = bf16[16,896]{1,0:T(8,128)(2,1)S(1)} collective-permute-done((bf16[16,896]{1,0:T(8,128)(2,1)S(1)}, bf16[16,896]{1,0:T(8,128)(2,1)S(1)}, u32[]{:S(2)}, u32[]{:S(2)}) %collective-permute-start.6) | collective-permute-done | bytes 28704 | tf_op jit(solution)/shard_map/ppermute | solution.py:22
  30.1 1.3 %collective-permute-done.7.rest_2_ = bf16[16,896]{1,0:T(8,128)(2,1)S(1)} collective-permute-done((bf16[16,896]{1,0:T(8,128)(2,1)S(1)}, bf16[16,896]{1,0:T(8,128)(2,1)S(1)}, u32[]{:S(2)}, u32[]{:S(2)}) %collective-permute-start.7) | collective-permute-done | bytes 28704 | tf_op jit(solution)/shard_map/ppermute | solution.py:22
  31.4 0.0 collective-permute-done.8.rest_3_
  31.5 0.9 %shard_map.120 = (f32[32,1,640]{2,1,0:T(1,128)}, f32[16,768]{1,0:T(8,128)S(1)}) custom-call(f32[1,16]{1,0:T(1,128)S(1)} %bitcast.21, f32[16,768]{1,0:T(8,128)S(1)} %bitcast.12, f32[16,768]{1,0:T(8,128)S(1)} %bitcast.19, f32[40,1024]{1,0:T(8,128)S(1)} %shard_map.119.cross_ref, f32[16,896]{1,0:T(8,128)S(1)} %get-tuple-element.33.rest_0_, ...), custom_call_target="tpu_custom_call" | custom-call | bytes 81920 | tf_op jit(solution)/shard_map/pallas_call | solution.py:369
  32.4 3.3 %all-to-all-start = ((f32[32,1,640]{2,1,0:T(1,128)}), f32[32,1,640]{2,1,0:T(1,128)S(1)}, u32[]{:S(2)}, u32[]{:S(2)}) async-start(f32[32,1,640]{2,1,0:T(1,128)} %get-tuple-element.39), calls=%async_computation | async-start | bytes 163840 | tf_op jit(solution)/shard_map/all_to_all | solution.py:487
  35.7 0.7 %shard_map.118 = (f32[16,768]{1,0:T(8,128)}, f32[16,768]{1,0:T(8,128)}, f32[16,128]{1,0:T(8,128)S(1)}) custom-call(f32[1,16]{1,0:T(1,128)S(1)} %bitcast.22, f32[16,768]{1,0:T(8,128)S(1)} %bitcast.13, f32[16,768]{1,0:T(8,128)S(1)} %bitcast.20, f32[16,768]{1,0:T(8,128)S(1)} %bitcast.17, f32[16,896]{1,0:T(8,128)S(1)} %get-tuple-element.33.rest_0_, ...), custom_call_target="tpu_custom_call" | custom-call | bytes 1048576 | tf_op jit(solution)/shard_map/pallas_call | solution.py:369
  36.5 6.9 %all-to-all-done.came_ref = f32[32,1,640]{2,1,0:T(1,128)S(1)} async-done(((f32[32,1,640]{2,1,0:T(1,128)}), f32[32,1,640]{2,1,0:T(1,128)S(1)}, u32[]{:S(2)}, u32[]{:S(2)}) %all-to-all-start) | async-done | bytes 81952 | tf_op jit(solution)/shard_map/all_to_all | solution.py:487
  43.3 0.8 %shard_map.121 = (f32[16,768]{1,0:T(8,128)}, f32[16,32]{1,0:T(8,128)}) custom-call(f32[32,1,640]{2,1,0:T(1,128)S(1)} %all-to-all-done.came_ref, f32[16,128]{1,0:T(8,128)S(1)} %get-tuple-element.40.stats_ref, f32[16,768]{1,0:T(8,128)S(1)} %get-tuple-element.41.res_ref, f32[16,768]{1,0:T(8,128)S(1)} %bitcast.14), custom_call_target="tpu_custom_call" | custom-call | tf_op jit(solution)/shard_map/pallas_call | solution.py:369
  (13 shorter events, 0.1 us)
Async XLA Ops:
  0.6 6.3 %collective-permute-start = (f32[16,768]{1,0:T(8,128)}, f32[16,768]{1,0:T(8,128)S(1)}, u32[]{:S(2)}, u32[]{:S(2)}) collective-permute-start(f32[16,768]{1,0:T(8,128)} %bitcast.8), channel_id=1, source_target_pairs={{0,8},{8,0},{16,24},{24,16},{1,9},{9,1},{17,25},{25,17},{2,10},{10... | collective-permute-start | bytes 147464 | tf_op jit(solution)/shard_map/ppermute | solution.py:22
  3.7 3.2 %copy-start.2 = (f32[768,16]{0,1:T(8,128)S(1)}, f32[768,16]{0,1:T(8,128)}, u32[]{:S(2)}) copy-start(f32[768,16]{0,1:T(8,128)} %param.15) | copy-start | bytes 147460
  3.7 6.5 %copy-start = (s32[768,3072]{1,0:T(8,128)S(1)}, s32[768,3072]{1,0:T(8,128)}, u32[]{:S(2)}) copy-start(s32[768,3072]{1,0:T(8,128)} %gen_ref.1) | copy-start | bytes 28311556
  7.0 6.4 %collective-permute-start.1 = (bf16[32,768]{1,0:T(8,128)(2,1)S(1)}, bf16[32,768]{1,0:T(8,128)(2,1)S(1)}, u32[]{:S(2)}, u32[]{:S(2)}) collective-permute-start(bf16[32,768]{1,0:T(8,128)(2,1)S(1)} %shard_map.111.pair_ref), channel_id=1, source_target_pairs={{0,16},{8,24},{16,0},{24,8},{1,17},{9,25},{17,1},{25,9},{2,18},{10... | collective-permute-start | bytes 147464 | tf_op jit(solution)/shard_map/ppermute | solution.py:22
  14.9 1.4 %collective-permute-start.2 = (f32[40,896]{1,0:T(8,128)S(1)}, f32[40,896]{1,0:T(8,128)S(1)}, u32[]{:S(2)}, u32[]{:S(2)}) collective-permute-start(f32[40,896]{1,0:T(8,128)S(1)} %shard_map.115.own_ref), channel_id=1, source_target_pairs={{0,1},{1,0},{2,3},{3,2},{4,5},{5,4},{6,7},{7,6},{8,9},{9,8},{10,11... | collective-permute-start | bytes 430088 | tf_op jit(solution)/shard_map/ppermute | solution.py:22
  16.4 4.9 %collective-permute-start.3 = (bf16[32,896]{1,0:T(8,128)(2,1)S(1)}, bf16[32,896]{1,0:T(8,128)(2,1)S(1)}, u32[]{:S(2)}, u32[]{:S(2)}) collective-permute-start(bf16[32,896]{1,0:T(8,128)(2,1)S(1)} %get-tuple-element.30), channel_id=1, source_target_pairs={{0,7},{1,6},{2,5},{3,4},{4,3},{5,2},{6,1},{7,0},{8,15},{9,14},{10,... | collective-permute-start | bytes 172040 | tf_op jit(solution)/shard_map/ppermute | solution.py:22
  18.6 3.8 %collective-permute-start.4 = (bf16[32,896]{1,0:T(8,128)(2,1)S(1)}, bf16[32,896]{1,0:T(8,128)(2,1)S(1)}, u32[]{:S(2)}, u32[]{:S(2)}) collective-permute-start(bf16[32,896]{1,0:T(8,128)(2,1)S(1)} %get-tuple-element.31), channel_id=1, source_target_pairs={{0,5},{1,4},{2,7},{3,6},{4,1},{5,0},{6,3},{7,2},{8,13},{9,12},{10,... | collective-permute-start | bytes 172040 | tf_op jit(solution)/shard_map/ppermute | solution.py:22
  19.1 3.9 %collective-permute-start.5 = (bf16[32,896]{1,0:T(8,128)(2,1)S(1)}, bf16[32,896]{1,0:T(8,128)(2,1)S(1)}, u32[]{:S(2)}, u32[]{:S(2)}) collective-permute-start(bf16[32,896]{1,0:T(8,128)(2,1)S(1)} %get-tuple-element.32), channel_id=1, source_target_pairs={{0,3},{1,2},{2,1},{3,0},{4,7},{5,6},{6,5},{7,4},{8,11},{9,10},{10,... | collective-permute-start | bytes 172040 | tf_op jit(solution)/shard_map/ppermute | solution.py:22
  23.0 5.8 %copy-start.1 = (s32[768,1024]{1,0:T(8,128)S(1)}, s32[768,1024]{1,0:T(8,128)}, u32[]{:S(2)}) copy-start(s32[768,1024]{1,0:T(8,128)} %dose_ref.1) | copy-start | bytes 9437188
  23.0 5.8 %copy-start.3 = (f32[768,16]{0,1:T(8,128)S(1)}, f32[768,16]{0,1:T(8,128)}, u32[]{:S(2)}) copy-start(f32[768,16]{0,1:T(8,128)} %param.13) | copy-start | bytes 147460
  23.0 5.8 %copy-start.5 = (s32[1,768]{1,0:T(1,128)S(1)}, s32[1,768]{1,0:T(1,128)}, u32[]{:S(2)}) copy-start(s32[1,768]{1,0:T(1,128)} %order_ref.1) | copy-start | bytes 9220
  23.0 8.5 %copy-start.4 = (f32[768,16]{0,1:T(8,128)S(1)}, f32[768,16]{0,1:T(8,128)}, u32[]{:S(2)}) copy-start(f32[768,16]{0,1:T(8,128)} %param.14) | copy-start | bytes 147460
  23.0 8.5 %copy-start.6 = (f32[16]{0:T(128)S(1)}, f32[16]{0:T(128)}, u32[]{:S(2)}) copy-start(f32[16]{0:T(128)} %param.12) | copy-start | bytes 196
  24.4 5.7 %collective-permute-start.6 = (bf16[16,896]{1,0:T(8,128)(2,1)S(1)}, bf16[16,896]{1,0:T(8,128)(2,1)S(1)}, u32[]{:S(2)}, u32[]{:S(2)}) collective-permute-start(bf16[16,896]{1,0:T(8,128)(2,1)S(1)} %get-tuple-element.34), channel_id=1, source_target_pairs={{0,24},{8,16},{16,8},{24,0},{1,25},{9,17},{17,9},{25,1},{2,26},{10... | collective-permute-start | bytes 86024 | tf_op jit(solution)/shard_map/ppermute | solution.py:22
  26.7 4.8 %collective-permute-start.7 = (bf16[16,896]{1,0:T(8,128)(2,1)S(1)}, bf16[16,896]{1,0:T(8,128)(2,1)S(1)}, u32[]{:S(2)}, u32[]{:S(2)}) collective-permute-start(bf16[16,896]{1,0:T(8,128)(2,1)S(1)} %get-tuple-element.35), channel_id=1, source_target_pairs={{0,16},{8,24},{16,0},{24,8},{1,17},{9,25},{17,1},{25,9},{2,18},{10... | collective-permute-start | bytes 86024 | tf_op jit(solution)/shard_map/ppermute | solution.py:22
  26.9 4.5 %collective-permute-start.8 = (bf16[16,896]{1,0:T(8,128)(2,1)S(1)}, bf16[16,896]{1,0:T(8,128)(2,1)S(1)}, u32[]{:S(2)}, u32[]{:S(2)}) collective-permute-start(bf16[16,896]{1,0:T(8,128)(2,1)S(1)} %get-tuple-element.36), channel_id=1, source_target_pairs={{0,8},{8,0},{16,24},{24,16},{1,9},{9,1},{17,25},{25,17},{2,10},{10... | collective-permute-start | bytes 86024 | tf_op jit(solution)/shard_map/ppermute | solution.py:22
  32.4 11.0 %all-to-all-start = ((f32[32,1,640]{2,1,0:T(1,128)}), f32[32,1,640]{2,1,0:T(1,128)S(1)}, u32[]{:S(2)}, u32[]{:S(2)}) async-start(f32[32,1,640]{2,1,0:T(1,128)} %get-tuple-element.39), calls=%async_computation | async-start | bytes 163840 | tf_op jit(solution)/shard_map/all_to_all | solution.py:487

commit v15 on v14

--- a/solution.py
+++ b/solution.py
@@ -60,7 +60,7 @@
     return jnp.sum(jnp.where(same, row, 0.0), axis=1, keepdims=True)
 
 
-BLOCK = 1024
+BLOCK = 512
 CHUNK = 256
 
 
@@ -168,18 +168,16 @@
             if after >= 0:
                 called[block] = mask
 
-        held = None
+        held = []
         for block in blocks(LANES, shard):
             mask = call[block].astype(F32).astype(BF16) if after >= 0 else mask_ref[block]
-            value = gen[block].astype(F32).astype(BF16) * mask
-            if held:
-                store(*held)
-            held = (block, value, mask)
-        store(*held)
+            held.append((block, gen[block].astype(F32).astype(BF16) * mask, mask))
+            if len(held) > 4:
+                store(*held.pop(0))
+        for item in held:
+            store(*item)
 
     for place in range(0, rows + CHUNK, CHUNK):
-        for part in range(place, min(place + CHUNK, rows), LANES):
-            convert(part)
         if place:
             before = place - CHUNK
             coded = product(w, coded_ref, before, CHUNK, samples)
@@ -188,6 +186,8 @@
             else:
                 called = product(w, called_ref, before - first, CHUNK, samples)
             out_ref[:, before:place] = rows_of(coded, called)
+        for part in range(place, min(place + CHUNK, rows), LANES):
+            convert(part)
 
 
 def forward_kernel(pair_ref, coded_ref, called_first, called_ref, half_ref, sums_ref, out_ref, w):

time: 44.3 us -> 44.3 us (level)
  transfers between devices with their start and end apart: 10 -> 10, of which waited for: 7 -> 7; matrix products, arithmetic and copies ran while one was open for 0% -> 0% of each run, Pallas kernels for 19% -> 18%
where the time goes in v15:
time: 44.3 us; the launch traced here: 44.1 us
  starting transfers between devices  16.6 us (37%)
  waiting for transfers between devices  14.1 us (32%)
  Pallas kernels  12.6 us (28%)
  between operations  0.74 us (2%)
    ppermute x9, starting transfers between devices, swap(): return lax.ppermute(values, axis, [(i, i ^ distance) for i in range(size)])  13.3 us
    pallas_call x11, Pallas kernels, call(): pl.pallas_call(kernel, out_shape=[jax.ShapeDtypeStruct(*o) if len(o) == 2...  12.6 us
    ppermute x9, waiting for transfers between devices, swap(): return lax.ppermute(values, axis, [(i, i ^ distance) for i in range(size)])  7.28 us
    all_to_all x1, waiting for transfers between devices, body(): lax.all_to_all(outgoing, ('var', 'samp'), split_axis=0, concat_axis=0)  6.86 us
    all_to_all x1, starting transfers between devices, body(): lax.all_to_all(outgoing, ('var', 'samp'), split_axis=0, concat_axis=0)  3.34 us
  transfers between devices with their start and end apart: 10, of which 7 were waited for; matrix products, arithmetic and copies ran while one was open for 0% of the time, Pallas kernels for 18%

profile of v15, /device:TPU:0, one launch (start us, length us, event | category | flops | bytes accessed | tf_op | source)
XLA Modules:
  0.0 44.1 jit_solution(1765638793151700049)
XLA Ops:
  0.6 3.1 %collective-permute-start = (f32[16,768]{1,0:T(8,128)}, f32[16,768]{1,0:T(8,128)S(1)}, u32[]{:S(2)}, u32[]{:S(2)}) collective-permute-start(f32[16,768]{1,0:T(8,128)} %bitcast.8), channel_id=1, source_target_pairs={{0,8},{8,0},{16,24},{24,16},{1,9},{9,1},{17,25},{25,17},{2,10},{10... | collective-permute-start | bytes 147464 | tf_op jit(solution)/shard_map/ppermute | solution.py:22
  3.7 3.2 %shard_map.112 = (bf16[512,3072]{1,0:T(8,128)(2,1)S(1)}, f32[8,128]{1,0:T(8,128)S(1)}) custom-call(f32[16,768]{1,0:T(8,128)} %bitcast.15, f32[16,768]{1,0:T(8,128)} %bitcast.9, f32[16,768]{1,0:T(8,128)} %bitcast.18, s32[768,3072]{1,0:T(8,128)} %call_hbm.3), custom_call_target="tpu_custom_call" | custom-call | bytes 6291456 | tf_op jit(solution)/shard_map/pallas_call | solution.py:369
  6.9 0.0 collective-permute-done.other_ref
  7.0 2.7 %collective-permute-start.1 = (bf16[32,768]{1,0:T(8,128)(2,1)S(1)}, bf16[32,768]{1,0:T(8,128)(2,1)S(1)}, u32[]{:S(2)}, u32[]{:S(2)}) collective-permute-start(bf16[32,768]{1,0:T(8,128)(2,1)S(1)} %shard_map.111.pair_ref), channel_id=1, source_target_pairs={{0,16},{8,24},{16,0},{24,8},{1,17},{9,25},{17,1},{25,9},{2,18},{10... | collective-permute-start | bytes 147464 | tf_op jit(solution)/shard_map/ppermute | solution.py:22
  9.6 0.6 %shard_map.113.done_ref = f32[32,512]{1,0:T(8,128)S(1)} custom-call(bf16[32,768]{1,0:T(8,128)(2,1)S(1)} %shard_map.111.pair_ref, bf16[512,3072]{1,0:T(8,128)(2,1)S(1)} %get-tuple-element.24.called_first), custom_call_target="tpu_custom_call" | custom-call | flops 402653184 | bytes 1572864 | tf_op jit(solution)/shard_map/pallas_call | solution.py:369
  10.2 0.0 copy-done
  10.2 2.8 %shard_map.114 = (bf16[768,3072]{1,0:T(8,128)(2,1)S(1)}, bf16[256,3072]{1,0:T(8,128)(2,1)S(1)}, f32[40,768]{1,0:T(8,128)S(1)}) custom-call(bf16[32,768]{1,0:T(8,128)(2,1)S(1)} %shard_map.111.pair_ref, bf16[512,3072]{1,0:T(8,128)(2,1)S(1)} %get-tuple-element.24.called_first, f32[32,512]{1,0:T(8,128)S(1)} %shard_map.113.done_ref, s32[768,3072]{1,0:T(8,128)S(1)} %copy-done, ...), custom_call_target="tpu_custom_call" | custom-call | flops 1207959552 | bytes 9437184 | tf_op jit(solution)/shard_map/pallas_call | solution.py:369
  13.0 0.0 collective-permute-done.1.pair_ref
  13.0 1.5 %shard_map.115.own_ref = f32[40,896]{1,0:T(8,128)S(1)} custom-call(bf16[32,768]{1,0:T(8,128)(2,1)S(1)} %collective-permute-done.1.pair_ref, bf16[768,3072]{1,0:T(8,128)(2,1)S(1)} %get-tuple-element.25.coded_ref, bf16[512,3072]{1,0:T(8,128)(2,1)S(1)} %get-tuple-element.24.called_first, bf16[256,3072]{1,0:T(8,128)(2,1)S(1)} %get-tuple-element.26.called_ref, ...), custom_call_target="tpu_custom_call" | custom-call | flops 1207959552 | bytes 4718592 | tf_op jit(solution)/shard_map/pallas_call | solution.py:369
  14.6 0.1 collective-permute-start.2
  14.6 1.4 %collective-permute-done.2.other_ref = f32[40,896]{1,0:T(8,128)S(1)} collective-permute-done((f32[40,896]{1,0:T(8,128)S(1)}, f32[40,896]{1,0:T(8,128)S(1)}, u32[]{:S(2)}, u32[]{:S(2)}) %collective-permute-start.2) | collective-permute-done | bytes 143392 | tf_op jit(solution)/shard_map/ppermute | solution.py:22
  16.0 2.3 %collective-permute-start.3 = (bf16[32,896]{1,0:T(8,128)(2,1)S(1)}, bf16[32,896]{1,0:T(8,128)(2,1)S(1)}, u32[]{:S(2)}, u32[]{:S(2)}) collective-permute-start(bf16[32,896]{1,0:T(8,128)(2,1)S(1)} %get-tuple-element.30), channel_id=1, source_target_pairs={{0,7},{1,6},{2,5},{3,4},{4,3},{5,2},{6,1},{7,0},{8,15},{9,14},{10,... | collective-permute-start | bytes 172040 | tf_op jit(solution)/shard_map/ppermute | solution.py:22
  18.3 0.5 %collective-permute-start.4 = (bf16[32,896]{1,0:T(8,128)(2,1)S(1)}, bf16[32,896]{1,0:T(8,128)(2,1)S(1)}, u32[]{:S(2)}, u32[]{:S(2)}) collective-permute-start(bf16[32,896]{1,0:T(8,128)(2,1)S(1)} %get-tuple-element.31), channel_id=1, source_target_pairs={{0,5},{1,4},{2,7},{3,6},{4,1},{5,0},{6,3},{7,2},{8,13},{9,12},{10,... | collective-permute-start | bytes 172040 | tf_op jit(solution)/shard_map/ppermute | solution.py:22
  18.8 0.3 collective-permute-start.5
  19.1 1.8 %collective-permute-done.3.rest_0_ = bf16[32,896]{1,0:T(8,128)(2,1)S(1)} collective-permute-done((bf16[32,896]{1,0:T(8,128)(2,1)S(1)}, bf16[32,896]{1,0:T(8,128)(2,1)S(1)}, u32[]{:S(2)}, u32[]{:S(2)}) %collective-permute-start.3) | collective-permute-done | bytes 57376 | tf_op jit(solution)/shard_map/ppermute | solution.py:22
  20.9 1.2 %collective-permute-done.4.rest_1_ = bf16[32,896]{1,0:T(8,128)(2,1)S(1)} collective-permute-done((bf16[32,896]{1,0:T(8,128)(2,1)S(1)}, bf16[32,896]{1,0:T(8,128)(2,1)S(1)}, u32[]{:S(2)}, u32[]{:S(2)}) %collective-permute-start.4) | collective-permute-done | bytes 57376 | tf_op jit(solution)/shard_map/ppermute | solution.py:22
  22.1 0.6 %collective-permute-done.5.rest_2_ = bf16[32,896]{1,0:T(8,128)(2,1)S(1)} collective-permute-done((bf16[32,896]{1,0:T(8,128)(2,1)S(1)}, bf16[32,896]{1,0:T(8,128)(2,1)S(1)}, u32[]{:S(2)}, u32[]{:S(2)}) %collective-permute-start.5) | collective-permute-done | bytes 57376 | tf_op jit(solution)/shard_map/ppermute | solution.py:22
  22.7 0.0 copy-start.6
  22.7 1.4 %shard_map.117 = (f32[16,896]{1,0:T(8,128)S(1)}, bf16[16,896]{1,0:T(8,128)(2,1)S(1)}, bf16[16,896]{1,0:T(8,128)(2,1)S(1)}, bf16[16,896]{1,0:T(8,128)(2,1)S(1)}) custom-call(f32[40,896]{1,0:T(8,128)S(1)} %get-tuple-element.29.total_ref.after_ref, bf16[768,3072]{1,0:T(8,128)(2,1)S(1)} %get-tuple-element.25.coded_ref, ...), custom_call_target="tpu_custom_call" | custom-call | flops 2415919104 | bytes 9437184 | tf_op jit(solution)/shard_map/pallas_call | solution.py:369
  24.0 2.6 %collective-permute-start.6 = (bf16[16,896]{1,0:T(8,128)(2,1)S(1)}, bf16[16,896]{1,0:T(8,128)(2,1)S(1)}, u32[]{:S(2)}, u32[]{:S(2)}) collective-permute-start(bf16[16,896]{1,0:T(8,128)(2,1)S(1)} %get-tuple-element.34), channel_id=1, source_target_pairs={{0,24},{8,16},{16,8},{24,0},{1,25},{9,17},{17,9},{25,1},{2,26},{10... | collective-permute-start | bytes 86024 | tf_op jit(solution)/shard_map/ppermute | solution.py:22
  26.7 0.0 collective-permute-start.7
  26.7 1.8 %collective-permute-start.8 = (bf16[16,896]{1,0:T(8,128)(2,1)S(1)}, bf16[16,896]{1,0:T(8,128)(2,1)S(1)}, u32[]{:S(2)}, u32[]{:S(2)}) collective-permute-start(bf16[16,896]{1,0:T(8,128)(2,1)S(1)} %get-tuple-element.36), channel_id=1, source_target_pairs={{0,8},{8,0},{16,24},{24,16},{1,9},{9,1},{17,25},{25,17},{2,10},{10... | collective-permute-start | bytes 86024 | tf_op jit(solution)/shard_map/ppermute | solution.py:22
  28.5 0.0 copy-done.3
  28.5 0.6 %shard_map.119.cross_ref = f32[40,1024]{1,0:T(8,128)S(1)} custom-call(s32[1,768]{1,0:T(1,128)S(1)} %copy-done.5, f32[16,768]{1,0:T(8,128)S(1)} %bitcast.16, f32[16,768]{1,0:T(8,128)S(1)} %bitcast.11, s32[768,1024]{1,0:T(8,128)S(1)} %copy-done.1, f32[40,896]{1,0:T(8,128)S(1)} %get-tuple-element.29.total_ref.after_ref), custom_call_target="tpu_custom_call" | custom-call | flops 220200960 | bytes 3145728 | tf_op jit(solution)/shard_map/pallas_call | solution.py:369
  29.1 0.7 %collective-permute-done.6.rest_1_ = bf16[16,896]{1,0:T(8,128)(2,1)S(1)} collective-permute-done((bf16[16,896]{1,0:T(8,128)(2,1)S(1)}, bf16[16,896]{1,0:T(8,128)(2,1)S(1)}, u32[]{:S(2)}, u32[]{:S(2)}) %collective-permute-start.6) | collective-permute-done | bytes 28704 | tf_op jit(solution)/shard_map/ppermute | solution.py:22
  29.8 1.7 %collective-permute-done.7.rest_2_ = bf16[16,896]{1,0:T(8,128)(2,1)S(1)} collective-permute-done((bf16[16,896]{1,0:T(8,128)(2,1)S(1)}, bf16[16,896]{1,0:T(8,128)(2,1)S(1)}, u32[]{:S(2)}, u32[]{:S(2)}) %collective-permute-start.7) | collective-permute-done | bytes 28704 | tf_op jit(solution)/shard_map/ppermute | solution.py:22
  31.4 0.0 collective-permute-done.8.rest_3_
  31.5 0.9 %shard_map.120 = (f32[32,1,640]{2,1,0:T(1,128)}, f32[16,768]{1,0:T(8,128)S(1)}) custom-call(f32[1,16]{1,0:T(1,128)S(1)} %bitcast.21, f32[16,768]{1,0:T(8,128)S(1)} %bitcast.12, f32[16,768]{1,0:T(8,128)S(1)} %bitcast.19, f32[40,1024]{1,0:T(8,128)S(1)} %shard_map.119.cross_ref, f32[16,896]{1,0:T(8,128)S(1)} %get-tuple-element.33.rest_0_, ...), custom_call_target="tpu_custom_call" | custom-call | bytes 81920 | tf_op jit(solution)/shard_map/pallas_call | solution.py:369
  32.4 3.3 %all-to-all-start = ((f32[32,1,640]{2,1,0:T(1,128)}), f32[32,1,640]{2,1,0:T(1,128)S(1)}, u32[]{:S(2)}, u32[]{:S(2)}) async-start(f32[32,1,640]{2,1,0:T(1,128)} %get-tuple-element.39), calls=%async_computation | async-start | bytes 163840 | tf_op jit(solution)/shard_map/all_to_all | solution.py:487
  35.7 0.7 %shard_map.118 = (f32[16,768]{1,0:T(8,128)}, f32[16,768]{1,0:T(8,128)}, f32[16,128]{1,0:T(8,128)S(1)}) custom-call(f32[1,16]{1,0:T(1,128)S(1)} %bitcast.22, f32[16,768]{1,0:T(8,128)S(1)} %bitcast.13, f32[16,768]{1,0:T(8,128)S(1)} %bitcast.20, f32[16,768]{1,0:T(8,128)S(1)} %bitcast.17, f32[16,896]{1,0:T(8,128)S(1)} %get-tuple-element.33.rest_0_, ...), custom_call_target="tpu_custom_call" | custom-call | bytes 1048576 | tf_op jit(solution)/shard_map/pallas_call | solution.py:369
  36.5 6.9 %all-to-all-done.came_ref = f32[32,1,640]{2,1,0:T(1,128)S(1)} async-done(((f32[32,1,640]{2,1,0:T(1,128)}), f32[32,1,640]{2,1,0:T(1,128)S(1)}, u32[]{:S(2)}, u32[]{:S(2)}) %all-to-all-start) | async-done | bytes 81952 | tf_op jit(solution)/shard_map/all_to_all | solution.py:487
  43.3 0.8 %shard_map.121 = (f32[16,768]{1,0:T(8,128)}, f32[16,32]{1,0:T(8,128)}) custom-call(f32[32,1,640]{2,1,0:T(1,128)S(1)} %all-to-all-done.came_ref, f32[16,128]{1,0:T(8,128)S(1)} %get-tuple-element.40.stats_ref, f32[16,768]{1,0:T(8,128)S(1)} %get-tuple-element.41.res_ref, f32[16,768]{1,0:T(8,128)S(1)} %bitcast.14), custom_call_target="tpu_custom_call" | custom-call | tf_op jit(solution)/shard_map/pallas_call | solution.py:369
  (13 shorter events, 0.1 us)
Async XLA Ops:
  0.6 6.3 %collective-permute-start = (f32[16,768]{1,0:T(8,128)}, f32[16,768]{1,0:T(8,128)S(1)}, u32[]{:S(2)}, u32[]{:S(2)}) collective-permute-start(f32[16,768]{1,0:T(8,128)} %bitcast.8), channel_id=1, source_target_pairs={{0,8},{8,0},{16,24},{24,16},{1,9},{9,1},{17,25},{25,17},{2,10},{10... | collective-permute-start | bytes 147464 | tf_op jit(solution)/shard_map/ppermute | solution.py:22
  3.7 3.2 %copy-start.2 = (f32[768,16]{0,1:T(8,128)S(1)}, f32[768,16]{0,1:T(8,128)}, u32[]{:S(2)}) copy-start(f32[768,16]{0,1:T(8,128)} %param.15) | copy-start | bytes 147460
  3.7 6.5 %copy-start = (s32[768,3072]{1,0:T(8,128)S(1)}, s32[768,3072]{1,0:T(8,128)}, u32[]{:S(2)}) copy-start(s32[768,3072]{1,0:T(8,128)} %gen_ref.1) | copy-start | bytes 28311556
  7.0 6.1 %collective-permute-start.1 = (bf16[32,768]{1,0:T(8,128)(2,1)S(1)}, bf16[32,768]{1,0:T(8,128)(2,1)S(1)}, u32[]{:S(2)}, u32[]{:S(2)}) collective-permute-start(bf16[32,768]{1,0:T(8,128)(2,1)S(1)} %shard_map.111.pair_ref), channel_id=1, source_target_pairs={{0,16},{8,24},{16,0},{24,8},{1,17},{9,25},{17,1},{25,9},{2,18},{10... | collective-permute-start | bytes 147464 | tf_op jit(solution)/shard_map/ppermute | solution.py:22
  14.6 1.4 %collective-permute-start.2 = (f32[40,896]{1,0:T(8,128)S(1)}, f32[40,896]{1,0:T(8,128)S(1)}, u32[]{:S(2)}, u32[]{:S(2)}) collective-permute-start(f32[40,896]{1,0:T(8,128)S(1)} %shard_map.115.own_ref), channel_id=1, source_target_pairs={{0,1},{1,0},{2,3},{3,2},{4,5},{5,4},{6,7},{7,6},{8,9},{9,8},{10,11... | collective-permute-start | bytes 430088 | tf_op jit(solution)/shard_map/ppermute | solution.py:22
  16.0 4.9 %collective-permute-start.3 = (bf16[32,896]{1,0:T(8,128)(2,1)S(1)}, bf16[32,896]{1,0:T(8,128)(2,1)S(1)}, u32[]{:S(2)}, u32[]{:S(2)}) collective-permute-start(bf16[32,896]{1,0:T(8,128)(2,1)S(1)} %get-tuple-element.30), channel_id=1, source_target_pairs={{0,7},{1,6},{2,5},{3,4},{4,3},{5,2},{6,1},{7,0},{8,15},{9,14},{10,... | collective-permute-start | bytes 172040 | tf_op jit(solution)/shard_map/ppermute | solution.py:22
  18.3 3.8 %collective-permute-start.4 = (bf16[32,896]{1,0:T(8,128)(2,1)S(1)}, bf16[32,896]{1,0:T(8,128)(2,1)S(1)}, u32[]{:S(2)}, u32[]{:S(2)}) collective-permute-start(bf16[32,896]{1,0:T(8,128)(2,1)S(1)} %get-tuple-element.31), channel_id=1, source_target_pairs={{0,5},{1,4},{2,7},{3,6},{4,1},{5,0},{6,3},{7,2},{8,13},{9,12},{10,... | collective-permute-start | bytes 172040 | tf_op jit(solution)/shard_map/ppermute | solution.py:22
  18.8 3.9 %collective-permute-start.5 = (bf16[32,896]{1,0:T(8,128)(2,1)S(1)}, bf16[32,896]{1,0:T(8,128)(2,1)S(1)}, u32[]{:S(2)}, u32[]{:S(2)}) collective-permute-start(bf16[32,896]{1,0:T(8,128)(2,1)S(1)} %get-tuple-element.32), channel_id=1, source_target_pairs={{0,3},{1,2},{2,1},{3,0},{4,7},{5,6},{6,5},{7,4},{8,11},{9,10},{10,... | collective-permute-start | bytes 172040 | tf_op jit(solution)/shard_map/ppermute | solution.py:22
  22.6 5.8 %copy-start.1 = (s32[768,1024]{1,0:T(8,128)S(1)}, s32[768,1024]{1,0:T(8,128)}, u32[]{:S(2)}) copy-start(s32[768,1024]{1,0:T(8,128)} %dose_ref.1) | copy-start | bytes 9437188
  22.6 5.8 %copy-start.3 = (f32[768,16]{0,1:T(8,128)S(1)}, f32[768,16]{0,1:T(8,128)}, u32[]{:S(2)}) copy-start(f32[768,16]{0,1:T(8,128)} %param.13) | copy-start | bytes 147460
  22.6 5.8 %copy-start.5 = (s32[1,768]{1,0:T(1,128)S(1)}, s32[1,768]{1,0:T(1,128)}, u32[]{:S(2)}) copy-start(s32[1,768]{1,0:T(1,128)} %order_ref.1) | copy-start | bytes 9220
  22.7 8.8 %copy-start.4 = (f32[768,16]{0,1:T(8,128)S(1)}, f32[768,16]{0,1:T(8,128)}, u32[]{:S(2)}) copy-start(f32[768,16]{0,1:T(8,128)} %param.14) | copy-start | bytes 147460
  22.7 8.8 %copy-start.6 = (f32[16]{0:T(128)S(1)}, f32[16]{0:T(128)}, u32[]{:S(2)}) copy-start(f32[16]{0:T(128)} %param.12) | copy-start | bytes 196
  24.0 5.7 %collective-permute-start.6 = (bf16[16,896]{1,0:T(8,128)(2,1)S(1)}, bf16[16,896]{1,0:T(8,128)(2,1)S(1)}, u32[]{:S(2)}, u32[]{:S(2)}) collective-permute-start(bf16[16,896]{1,0:T(8,128)(2,1)S(1)} %get-tuple-element.34), channel_id=1, source_target_pairs={{0,24},{8,16},{16,8},{24,0},{1,25},{9,17},{17,9},{25,1},{2,26},{10... | collective-permute-start | bytes 86024 | tf_op jit(solution)/shard_map/ppermute | solution.py:22
  26.7 4.8 %collective-permute-start.7 = (bf16[16,896]{1,0:T(8,128)(2,1)S(1)}, bf16[16,896]{1,0:T(8,128)(2,1)S(1)}, u32[]{:S(2)}, u32[]{:S(2)}) collective-permute-start(bf16[16,896]{1,0:T(8,128)(2,1)S(1)} %get-tuple-element.35), channel_id=1, source_target_pairs={{0,16},{8,24},{16,0},{24,8},{1,17},{9,25},{17,1},{25,9},{2,18},{10... | collective-permute-start | bytes 86024 | tf_op jit(solution)/shard_map/ppermute | solution.py:22
  26.7 4.8 %collective-permute-start.8 = (bf16[16,896]{1,0:T(8,128)(2,1)S(1)}, bf16[16,896]{1,0:T(8,128)(2,1)S(1)}, u32[]{:S(2)}, u32[]{:S(2)}) collective-permute-start(bf16[16,896]{1,0:T(8,128)(2,1)S(1)} %get-tuple-element.36), channel_id=1, source_target_pairs={{0,8},{8,0},{16,24},{24,16},{1,9},{9,1},{17,25},{25,17},{2,10},{10... | collective-permute-start | bytes 86024 | tf_op jit(solution)/shard_map/ppermute | solution.py:22
  32.4 11.0 %all-to-all-start = ((f32[32,1,640]{2,1,0:T(1,128)}), f32[32,1,640]{2,1,0:T(1,128)S(1)}, u32[]{:S(2)}, u32[]{:S(2)}) async-start(f32[32,1,640]{2,1,0:T(1,128)} %get-tuple-element.39), calls=%async_computation | async-start | bytes 163840 | tf_op jit(solution)/shard_map/all_to_all | solution.py:487

commit v16 on v15

--- a/solution.py
+++ b/solution.py
@@ -238,8 +238,23 @@
     cross_ref[2 * rhs :] = cross[4 * rhs : 4 * rhs + 8]
 
 
+def term(scaled_ref, coded_ref, called_first, called_ref, p, own, variants):
+    part = pl.ds(pl.multiple_of(p * own, LANES), own)
+    first = called_first.shape[0]
+    got = jnp.dot(scaled_ref[0:16], coded_ref[:, part], preferred_element_type=F32)
+    got = got + jnp.dot(scaled_ref[16:32, :first], called_first[:, part], preferred_element_type=F32)
+    got = got + jnp.dot(scaled_ref[16:32, first:], called_ref[:, part], preferred_element_type=F32)
+    return got / variants
+
+
+def sums_block(sums):
+    parts = [part.astype(F32) for part in thirds(sums)]
+    return jnp.concatenate(parts + [jnp.zeros((13, LANES), F32)], axis=0).astype(BF16)
+
+
 def back_kernel(variants, n_arrived, total_ref, coded_ref, called_first, called_ref, *rest):
-    arrived, own_ref, messages = rest[:n_arrived], rest[n_arrived], rest[n_arrived + 1 :]
+    arrived = rest[:n_arrived]
+    scaled_ref, sums_ref, *messages = rest[n_arrived:]
     var = lax.axis_index("var")
     rows = total_ref.shape[1] - LANES
 
@@ -263,28 +278,24 @@
     spread = jnp.sqrt(2.0 * frequency * (1.0 - frequency))
     loading = (main[0:16] - 2.0 * frequency * main[16:32]) / spread
     scaled = loading / spread
-    scaled_a = scaled.astype(BF16)
-    scaled_b = (-2.0 * frequency * scaled).astype(BF16)
+    scaled_ref[0:16] = scaled.astype(BF16)
+    scaled_ref[16:32] = (-2.0 * frequency * scaled).astype(BF16)
     square = as_row({6: jnp.sum(loading * loading, axis=1, keepdims=True)})
     sums = jnp.where(lane_of((1, LANES)) < 96, sums, square)
 
+    sums_ref[...] = jnp.broadcast_to(sums, sums_ref.shape)
+
+    for k, ref in enumerate(messages):
+        own = ref.shape[1] - LANES
+        ref[:, :own] = term(scaled_ref, coded_ref, called_first, called_ref, var ^ (k + 1), own, variants).astype(BF16)
+        ref[:, own:] = sums_block(sums)
+
+
+def own_kernel(variants, scaled_ref, sums_ref, coded_ref, called_first, called_ref, own_ref):
     own = own_ref.shape[1] - LANES
-
-    def term(p):
-        part = pl.ds(pl.multiple_of(p * own, LANES), own)
-        got = jnp.dot(scaled_a, coded_ref[:, part], preferred_element_type=F32)
-        first = called_first.shape[0]
-        got = got + jnp.dot(scaled_b[:, :first], called_first[:, part], preferred_element_type=F32)
-        got = got + jnp.dot(scaled_b[:, first:], called_ref[:, part], preferred_element_type=F32)
-        return got / variants
-
-    parts = [part.astype(F32) for part in thirds(sums)]
-    block = jnp.concatenate(parts + [jnp.zeros((13, LANES), F32)], axis=0).astype(BF16)
-    for k, ref in enumerate(messages):
-        ref[:, :own] = term(var ^ (k + 1)).astype(BF16)
-        ref[:, own:] = block
-    own_ref[:, :own] = term(var)
-    own_ref[:, own:] = jnp.concatenate([sums, jnp.zeros((15, LANES), F32)], axis=0)
+    p = lax.axis_index("var")
+    own_ref[:, :own] = term(scaled_ref, coded_ref, called_first, called_ref, p, own, variants)
+    own_ref[:, own:] = jnp.concatenate([sums_ref[0:1], jnp.zeros((15, LANES), F32)], axis=0)
 
 
 def step_of(refs, noise_row, variants):
@@ -456,6 +467,25 @@
         moved=1 * MIB,
     )
     arrived = [swap(messages[k], "samp", 2 * (k + 1) + 1) for k in reversed(range(n_chips - 1))]
+    wide = own + LANES
+    scaled, sums, *messages = call(
+        functools.partial(back_kernel, variants, len(arrived)),
+        [((2 * rhs, rows), BF16), ((8, LANES), F32)] + [((rhs, wide), BF16)] * (n_var - 1),
+        [VMEM] * (4 + len(arrived)),
+        (total, coded, called_a, called_b, *arrived),
+        flops=2 * rows * shard * 256,
+        moved=2 * rows * shard,
+    )
+    backs = [swap(messages[k], "var", k + 1) for k in reversed(range(n_var - 1))]
+    (mine_back,) = call(
+        functools.partial(own_kernel, variants),
+        [((rhs, wide), F32)],
+        [VMEM] * 5,
+        (scaled, sums, coded, called_a, called_b),
+        flops=rows * shard * 256,
+        moved=rows * shard,
+    )
+    backs = [mine_back] + backs
     (cross,) = call(
         dosage_kernel,
         [((2 * rhs + 8, imputed), F32)],
@@ -465,16 +495,6 @@
         moved=4 * own * imputed,
     )
 
-    wide = own + LANES
-    mine_back, *messages = call(
-        functools.partial(back_kernel, variants, len(arrived)),
-        [((rhs, wide), F32)] + [((rhs, wide), BF16)] * (n_var - 1),
-        [VMEM] * (4 + len(arrived)),
-        (total, coded, called_a, called_b, *arrived),
-        flops=4 * rows * shard * 256,
-        moved=4 * rows * shard,
-    )
-    backs = [mine_back] + [swap(messages[k], "var", k + 1) for k in reversed(range(n_var - 1))]
 
     n_all = n_var * n_samp
     outgoing, res_keep = call(

time: 44.3 us -> 44 us (level)
    ppermute x9, waiting for transfers between devices: 7.28 us -> 6.82 us  [swap(): return lax.ppermute(values, axis, [(i, i ^ distance) for i in range(size)])]
    pallas_call x11 -> x12, Pallas kernels: 12.6 us -> 12.7 us  [call(): pl.pallas_call(kernel, out_shape=[jax.ShapeDtypeStruct(*o) if len(o) == 2...]
  transfers between devices with their start and end apart: 10 -> 10, of which waited for: 7 -> 7; matrix products, arithmetic and copies ran while one was open for 0% -> 0% of each run, Pallas kernels for 18% -> 19%
where the time goes in v16:
time: 44 us; the launch traced here: 43.8 us
  starting transfers between devices  16.6 us (38%)
  waiting for transfers between devices  13.7 us (31%)
  Pallas kernels  12.7 us (29%)
  between operations  0.76 us (2%)
    ppermute x9, starting transfers between devices, swap(): return lax.ppermute(values, axis, [(i, i ^ distance) for i in range(size)])  13.3 us
    pallas_call x12, Pallas kernels, call(): pl.pallas_call(kernel, out_shape=[jax.ShapeDtypeStruct(*o) if len(o) == 2...  12.7 us
    all_to_all x1, waiting for transfers between devices, body(): lax.all_to_all(outgoing, ('var', 'samp'), split_axis=0, concat_axis=0)  6.86 us
    ppermute x9, waiting for transfers between devices, swap(): return lax.ppermute(values, axis, [(i, i ^ distance) for i in range(size)])  6.82 us
    all_to_all x1, starting transfers between devices, body(): lax.all_to_all(outgoing, ('var', 'samp'), split_axis=0, concat_axis=0)  3.34 us
  transfers between devices with their start and end apart: 10, of which 7 were waited for; matrix products, arithmetic and copies ran while one was open for 0% of the time, Pallas kernels for 19%

profile of v16, /device:TPU:0, one launch (start us, length us, event | category | flops | bytes accessed | tf_op | source)
XLA Modules:
  0.0 43.8 jit_solution(4805369215802498246)
XLA Ops:
  0.6 3.1 %collective-permute-start = (f32[16,768]{1,0:T(8,128)}, f32[16,768]{1,0:T(8,128)S(1)}, u32[]{:S(2)}, u32[]{:S(2)}) collective-permute-start(f32[16,768]{1,0:T(8,128)} %bitcast.8), channel_id=1, source_target_pairs={{0,8},{8,0},{16,24},{24,16},{1,9},{9,1},{17,25},{25,17},{2,10},{10... | collective-permute-start | bytes 147464 | tf_op jit(solution)/shard_map/ppermute | solution.py:22
  3.7 3.2 %shard_map.112 = (bf16[512,3072]{1,0:T(8,128)(2,1)S(1)}, f32[8,128]{1,0:T(8,128)S(1)}) custom-call(f32[16,768]{1,0:T(8,128)} %bitcast.15, f32[16,768]{1,0:T(8,128)} %bitcast.9, f32[16,768]{1,0:T(8,128)} %bitcast.18, s32[768,3072]{1,0:T(8,128)} %call_hbm.3), custom_call_target="tpu_custom_call" | custom-call | bytes 6291456 | tf_op jit(solution)/shard_map/pallas_call | solution.py:380
  6.9 0.0 collective-permute-done.other_ref
  7.0 2.7 %collective-permute-start.1 = (bf16[32,768]{1,0:T(8,128)(2,1)S(1)}, bf16[32,768]{1,0:T(8,128)(2,1)S(1)}, u32[]{:S(2)}, u32[]{:S(2)}) collective-permute-start(bf16[32,768]{1,0:T(8,128)(2,1)S(1)} %shard_map.111.pair_ref), channel_id=1, source_target_pairs={{0,16},{8,24},{16,0},{24,8},{1,17},{9,25},{17,1},{25,9},{2,18},{10... | collective-permute-start | bytes 147464 | tf_op jit(solution)/shard_map/ppermute | solution.py:22
  9.6 0.6 %shard_map.113.done_ref = f32[32,512]{1,0:T(8,128)S(1)} custom-call(bf16[32,768]{1,0:T(8,128)(2,1)S(1)} %shard_map.111.pair_ref, bf16[512,3072]{1,0:T(8,128)(2,1)S(1)} %get-tuple-element.25.called_first), custom_call_target="tpu_custom_call" | custom-call | flops 402653184 | bytes 1572864 | tf_op jit(solution)/shard_map/pallas_call | solution.py:380
  10.2 0.0 copy-done
  10.2 2.8 %shard_map.114 = (bf16[768,3072]{1,0:T(8,128)(2,1)S(1)}, bf16[256,3072]{1,0:T(8,128)(2,1)S(1)}, f32[40,768]{1,0:T(8,128)S(1)}) custom-call(bf16[32,768]{1,0:T(8,128)(2,1)S(1)} %shard_map.111.pair_ref, bf16[512,3072]{1,0:T(8,128)(2,1)S(1)} %get-tuple-element.25.called_first, f32[32,512]{1,0:T(8,128)S(1)} %shard_map.113.done_ref, s32[768,3072]{1,0:T(8,128)S(1)} %copy-done, ...), custom_call_target="tpu_custom_call" | custom-call | flops 1207959552 | bytes 9437184 | tf_op jit(solution)/shard_map/pallas_call | solution.py:380
  13.0 0.0 collective-permute-done.1.pair_ref
  13.0 0.0 copy-start.1
  13.1 0.0 copy-start.3
  13.1 0.0 copy-start.5
  13.1 1.5 %shard_map.115.own_ref = f32[40,896]{1,0:T(8,128)S(1)} custom-call(bf16[32,768]{1,0:T(8,128)(2,1)S(1)} %collective-permute-done.1.pair_ref, bf16[768,3072]{1,0:T(8,128)(2,1)S(1)} %get-tuple-element.26.coded_ref, bf16[512,3072]{1,0:T(8,128)(2,1)S(1)} %get-tuple-element.25.called_first, bf16[256,3072]{1,0:T(8,128)(2,1)S(1)} %get-tuple-element.27.called_ref, ...), custom_call_target="tpu_custom_call" | custom-call | flops 1207959552 | bytes 4718592 | tf_op jit(solution)/shard_map/pallas_call | solution.py:380
  14.6 0.1 collective-permute-start.2
  14.7 1.4 %collective-permute-done.2.other_ref = f32[40,896]{1,0:T(8,128)S(1)} collective-permute-done((f32[40,896]{1,0:T(8,128)S(1)}, f32[40,896]{1,0:T(8,128)S(1)}, u32[]{:S(2)}, u32[]{:S(2)}) %collective-permute-start.2) | collective-permute-done | bytes 143392 | tf_op jit(solution)/shard_map/ppermute | solution.py:22
  16.1 2.3 %collective-permute-start.3 = (bf16[32,896]{1,0:T(8,128)(2,1)S(1)}, bf16[32,896]{1,0:T(8,128)(2,1)S(1)}, u32[]{:S(2)}, u32[]{:S(2)}) collective-permute-start(bf16[32,896]{1,0:T(8,128)(2,1)S(1)} %get-tuple-element.31), channel_id=1, source_target_pairs={{0,7},{1,6},{2,5},{3,4},{4,3},{5,2},{6,1},{7,0},{8,15},{9,14},{10,... | collective-permute-start | bytes 172040 | tf_op jit(solution)/shard_map/ppermute | solution.py:22
  18.3 0.5 %collective-permute-start.4 = (bf16[32,896]{1,0:T(8,128)(2,1)S(1)}, bf16[32,896]{1,0:T(8,128)(2,1)S(1)}, u32[]{:S(2)}, u32[]{:S(2)}) collective-permute-start(bf16[32,896]{1,0:T(8,128)(2,1)S(1)} %get-tuple-element.32), channel_id=1, source_target_pairs={{0,5},{1,4},{2,7},{3,6},{4,1},{5,0},{6,3},{7,2},{8,13},{9,12},{10,... | collective-permute-start | bytes 172040 | tf_op jit(solution)/shard_map/ppermute | solution.py:22
  18.8 0.3 collective-permute-start.5
  19.1 0.6 %shard_map.120.cross_ref = f32[40,1024]{1,0:T(8,128)S(1)} custom-call(s32[1,768]{1,0:T(1,128)S(1)} %copy-done.5, f32[16,768]{1,0:T(8,128)S(1)} %bitcast.16, f32[16,768]{1,0:T(8,128)S(1)} %bitcast.11, s32[768,1024]{1,0:T(8,128)S(1)} %copy-done.1, f32[40,896]{1,0:T(8,128)S(1)} %get-tuple-element.30.total_ref.after_ref), custom_call_target="tpu_custom_call" | custom-call | flops 220200960 | bytes 3145728 | tf_op jit(solution)/shard_map/pallas_call | solution.py:380
  19.7 1.2 %collective-permute-done.3.rest_0_ = bf16[32,896]{1,0:T(8,128)(2,1)S(1)} collective-permute-done((bf16[32,896]{1,0:T(8,128)(2,1)S(1)}, bf16[32,896]{1,0:T(8,128)(2,1)S(1)}, u32[]{:S(2)}, u32[]{:S(2)}) %collective-permute-start.3) | collective-permute-done | bytes 57376 | tf_op jit(solution)/shard_map/ppermute | solution.py:22
  20.9 1.2 %collective-permute-done.4.rest_1_ = bf16[32,896]{1,0:T(8,128)(2,1)S(1)} collective-permute-done((bf16[32,896]{1,0:T(8,128)(2,1)S(1)}, bf16[32,896]{1,0:T(8,128)(2,1)S(1)}, u32[]{:S(2)}, u32[]{:S(2)}) %collective-permute-start.4) | collective-permute-done | bytes 57376 | tf_op jit(solution)/shard_map/ppermute | solution.py:22
  22.1 0.6 %collective-permute-done.5.rest_2_ = bf16[32,896]{1,0:T(8,128)(2,1)S(1)} collective-permute-done((bf16[32,896]{1,0:T(8,128)(2,1)S(1)}, bf16[32,896]{1,0:T(8,128)(2,1)S(1)}, u32[]{:S(2)}, u32[]{:S(2)}) %collective-permute-start.5) | collective-permute-done | bytes 57376 | tf_op jit(solution)/shard_map/ppermute | solution.py:22
  22.7 1.1 %shard_map.117 = (bf16[32,768]{1,0:T(8,128)(2,1)S(1)}, f32[8,128]{1,0:T(8,128)S(1)}, bf16[16,896]{1,0:T(8,128)(2,1)S(1)}, bf16[16,896]{1,0:T(8,128)(2,1)S(1)}, bf16[16,896]{1,0:T(8,128)(2,1)S(1)}) custom-call(f32[40,896]{1,0:T(8,128)S(1)} %get-tuple-element.30.total_ref.after_ref, bf16[768,3072]{1,0:T(8,128)(2,1)S(1)} %get-tuple-element.26.coded_ref, ...), custom_call_target="tpu_custom_call" | custom-call | flops 1207959552 | bytes 4718592 | tf_op jit(solution)/shard_map/pallas_call | solution.py:380
  23.8 2.6 %collective-permute-start.6 = (bf16[16,896]{1,0:T(8,128)(2,1)S(1)}, bf16[16,896]{1,0:T(8,128)(2,1)S(1)}, u32[]{:S(2)}, u32[]{:S(2)}) collective-permute-start(bf16[16,896]{1,0:T(8,128)(2,1)S(1)} %get-tuple-element.36), channel_id=1, source_target_pairs={{0,24},{8,16},{16,8},{24,0},{1,25},{9,17},{17,9},{25,1},{2,26},{10... | collective-permute-start | bytes 86024 | tf_op jit(solution)/shard_map/ppermute | solution.py:22
  26.4 1.8 %collective-permute-start.8 = (bf16[16,896]{1,0:T(8,128)(2,1)S(1)}, bf16[16,896]{1,0:T(8,128)(2,1)S(1)}, u32[]{:S(2)}, u32[]{:S(2)}) collective-permute-start(bf16[16,896]{1,0:T(8,128)(2,1)S(1)} %get-tuple-element.38), channel_id=1, source_target_pairs={{0,8},{8,0},{16,24},{24,16},{1,9},{9,1},{17,25},{25,17},{2,10},{10... | collective-permute-start | bytes 86024 | tf_op jit(solution)/shard_map/ppermute | solution.py:22
  28.2 0.4 shard_map.118.rest_0_
  28.6 0.9 %collective-permute-done.6.rest_1_ = bf16[16,896]{1,0:T(8,128)(2,1)S(1)} collective-permute-done((bf16[16,896]{1,0:T(8,128)(2,1)S(1)}, bf16[16,896]{1,0:T(8,128)(2,1)S(1)}, u32[]{:S(2)}, u32[]{:S(2)}) %collective-permute-start.6) | collective-permute-done | bytes 28704 | tf_op jit(solution)/shard_map/ppermute | solution.py:22
  29.5 1.6 %collective-permute-done.7.rest_2_ = bf16[16,896]{1,0:T(8,128)(2,1)S(1)} collective-permute-done((bf16[16,896]{1,0:T(8,128)(2,1)S(1)}, bf16[16,896]{1,0:T(8,128)(2,1)S(1)}, u32[]{:S(2)}, u32[]{:S(2)}) %collective-permute-start.7) | collective-permute-done | bytes 28704 | tf_op jit(solution)/shard_map/ppermute | solution.py:22
  31.2 0.9 %shard_map.121 = (f32[32,1,640]{2,1,0:T(1,128)}, f32[16,768]{1,0:T(8,128)S(1)}) custom-call(f32[1,16]{1,0:T(1,128)S(1)} %bitcast.21, f32[16,768]{1,0:T(8,128)S(1)} %bitcast.12, f32[16,768]{1,0:T(8,128)S(1)} %bitcast.19, f32[40,1024]{1,0:T(8,128)S(1)} %shard_map.120.cross_ref, f32[16,896]{1,0:T(8,128)S(1)} %shard_map.118.rest_0_, ...), custom_call_target="tpu_custom_call" | custom-call | bytes 81920 | tf_op jit(solution)/shard_map/pallas_call | solution.py:380
  32.1 3.3 %all-to-all-start = ((f32[32,1,640]{2,1,0:T(1,128)}), f32[32,1,640]{2,1,0:T(1,128)S(1)}, u32[]{:S(2)}, u32[]{:S(2)}) async-start(f32[32,1,640]{2,1,0:T(1,128)} %get-tuple-element.41), calls=%async_computation | async-start | bytes 163840 | tf_op jit(solution)/shard_map/all_to_all | solution.py:507
  35.4 0.7 %shard_map.119 = (f32[16,768]{1,0:T(8,128)}, f32[16,768]{1,0:T(8,128)}, f32[16,128]{1,0:T(8,128)S(1)}) custom-call(f32[1,16]{1,0:T(1,128)S(1)} %bitcast.22, f32[16,768]{1,0:T(8,128)S(1)} %bitcast.13, f32[16,768]{1,0:T(8,128)S(1)} %bitcast.20, f32[16,768]{1,0:T(8,128)S(1)} %bitcast.17, f32[16,896]{1,0:T(8,128)S(1)} %shard_map.118.rest_0_, ...), custom_call_target="tpu_custom_call" | custom-call | bytes 1048576 | tf_op jit(solution)/shard_map/pallas_call | solution.py:380
  36.1 6.9 %all-to-all-done.came_ref = f32[32,1,640]{2,1,0:T(1,128)S(1)} async-done(((f32[32,1,640]{2,1,0:T(1,128)}), f32[32,1,640]{2,1,0:T(1,128)S(1)}, u32[]{:S(2)}, u32[]{:S(2)}) %all-to-all-start) | async-done | bytes 81952 | tf_op jit(solution)/shard_map/all_to_all | solution.py:507
  43.0 0.8 %shard_map.122 = (f32[16,768]{1,0:T(8,128)}, f32[16,32]{1,0:T(8,128)}) custom-call(f32[32,1,640]{2,1,0:T(1,128)S(1)} %all-to-all-done.came_ref, f32[16,128]{1,0:T(8,128)S(1)} %get-tuple-element.42.stats_ref, f32[16,768]{1,0:T(8,128)S(1)} %get-tuple-element.43.res_ref, f32[16,768]{1,0:T(8,128)S(1)} %bitcast.14), custom_call_target="tpu_custom_call" | custom-call | tf_op jit(solution)/shard_map/pallas_call | solution.py:380
  (14 shorter events, 0.1 us)
Async XLA Ops:
  0.6 6.3 %collective-permute-start = (f32[16,768]{1,0:T(8,128)}, f32[16,768]{1,0:T(8,128)S(1)}, u32[]{:S(2)}, u32[]{:S(2)}) collective-permute-start(f32[16,768]{1,0:T(8,128)} %bitcast.8), channel_id=1, source_target_pairs={{0,8},{8,0},{16,24},{24,16},{1,9},{9,1},{17,25},{25,17},{2,10},{10... | collective-permute-start | bytes 147464 | tf_op jit(solution)/shard_map/ppermute | solution.py:22
  3.7 3.2 %copy-start.2 = (f32[768,16]{0,1:T(8,128)S(1)}, f32[768,16]{0,1:T(8,128)}, u32[]{:S(2)}) copy-start(f32[768,16]{0,1:T(8,128)} %param.15) | copy-start | bytes 147460
  3.7 6.5 %copy-start = (s32[768,3072]{1,0:T(8,128)S(1)}, s32[768,3072]{1,0:T(8,128)}, u32[]{:S(2)}) copy-start(s32[768,3072]{1,0:T(8,128)} %gen_ref.1) | copy-start | bytes 28311556
  7.0 6.1 %collective-permute-start.1 = (bf16[32,768]{1,0:T(8,128)(2,1)S(1)}, bf16[32,768]{1,0:T(8,128)(2,1)S(1)}, u32[]{:S(2)}, u32[]{:S(2)}) collective-permute-start(bf16[32,768]{1,0:T(8,128)(2,1)S(1)} %shard_map.111.pair_ref), channel_id=1, source_target_pairs={{0,16},{8,24},{16,0},{24,8},{1,17},{9,25},{17,1},{25,9},{2,18},{10... | collective-permute-start | bytes 147464 | tf_op jit(solution)/shard_map/ppermute | solution.py:22
  13.0 6.1 %copy-start.1 = (s32[768,1024]{1,0:T(8,128)S(1)}, s32[768,1024]{1,0:T(8,128)}, u32[]{:S(2)}) copy-start(s32[768,1024]{1,0:T(8,128)} %dose_ref.1) | copy-start | bytes 9437188
  13.1 6.0 %copy-start.3 = (f32[768,16]{0,1:T(8,128)S(1)}, f32[768,16]{0,1:T(8,128)}, u32[]{:S(2)}) copy-start(f32[768,16]{0,1:T(8,128)} %param.13) | copy-start | bytes 147460
  13.1 6.0 %copy-start.5 = (s32[1,768]{1,0:T(1,128)S(1)}, s32[1,768]{1,0:T(1,128)}, u32[]{:S(2)}) copy-start(s32[1,768]{1,0:T(1,128)} %order_ref.1) | copy-start | bytes 9220
  14.6 1.4 %collective-permute-start.2 = (f32[40,896]{1,0:T(8,128)S(1)}, f32[40,896]{1,0:T(8,128)S(1)}, u32[]{:S(2)}, u32[]{:S(2)}) collective-permute-start(f32[40,896]{1,0:T(8,128)S(1)} %shard_map.115.own_ref), channel_id=1, source_target_pairs={{0,1},{1,0},{2,3},{3,2},{4,5},{5,4},{6,7},{7,6},{8,9},{9,8},{10,11... | collective-permute-start | bytes 430088 | tf_op jit(solution)/shard_map/ppermute | solution.py:22
  16.1 4.9 %collective-permute-start.3 = (bf16[32,896]{1,0:T(8,128)(2,1)S(1)}, bf16[32,896]{1,0:T(8,128)(2,1)S(1)}, u32[]{:S(2)}, u32[]{:S(2)}) collective-permute-start(bf16[32,896]{1,0:T(8,128)(2,1)S(1)} %get-tuple-element.31), channel_id=1, source_target_pairs={{0,7},{1,6},{2,5},{3,4},{4,3},{5,2},{6,1},{7,0},{8,15},{9,14},{10,... | collective-permute-start | bytes 172040 | tf_op jit(solution)/shard_map/ppermute | solution.py:22
  18.3 3.8 %collective-permute-start.4 = (bf16[32,896]{1,0:T(8,128)(2,1)S(1)}, bf16[32,896]{1,0:T(8,128)(2,1)S(1)}, u32[]{:S(2)}, u32[]{:S(2)}) collective-permute-start(bf16[32,896]{1,0:T(8,128)(2,1)S(1)} %get-tuple-element.32), channel_id=1, source_target_pairs={{0,5},{1,4},{2,7},{3,6},{4,1},{5,0},{6,3},{7,2},{8,13},{9,12},{10,... | collective-permute-start | bytes 172040 | tf_op jit(solution)/shard_map/ppermute | solution.py:22
  18.8 3.9 %collective-permute-start.5 = (bf16[32,896]{1,0:T(8,128)(2,1)S(1)}, bf16[32,896]{1,0:T(8,128)(2,1)S(1)}, u32[]{:S(2)}, u32[]{:S(2)}) collective-permute-start(bf16[32,896]{1,0:T(8,128)(2,1)S(1)} %get-tuple-element.33), channel_id=1, source_target_pairs={{0,3},{1,2},{2,1},{3,0},{4,7},{5,6},{6,5},{7,4},{8,11},{9,10},{10,... | collective-permute-start | bytes 172040 | tf_op jit(solution)/shard_map/ppermute | solution.py:22
  23.8 5.7 %collective-permute-start.6 = (bf16[16,896]{1,0:T(8,128)(2,1)S(1)}, bf16[16,896]{1,0:T(8,128)(2,1)S(1)}, u32[]{:S(2)}, u32[]{:S(2)}) collective-permute-start(bf16[16,896]{1,0:T(8,128)(2,1)S(1)} %get-tuple-element.36), channel_id=1, source_target_pairs={{0,24},{8,16},{16,8},{24,0},{1,25},{9,17},{17,9},{25,1},{2,26},{10... | collective-permute-start | bytes 86024 | tf_op jit(solution)/shard_map/ppermute | solution.py:22
  26.4 4.8 %collective-permute-start.7 = (bf16[16,896]{1,0:T(8,128)(2,1)S(1)}, bf16[16,896]{1,0:T(8,128)(2,1)S(1)}, u32[]{:S(2)}, u32[]{:S(2)}) collective-permute-start(bf16[16,896]{1,0:T(8,128)(2,1)S(1)} %get-tuple-element.37), channel_id=1, source_target_pairs={{0,16},{8,24},{16,0},{24,8},{1,17},{9,25},{17,1},{25,9},{2,18},{10... | collective-permute-start | bytes 86024 | tf_op jit(solution)/shard_map/ppermute | solution.py:22
  26.4 4.8 %collective-permute-start.8 = (bf16[16,896]{1,0:T(8,128)(2,1)S(1)}, bf16[16,896]{1,0:T(8,128)(2,1)S(1)}, u32[]{:S(2)}, u32[]{:S(2)}) collective-permute-start(bf16[16,896]{1,0:T(8,128)(2,1)S(1)} %get-tuple-element.38), channel_id=1, source_target_pairs={{0,8},{8,0},{16,24},{24,16},{1,9},{9,1},{17,25},{25,17},{2,10},{10... | collective-permute-start | bytes 86024 | tf_op jit(solution)/shard_map/ppermute | solution.py:22
  28.2 3.0 %copy-start.4 = (f32[768,16]{0,1:T(8,128)S(1)}, f32[768,16]{0,1:T(8,128)}, u32[]{:S(2)}) copy-start(f32[768,16]{0,1:T(8,128)} %param.14) | copy-start | bytes 147460
  28.2 3.0 %copy-start.6 = (f32[16]{0:T(128)S(1)}, f32[16]{0:T(128)}, u32[]{:S(2)}) copy-start(f32[16]{0:T(128)} %param.12) | copy-start | bytes 196
  32.1 11.0 %all-to-all-start = ((f32[32,1,640]{2,1,0:T(1,128)}), f32[32,1,640]{2,1,0:T(1,128)S(1)}, u32[]{:S(2)}, u32[]{:S(2)}) async-start(f32[32,1,640]{2,1,0:T(1,128)} %get-tuple-element.41), calls=%async_computation | async-start | bytes 163840 | tf_op jit(solution)/shard_map/all_to_all | solution.py:507

commit v17 on v16

--- a/solution.py
+++ b/solution.py
@@ -62,6 +62,17 @@
 
 BLOCK = 512
 CHUNK = 256
+
+
+def pieces(*ends):
+    found = []
+    at = 0
+    for end in ends:
+        while at < end:
+            size = min(CHUNK, end - at)
+            found.append((at, size))
+            at += size
+    return found
 
 
 def blocks(rows, samples):
@@ -140,8 +151,8 @@
     own = pair_ref.shape[1]
     samples = pair_samples(lax.axis_index("var") // 2, own)
     weights(pair_ref, w)
-    for place in range(0, called_first.shape[0], CHUNK):
-        out_ref[:, place : place + CHUNK] = product(w, called_first, place, CHUNK, samples)
+    for place, size in pieces(called_first.shape[0]):
+        out_ref[:, place : place + size] = product(w, called_first, place, size, samples)
 
 
 def mask_kernel(pair_ref, called_first, done_ref, gen_ref, call_hbm, coded_ref, called_ref, out_ref, cbuf, w, sems):
@@ -177,17 +188,19 @@
         for item in held:
             store(*item)
 
-    for place in range(0, rows + CHUNK, CHUNK):
-        if place:
-            before = place - CHUNK
-            coded = product(w, coded_ref, before, CHUNK, samples)
-            if before < first:
-                called = done_ref[:, before:place]
+    before = None
+    for place, size in pieces(first, rows) + [(rows, 0)]:
+        if before:
+            at, count = before
+            coded = product(w, coded_ref, at, count, samples)
+            if at < first:
+                called = done_ref[:, at : at + count]
             else:
-                called = product(w, called_ref, before - first, CHUNK, samples)
-            out_ref[:, before:place] = rows_of(coded, called)
-        for part in range(place, min(place + CHUNK, rows), LANES):
+                called = product(w, called_ref, at - first, count, samples)
+            out_ref[:, at : at + count] = rows_of(coded, called)
+        for part in range(place, place + size, LANES):
             convert(part)
+        before = (place, size)
 
 
 def forward_kernel(pair_ref, coded_ref, called_first, called_ref, half_ref, sums_ref, out_ref, w):
@@ -195,10 +208,10 @@
     rows = coded_ref.shape[0]
     samples = pair_samples((lax.axis_index("var") // 2) ^ 1, own)
     weights(pair_ref, w)
-    for place in range(0, rows, CHUNK):
-        here = slice(place, place + CHUNK)
-        coded = product(w, coded_ref, place, CHUNK, samples)
-        called = split_product(w, called_first, called_ref, place, CHUNK, samples)
+    for place, size in pieces(called_first.shape[0], rows):
+        here = slice(place, place + size)
+        coded = product(w, coded_ref, place, size, samples)
+        called = split_product(w, called_first, called_ref, place, size, samples)
         out_ref[:, here] = half_ref[:, here] + rows_of(coded, called)
     out_ref[:, rows:] = jnp.zeros((out_ref.shape[0], LANES), F32)
     out_ref[0:8, rows:] = sums_ref[...]
@@ -252,6 +265,11 @@
     return jnp.concatenate(parts + [jnp.zeros((13, LANES), F32)], axis=0).astype(BF16)
 
 
+def var_distances(n_var):
+    far = list(reversed(range(1, n_var)))
+    return list(zip(far, far[-1:] + far[:-1]))
+
+
 def back_kernel(variants, n_arrived, total_ref, coded_ref, called_first, called_ref, *rest):
     arrived = rest[:n_arrived]
     scaled_ref, sums_ref, *messages = rest[n_arrived:]
@@ -285,9 +303,11 @@
 
     sums_ref[...] = jnp.broadcast_to(sums, sums_ref.shape)
 
-    for k, ref in enumerate(messages):
+    core = lax.axis_index("samp") % 2
+    for (zero, one), ref in zip(var_distances(len(messages) + 1), messages):
         own = ref.shape[1] - LANES
-        ref[:, :own] = term(scaled_ref, coded_ref, called_first, called_ref, var ^ (k + 1), own, variants).astype(BF16)
+        p = var ^ jnp.where(core == 0, zero, one)
+        ref[:, :own] = term(scaled_ref, coded_ref, called_first, called_ref, p, own, variants).astype(BF16)
         ref[:, own:] = sums_block(sums)
 
 
@@ -400,7 +420,7 @@
     noise = noise_ratio[None]
 
     dire, res, sol = direction.T, residual.T, solution.T
-    first, chunk = rows // 3 * 2, 128
+    first, chunk = rows // 2, 128
     matrix = lambda n: ((n, shard), BF16, pltpu.VMEM)
 
     neighbour = swap(dire, "var", 1)
@@ -476,7 +496,10 @@
         flops=2 * rows * shard * 256,
         moved=2 * rows * shard,
     )
-    backs = [swap(messages[k], "var", k + 1) for k in reversed(range(n_var - 1))]
+    backs = []
+    for distances, m in zip(var_distances(n_var), messages):
+        pairs = [(i, i ^ (distances[i % 2] * n_samp)) for i in range(n_var * n_samp)]
+        backs.append(lax.ppermute(m, ("var", "samp"), pairs))
     (mine_back,) = call(
         functools.partial(own_kernel, variants),
         [((rhs, wide), F32)],

time: 44 us -> 44.4 us (level)
    ppermute x9 -> x6, starting transfers between devices: 13.3 us -> 8.85 us  [swap(): return lax.ppermute(values, axis, [(i, i ^ distance) for i in range(size)])]
    ppermute x0 -> x3, starting transfers between devices: none -> 4.42 us  [body(): backs.append(lax.ppermute(m, ('var', 'samp'), pairs))]
    ppermute x0 -> x3, waiting for transfers between devices: none -> 2.66 us  [body(): backs.append(lax.ppermute(m, ('var', 'samp'), pairs))]
    ppermute x9 -> x6, waiting for transfers between devices: 6.82 us -> 4.3 us  [swap(): return lax.ppermute(values, axis, [(i, i ^ distance) for i in range(size)])]
where the time goes in v17:
time: 44.4 us; the launch traced here: 44.1 us
  starting transfers between devices  16.5 us (37%)
  waiting for transfers between devices  13.8 us (31%)
  Pallas kernels  13 us (29%)
  between operations  0.75 us (2%)
    pallas_call x12, Pallas kernels, call(): pl.pallas_call(kernel, out_shape=[jax.ShapeDtypeStruct(*o) if len(o) == 2...  13 us
    ppermute x6, starting transfers between devices, swap(): return lax.ppermute(values, axis, [(i, i ^ distance) for i in range(size)])  8.85 us
    all_to_all x1, waiting for transfers between devices, body(): lax.all_to_all(outgoing, ('var', 'samp'), split_axis=0, concat_axis=0)  6.86 us
    ppermute x3, starting transfers between devices, body(): backs.append(lax.ppermute(m, ('var', 'samp'), pairs))  4.42 us
    ppermute x6, waiting for transfers between devices, swap(): return lax.ppermute(values, axis, [(i, i ^ distance) for i in range(size)])  4.3 us
    all_to_all x1, starting transfers between devices, body(): lax.all_to_all(outgoing, ('var', 'samp'), split_axis=0, concat_axis=0)  3.25 us
    ppermute x3, waiting for transfers between devices, body(): backs.append(lax.ppermute(m, ('var', 'samp'), pairs))  2.66 us
  transfers between devices with their start and end apart: 10, of which 7 were waited for; matrix products, arithmetic and copies ran while one was open for 0% of the time, Pallas kernels for 19%

profile of v17, /device:TPU:0, one launch (start us, length us, event | category | flops | bytes accessed | tf_op | source)
XLA Modules:
  0.0 44.1 jit_solution(5247896627816177915)
XLA Ops:
  0.6 3.1 %collective-permute-start = (f32[16,768]{1,0:T(8,128)}, f32[16,768]{1,0:T(8,128)S(1)}, u32[]{:S(2)}, u32[]{:S(2)}) collective-permute-start(f32[16,768]{1,0:T(8,128)} %bitcast.8), channel_id=1, source_target_pairs={{0,8},{8,0},{16,24},{24,16},{1,9},{9,1},{17,25},{25,17},{2,10},{10... | collective-permute-start | bytes 147464 | tf_op jit(solution)/shard_map/ppermute | solution.py:22
  3.7 2.7 %shard_map.112 = (bf16[384,3072]{1,0:T(8,128)(2,1)S(1)}, f32[8,128]{1,0:T(8,128)S(1)}) custom-call(f32[16,768]{1,0:T(8,128)} %bitcast.15, f32[16,768]{1,0:T(8,128)} %bitcast.9, f32[16,768]{1,0:T(8,128)} %bitcast.18, s32[768,3072]{1,0:T(8,128)} %call_hbm.3), custom_call_target="tpu_custom_call" | custom-call | bytes 4718592 | tf_op jit(solution)/shard_map/pallas_call | solution.py:400
  6.5 2.7 %collective-permute-start.1 = (bf16[32,768]{1,0:T(8,128)(2,1)S(1)}, bf16[32,768]{1,0:T(8,128)(2,1)S(1)}, u32[]{:S(2)}, u32[]{:S(2)}) collective-permute-start(bf16[32,768]{1,0:T(8,128)(2,1)S(1)} %shard_map.111.pair_ref), channel_id=1, source_target_pairs={{0,16},{8,24},{16,0},{24,8},{1,17},{9,25},{17,1},{25,9},{2,18},{10... | collective-permute-start | bytes 147464 | tf_op jit(solution)/shard_map/ppermute | solution.py:22
  9.1 0.5 %shard_map.113.done_ref = f32[32,384]{1,0:T(8,128)S(1)} custom-call(bf16[32,768]{1,0:T(8,128)(2,1)S(1)} %shard_map.111.pair_ref, bf16[384,3072]{1,0:T(8,128)(2,1)S(1)} %get-tuple-element.25.called_first), custom_call_target="tpu_custom_call" | custom-call | flops 301989888 | bytes 1179648 | tf_op jit(solution)/shard_map/pallas_call | solution.py:400
  9.6 0.0 copy-done
  9.6 3.6 %shard_map.114 = (bf16[768,3072]{1,0:T(8,128)(2,1)S(1)}, bf16[384,3072]{1,0:T(8,128)(2,1)S(1)}, f32[40,768]{1,0:T(8,128)S(1)}) custom-call(bf16[32,768]{1,0:T(8,128)(2,1)S(1)} %shard_map.111.pair_ref, bf16[384,3072]{1,0:T(8,128)(2,1)S(1)} %get-tuple-element.25.called_first, f32[32,384]{1,0:T(8,128)S(1)} %shard_map.113.done_ref, s32[768,3072]{1,0:T(8,128)S(1)} %copy-done, ...), custom_call_target="tpu_custom_call" | custom-call | flops 1207959552 | bytes 9437184 | tf_op jit(solution)/shard_map/pallas_call | solution.py:400
  13.3 0.0 copy-start.1
  13.3 0.0 copy-start.3
  13.3 0.0 copy-start.5
  13.3 1.6 %shard_map.115.own_ref = f32[40,896]{1,0:T(8,128)S(1)} custom-call(bf16[32,768]{1,0:T(8,128)(2,1)S(1)} %collective-permute-done.1.pair_ref, bf16[768,3072]{1,0:T(8,128)(2,1)S(1)} %get-tuple-element.26.coded_ref, bf16[384,3072]{1,0:T(8,128)(2,1)S(1)} %get-tuple-element.25.called_first, bf16[384,3072]{1,0:T(8,128)(2,1)S(1)} %get-tuple-element.27.called_ref, ...), custom_call_target="tpu_custom_call" | custom-call | flops 1207959552 | bytes 4718592 | tf_op jit(solution)/shard_map/pallas_call | solution.py:400
  14.9 0.1 collective-permute-start.2
  14.9 1.4 %collective-permute-done.2.other_ref = f32[40,896]{1,0:T(8,128)S(1)} collective-permute-done((f32[40,896]{1,0:T(8,128)S(1)}, f32[40,896]{1,0:T(8,128)S(1)}, u32[]{:S(2)}, u32[]{:S(2)}) %collective-permute-start.2) | collective-permute-done | bytes 143392 | tf_op jit(solution)/shard_map/ppermute | solution.py:22
  16.3 2.3 %collective-permute-start.3 = (bf16[32,896]{1,0:T(8,128)(2,1)S(1)}, bf16[32,896]{1,0:T(8,128)(2,1)S(1)}, u32[]{:S(2)}, u32[]{:S(2)}) collective-permute-start(bf16[32,896]{1,0:T(8,128)(2,1)S(1)} %get-tuple-element.31), channel_id=1, source_target_pairs={{0,7},{1,6},{2,5},{3,4},{4,3},{5,2},{6,1},{7,0},{8,15},{9,14},{10,... | collective-permute-start | bytes 172040 | tf_op jit(solution)/shard_map/ppermute | solution.py:22
  18.6 0.5 %collective-permute-start.4 = (bf16[32,896]{1,0:T(8,128)(2,1)S(1)}, bf16[32,896]{1,0:T(8,128)(2,1)S(1)}, u32[]{:S(2)}, u32[]{:S(2)}) collective-permute-start(bf16[32,896]{1,0:T(8,128)(2,1)S(1)} %get-tuple-element.32), channel_id=1, source_target_pairs={{0,5},{1,4},{2,7},{3,6},{4,1},{5,0},{6,3},{7,2},{8,13},{9,12},{10,... | collective-permute-start | bytes 172040 | tf_op jit(solution)/shard_map/ppermute | solution.py:22
  19.1 0.3 collective-permute-start.5
  19.4 0.6 %shard_map.120.cross_ref = f32[40,1024]{1,0:T(8,128)S(1)} custom-call(s32[1,768]{1,0:T(1,128)S(1)} %copy-done.5, f32[16,768]{1,0:T(8,128)S(1)} %bitcast.16, f32[16,768]{1,0:T(8,128)S(1)} %bitcast.11, s32[768,1024]{1,0:T(8,128)S(1)} %copy-done.1, f32[40,896]{1,0:T(8,128)S(1)} %get-tuple-element.30.total_ref.after_ref), custom_call_target="tpu_custom_call" | custom-call | flops 220200960 | bytes 3145728 | tf_op jit(solution)/shard_map/pallas_call | solution.py:400
  20.0 1.2 %collective-permute-done.3.rest_0_ = bf16[32,896]{1,0:T(8,128)(2,1)S(1)} collective-permute-done((bf16[32,896]{1,0:T(8,128)(2,1)S(1)}, bf16[32,896]{1,0:T(8,128)(2,1)S(1)}, u32[]{:S(2)}, u32[]{:S(2)}) %collective-permute-start.3) | collective-permute-done | bytes 57376 | tf_op jit(solution)/shard_map/ppermute | solution.py:22
  21.2 1.2 %collective-permute-done.4.rest_1_ = bf16[32,896]{1,0:T(8,128)(2,1)S(1)} collective-permute-done((bf16[32,896]{1,0:T(8,128)(2,1)S(1)}, bf16[32,896]{1,0:T(8,128)(2,1)S(1)}, u32[]{:S(2)}, u32[]{:S(2)}) %collective-permute-start.4) | collective-permute-done | bytes 57376 | tf_op jit(solution)/shard_map/ppermute | solution.py:22
  22.3 0.6 %collective-permute-done.5.rest_2_ = bf16[32,896]{1,0:T(8,128)(2,1)S(1)} collective-permute-done((bf16[32,896]{1,0:T(8,128)(2,1)S(1)}, bf16[32,896]{1,0:T(8,128)(2,1)S(1)}, u32[]{:S(2)}, u32[]{:S(2)}) %collective-permute-start.5) | collective-permute-done | bytes 57376 | tf_op jit(solution)/shard_map/ppermute | solution.py:22
  22.9 1.1 %shard_map.117 = (bf16[32,768]{1,0:T(8,128)(2,1)S(1)}, f32[8,128]{1,0:T(8,128)S(1)}, bf16[16,896]{1,0:T(8,128)(2,1)S(1)}, bf16[16,896]{1,0:T(8,128)(2,1)S(1)}, bf16[16,896]{1,0:T(8,128)(2,1)S(1)}) custom-call(f32[40,896]{1,0:T(8,128)S(1)} %get-tuple-element.30.total_ref.after_ref, bf16[768,3072]{1,0:T(8,128)(2,1)S(1)} %get-tuple-element.26.coded_ref, ...), custom_call_target="tpu_custom_call" | custom-call | flops 1207959552 | bytes 4718592 | tf_op jit(solution)/shard_map/pallas_call | solution.py:400
  24.1 2.3 %collective-permute-start.6 = (bf16[16,896]{1,0:T(8,128)(2,1)S(1)}, bf16[16,896]{1,0:T(8,128)(2,1)S(1)}, u32[]{:S(2)}, u32[]{:S(2)}) collective-permute-start(bf16[16,896]{1,0:T(8,128)(2,1)S(1)} %get-tuple-element.36), channel_id=1, source_target_pairs={{0,24},{1,9},{2,26},{3,11},{4,28},{5,13},{6,30},{7,15},{8,16},{9,1... | collective-permute-start | bytes 86024 | tf_op jit(solution)/shard_map/ppermute | solution.py:502
  26.3 0.8 %collective-permute-start.7 = (bf16[16,896]{1,0:T(8,128)(2,1)S(1)}, bf16[16,896]{1,0:T(8,128)(2,1)S(1)}, u32[]{:S(2)}, u32[]{:S(2)}) collective-permute-start(bf16[16,896]{1,0:T(8,128)(2,1)S(1)} %get-tuple-element.37), channel_id=1, source_target_pairs={{0,16},{1,25},{2,18},{3,27},{4,20},{5,29},{6,22},{7,31},{8,24},{9,... | collective-permute-start | bytes 86024 | tf_op jit(solution)/shard_map/ppermute | solution.py:502
  27.1 1.4 %collective-permute-start.8 = (bf16[16,896]{1,0:T(8,128)(2,1)S(1)}, bf16[16,896]{1,0:T(8,128)(2,1)S(1)}, u32[]{:S(2)}, u32[]{:S(2)}) collective-permute-start(bf16[16,896]{1,0:T(8,128)(2,1)S(1)} %get-tuple-element.38), channel_id=1, source_target_pairs={{0,8},{1,17},{2,10},{3,19},{4,12},{5,21},{6,14},{7,23},{8,0},{9,25... | collective-permute-start | bytes 86024 | tf_op jit(solution)/shard_map/ppermute | solution.py:502
  28.5 0.4 shard_map.118.rest_0_
  28.9 0.8 %collective-permute-done.6.rest_1_ = bf16[16,896]{1,0:T(8,128)(2,1)S(1)} collective-permute-done((bf16[16,896]{1,0:T(8,128)(2,1)S(1)}, bf16[16,896]{1,0:T(8,128)(2,1)S(1)}, u32[]{:S(2)}, u32[]{:S(2)}) %collective-permute-start.6) | collective-permute-done | bytes 28704 | tf_op jit(solution)/shard_map/ppermute | solution.py:502
  29.8 1.8 %collective-permute-done.7.rest_2_ = bf16[16,896]{1,0:T(8,128)(2,1)S(1)} collective-permute-done((bf16[16,896]{1,0:T(8,128)(2,1)S(1)}, bf16[16,896]{1,0:T(8,128)(2,1)S(1)}, u32[]{:S(2)}, u32[]{:S(2)}) %collective-permute-start.7) | collective-permute-done | bytes 28704 | tf_op jit(solution)/shard_map/ppermute | solution.py:502
  31.5 0.0 collective-permute-done.8.rest_3_
  31.6 0.9 %shard_map.121 = (f32[32,1,640]{2,1,0:T(1,128)}, f32[16,768]{1,0:T(8,128)S(1)}) custom-call(f32[1,16]{1,0:T(1,128)S(1)} %bitcast.21, f32[16,768]{1,0:T(8,128)S(1)} %bitcast.12, f32[16,768]{1,0:T(8,128)S(1)} %bitcast.19, f32[40,1024]{1,0:T(8,128)S(1)} %shard_map.120.cross_ref, f32[16,896]{1,0:T(8,128)S(1)} %shard_map.118.rest_0_, ...), custom_call_target="tpu_custom_call" | custom-call | bytes 81920 | tf_op jit(solution)/shard_map/pallas_call | solution.py:400
  32.5 3.2 %all-to-all-start = ((f32[32,1,640]{2,1,0:T(1,128)}), f32[32,1,640]{2,1,0:T(1,128)S(1)}, u32[]{:S(2)}, u32[]{:S(2)}) async-start(f32[32,1,640]{2,1,0:T(1,128)} %get-tuple-element.41), calls=%async_computation | async-start | bytes 163840 | tf_op jit(solution)/shard_map/all_to_all | solution.py:530
  35.7 0.7 %shard_map.119 = (f32[16,768]{1,0:T(8,128)}, f32[16,768]{1,0:T(8,128)}, f32[16,128]{1,0:T(8,128)S(1)}) custom-call(f32[1,16]{1,0:T(1,128)S(1)} %bitcast.22, f32[16,768]{1,0:T(8,128)S(1)} %bitcast.13, f32[16,768]{1,0:T(8,128)S(1)} %bitcast.20, f32[16,768]{1,0:T(8,128)S(1)} %bitcast.17, f32[16,896]{1,0:T(8,128)S(1)} %shard_map.118.rest_0_, ...), custom_call_target="tpu_custom_call" | custom-call | bytes 1048576 | tf_op jit(solution)/shard_map/pallas_call | solution.py:400
  36.5 6.9 %all-to-all-done.came_ref = f32[32,1,640]{2,1,0:T(1,128)S(1)} async-done(((f32[32,1,640]{2,1,0:T(1,128)}), f32[32,1,640]{2,1,0:T(1,128)S(1)}, u32[]{:S(2)}, u32[]{:S(2)}) %all-to-all-start) | async-done | bytes 81952 | tf_op jit(solution)/shard_map/all_to_all | solution.py:530
  43.3 0.8 %shard_map.122 = (f32[16,768]{1,0:T(8,128)}, f32[16,32]{1,0:T(8,128)}) custom-call(f32[32,1,640]{2,1,0:T(1,128)S(1)} %all-to-all-done.came_ref, f32[16,128]{1,0:T(8,128)S(1)} %get-tuple-element.42.stats_ref, f32[16,768]{1,0:T(8,128)S(1)} %get-tuple-element.43.res_ref, f32[16,768]{1,0:T(8,128)S(1)} %bitcast.14), custom_call_target="tpu_custom_call" | custom-call | tf_op jit(solution)/shard_map/pallas_call | solution.py:400
  (14 shorter events, 0.1 us)
Async XLA Ops:
  0.6 5.8 %collective-permute-start = (f32[16,768]{1,0:T(8,128)}, f32[16,768]{1,0:T(8,128)S(1)}, u32[]{:S(2)}, u32[]{:S(2)}) collective-permute-start(f32[16,768]{1,0:T(8,128)} %bitcast.8), channel_id=1, source_target_pairs={{0,8},{8,0},{16,24},{24,16},{1,9},{9,1},{17,25},{25,17},{2,10},{10... | collective-permute-start | bytes 147464 | tf_op jit(solution)/shard_map/ppermute | solution.py:22
  3.7 2.7 %copy-start.2 = (f32[768,16]{0,1:T(8,128)S(1)}, f32[768,16]{0,1:T(8,128)}, u32[]{:S(2)}) copy-start(f32[768,16]{0,1:T(8,128)} %param.15) | copy-start | bytes 147460
  3.7 5.9 %copy-start = (s32[768,3072]{1,0:T(8,128)S(1)}, s32[768,3072]{1,0:T(8,128)}, u32[]{:S(2)}) copy-start(s32[768,3072]{1,0:T(8,128)} %gen_ref.1) | copy-start | bytes 28311556
  6.5 6.8 %collective-permute-start.1 = (bf16[32,768]{1,0:T(8,128)(2,1)S(1)}, bf16[32,768]{1,0:T(8,128)(2,1)S(1)}, u32[]{:S(2)}, u32[]{:S(2)}) collective-permute-start(bf16[32,768]{1,0:T(8,128)(2,1)S(1)} %shard_map.111.pair_ref), channel_id=1, source_target_pairs={{0,16},{8,24},{16,0},{24,8},{1,17},{9,25},{17,1},{25,9},{2,18},{10... | collective-permute-start | bytes 147464 | tf_op jit(solution)/shard_map/ppermute | solution.py:22
  13.3 6.1 %copy-start.1 = (s32[768,1024]{1,0:T(8,128)S(1)}, s32[768,1024]{1,0:T(8,128)}, u32[]{:S(2)}) copy-start(s32[768,1024]{1,0:T(8,128)} %dose_ref.1) | copy-start | bytes 9437188
  13.3 6.1 %copy-start.3 = (f32[768,16]{0,1:T(8,128)S(1)}, f32[768,16]{0,1:T(8,128)}, u32[]{:S(2)}) copy-start(f32[768,16]{0,1:T(8,128)} %param.13) | copy-start | bytes 147460
  13.3 6.1 %copy-start.5 = (s32[1,768]{1,0:T(1,128)S(1)}, s32[1,768]{1,0:T(1,128)}, u32[]{:S(2)}) copy-start(s32[1,768]{1,0:T(1,128)} %order_ref.1) | copy-start | bytes 9220
  14.9 1.4 %collective-permute-start.2 = (f32[40,896]{1,0:T(8,128)S(1)}, f32[40,896]{1,0:T(8,128)S(1)}, u32[]{:S(2)}, u32[]{:S(2)}) collective-permute-start(f32[40,896]{1,0:T(8,128)S(1)} %shard_map.115.own_ref), channel_id=1, source_target_pairs={{0,1},{1,0},{2,3},{3,2},{4,5},{5,4},{6,7},{7,6},{8,9},{9,8},{10,11... | collective-permute-start | bytes 430088 | tf_op jit(solution)/shard_map/ppermute | solution.py:22
  16.3 4.9 %collective-permute-start.3 = (bf16[32,896]{1,0:T(8,128)(2,1)S(1)}, bf16[32,896]{1,0:T(8,128)(2,1)S(1)}, u32[]{:S(2)}, u32[]{:S(2)}) collective-permute-start(bf16[32,896]{1,0:T(8,128)(2,1)S(1)} %get-tuple-element.31), channel_id=1, source_target_pairs={{0,7},{1,6},{2,5},{3,4},{4,3},{5,2},{6,1},{7,0},{8,15},{9,14},{10,... | collective-permute-start | bytes 172040 | tf_op jit(solution)/shard_map/ppermute | solution.py:22
  18.6 3.8 %collective-permute-start.4 = (bf16[32,896]{1,0:T(8,128)(2,1)S(1)}, bf16[32,896]{1,0:T(8,128)(2,1)S(1)}, u32[]{:S(2)}, u32[]{:S(2)}) collective-permute-start(bf16[32,896]{1,0:T(8,128)(2,1)S(1)} %get-tuple-element.32), channel_id=1, source_target_pairs={{0,5},{1,4},{2,7},{3,6},{4,1},{5,0},{6,3},{7,2},{8,13},{9,12},{10,... | collective-permute-start | bytes 172040 | tf_op jit(solution)/shard_map/ppermute | solution.py:22
  19.1 3.9 %collective-permute-start.5 = (bf16[32,896]{1,0:T(8,128)(2,1)S(1)}, bf16[32,896]{1,0:T(8,128)(2,1)S(1)}, u32[]{:S(2)}, u32[]{:S(2)}) collective-permute-start(bf16[32,896]{1,0:T(8,128)(2,1)S(1)} %get-tuple-element.33), channel_id=1, source_target_pairs={{0,3},{1,2},{2,1},{3,0},{4,7},{5,6},{6,5},{7,4},{8,11},{9,10},{10,... | collective-permute-start | bytes 172040 | tf_op jit(solution)/shard_map/ppermute | solution.py:22
  24.1 5.7 %collective-permute-start.6 = (bf16[16,896]{1,0:T(8,128)(2,1)S(1)}, bf16[16,896]{1,0:T(8,128)(2,1)S(1)}, u32[]{:S(2)}, u32[]{:S(2)}) collective-permute-start(bf16[16,896]{1,0:T(8,128)(2,1)S(1)} %get-tuple-element.36), channel_id=1, source_target_pairs={{0,24},{1,9},{2,26},{3,11},{4,28},{5,13},{6,30},{7,15},{8,16},{9,1... | collective-permute-start | bytes 86024 | tf_op jit(solution)/shard_map/ppermute | solution.py:502
  26.3 5.2 %collective-permute-start.7 = (bf16[16,896]{1,0:T(8,128)(2,1)S(1)}, bf16[16,896]{1,0:T(8,128)(2,1)S(1)}, u32[]{:S(2)}, u32[]{:S(2)}) collective-permute-start(bf16[16,896]{1,0:T(8,128)(2,1)S(1)} %get-tuple-element.37), channel_id=1, source_target_pairs={{0,16},{1,25},{2,18},{3,27},{4,20},{5,29},{6,22},{7,31},{8,24},{9,... | collective-permute-start | bytes 86024 | tf_op jit(solution)/shard_map/ppermute | solution.py:502
  27.1 4.5 %collective-permute-start.8 = (bf16[16,896]{1,0:T(8,128)(2,1)S(1)}, bf16[16,896]{1,0:T(8,128)(2,1)S(1)}, u32[]{:S(2)}, u32[]{:S(2)}) collective-permute-start(bf16[16,896]{1,0:T(8,128)(2,1)S(1)} %get-tuple-element.38), channel_id=1, source_target_pairs={{0,8},{1,17},{2,10},{3,19},{4,12},{5,21},{6,14},{7,23},{8,0},{9,25... | collective-permute-start | bytes 86024 | tf_op jit(solution)/shard_map/ppermute | solution.py:502
  28.5 3.1 %copy-start.4 = (f32[768,16]{0,1:T(8,128)S(1)}, f32[768,16]{0,1:T(8,128)}, u32[]{:S(2)}) copy-start(f32[768,16]{0,1:T(8,128)} %param.14) | copy-start | bytes 147460
  28.5 3.1 %copy-start.6 = (f32[16]{0:T(128)S(1)}, f32[16]{0:T(128)}, u32[]{:S(2)}) copy-start(f32[16]{0:T(128)} %param.12) | copy-start | bytes 196
  32.5 10.9 %all-to-all-start = ((f32[32,1,640]{2,1,0:T(1,128)}), f32[32,1,640]{2,1,0:T(1,128)S(1)}, u32[]{:S(2)}, u32[]{:S(2)}) async-start(f32[32,1,640]{2,1,0:T(1,128)} %get-tuple-element.41), calls=%async_computation | async-start | bytes 163840 | tf_op jit(solution)/shard_map/all_to_all | solution.py:530

commit v18 on v16

--- a/solution.py
+++ b/solution.py
@@ -291,7 +291,9 @@
         ref[:, own:] = sums_block(sums)
 
 
-def own_kernel(variants, scaled_ref, sums_ref, coded_ref, called_first, called_ref, own_ref):
+def own_kernel(variants, scaled_ref, sums_ref, coded_ref, called_first, called_ref,
+               cross_ref, other_ref, own_ref, both_ref):
+    both_ref[...] = cross_ref[...] + other_ref[...]
     own = own_ref.shape[1] - LANES
     p = lax.axis_index("var")
     own_ref[:, :own] = term(scaled_ref, coded_ref, called_first, called_ref, p, own, variants)
@@ -312,16 +314,19 @@
     return back, column, noise, step
 
 
-def norm_kernel(variants, width, noise_ref, dir_ref, res_ref, cross_ref, *rest):
+def norm_kernel(variants, width, noise_ref, dir_ref, res_ref, both_ref, *rest):
     refs, (out_ref, new_ref) = rest[:-2], rest[-2:]
     back, _, noise, step = step_of(refs, noise_ref[...], variants)
     new = res_ref[...] - step * (noise * dir_ref[...] + back)
     new_ref[...] = new
     norm = as_row({6: jnp.sum(new * new, axis=1, keepdims=True)})
-    cross = cross_ref[0:16] + step * cross_ref[16:32]
-    dose = cross_ref[32:40]
-    lane = lane_of((16, LANES))
-    row = lax.broadcasted_iota(jnp.int32, (16, LANES), 0)
+    both = both_ref[...]
+    core = lax.axis_index("samp") % 2
+    half = lambda x: jnp.where(core == 0, x[0:8], x[8:16])
+    cross = half(both[0:16]) + half(step) * half(both[16:32])
+    dose = both[32:40]
+    lane = lane_of((8, LANES))
+    row = lax.broadcasted_iota(jnp.int32, (8, LANES), 0)
     turned = {}
 
     def turn(values, name, tile, by):
@@ -332,16 +337,16 @@
 
     for j in range(out_ref.shape[0]):
         tile, inside = (j * width) // LANES * LANES, (j * width) % LANES
-        block = jnp.zeros((16, LANES), F32)
+        block = jnp.zeros((8, LANES), F32)
         for m in range(4):
-            here = (row // 4 == m) & (lane >= 32 * m) & (lane < 32 * m + width)
+            here = (row // 2 == m) & (lane >= 32 * m) & (lane < 32 * m + width)
             block = jnp.where(here, turn(cross, "cross", tile, (32 * m - inside) % LANES), block)
-        block = block[0:8] + block[8:16]
         block = block[0:4] + block[4:8]
+        block = block[0:2] + block[2:4]
         last = jnp.where(lane[0:1] < width, turn(dose, "dose", tile, -inside % LANES)[0:1], norm)
-        for k in range(4):
+        for k in range(2):
             out_ref[j, :, k * LANES : (k + 1) * LANES] = block[k : k + 1]
-        out_ref[j, :, 4 * LANES :] = last
+        out_ref[j, :, 2 * LANES :] = last
 
 
 def new_kernel(variants, noise_ref, dir_ref, res_ref, sol_ref, *rest):
@@ -357,17 +362,22 @@
 
 
 def last_kernel(samples, width, came_ref, stats_ref, res_ref, dir_ref, out_ref, score_out):
-    total = jnp.sum(came_ref[...], axis=0)
-    last = total[:, 4 * LANES :]
-    out_ref[...] = res_ref[...] + (as_column(last, 6) / (stats_ref[:, 0:1] + 1e-06)) * dir_ref[...]
-    row = lax.broadcasted_iota(jnp.int32, (16, LANES), 0)
-    spread = jnp.zeros((16, LANES), F32)
-    for k in range(4):
-        spread = jnp.where(row % 4 == k, total[:, k * LANES : (k + 1) * LANES], spread)
-    cross = spread
-    for m in range(1, 4):
-        cross = jnp.where(row // 4 == m, pltpu.roll(spread, LANES - 32 * m, 1), cross)
-    dose = last
+    row = lax.broadcasted_iota(jnp.int32, (8, LANES), 0)
+    halves_of, lasts = [], []
+    for core in range(2):
+        total = came_ref[core]
+        for i in range(core + 2, came_ref.shape[0], 2):
+            total = total + came_ref[i]
+        spread = jnp.where(row % 2 == 0, total[:, :LANES], total[:, LANES : 2 * LANES])
+        part = spread
+        for m in range(1, 4):
+            part = jnp.where(row // 2 == m, pltpu.roll(spread, LANES - 32 * m, 1), part)
+        halves_of.append(part)
+        lasts.append(total[:, 2 * LANES :])
+    new_norm = as_column(lasts[0] + lasts[1], 6)
+    out_ref[...] = res_ref[...] + (new_norm / (stats_ref[:, 0:1] + 1e-06)) * dir_ref[...]
+    cross = jnp.concatenate(halves_of, axis=0)
+    dose = lasts[0]
     sol_sum, sol_square = stats_ref[:, 1:2], stats_ref[:, 2:3]
     dose_freq = (dose / 100.0 + 1.0) / (2.0 * samples + 2.0)
     dose_spread = jnp.sqrt(2.0 * dose_freq * (1.0 - dose_freq))
@@ -467,6 +477,16 @@
         moved=1 * MIB,
     )
     arrived = [swap(messages[k], "samp", 2 * (k + 1) + 1) for k in reversed(range(n_chips - 1))]
+    (cross,) = call(
+        dosage_kernel,
+        [((2 * rhs + 8, imputed), F32)],
+        [VMEM] * 5,
+        (sample_order, sol, dire, dosage, total),
+        flops=2 * 80 * own * (own + imputed),
+        moved=4 * own * imputed,
+    )
+    cross_other = swap(cross, "samp", 1)
+
     wide = own + LANES
     scaled, sums, *messages = call(
         functools.partial(back_kernel, variants, len(arrived)),
@@ -477,32 +497,24 @@
         moved=2 * rows * shard,
     )
     backs = [swap(messages[k], "var", k + 1) for k in reversed(range(n_var - 1))]
-    (mine_back,) = call(
+    mine_back, both = call(
         functools.partial(own_kernel, variants),
-        [((rhs, wide), F32)],
-        [VMEM] * 5,
-        (scaled, sums, coded, called_a, called_b),
+        [((rhs, wide), F32), (cross.shape, F32)],
+        [VMEM] * 7,
+        (scaled, sums, coded, called_a, called_b, cross, cross_other),
         flops=rows * shard * 256,
         moved=rows * shard,
     )
     backs = [mine_back] + backs
-    (cross,) = call(
-        dosage_kernel,
-        [((2 * rhs + 8, imputed), F32)],
-        [VMEM] * 5,
-        (sample_order, sol, dire, dosage, total),
-        flops=2 * 80 * own * (own + imputed),
-        moved=4 * own * imputed,
-    )
 
 
     n_all = n_var * n_samp
     outgoing, res_keep = call(
         functools.partial(norm_kernel, variants, width),
-        [((n_all, 1, 5 * LANES), F32), ((rhs, own), F32)],
+        [((n_all, 1, 3 * LANES), F32), ((rhs, own), F32)],
         [VMEM] * (4 + n_var),
-        (noise, dire, res, cross, *backs),
-        moved=4 * 5 * n_all * LANES,
+        (noise, dire, res, both, *backs),
+        moved=4 * 3 * n_all * LANES,
     )
     came = lax.all_to_all(outgoing, ("var", "samp"), split_axis=0, concat_axis=0)
     sol_new, res_new, stats = call(

time: 44 us -> 43.7 us (level)
  waiting for transfers between devices: 13.7 us -> 13 us
    ppermute x9 -> x10, waiting for transfers between devices: 6.82 us -> 6.39 us  [swap(): return lax.ppermute(values, axis, [(i, i ^ distance) for i in range(size)])]
    ppermute x9 -> x10, starting transfers between devices: 13.3 us -> 13.7 us  [swap(): return lax.ppermute(values, axis, [(i, i ^ distance) for i in range(size)])]
  transfers between devices with their start and end apart: 10 -> 11, of which waited for: 7 -> 7; matrix products, arithmetic and copies ran while one was open for 0% -> 0% of each run, Pallas kernels for 19% -> 22%
where the time goes in v18:
time: 43.7 us; the launch traced here: 43.5 us
  starting transfers between devices  17 us (39%)
  waiting for transfers between devices  13 us (30%)
  Pallas kernels  12.7 us (29%)
  between operations  0.76 us (2%)
    ppermute x10, starting transfers between devices, swap(): return lax.ppermute(values, axis, [(i, i ^ distance) for i in range(size)])  13.7 us
    pallas_call x12, Pallas kernels, call(): pl.pallas_call(kernel, out_shape=[jax.ShapeDtypeStruct(*o) if len(o) == 2...  12.7 us
    all_to_all x1, waiting for transfers between devices, body(): lax.all_to_all(outgoing, ('var', 'samp'), split_axis=0, concat_axis=0)  6.59 us
    ppermute x10, waiting for transfers between devices, swap(): return lax.ppermute(values, axis, [(i, i ^ distance) for i in range(size)])  6.39 us
    all_to_all x1, starting transfers between devices, body(): lax.all_to_all(outgoing, ('var', 'samp'), split_axis=0, concat_axis=0)  3.34 us
  transfers between devices with their start and end apart: 11, of which 7 were waited for; matrix products, arithmetic and copies ran while one was open for 0% of the time, Pallas kernels for 22%

profile of v18, /device:TPU:0, one launch (start us, length us, event | category | flops | bytes accessed | tf_op | source)
XLA Modules:
  0.0 43.5 jit_solution(3900799455436701062)
XLA Ops:
  0.6 3.1 %collective-permute-start = (f32[16,768]{1,0:T(8,128)}, f32[16,768]{1,0:T(8,128)S(1)}, u32[]{:S(2)}, u32[]{:S(2)}) collective-permute-start(f32[16,768]{1,0:T(8,128)} %bitcast.8), channel_id=1, source_target_pairs={{0,8},{8,0},{16,24},{24,16},{1,9},{9,1},{17,25},{25,17},{2,10},{10... | collective-permute-start | bytes 147464 | tf_op jit(solution)/shard_map/ppermute | solution.py:22
  3.7 3.2 %shard_map.112 = (bf16[512,3072]{1,0:T(8,128)(2,1)S(1)}, f32[8,128]{1,0:T(8,128)S(1)}) custom-call(f32[16,768]{1,0:T(8,128)} %bitcast.15, f32[16,768]{1,0:T(8,128)} %bitcast.9, f32[16,768]{1,0:T(8,128)} %bitcast.18, s32[768,3072]{1,0:T(8,128)} %call_hbm.3), custom_call_target="tpu_custom_call" | custom-call | bytes 6291456 | tf_op jit(solution)/shard_map/pallas_call | solution.py:390
  7.0 2.7 %collective-permute-start.1 = (bf16[32,768]{1,0:T(8,128)(2,1)S(1)}, bf16[32,768]{1,0:T(8,128)(2,1)S(1)}, u32[]{:S(2)}, u32[]{:S(2)}) collective-permute-start(bf16[32,768]{1,0:T(8,128)(2,1)S(1)} %shard_map.111.pair_ref), channel_id=1, source_target_pairs={{0,16},{8,24},{16,0},{24,8},{1,17},{9,25},{17,1},{25,9},{2,18},{10... | collective-permute-start | bytes 147464 | tf_op jit(solution)/shard_map/ppermute | solution.py:22
  9.6 0.6 %shard_map.113.done_ref = f32[32,512]{1,0:T(8,128)S(1)} custom-call(bf16[32,768]{1,0:T(8,128)(2,1)S(1)} %shard_map.111.pair_ref, bf16[512,3072]{1,0:T(8,128)(2,1)S(1)} %get-tuple-element.27.called_first), custom_call_target="tpu_custom_call" | custom-call | flops 402653184 | bytes 1572864 | tf_op jit(solution)/shard_map/pallas_call | solution.py:390
  10.2 0.0 copy-done
  10.2 2.8 %shard_map.114 = (bf16[768,3072]{1,0:T(8,128)(2,1)S(1)}, bf16[256,3072]{1,0:T(8,128)(2,1)S(1)}, f32[40,768]{1,0:T(8,128)S(1)}) custom-call(bf16[32,768]{1,0:T(8,128)(2,1)S(1)} %shard_map.111.pair_ref, bf16[512,3072]{1,0:T(8,128)(2,1)S(1)} %get-tuple-element.27.called_first, f32[32,512]{1,0:T(8,128)S(1)} %shard_map.113.done_ref, s32[768,3072]{1,0:T(8,128)S(1)} %copy-done, ...), custom_call_target="tpu_custom_call" | custom-call | flops 1207959552 | bytes 9437184 | tf_op jit(solution)/shard_map/pallas_call | solution.py:390
  13.0 0.0 collective-permute-done.1.pair_ref
  13.0 0.0 copy-start.1
  13.1 0.0 copy-start.3
  13.1 0.0 copy-start.5
  13.1 1.5 %shard_map.115.own_ref = f32[40,896]{1,0:T(8,128)S(1)} custom-call(bf16[32,768]{1,0:T(8,128)(2,1)S(1)} %collective-permute-done.1.pair_ref, bf16[768,3072]{1,0:T(8,128)(2,1)S(1)} %get-tuple-element.28.coded_ref, bf16[512,3072]{1,0:T(8,128)(2,1)S(1)} %get-tuple-element.27.called_first, bf16[256,3072]{1,0:T(8,128)(2,1)S(1)} %get-tuple-element.29.called_ref, ...), custom_call_target="tpu_custom_call" | custom-call | flops 1207959552 | bytes 4718592 | tf_op jit(solution)/shard_map/pallas_call | solution.py:390
  14.6 0.1 collective-permute-start.2
  14.7 1.4 %collective-permute-done.2.other_ref = f32[40,896]{1,0:T(8,128)S(1)} collective-permute-done((f32[40,896]{1,0:T(8,128)S(1)}, f32[40,896]{1,0:T(8,128)S(1)}, u32[]{:S(2)}, u32[]{:S(2)}) %collective-permute-start.2) | collective-permute-done | bytes 143392 | tf_op jit(solution)/shard_map/ppermute | solution.py:22
  16.1 2.3 %collective-permute-start.3 = (bf16[32,896]{1,0:T(8,128)(2,1)S(1)}, bf16[32,896]{1,0:T(8,128)(2,1)S(1)}, u32[]{:S(2)}, u32[]{:S(2)}) collective-permute-start(bf16[32,896]{1,0:T(8,128)(2,1)S(1)} %get-tuple-element.33), channel_id=1, source_target_pairs={{0,7},{1,6},{2,5},{3,4},{4,3},{5,2},{6,1},{7,0},{8,15},{9,14},{10,... | collective-permute-start | bytes 172040 | tf_op jit(solution)/shard_map/ppermute | solution.py:22
  18.3 0.5 %collective-permute-start.4 = (bf16[32,896]{1,0:T(8,128)(2,1)S(1)}, bf16[32,896]{1,0:T(8,128)(2,1)S(1)}, u32[]{:S(2)}, u32[]{:S(2)}) collective-permute-start(bf16[32,896]{1,0:T(8,128)(2,1)S(1)} %get-tuple-element.34), channel_id=1, source_target_pairs={{0,5},{1,4},{2,7},{3,6},{4,1},{5,0},{6,3},{7,2},{8,13},{9,12},{10,... | collective-permute-start | bytes 172040 | tf_op jit(solution)/shard_map/ppermute | solution.py:22
  18.8 0.3 collective-permute-start.5
  19.1 0.6 %shard_map.118.cross_ref = f32[40,1024]{1,0:T(8,128)S(1)} custom-call(s32[1,768]{1,0:T(1,128)S(1)} %copy-done.5, f32[16,768]{1,0:T(8,128)S(1)} %bitcast.16, f32[16,768]{1,0:T(8,128)S(1)} %bitcast.11, s32[768,1024]{1,0:T(8,128)S(1)} %copy-done.1, f32[40,896]{1,0:T(8,128)S(1)} %get-tuple-element.32.total_ref.after_ref), custom_call_target="tpu_custom_call" | custom-call | flops 220200960 | bytes 3145728 | tf_op jit(solution)/shard_map/pallas_call | solution.py:390
  19.7 0.4 collective-permute-start.6
  20.2 0.8 %collective-permute-done.3.rest_0_ = bf16[32,896]{1,0:T(8,128)(2,1)S(1)} collective-permute-done((bf16[32,896]{1,0:T(8,128)(2,1)S(1)}, bf16[32,896]{1,0:T(8,128)(2,1)S(1)}, u32[]{:S(2)}, u32[]{:S(2)}) %collective-permute-start.3) | collective-permute-done | bytes 57376 | tf_op jit(solution)/shard_map/ppermute | solution.py:22
  20.9 1.2 %collective-permute-done.4.rest_1_ = bf16[32,896]{1,0:T(8,128)(2,1)S(1)} collective-permute-done((bf16[32,896]{1,0:T(8,128)(2,1)S(1)}, bf16[32,896]{1,0:T(8,128)(2,1)S(1)}, u32[]{:S(2)}, u32[]{:S(2)}) %collective-permute-start.4) | collective-permute-done | bytes 57376 | tf_op jit(solution)/shard_map/ppermute | solution.py:22
  22.1 0.6 %collective-permute-done.5.rest_2_ = bf16[32,896]{1,0:T(8,128)(2,1)S(1)} collective-permute-done((bf16[32,896]{1,0:T(8,128)(2,1)S(1)}, bf16[32,896]{1,0:T(8,128)(2,1)S(1)}, u32[]{:S(2)}, u32[]{:S(2)}) %collective-permute-start.5) | collective-permute-done | bytes 57376 | tf_op jit(solution)/shard_map/ppermute | solution.py:22
  22.7 1.1 %shard_map.117 = (bf16[32,768]{1,0:T(8,128)(2,1)S(1)}, f32[8,128]{1,0:T(8,128)S(1)}, bf16[16,896]{1,0:T(8,128)(2,1)S(1)}, bf16[16,896]{1,0:T(8,128)(2,1)S(1)}, bf16[16,896]{1,0:T(8,128)(2,1)S(1)}) custom-call(f32[40,896]{1,0:T(8,128)S(1)} %get-tuple-element.32.total_ref.after_ref, bf16[768,3072]{1,0:T(8,128)(2,1)S(1)} %get-tuple-element.28.coded_ref, ...), custom_call_target="tpu_custom_call" | custom-call | flops 1207959552 | bytes 4718592 | tf_op jit(solution)/shard_map/pallas_call | solution.py:390
  23.8 2.6 %collective-permute-start.7 = (bf16[16,896]{1,0:T(8,128)(2,1)S(1)}, bf16[16,896]{1,0:T(8,128)(2,1)S(1)}, u32[]{:S(2)}, u32[]{:S(2)}) collective-permute-start(bf16[16,896]{1,0:T(8,128)(2,1)S(1)} %get-tuple-element.39), channel_id=1, source_target_pairs={{0,24},{8,16},{16,8},{24,0},{1,25},{9,17},{17,9},{25,1},{2,26},{10... | collective-permute-start | bytes 86024 | tf_op jit(solution)/shard_map/ppermute | solution.py:22
  26.4 1.8 %collective-permute-start.9 = (bf16[16,896]{1,0:T(8,128)(2,1)S(1)}, bf16[16,896]{1,0:T(8,128)(2,1)S(1)}, u32[]{:S(2)}, u32[]{:S(2)}) collective-permute-start(bf16[16,896]{1,0:T(8,128)(2,1)S(1)} %get-tuple-element.41), channel_id=1, source_target_pairs={{0,8},{8,0},{16,24},{24,16},{1,9},{9,1},{17,25},{25,17},{2,10},{10... | collective-permute-start | bytes 86024 | tf_op jit(solution)/shard_map/ppermute | solution.py:22
  28.2 0.4 %shard_map.119 = (f32[16,896]{1,0:T(8,128)S(1)}, f32[40,1024]{1,0:T(8,128)S(1)}) custom-call(bf16[32,768]{1,0:T(8,128)(2,1)S(1)} %get-tuple-element.36.scaled_ref, f32[8,128]{1,0:T(8,128)S(1)} %get-tuple-element.37.sums_ref, bf16[768,3072]{1,0:T(8,128)(2,1)S(1)} %get-tuple-element.28.coded_ref, bf16[512,3072]{1,0:T(8,128)(2,1)S(1)} %get-tuple-element.27.called_first, ...), custom_call_target="tpu_custom_call" | custom-call | flops 603979776 | bytes 2359296 | tf_op jit(solution)/shard_map/pallas_call | solution.py:390
  28.6 0.9 %collective-permute-done.7.rest_1_ = bf16[16,896]{1,0:T(8,128)(2,1)S(1)} collective-permute-done((bf16[16,896]{1,0:T(8,128)(2,1)S(1)}, bf16[16,896]{1,0:T(8,128)(2,1)S(1)}, u32[]{:S(2)}, u32[]{:S(2)}) %collective-permute-start.7) | collective-permute-done | bytes 28704 | tf_op jit(solution)/shard_map/ppermute | solution.py:22
  29.5 1.6 %collective-permute-done.8.rest_2_ = bf16[16,896]{1,0:T(8,128)(2,1)S(1)} collective-permute-done((bf16[16,896]{1,0:T(8,128)(2,1)S(1)}, bf16[16,896]{1,0:T(8,128)(2,1)S(1)}, u32[]{:S(2)}, u32[]{:S(2)}) %collective-permute-start.8) | collective-permute-done | bytes 28704 | tf_op jit(solution)/shard_map/ppermute | solution.py:22
  31.2 0.9 %shard_map.121 = (f32[32,1,384]{2,1,0:T(1,128)}, f32[16,768]{1,0:T(8,128)S(1)}) custom-call(f32[1,16]{1,0:T(1,128)S(1)} %bitcast.21, f32[16,768]{1,0:T(8,128)S(1)} %bitcast.12, f32[16,768]{1,0:T(8,128)S(1)} %bitcast.19, f32[40,1024]{1,0:T(8,128)S(1)} %get-tuple-element.44.both_ref, f32[16,896]{1,0:T(8,128)S(1)} %get-tuple-element.38.rest_0_, ...), custom_call_target="tpu_custom_call" | custom-call | bytes 49152 | tf_op jit(solution)/shard_map/pallas_call | solution.py:390
  32.0 3.3 %all-to-all-start = ((f32[32,1,384]{2,1,0:T(1,128)}), f32[32,1,384]{2,1,0:T(1,128)S(1)}, u32[]{:S(2)}, u32[]{:S(2)}) async-start(f32[32,1,384]{2,1,0:T(1,128)} %get-tuple-element.45), calls=%async_computation | async-start | bytes 98304 | tf_op jit(solution)/shard_map/all_to_all | solution.py:519
  35.4 0.7 %shard_map.120 = (f32[16,768]{1,0:T(8,128)}, f32[16,768]{1,0:T(8,128)}, f32[16,128]{1,0:T(8,128)S(1)}) custom-call(f32[1,16]{1,0:T(1,128)S(1)} %bitcast.22, f32[16,768]{1,0:T(8,128)S(1)} %bitcast.13, f32[16,768]{1,0:T(8,128)S(1)} %bitcast.20, f32[16,768]{1,0:T(8,128)S(1)} %bitcast.17, f32[16,896]{1,0:T(8,128)S(1)} %get-tuple-element.38.rest_0_, ...), custom_call_target="tpu_custom_call" | custom-call | bytes 1048576 | tf_op jit(solution)/shard_map/pallas_call | solution.py:390
  36.1 6.6 %all-to-all-done.came_ref = f32[32,1,384]{2,1,0:T(1,128)S(1)} async-done(((f32[32,1,384]{2,1,0:T(1,128)}), f32[32,1,384]{2,1,0:T(1,128)S(1)}, u32[]{:S(2)}, u32[]{:S(2)}) %all-to-all-start) | async-done | bytes 49184 | tf_op jit(solution)/shard_map/all_to_all | solution.py:519
  42.7 0.8 %shard_map.122 = (f32[16,768]{1,0:T(8,128)}, f32[16,32]{1,0:T(8,128)}) custom-call(f32[32,1,384]{2,1,0:T(1,128)S(1)} %all-to-all-done.came_ref, f32[16,128]{1,0:T(8,128)S(1)} %get-tuple-element.46.stats_ref, f32[16,768]{1,0:T(8,128)S(1)} %get-tuple-element.47.res_ref, f32[16,768]{1,0:T(8,128)S(1)} %bitcast.14), custom_call_target="tpu_custom_call" | custom-call | tf_op jit(solution)/shard_map/pallas_call | solution.py:390
  (16 shorter events, 0.1 us)
Async XLA Ops:
  0.6 6.3 %collective-permute-start = (f32[16,768]{1,0:T(8,128)}, f32[16,768]{1,0:T(8,128)S(1)}, u32[]{:S(2)}, u32[]{:S(2)}) collective-permute-start(f32[16,768]{1,0:T(8,128)} %bitcast.8), channel_id=1, source_target_pairs={{0,8},{8,0},{16,24},{24,16},{1,9},{9,1},{17,25},{25,17},{2,10},{10... | collective-permute-start | bytes 147464 | tf_op jit(solution)/shard_map/ppermute | solution.py:22
  3.7 3.2 %copy-start.2 = (f32[768,16]{0,1:T(8,128)S(1)}, f32[768,16]{0,1:T(8,128)}, u32[]{:S(2)}) copy-start(f32[768,16]{0,1:T(8,128)} %param.15) | copy-start | bytes 147460
  3.7 6.5 %copy-start = (s32[768,3072]{1,0:T(8,128)S(1)}, s32[768,3072]{1,0:T(8,128)}, u32[]{:S(2)}) copy-start(s32[768,3072]{1,0:T(8,128)} %gen_ref.1) | copy-start | bytes 28311556
  7.0 6.1 %collective-permute-start.1 = (bf16[32,768]{1,0:T(8,128)(2,1)S(1)}, bf16[32,768]{1,0:T(8,128)(2,1)S(1)}, u32[]{:S(2)}, u32[]{:S(2)}) collective-permute-start(bf16[32,768]{1,0:T(8,128)(2,1)S(1)} %shard_map.111.pair_ref), channel_id=1, source_target_pairs={{0,16},{8,24},{16,0},{24,8},{1,17},{9,25},{17,1},{25,9},{2,18},{10... | collective-permute-start | bytes 147464 | tf_op jit(solution)/shard_map/ppermute | solution.py:22
  13.0 6.1 %copy-start.1 = (s32[768,1024]{1,0:T(8,128)S(1)}, s32[768,1024]{1,0:T(8,128)}, u32[]{:S(2)}) copy-start(s32[768,1024]{1,0:T(8,128)} %dose_ref.1) | copy-start | bytes 9437188
  13.1 6.0 %copy-start.3 = (f32[768,16]{0,1:T(8,128)S(1)}, f32[768,16]{0,1:T(8,128)}, u32[]{:S(2)}) copy-start(f32[768,16]{0,1:T(8,128)} %param.13) | copy-start | bytes 147460
  13.1 6.0 %copy-start.5 = (s32[1,768]{1,0:T(1,128)S(1)}, s32[1,768]{1,0:T(1,128)}, u32[]{:S(2)}) copy-start(s32[1,768]{1,0:T(1,128)} %order_ref.1) | copy-start | bytes 9220
  14.6 1.4 %collective-permute-start.2 = (f32[40,896]{1,0:T(8,128)S(1)}, f32[40,896]{1,0:T(8,128)S(1)}, u32[]{:S(2)}, u32[]{:S(2)}) collective-permute-start(f32[40,896]{1,0:T(8,128)S(1)} %shard_map.115.own_ref), channel_id=1, source_target_pairs={{0,1},{1,0},{2,3},{3,2},{4,5},{5,4},{6,7},{7,6},{8,9},{9,8},{10,11... | collective-permute-start | bytes 430088 | tf_op jit(solution)/shard_map/ppermute | solution.py:22
  16.1 4.9 %collective-permute-start.3 = (bf16[32,896]{1,0:T(8,128)(2,1)S(1)}, bf16[32,896]{1,0:T(8,128)(2,1)S(1)}, u32[]{:S(2)}, u32[]{:S(2)}) collective-permute-start(bf16[32,896]{1,0:T(8,128)(2,1)S(1)} %get-tuple-element.33), channel_id=1, source_target_pairs={{0,7},{1,6},{2,5},{3,4},{4,3},{5,2},{6,1},{7,0},{8,15},{9,14},{10,... | collective-permute-start | bytes 172040 | tf_op jit(solution)/shard_map/ppermute | solution.py:22
  18.3 3.8 %collective-permute-start.4 = (bf16[32,896]{1,0:T(8,128)(2,1)S(1)}, bf16[32,896]{1,0:T(8,128)(2,1)S(1)}, u32[]{:S(2)}, u32[]{:S(2)}) collective-permute-start(bf16[32,896]{1,0:T(8,128)(2,1)S(1)} %get-tuple-element.34), channel_id=1, source_target_pairs={{0,5},{1,4},{2,7},{3,6},{4,1},{5,0},{6,3},{7,2},{8,13},{9,12},{10,... | collective-permute-start | bytes 172040 | tf_op jit(solution)/shard_map/ppermute | solution.py:22
  18.8 3.9 %collective-permute-start.5 = (bf16[32,896]{1,0:T(8,128)(2,1)S(1)}, bf16[32,896]{1,0:T(8,128)(2,1)S(1)}, u32[]{:S(2)}, u32[]{:S(2)}) collective-permute-start(bf16[32,896]{1,0:T(8,128)(2,1)S(1)} %get-tuple-element.35), channel_id=1, source_target_pairs={{0,3},{1,2},{2,1},{3,0},{4,7},{5,6},{6,5},{7,4},{8,11},{9,10},{10,... | collective-permute-start | bytes 172040 | tf_op jit(solution)/shard_map/ppermute | solution.py:22
  19.7 8.5 %collective-permute-start.6 = (f32[40,1024]{1,0:T(8,128)S(1)}, f32[40,1024]{1,0:T(8,128)S(1)}, u32[]{:S(2)}, u32[]{:S(2)}) collective-permute-start(f32[40,1024]{1,0:T(8,128)S(1)} %shard_map.118.cross_ref), channel_id=1, source_target_pairs={{0,1},{1,0},{2,3},{3,2},{4,5},{5,4},{6,7},{7,6},{8,9},{9,8},{10,11... | collective-permute-start | bytes 491528 | tf_op jit(solution)/shard_map/ppermute | solution.py:22
  23.8 5.7 %collective-permute-start.7 = (bf16[16,896]{1,0:T(8,128)(2,1)S(1)}, bf16[16,896]{1,0:T(8,128)(2,1)S(1)}, u32[]{:S(2)}, u32[]{:S(2)}) collective-permute-start(bf16[16,896]{1,0:T(8,128)(2,1)S(1)} %get-tuple-element.39), channel_id=1, source_target_pairs={{0,24},{8,16},{16,8},{24,0},{1,25},{9,17},{17,9},{25,1},{2,26},{10... | collective-permute-start | bytes 86024 | tf_op jit(solution)/shard_map/ppermute | solution.py:22
  26.4 4.8 %collective-permute-start.8 = (bf16[16,896]{1,0:T(8,128)(2,1)S(1)}, bf16[16,896]{1,0:T(8,128)(2,1)S(1)}, u32[]{:S(2)}, u32[]{:S(2)}) collective-permute-start(bf16[16,896]{1,0:T(8,128)(2,1)S(1)} %get-tuple-element.40), channel_id=1, source_target_pairs={{0,16},{8,24},{16,0},{24,8},{1,17},{9,25},{17,1},{25,9},{2,18},{10... | collective-permute-start | bytes 86024 | tf_op jit(solution)/shard_map/ppermute | solution.py:22
  26.4 4.8 %collective-permute-start.9 = (bf16[16,896]{1,0:T(8,128)(2,1)S(1)}, bf16[16,896]{1,0:T(8,128)(2,1)S(1)}, u32[]{:S(2)}, u32[]{:S(2)}) collective-permute-start(bf16[16,896]{1,0:T(8,128)(2,1)S(1)} %get-tuple-element.41), channel_id=1, source_target_pairs={{0,8},{8,0},{16,24},{24,16},{1,9},{9,1},{17,25},{25,17},{2,10},{10... | collective-permute-start | bytes 86024 | tf_op jit(solution)/shard_map/ppermute | solution.py:22
  28.2 3.0 %copy-start.4 = (f32[768,16]{0,1:T(8,128)S(1)}, f32[768,16]{0,1:T(8,128)}, u32[]{:S(2)}) copy-start(f32[768,16]{0,1:T(8,128)} %param.14) | copy-start | bytes 147460
  28.2 3.0 %copy-start.6 = (f32[16]{0:T(128)S(1)}, f32[16]{0:T(128)}, u32[]{:S(2)}) copy-start(f32[16]{0:T(128)} %param.12) | copy-start | bytes 196
  32.0 10.7 %all-to-all-start = ((f32[32,1,384]{2,1,0:T(1,128)}), f32[32,1,384]{2,1,0:T(1,128)S(1)}, u32[]{:S(2)}, u32[]{:S(2)}) async-start(f32[32,1,384]{2,1,0:T(1,128)} %get-tuple-element.45), calls=%async_computation | async-start | bytes 98304 | tf_op jit(solution)/shard_map/all_to_all | solution.py:519

commit v19 on v18

--- a/solution.py
+++ b/solution.py
@@ -410,7 +410,7 @@
     noise = noise_ratio[None]
 
     dire, res, sol = direction.T, residual.T, solution.T
-    first, chunk = rows // 3 * 2, 128
+    first, chunk = rows // 3 * 2, 64
     matrix = lambda n: ((n, shard), BF16, pltpu.VMEM)
 
     neighbour = swap(dire, "var", 1)

time: 43.7 us -> 43.2 us (0.989)
  waiting for transfers between devices: 13 us -> 12.4 us
    ppermute x10, waiting for transfers between devices: 6.39 us -> 5.85 us  [swap(): return lax.ppermute(values, axis, [(i, i ^ distance) for i in range(size)])]
where the time goes in v19:
time: 43.2 us; the launch traced here: 43 us
  starting transfers between devices  17 us (39%)
  Pallas kernels  12.7 us (29%)
  waiting for transfers between devices  12.4 us (29%)
  between operations  0.76 us (2%)
    ppermute x10, starting transfers between devices, swap(): return lax.ppermute(values, axis, [(i, i ^ distance) for i in range(size)])  13.7 us
    pallas_call x12, Pallas kernels, call(): pl.pallas_call(kernel, out_shape=[jax.ShapeDtypeStruct(*o) if len(o) == 2...  12.7 us
    all_to_all x1, waiting for transfers between devices, body(): lax.all_to_all(outgoing, ('var', 'samp'), split_axis=0, concat_axis=0)  6.59 us
    ppermute x10, waiting for transfers between devices, swap(): return lax.ppermute(values, axis, [(i, i ^ distance) for i in range(size)])  5.85 us
    all_to_all x1, starting transfers between devices, body(): lax.all_to_all(outgoing, ('var', 'samp'), split_axis=0, concat_axis=0)  3.34 us
  transfers between devices with their start and end apart: 11, of which 7 were waited for; matrix products, arithmetic and copies ran while one was open for 0% of the time, Pallas kernels for 22%

profile of v19, /device:TPU:0, one launch (start us, length us, event | category | flops | bytes accessed | tf_op | source)
XLA Modules:
  0.0 43.0 jit_solution(5105799221887067886)
XLA Ops:
  0.6 3.1 %collective-permute-start = (f32[16,768]{1,0:T(8,128)}, f32[16,768]{1,0:T(8,128)S(1)}, u32[]{:S(2)}, u32[]{:S(2)}) collective-permute-start(f32[16,768]{1,0:T(8,128)} %bitcast.8), channel_id=1, source_target_pairs={{0,8},{8,0},{16,24},{24,16},{1,9},{9,1},{17,25},{25,17},{2,10},{10... | collective-permute-start | bytes 147464 | tf_op jit(solution)/shard_map/ppermute | solution.py:22
  3.7 3.2 %shard_map.112 = (bf16[512,3072]{1,0:T(8,128)(2,1)S(1)}, f32[8,128]{1,0:T(8,128)S(1)}) custom-call(f32[16,768]{1,0:T(8,128)} %bitcast.15, f32[16,768]{1,0:T(8,128)} %bitcast.9, f32[16,768]{1,0:T(8,128)} %bitcast.18, s32[768,3072]{1,0:T(8,128)} %call_hbm.3), custom_call_target="tpu_custom_call" | custom-call | bytes 6291456 | tf_op jit(solution)/shard_map/pallas_call | solution.py:390
  7.0 2.7 %collective-permute-start.1 = (bf16[32,768]{1,0:T(8,128)(2,1)S(1)}, bf16[32,768]{1,0:T(8,128)(2,1)S(1)}, u32[]{:S(2)}, u32[]{:S(2)}) collective-permute-start(bf16[32,768]{1,0:T(8,128)(2,1)S(1)} %shard_map.111.pair_ref), channel_id=1, source_target_pairs={{0,16},{8,24},{16,0},{24,8},{1,17},{9,25},{17,1},{25,9},{2,18},{10... | collective-permute-start | bytes 147464 | tf_op jit(solution)/shard_map/ppermute | solution.py:22
  9.7 0.6 %shard_map.113.done_ref = f32[32,512]{1,0:T(8,128)S(1)} custom-call(bf16[32,768]{1,0:T(8,128)(2,1)S(1)} %shard_map.111.pair_ref, bf16[512,3072]{1,0:T(8,128)(2,1)S(1)} %get-tuple-element.27.called_first), custom_call_target="tpu_custom_call" | custom-call | flops 402653184 | bytes 1572864 | tf_op jit(solution)/shard_map/pallas_call | solution.py:390
  10.2 0.0 copy-done
  10.2 2.8 %shard_map.114 = (bf16[768,3072]{1,0:T(8,128)(2,1)S(1)}, bf16[256,3072]{1,0:T(8,128)(2,1)S(1)}, f32[40,768]{1,0:T(8,128)S(1)}) custom-call(bf16[32,768]{1,0:T(8,128)(2,1)S(1)} %shard_map.111.pair_ref, bf16[512,3072]{1,0:T(8,128)(2,1)S(1)} %get-tuple-element.27.called_first, f32[32,512]{1,0:T(8,128)S(1)} %shard_map.113.done_ref, s32[768,3072]{1,0:T(8,128)S(1)} %copy-done, ...), custom_call_target="tpu_custom_call" | custom-call | flops 1207959552 | bytes 9437184 | tf_op jit(solution)/shard_map/pallas_call | solution.py:390
  13.1 0.0 copy-start.1
  13.1 0.0 copy-start.3
  13.1 0.0 copy-start.5
  13.1 1.5 %shard_map.115.own_ref = f32[40,896]{1,0:T(8,128)S(1)} custom-call(bf16[32,768]{1,0:T(8,128)(2,1)S(1)} %collective-permute-done.1.pair_ref, bf16[768,3072]{1,0:T(8,128)(2,1)S(1)} %get-tuple-element.28.coded_ref, bf16[512,3072]{1,0:T(8,128)(2,1)S(1)} %get-tuple-element.27.called_first, bf16[256,3072]{1,0:T(8,128)(2,1)S(1)} %get-tuple-element.29.called_ref, ...), custom_call_target="tpu_custom_call" | custom-call | flops 1207959552 | bytes 4718592 | tf_op jit(solution)/shard_map/pallas_call | solution.py:390
  14.6 0.1 collective-permute-start.2
  14.7 1.4 %collective-permute-done.2.other_ref = f32[40,896]{1,0:T(8,128)S(1)} collective-permute-done((f32[40,896]{1,0:T(8,128)S(1)}, f32[40,896]{1,0:T(8,128)S(1)}, u32[]{:S(2)}, u32[]{:S(2)}) %collective-permute-start.2) | collective-permute-done | bytes 143392 | tf_op jit(solution)/shard_map/ppermute | solution.py:22
  16.1 2.3 %collective-permute-start.3 = (bf16[32,896]{1,0:T(8,128)(2,1)S(1)}, bf16[32,896]{1,0:T(8,128)(2,1)S(1)}, u32[]{:S(2)}, u32[]{:S(2)}) collective-permute-start(bf16[32,896]{1,0:T(8,128)(2,1)S(1)} %get-tuple-element.33), channel_id=1, source_target_pairs={{0,7},{1,6},{2,5},{3,4},{4,3},{5,2},{6,1},{7,0},{8,15},{9,14},{10,... | collective-permute-start | bytes 172040 | tf_op jit(solution)/shard_map/ppermute | solution.py:22
  18.4 0.5 %collective-permute-start.4 = (bf16[32,896]{1,0:T(8,128)(2,1)S(1)}, bf16[32,896]{1,0:T(8,128)(2,1)S(1)}, u32[]{:S(2)}, u32[]{:S(2)}) collective-permute-start(bf16[32,896]{1,0:T(8,128)(2,1)S(1)} %get-tuple-element.34), channel_id=1, source_target_pairs={{0,5},{1,4},{2,7},{3,6},{4,1},{5,0},{6,3},{7,2},{8,13},{9,12},{10,... | collective-permute-start | bytes 172040 | tf_op jit(solution)/shard_map/ppermute | solution.py:22
  18.8 0.3 collective-permute-start.5
  19.1 0.6 %shard_map.118.cross_ref = f32[40,1024]{1,0:T(8,128)S(1)} custom-call(s32[1,768]{1,0:T(1,128)S(1)} %copy-done.5, f32[16,768]{1,0:T(8,128)S(1)} %bitcast.16, f32[16,768]{1,0:T(8,128)S(1)} %bitcast.11, s32[768,1024]{1,0:T(8,128)S(1)} %copy-done.1, f32[40,896]{1,0:T(8,128)S(1)} %get-tuple-element.32.total_ref.after_ref), custom_call_target="tpu_custom_call" | custom-call | flops 220200960 | bytes 3145728 | tf_op jit(solution)/shard_map/pallas_call | solution.py:390
  19.8 0.4 collective-permute-start.6
  20.2 0.8 %collective-permute-done.3.rest_0_ = bf16[32,896]{1,0:T(8,128)(2,1)S(1)} collective-permute-done((bf16[32,896]{1,0:T(8,128)(2,1)S(1)}, bf16[32,896]{1,0:T(8,128)(2,1)S(1)}, u32[]{:S(2)}, u32[]{:S(2)}) %collective-permute-start.3) | collective-permute-done | bytes 57376 | tf_op jit(solution)/shard_map/ppermute | solution.py:22
  20.9 1.2 %collective-permute-done.4.rest_1_ = bf16[32,896]{1,0:T(8,128)(2,1)S(1)} collective-permute-done((bf16[32,896]{1,0:T(8,128)(2,1)S(1)}, bf16[32,896]{1,0:T(8,128)(2,1)S(1)}, u32[]{:S(2)}, u32[]{:S(2)}) %collective-permute-start.4) | collective-permute-done | bytes 57376 | tf_op jit(solution)/shard_map/ppermute | solution.py:22
  22.1 0.6 %collective-permute-done.5.rest_2_ = bf16[32,896]{1,0:T(8,128)(2,1)S(1)} collective-permute-done((bf16[32,896]{1,0:T(8,128)(2,1)S(1)}, bf16[32,896]{1,0:T(8,128)(2,1)S(1)}, u32[]{:S(2)}, u32[]{:S(2)}) %collective-permute-start.5) | collective-permute-done | bytes 57376 | tf_op jit(solution)/shard_map/ppermute | solution.py:22
  22.7 1.1 %shard_map.117 = (bf16[32,768]{1,0:T(8,128)(2,1)S(1)}, f32[8,128]{1,0:T(8,128)S(1)}, bf16[16,896]{1,0:T(8,128)(2,1)S(1)}, bf16[16,896]{1,0:T(8,128)(2,1)S(1)}, bf16[16,896]{1,0:T(8,128)(2,1)S(1)}) custom-call(f32[40,896]{1,0:T(8,128)S(1)} %get-tuple-element.32.total_ref.after_ref, bf16[768,3072]{1,0:T(8,128)(2,1)S(1)} %get-tuple-element.28.coded_ref, ...), custom_call_target="tpu_custom_call" | custom-call | flops 1207959552 | bytes 4718592 | tf_op jit(solution)/shard_map/pallas_call | solution.py:390
  23.8 2.1 %collective-permute-start.7 = (bf16[16,896]{1,0:T(8,128)(2,1)S(1)}, bf16[16,896]{1,0:T(8,128)(2,1)S(1)}, u32[]{:S(2)}, u32[]{:S(2)}) collective-permute-start(bf16[16,896]{1,0:T(8,128)(2,1)S(1)} %get-tuple-element.39), channel_id=1, source_target_pairs={{0,24},{8,16},{16,8},{24,0},{1,25},{9,17},{17,9},{25,1},{2,26},{10... | collective-permute-start | bytes 86024 | tf_op jit(solution)/shard_map/ppermute | solution.py:22
  25.9 0.5 %collective-permute-start.8 = (bf16[16,896]{1,0:T(8,128)(2,1)S(1)}, bf16[16,896]{1,0:T(8,128)(2,1)S(1)}, u32[]{:S(2)}, u32[]{:S(2)}) collective-permute-start(bf16[16,896]{1,0:T(8,128)(2,1)S(1)} %get-tuple-element.40), channel_id=1, source_target_pairs={{0,16},{8,24},{16,0},{24,8},{1,17},{9,25},{17,1},{25,9},{2,18},{10... | collective-permute-start | bytes 86024 | tf_op jit(solution)/shard_map/ppermute | solution.py:22
  26.3 1.9 %collective-permute-start.9 = (bf16[16,896]{1,0:T(8,128)(2,1)S(1)}, bf16[16,896]{1,0:T(8,128)(2,1)S(1)}, u32[]{:S(2)}, u32[]{:S(2)}) collective-permute-start(bf16[16,896]{1,0:T(8,128)(2,1)S(1)} %get-tuple-element.41), channel_id=1, source_target_pairs={{0,8},{8,0},{16,24},{24,16},{1,9},{9,1},{17,25},{25,17},{2,10},{10... | collective-permute-start | bytes 86024 | tf_op jit(solution)/shard_map/ppermute | solution.py:22
  28.2 0.4 %shard_map.119 = (f32[16,896]{1,0:T(8,128)S(1)}, f32[40,1024]{1,0:T(8,128)S(1)}) custom-call(bf16[32,768]{1,0:T(8,128)(2,1)S(1)} %get-tuple-element.36.scaled_ref, f32[8,128]{1,0:T(8,128)S(1)} %get-tuple-element.37.sums_ref, bf16[768,3072]{1,0:T(8,128)(2,1)S(1)} %get-tuple-element.28.coded_ref, bf16[512,3072]{1,0:T(8,128)(2,1)S(1)} %get-tuple-element.27.called_first, ...), custom_call_target="tpu_custom_call" | custom-call | flops 603979776 | bytes 2359296 | tf_op jit(solution)/shard_map/pallas_call | solution.py:390
  28.7 0.9 %collective-permute-done.7.rest_1_ = bf16[16,896]{1,0:T(8,128)(2,1)S(1)} collective-permute-done((bf16[16,896]{1,0:T(8,128)(2,1)S(1)}, bf16[16,896]{1,0:T(8,128)(2,1)S(1)}, u32[]{:S(2)}, u32[]{:S(2)}) %collective-permute-start.7) | collective-permute-done | bytes 28704 | tf_op jit(solution)/shard_map/ppermute | solution.py:22
  29.5 1.1 %collective-permute-done.8.rest_2_ = bf16[16,896]{1,0:T(8,128)(2,1)S(1)} collective-permute-done((bf16[16,896]{1,0:T(8,128)(2,1)S(1)}, bf16[16,896]{1,0:T(8,128)(2,1)S(1)}, u32[]{:S(2)}, u32[]{:S(2)}) %collective-permute-start.8) | collective-permute-done | bytes 28704 | tf_op jit(solution)/shard_map/ppermute | solution.py:22
  30.6 0.9 %shard_map.121 = (f32[32,1,384]{2,1,0:T(1,128)}, f32[16,768]{1,0:T(8,128)S(1)}) custom-call(f32[1,16]{1,0:T(1,128)S(1)} %bitcast.21, f32[16,768]{1,0:T(8,128)S(1)} %bitcast.12, f32[16,768]{1,0:T(8,128)S(1)} %bitcast.19, f32[40,1024]{1,0:T(8,128)S(1)} %get-tuple-element.44.both_ref, f32[16,896]{1,0:T(8,128)S(1)} %get-tuple-element.38.rest_0_, ...), custom_call_target="tpu_custom_call" | custom-call | bytes 49152 | tf_op jit(solution)/shard_map/pallas_call | solution.py:390
  31.5 3.3 %all-to-all-start = ((f32[32,1,384]{2,1,0:T(1,128)}), f32[32,1,384]{2,1,0:T(1,128)S(1)}, u32[]{:S(2)}, u32[]{:S(2)}) async-start(f32[32,1,384]{2,1,0:T(1,128)} %get-tuple-element.45), calls=%async_computation | async-start | bytes 98304 | tf_op jit(solution)/shard_map/all_to_all | solution.py:519
  34.9 0.7 %shard_map.120 = (f32[16,768]{1,0:T(8,128)}, f32[16,768]{1,0:T(8,128)}, f32[16,128]{1,0:T(8,128)S(1)}) custom-call(f32[1,16]{1,0:T(1,128)S(1)} %bitcast.22, f32[16,768]{1,0:T(8,128)S(1)} %bitcast.13, f32[16,768]{1,0:T(8,128)S(1)} %bitcast.20, f32[16,768]{1,0:T(8,128)S(1)} %bitcast.17, f32[16,896]{1,0:T(8,128)S(1)} %get-tuple-element.38.rest_0_, ...), custom_call_target="tpu_custom_call" | custom-call | bytes 1048576 | tf_op jit(solution)/shard_map/pallas_call | solution.py:390
  35.6 6.6 %all-to-all-done.came_ref = f32[32,1,384]{2,1,0:T(1,128)S(1)} async-done(((f32[32,1,384]{2,1,0:T(1,128)}), f32[32,1,384]{2,1,0:T(1,128)S(1)}, u32[]{:S(2)}, u32[]{:S(2)}) %all-to-all-start) | async-done | bytes 49184 | tf_op jit(solution)/shard_map/all_to_all | solution.py:519
  42.2 0.8 %shard_map.122 = (f32[16,768]{1,0:T(8,128)}, f32[16,32]{1,0:T(8,128)}) custom-call(f32[32,1,384]{2,1,0:T(1,128)S(1)} %all-to-all-done.came_ref, f32[16,128]{1,0:T(8,128)S(1)} %get-tuple-element.46.stats_ref, f32[16,768]{1,0:T(8,128)S(1)} %get-tuple-element.47.res_ref, f32[16,768]{1,0:T(8,128)S(1)} %bitcast.14), custom_call_target="tpu_custom_call" | custom-call | tf_op jit(solution)/shard_map/pallas_call | solution.py:390
  (16 shorter events, 0.1 us)
Async XLA Ops:
  0.6 6.3 %collective-permute-start = (f32[16,768]{1,0:T(8,128)}, f32[16,768]{1,0:T(8,128)S(1)}, u32[]{:S(2)}, u32[]{:S(2)}) collective-permute-start(f32[16,768]{1,0:T(8,128)} %bitcast.8), channel_id=1, source_target_pairs={{0,8},{8,0},{16,24},{24,16},{1,9},{9,1},{17,25},{25,17},{2,10},{10... | collective-permute-start | bytes 147464 | tf_op jit(solution)/shard_map/ppermute | solution.py:22
  3.7 3.3 %copy-start.2 = (f32[768,16]{0,1:T(8,128)S(1)}, f32[768,16]{0,1:T(8,128)}, u32[]{:S(2)}) copy-start(f32[768,16]{0,1:T(8,128)} %param.15) | copy-start | bytes 147460
  3.7 6.5 %copy-start = (s32[768,3072]{1,0:T(8,128)S(1)}, s32[768,3072]{1,0:T(8,128)}, u32[]{:S(2)}) copy-start(s32[768,3072]{1,0:T(8,128)} %gen_ref.1) | copy-start | bytes 28311556
  7.0 6.1 %collective-permute-start.1 = (bf16[32,768]{1,0:T(8,128)(2,1)S(1)}, bf16[32,768]{1,0:T(8,128)(2,1)S(1)}, u32[]{:S(2)}, u32[]{:S(2)}) collective-permute-start(bf16[32,768]{1,0:T(8,128)(2,1)S(1)} %shard_map.111.pair_ref), channel_id=1, source_target_pairs={{0,16},{8,24},{16,0},{24,8},{1,17},{9,25},{17,1},{25,9},{2,18},{10... | collective-permute-start | bytes 147464 | tf_op jit(solution)/shard_map/ppermute | solution.py:22
  13.1 6.1 %copy-start.1 = (s32[768,1024]{1,0:T(8,128)S(1)}, s32[768,1024]{1,0:T(8,128)}, u32[]{:S(2)}) copy-start(s32[768,1024]{1,0:T(8,128)} %dose_ref.1) | copy-start | bytes 9437188
  13.1 6.0 %copy-start.3 = (f32[768,16]{0,1:T(8,128)S(1)}, f32[768,16]{0,1:T(8,128)}, u32[]{:S(2)}) copy-start(f32[768,16]{0,1:T(8,128)} %param.13) | copy-start | bytes 147460
  13.1 6.0 %copy-start.5 = (s32[1,768]{1,0:T(1,128)S(1)}, s32[1,768]{1,0:T(1,128)}, u32[]{:S(2)}) copy-start(s32[1,768]{1,0:T(1,128)} %order_ref.1) | copy-start | bytes 9220
  14.6 1.4 %collective-permute-start.2 = (f32[40,896]{1,0:T(8,128)S(1)}, f32[40,896]{1,0:T(8,128)S(1)}, u32[]{:S(2)}, u32[]{:S(2)}) collective-permute-start(f32[40,896]{1,0:T(8,128)S(1)} %shard_map.115.own_ref), channel_id=1, source_target_pairs={{0,1},{1,0},{2,3},{3,2},{4,5},{5,4},{6,7},{7,6},{8,9},{9,8},{10,11... | collective-permute-start | bytes 430088 | tf_op jit(solution)/shard_map/ppermute | solution.py:22
  16.1 4.9 %collective-permute-start.3 = (bf16[32,896]{1,0:T(8,128)(2,1)S(1)}, bf16[32,896]{1,0:T(8,128)(2,1)S(1)}, u32[]{:S(2)}, u32[]{:S(2)}) collective-permute-start(bf16[32,896]{1,0:T(8,128)(2,1)S(1)} %get-tuple-element.33), channel_id=1, source_target_pairs={{0,7},{1,6},{2,5},{3,4},{4,3},{5,2},{6,1},{7,0},{8,15},{9,14},{10,... | collective-permute-start | bytes 172040 | tf_op jit(solution)/shard_map/ppermute | solution.py:22
  18.4 3.8 %collective-permute-start.4 = (bf16[32,896]{1,0:T(8,128)(2,1)S(1)}, bf16[32,896]{1,0:T(8,128)(2,1)S(1)}, u32[]{:S(2)}, u32[]{:S(2)}) collective-permute-start(bf16[32,896]{1,0:T(8,128)(2,1)S(1)} %get-tuple-element.34), channel_id=1, source_target_pairs={{0,5},{1,4},{2,7},{3,6},{4,1},{5,0},{6,3},{7,2},{8,13},{9,12},{10,... | collective-permute-start | bytes 172040 | tf_op jit(solution)/shard_map/ppermute | solution.py:22
  18.8 3.9 %collective-permute-start.5 = (bf16[32,896]{1,0:T(8,128)(2,1)S(1)}, bf16[32,896]{1,0:T(8,128)(2,1)S(1)}, u32[]{:S(2)}, u32[]{:S(2)}) collective-permute-start(bf16[32,896]{1,0:T(8,128)(2,1)S(1)} %get-tuple-element.35), channel_id=1, source_target_pairs={{0,3},{1,2},{2,1},{3,0},{4,7},{5,6},{6,5},{7,4},{8,11},{9,10},{10,... | collective-permute-start | bytes 172040 | tf_op jit(solution)/shard_map/ppermute | solution.py:22
  19.8 8.5 %collective-permute-start.6 = (f32[40,1024]{1,0:T(8,128)S(1)}, f32[40,1024]{1,0:T(8,128)S(1)}, u32[]{:S(2)}, u32[]{:S(2)}) collective-permute-start(f32[40,1024]{1,0:T(8,128)S(1)} %shard_map.118.cross_ref), channel_id=1, source_target_pairs={{0,1},{1,0},{2,3},{3,2},{4,5},{5,4},{6,7},{7,6},{8,9},{9,8},{10,11... | collective-permute-start | bytes 491528 | tf_op jit(solution)/shard_map/ppermute | solution.py:22
  23.8 5.7 %collective-permute-start.7 = (bf16[16,896]{1,0:T(8,128)(2,1)S(1)}, bf16[16,896]{1,0:T(8,128)(2,1)S(1)}, u32[]{:S(2)}, u32[]{:S(2)}) collective-permute-start(bf16[16,896]{1,0:T(8,128)(2,1)S(1)} %get-tuple-element.39), channel_id=1, source_target_pairs={{0,24},{8,16},{16,8},{24,0},{1,25},{9,17},{17,9},{25,1},{2,26},{10... | collective-permute-start | bytes 86024 | tf_op jit(solution)/shard_map/ppermute | solution.py:22
  25.9 4.8 %collective-permute-start.8 = (bf16[16,896]{1,0:T(8,128)(2,1)S(1)}, bf16[16,896]{1,0:T(8,128)(2,1)S(1)}, u32[]{:S(2)}, u32[]{:S(2)}) collective-permute-start(bf16[16,896]{1,0:T(8,128)(2,1)S(1)} %get-tuple-element.40), channel_id=1, source_target_pairs={{0,16},{8,24},{16,0},{24,8},{1,17},{9,25},{17,1},{25,9},{2,18},{10... | collective-permute-start | bytes 86024 | tf_op jit(solution)/shard_map/ppermute | solution.py:22
  26.3 4.3 %collective-permute-start.9 = (bf16[16,896]{1,0:T(8,128)(2,1)S(1)}, bf16[16,896]{1,0:T(8,128)(2,1)S(1)}, u32[]{:S(2)}, u32[]{:S(2)}) collective-permute-start(bf16[16,896]{1,0:T(8,128)(2,1)S(1)} %get-tuple-element.41), channel_id=1, source_target_pairs={{0,8},{8,0},{16,24},{24,16},{1,9},{9,1},{17,25},{25,17},{2,10},{10... | collective-permute-start | bytes 86024 | tf_op jit(solution)/shard_map/ppermute | solution.py:22
  28.2 2.4 %copy-start.4 = (f32[768,16]{0,1:T(8,128)S(1)}, f32[768,16]{0,1:T(8,128)}, u32[]{:S(2)}) copy-start(f32[768,16]{0,1:T(8,128)} %param.14) | copy-start | bytes 147460
  28.2 2.4 %copy-start.6 = (f32[16]{0:T(128)S(1)}, f32[16]{0:T(128)}, u32[]{:S(2)}) copy-start(f32[16]{0:T(128)} %param.12) | copy-start | bytes 196
  31.5 10.7 %all-to-all-start = ((f32[32,1,384]{2,1,0:T(1,128)}), f32[32,1,384]{2,1,0:T(1,128)S(1)}, u32[]{:S(2)}, u32[]{:S(2)}) async-start(f32[32,1,384]{2,1,0:T(1,128)} %get-tuple-element.45), calls=%async_computation | async-start | bytes 98304 | tf_op jit(solution)/shard_map/all_to_all | solution.py:519

commit v20 on v19

--- a/solution.py
+++ b/solution.py
@@ -172,7 +172,7 @@
         for block in blocks(LANES, shard):
             mask = call[block].astype(F32).astype(BF16) if after >= 0 else mask_ref[block]
             held.append((block, gen[block].astype(F32).astype(BF16) * mask, mask))
-            if len(held) > 4:
+            if len(held) > 6:
                 store(*held.pop(0))
         for item in held:
             store(*item)

time: 43.2 us -> 43.2 us (level)
  no operation moved by 1% of the time
where the time goes in v20:
time: 43.2 us; the launch traced here: 43 us
  starting transfers between devices  17 us (39%)
  Pallas kernels  12.7 us (29%)
  waiting for transfers between devices  12.4 us (29%)
  between operations  0.76 us (2%)
    ppermute x10, starting transfers between devices, swap(): return lax.ppermute(values, axis, [(i, i ^ distance) for i in range(size)])  13.7 us
    pallas_call x12, Pallas kernels, call(): pl.pallas_call(kernel, out_shape=[jax.ShapeDtypeStruct(*o) if len(o) == 2...  12.7 us
    all_to_all x1, waiting for transfers between devices, body(): lax.all_to_all(outgoing, ('var', 'samp'), split_axis=0, concat_axis=0)  6.59 us
    ppermute x10, waiting for transfers between devices, swap(): return lax.ppermute(values, axis, [(i, i ^ distance) for i in range(size)])  5.84 us
    all_to_all x1, starting transfers between devices, body(): lax.all_to_all(outgoing, ('var', 'samp'), split_axis=0, concat_axis=0)  3.34 us
  transfers between devices with their start and end apart: 11, of which 7 were waited for; matrix products, arithmetic and copies ran while one was open for 0% of the time, Pallas kernels for 22%

profile of v20, /device:TPU:0, one launch (start us, length us, event | category | flops | bytes accessed | tf_op | source)
XLA Modules:
  0.0 43.0 jit_solution(8360674197139177627)
XLA Ops:
  0.6 3.1 %collective-permute-start = (f32[16,768]{1,0:T(8,128)}, f32[16,768]{1,0:T(8,128)S(1)}, u32[]{:S(2)}, u32[]{:S(2)}) collective-permute-start(f32[16,768]{1,0:T(8,128)} %bitcast.8), channel_id=1, source_target_pairs={{0,8},{8,0},{16,24},{24,16},{1,9},{9,1},{17,25},{25,17},{2,10},{10... | collective-permute-start | bytes 147464 | tf_op jit(solution)/shard_map/ppermute | solution.py:22
  3.7 3.2 %shard_map.112 = (bf16[512,3072]{1,0:T(8,128)(2,1)S(1)}, f32[8,128]{1,0:T(8,128)S(1)}) custom-call(f32[16,768]{1,0:T(8,128)} %bitcast.15, f32[16,768]{1,0:T(8,128)} %bitcast.9, f32[16,768]{1,0:T(8,128)} %bitcast.18, s32[768,3072]{1,0:T(8,128)} %call_hbm.3), custom_call_target="tpu_custom_call" | custom-call | bytes 6291456 | tf_op jit(solution)/shard_map/pallas_call | solution.py:390
  7.0 2.7 %collective-permute-start.1 = (bf16[32,768]{1,0:T(8,128)(2,1)S(1)}, bf16[32,768]{1,0:T(8,128)(2,1)S(1)}, u32[]{:S(2)}, u32[]{:S(2)}) collective-permute-start(bf16[32,768]{1,0:T(8,128)(2,1)S(1)} %shard_map.111.pair_ref), channel_id=1, source_target_pairs={{0,16},{8,24},{16,0},{24,8},{1,17},{9,25},{17,1},{25,9},{2,18},{10... | collective-permute-start | bytes 147464 | tf_op jit(solution)/shard_map/ppermute | solution.py:22
  9.7 0.6 %shard_map.113.done_ref = f32[32,512]{1,0:T(8,128)S(1)} custom-call(bf16[32,768]{1,0:T(8,128)(2,1)S(1)} %shard_map.111.pair_ref, bf16[512,3072]{1,0:T(8,128)(2,1)S(1)} %get-tuple-element.27.called_first), custom_call_target="tpu_custom_call" | custom-call | flops 402653184 | bytes 1572864 | tf_op jit(solution)/shard_map/pallas_call | solution.py:390
  10.2 0.0 copy-done
  10.2 2.8 %shard_map.114 = (bf16[768,3072]{1,0:T(8,128)(2,1)S(1)}, bf16[256,3072]{1,0:T(8,128)(2,1)S(1)}, f32[40,768]{1,0:T(8,128)S(1)}) custom-call(bf16[32,768]{1,0:T(8,128)(2,1)S(1)} %shard_map.111.pair_ref, bf16[512,3072]{1,0:T(8,128)(2,1)S(1)} %get-tuple-element.27.called_first, f32[32,512]{1,0:T(8,128)S(1)} %shard_map.113.done_ref, s32[768,3072]{1,0:T(8,128)S(1)} %copy-done, ...), custom_call_target="tpu_custom_call" | custom-call | flops 1207959552 | bytes 9437184 | tf_op jit(solution)/shard_map/pallas_call | solution.py:390
  13.1 0.0 copy-start.1
  13.1 0.0 copy-start.3
  13.1 0.0 copy-start.5
  13.1 1.5 %shard_map.115.own_ref = f32[40,896]{1,0:T(8,128)S(1)} custom-call(bf16[32,768]{1,0:T(8,128)(2,1)S(1)} %collective-permute-done.1.pair_ref, bf16[768,3072]{1,0:T(8,128)(2,1)S(1)} %get-tuple-element.28.coded_ref, bf16[512,3072]{1,0:T(8,128)(2,1)S(1)} %get-tuple-element.27.called_first, bf16[256,3072]{1,0:T(8,128)(2,1)S(1)} %get-tuple-element.29.called_ref, ...), custom_call_target="tpu_custom_call" | custom-call | flops 1207959552 | bytes 4718592 | tf_op jit(solution)/shard_map/pallas_call | solution.py:390
  14.6 0.1 collective-permute-start.2
  14.7 1.4 %collective-permute-done.2.other_ref = f32[40,896]{1,0:T(8,128)S(1)} collective-permute-done((f32[40,896]{1,0:T(8,128)S(1)}, f32[40,896]{1,0:T(8,128)S(1)}, u32[]{:S(2)}, u32[]{:S(2)}) %collective-permute-start.2) | collective-permute-done | bytes 143392 | tf_op jit(solution)/shard_map/ppermute | solution.py:22
  16.1 2.3 %collective-permute-start.3 = (bf16[32,896]{1,0:T(8,128)(2,1)S(1)}, bf16[32,896]{1,0:T(8,128)(2,1)S(1)}, u32[]{:S(2)}, u32[]{:S(2)}) collective-permute-start(bf16[32,896]{1,0:T(8,128)(2,1)S(1)} %get-tuple-element.33), channel_id=1, source_target_pairs={{0,7},{1,6},{2,5},{3,4},{4,3},{5,2},{6,1},{7,0},{8,15},{9,14},{10,... | collective-permute-start | bytes 172040 | tf_op jit(solution)/shard_map/ppermute | solution.py:22
  18.4 0.5 %collective-permute-start.4 = (bf16[32,896]{1,0:T(8,128)(2,1)S(1)}, bf16[32,896]{1,0:T(8,128)(2,1)S(1)}, u32[]{:S(2)}, u32[]{:S(2)}) collective-permute-start(bf16[32,896]{1,0:T(8,128)(2,1)S(1)} %get-tuple-element.34), channel_id=1, source_target_pairs={{0,5},{1,4},{2,7},{3,6},{4,1},{5,0},{6,3},{7,2},{8,13},{9,12},{10,... | collective-permute-start | bytes 172040 | tf_op jit(solution)/shard_map/ppermute | solution.py:22
  18.8 0.3 collective-permute-start.5
  19.1 0.6 %shard_map.118.cross_ref = f32[40,1024]{1,0:T(8,128)S(1)} custom-call(s32[1,768]{1,0:T(1,128)S(1)} %copy-done.5, f32[16,768]{1,0:T(8,128)S(1)} %bitcast.16, f32[16,768]{1,0:T(8,128)S(1)} %bitcast.11, s32[768,1024]{1,0:T(8,128)S(1)} %copy-done.1, f32[40,896]{1,0:T(8,128)S(1)} %get-tuple-element.32.total_ref.after_ref), custom_call_target="tpu_custom_call" | custom-call | flops 220200960 | bytes 3145728 | tf_op jit(solution)/shard_map/pallas_call | solution.py:390
  19.8 0.4 collective-permute-start.6
  20.2 0.8 %collective-permute-done.3.rest_0_ = bf16[32,896]{1,0:T(8,128)(2,1)S(1)} collective-permute-done((bf16[32,896]{1,0:T(8,128)(2,1)S(1)}, bf16[32,896]{1,0:T(8,128)(2,1)S(1)}, u32[]{:S(2)}, u32[]{:S(2)}) %collective-permute-start.3) | collective-permute-done | bytes 57376 | tf_op jit(solution)/shard_map/ppermute | solution.py:22
  20.9 1.2 %collective-permute-done.4.rest_1_ = bf16[32,896]{1,0:T(8,128)(2,1)S(1)} collective-permute-done((bf16[32,896]{1,0:T(8,128)(2,1)S(1)}, bf16[32,896]{1,0:T(8,128)(2,1)S(1)}, u32[]{:S(2)}, u32[]{:S(2)}) %collective-permute-start.4) | collective-permute-done | bytes 57376 | tf_op jit(solution)/shard_map/ppermute | solution.py:22
  22.1 0.6 %collective-permute-done.5.rest_2_ = bf16[32,896]{1,0:T(8,128)(2,1)S(1)} collective-permute-done((bf16[32,896]{1,0:T(8,128)(2,1)S(1)}, bf16[32,896]{1,0:T(8,128)(2,1)S(1)}, u32[]{:S(2)}, u32[]{:S(2)}) %collective-permute-start.5) | collective-permute-done | bytes 57376 | tf_op jit(solution)/shard_map/ppermute | solution.py:22
  22.7 1.1 %shard_map.117 = (bf16[32,768]{1,0:T(8,128)(2,1)S(1)}, f32[8,128]{1,0:T(8,128)S(1)}, bf16[16,896]{1,0:T(8,128)(2,1)S(1)}, bf16[16,896]{1,0:T(8,128)(2,1)S(1)}, bf16[16,896]{1,0:T(8,128)(2,1)S(1)}) custom-call(f32[40,896]{1,0:T(8,128)S(1)} %get-tuple-element.32.total_ref.after_ref, bf16[768,3072]{1,0:T(8,128)(2,1)S(1)} %get-tuple-element.28.coded_ref, ...), custom_call_target="tpu_custom_call" | custom-call | flops 1207959552 | bytes 4718592 | tf_op jit(solution)/shard_map/pallas_call | solution.py:390
  23.8 2.0 %collective-permute-start.7 = (bf16[16,896]{1,0:T(8,128)(2,1)S(1)}, bf16[16,896]{1,0:T(8,128)(2,1)S(1)}, u32[]{:S(2)}, u32[]{:S(2)}) collective-permute-start(bf16[16,896]{1,0:T(8,128)(2,1)S(1)} %get-tuple-element.39), channel_id=1, source_target_pairs={{0,24},{8,16},{16,8},{24,0},{1,25},{9,17},{17,9},{25,1},{2,26},{10... | collective-permute-start | bytes 86024 | tf_op jit(solution)/shard_map/ppermute | solution.py:22
  25.9 0.5 %collective-permute-start.8 = (bf16[16,896]{1,0:T(8,128)(2,1)S(1)}, bf16[16,896]{1,0:T(8,128)(2,1)S(1)}, u32[]{:S(2)}, u32[]{:S(2)}) collective-permute-start(bf16[16,896]{1,0:T(8,128)(2,1)S(1)} %get-tuple-element.40), channel_id=1, source_target_pairs={{0,16},{8,24},{16,0},{24,8},{1,17},{9,25},{17,1},{25,9},{2,18},{10... | collective-permute-start | bytes 86024 | tf_op jit(solution)/shard_map/ppermute | solution.py:22
  26.3 1.9 %collective-permute-start.9 = (bf16[16,896]{1,0:T(8,128)(2,1)S(1)}, bf16[16,896]{1,0:T(8,128)(2,1)S(1)}, u32[]{:S(2)}, u32[]{:S(2)}) collective-permute-start(bf16[16,896]{1,0:T(8,128)(2,1)S(1)} %get-tuple-element.41), channel_id=1, source_target_pairs={{0,8},{8,0},{16,24},{24,16},{1,9},{9,1},{17,25},{25,17},{2,10},{10... | collective-permute-start | bytes 86024 | tf_op jit(solution)/shard_map/ppermute | solution.py:22
  28.2 0.4 %shard_map.119 = (f32[16,896]{1,0:T(8,128)S(1)}, f32[40,1024]{1,0:T(8,128)S(1)}) custom-call(bf16[32,768]{1,0:T(8,128)(2,1)S(1)} %get-tuple-element.36.scaled_ref, f32[8,128]{1,0:T(8,128)S(1)} %get-tuple-element.37.sums_ref, bf16[768,3072]{1,0:T(8,128)(2,1)S(1)} %get-tuple-element.28.coded_ref, bf16[512,3072]{1,0:T(8,128)(2,1)S(1)} %get-tuple-element.27.called_first, ...), custom_call_target="tpu_custom_call" | custom-call | flops 603979776 | bytes 2359296 | tf_op jit(solution)/shard_map/pallas_call | solution.py:390
  28.7 0.9 %collective-permute-done.7.rest_1_ = bf16[16,896]{1,0:T(8,128)(2,1)S(1)} collective-permute-done((bf16[16,896]{1,0:T(8,128)(2,1)S(1)}, bf16[16,896]{1,0:T(8,128)(2,1)S(1)}, u32[]{:S(2)}, u32[]{:S(2)}) %collective-permute-start.7) | collective-permute-done | bytes 28704 | tf_op jit(solution)/shard_map/ppermute | solution.py:22
  29.5 1.1 %collective-permute-done.8.rest_2_ = bf16[16,896]{1,0:T(8,128)(2,1)S(1)} collective-permute-done((bf16[16,896]{1,0:T(8,128)(2,1)S(1)}, bf16[16,896]{1,0:T(8,128)(2,1)S(1)}, u32[]{:S(2)}, u32[]{:S(2)}) %collective-permute-start.8) | collective-permute-done | bytes 28704 | tf_op jit(solution)/shard_map/ppermute | solution.py:22
  30.6 0.9 %shard_map.121 = (f32[32,1,384]{2,1,0:T(1,128)}, f32[16,768]{1,0:T(8,128)S(1)}) custom-call(f32[1,16]{1,0:T(1,128)S(1)} %bitcast.21, f32[16,768]{1,0:T(8,128)S(1)} %bitcast.12, f32[16,768]{1,0:T(8,128)S(1)} %bitcast.19, f32[40,1024]{1,0:T(8,128)S(1)} %get-tuple-element.44.both_ref, f32[16,896]{1,0:T(8,128)S(1)} %get-tuple-element.38.rest_0_, ...), custom_call_target="tpu_custom_call" | custom-call | bytes 49152 | tf_op jit(solution)/shard_map/pallas_call | solution.py:390
  31.5 3.3 %all-to-all-start = ((f32[32,1,384]{2,1,0:T(1,128)}), f32[32,1,384]{2,1,0:T(1,128)S(1)}, u32[]{:S(2)}, u32[]{:S(2)}) async-start(f32[32,1,384]{2,1,0:T(1,128)} %get-tuple-element.45), calls=%async_computation | async-start | bytes 98304 | tf_op jit(solution)/shard_map/all_to_all | solution.py:519
  34.9 0.7 %shard_map.120 = (f32[16,768]{1,0:T(8,128)}, f32[16,768]{1,0:T(8,128)}, f32[16,128]{1,0:T(8,128)S(1)}) custom-call(f32[1,16]{1,0:T(1,128)S(1)} %bitcast.22, f32[16,768]{1,0:T(8,128)S(1)} %bitcast.13, f32[16,768]{1,0:T(8,128)S(1)} %bitcast.20, f32[16,768]{1,0:T(8,128)S(1)} %bitcast.17, f32[16,896]{1,0:T(8,128)S(1)} %get-tuple-element.38.rest_0_, ...), custom_call_target="tpu_custom_call" | custom-call | bytes 1048576 | tf_op jit(solution)/shard_map/pallas_call | solution.py:390
  35.6 6.6 %all-to-all-done.came_ref = f32[32,1,384]{2,1,0:T(1,128)S(1)} async-done(((f32[32,1,384]{2,1,0:T(1,128)}), f32[32,1,384]{2,1,0:T(1,128)S(1)}, u32[]{:S(2)}, u32[]{:S(2)}) %all-to-all-start) | async-done | bytes 49184 | tf_op jit(solution)/shard_map/all_to_all | solution.py:519
  42.2 0.8 %shard_map.122 = (f32[16,768]{1,0:T(8,128)}, f32[16,32]{1,0:T(8,128)}) custom-call(f32[32,1,384]{2,1,0:T(1,128)S(1)} %all-to-all-done.came_ref, f32[16,128]{1,0:T(8,128)S(1)} %get-tuple-element.46.stats_ref, f32[16,768]{1,0:T(8,128)S(1)} %get-tuple-element.47.res_ref, f32[16,768]{1,0:T(8,128)S(1)} %bitcast.14), custom_call_target="tpu_custom_call" | custom-call | tf_op jit(solution)/shard_map/pallas_call | solution.py:390
  (16 shorter events, 0.1 us)
Async XLA Ops:
  0.6 6.3 %collective-permute-start = (f32[16,768]{1,0:T(8,128)}, f32[16,768]{1,0:T(8,128)S(1)}, u32[]{:S(2)}, u32[]{:S(2)}) collective-permute-start(f32[16,768]{1,0:T(8,128)} %bitcast.8), channel_id=1, source_target_pairs={{0,8},{8,0},{16,24},{24,16},{1,9},{9,1},{17,25},{25,17},{2,10},{10... | collective-permute-start | bytes 147464 | tf_op jit(solution)/shard_map/ppermute | solution.py:22
  3.7 3.3 %copy-start.2 = (f32[768,16]{0,1:T(8,128)S(1)}, f32[768,16]{0,1:T(8,128)}, u32[]{:S(2)}) copy-start(f32[768,16]{0,1:T(8,128)} %param.15) | copy-start | bytes 147460
  3.7 6.5 %copy-start = (s32[768,3072]{1,0:T(8,128)S(1)}, s32[768,3072]{1,0:T(8,128)}, u32[]{:S(2)}) copy-start(s32[768,3072]{1,0:T(8,128)} %gen_ref.1) | copy-start | bytes 28311556
  7.0 6.1 %collective-permute-start.1 = (bf16[32,768]{1,0:T(8,128)(2,1)S(1)}, bf16[32,768]{1,0:T(8,128)(2,1)S(1)}, u32[]{:S(2)}, u32[]{:S(2)}) collective-permute-start(bf16[32,768]{1,0:T(8,128)(2,1)S(1)} %shard_map.111.pair_ref), channel_id=1, source_target_pairs={{0,16},{8,24},{16,0},{24,8},{1,17},{9,25},{17,1},{25,9},{2,18},{10... | collective-permute-start | bytes 147464 | tf_op jit(solution)/shard_map/ppermute | solution.py:22
  13.1 6.1 %copy-start.1 = (s32[768,1024]{1,0:T(8,128)S(1)}, s32[768,1024]{1,0:T(8,128)}, u32[]{:S(2)}) copy-start(s32[768,1024]{1,0:T(8,128)} %dose_ref.1) | copy-start | bytes 9437188
  13.1 6.1 %copy-start.3 = (f32[768,16]{0,1:T(8,128)S(1)}, f32[768,16]{0,1:T(8,128)}, u32[]{:S(2)}) copy-start(f32[768,16]{0,1:T(8,128)} %param.13) | copy-start | bytes 147460
  13.1 6.0 %copy-start.5 = (s32[1,768]{1,0:T(1,128)S(1)}, s32[1,768]{1,0:T(1,128)}, u32[]{:S(2)}) copy-start(s32[1,768]{1,0:T(1,128)} %order_ref.1) | copy-start | bytes 9220
  14.6 1.4 %collective-permute-start.2 = (f32[40,896]{1,0:T(8,128)S(1)}, f32[40,896]{1,0:T(8,128)S(1)}, u32[]{:S(2)}, u32[]{:S(2)}) collective-permute-start(f32[40,896]{1,0:T(8,128)S(1)} %shard_map.115.own_ref), channel_id=1, source_target_pairs={{0,1},{1,0},{2,3},{3,2},{4,5},{5,4},{6,7},{7,6},{8,9},{9,8},{10,11... | collective-permute-start | bytes 430088 | tf_op jit(solution)/shard_map/ppermute | solution.py:22
  16.1 4.9 %collective-permute-start.3 = (bf16[32,896]{1,0:T(8,128)(2,1)S(1)}, bf16[32,896]{1,0:T(8,128)(2,1)S(1)}, u32[]{:S(2)}, u32[]{:S(2)}) collective-permute-start(bf16[32,896]{1,0:T(8,128)(2,1)S(1)} %get-tuple-element.33), channel_id=1, source_target_pairs={{0,7},{1,6},{2,5},{3,4},{4,3},{5,2},{6,1},{7,0},{8,15},{9,14},{10,... | collective-permute-start | bytes 172040 | tf_op jit(solution)/shard_map/ppermute | solution.py:22
  18.4 3.8 %collective-permute-start.4 = (bf16[32,896]{1,0:T(8,128)(2,1)S(1)}, bf16[32,896]{1,0:T(8,128)(2,1)S(1)}, u32[]{:S(2)}, u32[]{:S(2)}) collective-permute-start(bf16[32,896]{1,0:T(8,128)(2,1)S(1)} %get-tuple-element.34), channel_id=1, source_target_pairs={{0,5},{1,4},{2,7},{3,6},{4,1},{5,0},{6,3},{7,2},{8,13},{9,12},{10,... | collective-permute-start | bytes 172040 | tf_op jit(solution)/shard_map/ppermute | solution.py:22
  18.8 3.9 %collective-permute-start.5 = (bf16[32,896]{1,0:T(8,128)(2,1)S(1)}, bf16[32,896]{1,0:T(8,128)(2,1)S(1)}, u32[]{:S(2)}, u32[]{:S(2)}) collective-permute-start(bf16[32,896]{1,0:T(8,128)(2,1)S(1)} %get-tuple-element.35), channel_id=1, source_target_pairs={{0,3},{1,2},{2,1},{3,0},{4,7},{5,6},{6,5},{7,4},{8,11},{9,10},{10,... | collective-permute-start | bytes 172040 | tf_op jit(solution)/shard_map/ppermute | solution.py:22
  19.8 8.5 %collective-permute-start.6 = (f32[40,1024]{1,0:T(8,128)S(1)}, f32[40,1024]{1,0:T(8,128)S(1)}, u32[]{:S(2)}, u32[]{:S(2)}) collective-permute-start(f32[40,1024]{1,0:T(8,128)S(1)} %shard_map.118.cross_ref), channel_id=1, source_target_pairs={{0,1},{1,0},{2,3},{3,2},{4,5},{5,4},{6,7},{7,6},{8,9},{9,8},{10,11... | collective-permute-start | bytes 491528 | tf_op jit(solution)/shard_map/ppermute | solution.py:22
  23.8 5.7 %collective-permute-start.7 = (bf16[16,896]{1,0:T(8,128)(2,1)S(1)}, bf16[16,896]{1,0:T(8,128)(2,1)S(1)}, u32[]{:S(2)}, u32[]{:S(2)}) collective-permute-start(bf16[16,896]{1,0:T(8,128)(2,1)S(1)} %get-tuple-element.39), channel_id=1, source_target_pairs={{0,24},{8,16},{16,8},{24,0},{1,25},{9,17},{17,9},{25,1},{2,26},{10... | collective-permute-start | bytes 86024 | tf_op jit(solution)/shard_map/ppermute | solution.py:22
  25.9 4.8 %collective-permute-start.8 = (bf16[16,896]{1,0:T(8,128)(2,1)S(1)}, bf16[16,896]{1,0:T(8,128)(2,1)S(1)}, u32[]{:S(2)}, u32[]{:S(2)}) collective-permute-start(bf16[16,896]{1,0:T(8,128)(2,1)S(1)} %get-tuple-element.40), channel_id=1, source_target_pairs={{0,16},{8,24},{16,0},{24,8},{1,17},{9,25},{17,1},{25,9},{2,18},{10... | collective-permute-start | bytes 86024 | tf_op jit(solution)/shard_map/ppermute | solution.py:22
  26.3 4.3 %collective-permute-start.9 = (bf16[16,896]{1,0:T(8,128)(2,1)S(1)}, bf16[16,896]{1,0:T(8,128)(2,1)S(1)}, u32[]{:S(2)}, u32[]{:S(2)}) collective-permute-start(bf16[16,896]{1,0:T(8,128)(2,1)S(1)} %get-tuple-element.41), channel_id=1, source_target_pairs={{0,8},{8,0},{16,24},{24,16},{1,9},{9,1},{17,25},{25,17},{2,10},{10... | collective-permute-start | bytes 86024 | tf_op jit(solution)/shard_map/ppermute | solution.py:22
  28.2 2.4 %copy-start.4 = (f32[768,16]{0,1:T(8,128)S(1)}, f32[768,16]{0,1:T(8,128)}, u32[]{:S(2)}) copy-start(f32[768,16]{0,1:T(8,128)} %param.14) | copy-start | bytes 147460
  28.2 2.4 %copy-start.6 = (f32[16]{0:T(128)S(1)}, f32[16]{0:T(128)}, u32[]{:S(2)}) copy-start(f32[16]{0:T(128)} %param.12) | copy-start | bytes 196
  31.5 10.7 %all-to-all-start = ((f32[32,1,384]{2,1,0:T(1,128)}), f32[32,1,384]{2,1,0:T(1,128)S(1)}, u32[]{:S(2)}, u32[]{:S(2)}) async-start(f32[32,1,384]{2,1,0:T(1,128)} %get-tuple-element.45), calls=%async_computation | async-start | bytes 98304 | tf_op jit(solution)/shard_map/all_to_all | solution.py:519
